TPU v7x, 32 devices: a whole 2x2x4 slice. The times are simulated.
32 devices in a mesh: groups: 2 (over y), dp: 4 (over z), mp: 2 (over x), sub: 2 (over core).
Axes of the slice: x: 2, y: 2, z: 4, core: 2. Of those that a mesh axis runs over, the one named last changes fastest.
Arguments:
- hidden: bfloat16 [4096, 14336], P(('groups', 'dp', 'sub'), 'mp'), parts along dimension 0, may hold values from -6 to 6
- out_grad: bfloat16 [4096, 4096], P(('groups', 'dp', 'sub'), 'mp'), parts along dimension 0, may hold values from -80 to 80
- lengths: int32 [64], P(('groups', 'dp', 'sub')), parts along dimension 0, may hold values from 16 to 64
- proj_in: bfloat16 [14336, 32], P('mp'), may hold values from -0.005859375 to 0.005859375
- proj_out: bfloat16 [4096, 32], P('mp'), may hold values from -0.09375 to 0.09375
- test_proj: bfloat16 [2048, 1024], P(('mp', 'sub')), may hold values from -6 to 6
Outputs:
- covariance: float32 [2048, 1024], P(('groups', 'dp', 'sub')), parts along dimension 0
- scores: float32 [64, 2048], P(('groups', 'dp', 'sub'), 'mp'), parts along dimension 0
There are 2 independent parts, one for each index of `groups`. A program takes and returns all parts, laid end to end along the dimension named above; an argument that names none is the same for every part. Nothing has to cross between parts.
All inputs are finite; a program needn't handle non-finite values.
Results may differ from a plain program's by a relative error of at most 0.004.
Values may be sent and summed in bfloat16 or wider, within the bound.
No kernel may reach another device: no remote copies, remote signals or barrier semaphores. Data moves between devices by JAX's collectives and lax.ppermute only.
A program may use at most 64 MiB of HBM per device.

v0:
```python
import functools

import jax
import jax.numpy as jnp
from jax import lax
from jax.experimental import pallas as pl
from jax.experimental.pallas import tpu as pltpu
from jax.sharding import PartitionSpec as P

SEQ = 64
DEPTH = 256
SENDS = ((6, 3, 7, 4, 0, 5, 2, 1), (0, 5, 2, 1, 6, 3, 4, 7))
CONTRACT_LAST = (((1,), (1,)), ((), ()))
CONTRACT_FIRST = (((0,), (0,)), ((), ()))


def chunk_of(width):
    return next(size for size in (1024, 512, 256, 128) if width % size == 0)


def tree_sum(terms):
    while len(terms) > 1:
        terms = [a + b for a, b in zip(terms[::2], terms[1::2])] + terms[len(terms) // 2 * 2:]
    return terms[0]


def project_kernel(scales, hidden, out_grad, proj_in, proj_out, out, hid, og, pin, pout, sems):
    k_in = pin.shape[0]
    sides = ((out_grad, proj_out, og, pout), (hidden, proj_in, hid, pin))

    def part_copy(which, n):
        src, _, dst, _ = sides[which]
        size = chunk_of(src.shape[1])
        lanes = pl.ds(n * size if isinstance(n, int) else pl.multiple_of(n * size, size), size)
        return pltpu.make_async_copy(src.at[:, lanes], dst.at[:, lanes], sems.at[which, 1 + n])

    def weight_copy(which):
        return pltpu.make_async_copy(sides[which][1], sides[which][3], sems.at[which, 0])

    counts = [side[0].shape[1] // chunk_of(side[0].shape[1]) for side in sides]
    for which in (0, 1):
        weight_copy(which).start()
        for n in range(counts[which]):
            part_copy(which, n).start()
    for which in (0, 1):
        _, _, dst, dst_w = sides[which]
        size = chunk_of(dst.shape[1])
        depth = min(size, DEPTH)
        weight_copy(which).wait()

        def step(n, total):
            part_copy(which, n).wait()
            terms = []
            for k in range(0, size, depth):
                lanes = pl.ds(pl.multiple_of(n * size + k, depth), depth)
                terms.append(lax.dot_general(dst_w[:, lanes], dst[:, lanes], CONTRACT_LAST,
                                             preferred_element_type=jnp.float32))
            return total + tree_sum(terms)

        zero = jnp.zeros((dst_w.shape[0], dst.shape[0]), jnp.float32)
        total = lax.fori_loop(0, counts[which], step, zero)
        if which == 0:
            out[k_in:] = total * scales[1]
        else:
            out[:k_in] = total * scales[0]


def project(hidden, out_grad, proj_in, proj_out, scales):
    rows, width = hidden.shape
    narrow = out_grad.shape[1]
    k_in, k_out = proj_in.shape[1], proj_out.shape[1]
    return pl.pallas_call(
        functools.partial(project_kernel, scales),
        out_shape=jax.ShapeDtypeStruct((k_in + k_out, rows), jnp.float32),
        in_specs=[pl.BlockSpec(memory_space=pltpu.HBM)] * 4,
        out_specs=pl.BlockSpec(memory_space=pltpu.VMEM),
        scratch_shapes=[
            pltpu.VMEM((rows, width), jnp.bfloat16),
            pltpu.VMEM((rows, narrow), jnp.bfloat16),
            pltpu.VMEM((k_in, width), jnp.bfloat16),
            pltpu.VMEM((k_out, narrow), jnp.bfloat16),
            pltpu.SemaphoreType.DMA((2, 1 + max(width // chunk_of(width), narrow // chunk_of(narrow)))),
        ],
        compiler_params=pltpu.CompilerParams(vmem_limit_bytes=24 << 20),
        cost_estimate=pl.CostEstimate(
            flops=2 * rows * (width * k_in + narrow * k_out),
            bytes_accessed=2 * rows * (width + narrow) + 2 * (width * k_in + narrow * k_out),
            transcendentals=0,
        ),
    )(*(pltpu.with_memory_space_constraint(x, pltpu.HBM) for x in (hidden, out_grad, proj_in.T, proj_out.T)))


def grads_kernel(k_in, scales, mask, *refs):
    *pieces, out = refs
    both = pieces[0][...]
    for piece in pieces[1:]:
        both = both + piece[...]
    rows = both.shape[1]
    act = both[:k_in] * (mask[...] * (1.0 / scales[0]))
    grad = both[k_in:] * (1.0 / scales[1])
    row = lax.broadcasted_iota(jnp.int32, (16, rows), 0)
    col = lax.broadcasted_iota(jnp.int32, (16, rows), 1)
    pick = jnp.where((col >= row * SEQ) & (col < (row + 1) * SEQ), 1.0, 0.0).astype(jnp.bfloat16)
    per = 8
    k_out = grad.shape[0]
    for at in range(0, k_in, per):
        rest = jnp.concatenate([act[i:i + 1] * grad for i in range(at, at + per)], axis=0)
        total = None
        for _ in range(3):
            high = rest.astype(jnp.bfloat16)
            rest = rest - high.astype(jnp.float32)
            part = lax.dot_general(pick, high, CONTRACT_LAST, preferred_element_type=jnp.float32)
            total = part if total is None else total + part
        out[:, at * k_out:(at + per) * k_out] = total[:out.shape[0]].astype(jnp.bfloat16)


def example_grads(mask, pieces, k_in, k_out, scales):
    vmem = pl.BlockSpec(memory_space=pltpu.VMEM)
    return pl.pallas_call(
        functools.partial(grads_kernel, k_in, scales),
        out_shape=jax.ShapeDtypeStruct((mask.shape[1] // SEQ, k_in * k_out), jnp.bfloat16),
        in_specs=[vmem] * (1 + len(pieces)),
        out_specs=vmem,
        compiler_params=pltpu.CompilerParams(vmem_limit_bytes=6 << 20),
        cost_estimate=pl.CostEstimate(flops=1 << 33, bytes_accessed=0, transcendentals=0),
    )(mask, *pieces)


def finish_kernel(examples, n_pieces, n_raw, *refs):
    pieces, raw = refs[:n_pieces], refs[n_pieces:n_pieces + n_raw]
    cov, scores = refs[n_pieces + n_raw:]
    own_rows = cov.shape[0]
    place = lax.axis_index(("dp", "sub"))
    every = jnp.concatenate([p[...] for p in pieces], axis=0)
    if own_rows % 128 == 0:
        at = pl.multiple_of(place * own_rows, own_rows)
        own = jnp.concatenate([p[:, pl.ds(at, own_rows)] for p in pieces], axis=0)
    else:
        at = pl.multiple_of((place * own_rows) // 128 * 128, 128)
        wider = jnp.concatenate([p[:, pl.ds(at, 128)] for p in pieces], axis=0)
        own = pltpu.roll(wider.astype(jnp.float32), at - place * own_rows + 128, 1)[:, :own_rows].astype(jnp.bfloat16)
    wide = every.astype(jnp.float32)
    factor = lax.rsqrt(jnp.sum(wide * wide) / examples + 1e-06)
    if n_raw == 2:
        near, far = raw[0][...], raw[1][...]
        first = lax.axis_index("sub") == 0
        half = near.shape[1]
        scores[:, :half] = jnp.where(first, near, far) * factor
        scores[:, half:] = jnp.where(first, far, near) * factor
    else:
        scores[...] = raw[0][...] * factor
    cov[...] = lax.dot_general(own, every, CONTRACT_FIRST, preferred_element_type=jnp.float32) * (1.0 / examples)


def finish(examples, own_rows, pieces, raw):
    flat = pieces[0].shape[1]
    vmem = pl.BlockSpec(memory_space=pltpu.VMEM)
    return pl.pallas_call(
        functools.partial(finish_kernel, examples, len(pieces), len(raw)),
        out_shape=(
            jax.ShapeDtypeStruct((own_rows, flat), jnp.float32),
            jax.ShapeDtypeStruct((raw[0].shape[0], sum(r.shape[1] for r in raw)), jnp.float32),
        ),
        in_specs=[vmem] * (len(pieces) + len(raw)),
        out_specs=(vmem, vmem),
        compiler_params=pltpu.CompilerParams(vmem_limit_bytes=8 << 20),
    )(*pieces, *raw)


def per_device(hidden, out_grad, lengths, proj_in, proj_out, test_proj):
    k_in, k_out = proj_in.shape[1], proj_out.shape[1]
    flat = k_in * k_out
    rows = hidden.shape[0]
    group = ("dp", "sub")
    sharers = lax.axis_size(group)
    examples = lengths.shape[0] * sharers
    n_sub = lax.axis_size("sub")

    paired = lax.axis_size("mp") == 2
    scales = (128.0, 4.0) if paired else (1.0, 1.0)
    both = project(hidden, out_grad, proj_in, proj_out, scales)
    if paired:
        sent = lax.optimization_barrier(both.astype(jnp.float16))
        came = lax.ppermute(sent, "mp", [(0, 1), (1, 0)])
        pieces = [sent.astype(jnp.float32), came.astype(jnp.float32)]
    else:
        pieces = [lax.psum(both, "mp")]
    lengths, _ = lax.optimization_barrier((lengths, both))
    slots = jnp.arange(SEQ, dtype=jnp.int32)
    mask = (slots[None, :] < lengths[:, None]).astype(jnp.float32).reshape(1, rows)
    grads = example_grads(mask, pieces, k_in, k_out, scales)

    if n_sub == 2 and lax.axis_size("dp") == 4:
        swap = [(i, i ^ 1) for i in range(sharers)]
        came = lax.ppermute(grads, group, swap)
        held = jnp.concatenate([grads, came], axis=0)
        place = lax.axis_index(group)
        fetched = []
        for targets in reversed(SENDS):
            block = lax.ppermute(held, group, list(enumerate(targets)))
            kept = sum(1 << i for i, target in enumerate(targets) if i != target)
            fetched.append(jnp.where(((kept >> place) & 1) == 1, block, 0))
        fetched = jnp.concatenate(fetched, axis=0)
        gathered = [held, fetched, lax.ppermute(fetched, group, swap)]
        near = jnp.einsum("ep,qp->eq", grads, test_proj, preferred_element_type=jnp.float32)
        for_other = jnp.einsum("ep,qp->eq", came, test_proj, preferred_element_type=jnp.float32)
        raw = [near, lax.ppermute(for_other, group, swap)]
    else:
        tests = lax.all_gather(test_proj, "sub", axis=0, tiled=True)
        raw = [jnp.einsum("ep,qp->eq", grads, tests, preferred_element_type=jnp.float32)]
        gathered = [lax.all_gather(grads, group, axis=0, tiled=True)]
    return finish(examples, flat // sharers, gathered, raw)


def solution(mesh):
    in_specs = (
        P(("groups", "dp", "sub"), "mp"),
        P(("groups", "dp", "sub"), "mp"),
        P(("groups", "dp", "sub")),
        P("mp", None),
        P("mp", None),
        P(("mp", "sub"), None),
    )
    out_specs = (P(("groups", "dp", "sub"), None), P(("groups", "dp", "sub"), "mp"))
    return jax.shard_map(
        per_device, mesh=mesh, in_specs=in_specs, out_specs=out_specs, check_vma=False
    )
```

profile of v0, /device:TPU:0, one launch (start us, length us, event | category | flops | bytes accessed | tf_op | source)
XLA Modules:
  0.0 21.6 jit_solution(12672861458993982663)
XLA Ops:
  0.6 0.0 copy-start
  0.6 0.0 copy-start.1
  0.7 3.8 %shard_map.77 = f32[64,256]{1,0:T(8,128)S(1)} custom-call(bf16[256,7168]{1,0:T(8,128)(2,1)} %hidden.1, bf16[256,2048]{1,0:T(8,128)(2,1)} %out_grad.1, bf16[32,7168]{1,0:T(8,128)(2,1)} %bitcast.6, bf16[32,2048]{1,0:T(8,128)(2,1)} %bitcast.7), custom_call_target="tpu_custom_call" | custom-call | flops 150994944 | bytes 5308416 | tf_op jit(solution)/shard_map/pallas_call | solution.py:72
  4.5 3.0 %collective-permute-start = (f16[64,256]{1,0:T(8,128)(2,1)S(1)}, f16[64,256]{1,0:T(8,128)(2,1)S(1)}, u32[]{:S(2)}, u32[]{:S(2)}) collective-permute-start(f16[64,256]{1,0:T(8,128)(2,1)S(1)} %convert_element_type.27), channel_id=1, source_target_pairs={{0,2},{2,0},{1,3},{3,1},{4,6},{6,4},{5,7},{7,5},{8,10},{10,8},{9,1... | collective-permute-start | bytes 98312 | tf_op jit(solution)/shard_map/ppermute | solution.py:184
  7.5 0.0 copy-done.1
  7.5 0.1 fusion
  7.5 0.1 reshape.33.mask
  7.6 1.7 %collective-permute-done = f16[64,256]{1,0:T(8,128)(2,1)S(1)} collective-permute-done((f16[64,256]{1,0:T(8,128)(2,1)S(1)}, f16[64,256]{1,0:T(8,128)(2,1)S(1)}, u32[]{:S(2)}, u32[]{:S(2)}) %collective-permute-start) | collective-permute-done | bytes 32800 | tf_op jit(solution)/shard_map/ppermute | solution.py:184
  9.4 0.6 %shard_map.78 = bf16[4,1024]{1,0:T(4,128)(2,1)S(1)} custom-call(f32[1,256]{1,0:T(1,128)S(1)} %reshape.33.mask, f32[64,256]{1,0:T(8,128)S(1)} %convert_element_type.28.refs_0_, f32[64,256]{1,0:T(8,128)S(1)} %convert_element_type.29.refs_1_), custom_call_target="tpu_custom_call" | custom-call | flops 8589934592 | tf_op jit(solution)/shard_map/pallas_call | solution.py:119
  9.9 0.0 collective-permute-start.1
  9.9 1.2 %collective-permute-done.1 = bf16[4,1024]{1,0:T(4,128)(2,1)S(1)} collective-permute-done((bf16[4,1024]{1,0:T(4,128)(2,1)S(1)}, bf16[4,1024]{1,0:T(4,128)(2,1)S(1)}, u32[]{:S(2)}, u32[]{:S(2)}) %collective-permute-start.1) | collective-permute-done | bytes 8224 | tf_op jit(solution)/shard_map/ppermute | solution.py:195
  11.1 6.0 %collective-permute-start.3 = (bf16[8,1024]{1,0:T(8,128)(2,1)S(1)}, bf16[8,1024]{1,0:T(8,128)(2,1)S(1)}, u32[]{:S(2)}, u32[]{:S(2)}) collective-permute-start(bf16[8,1024]{1,0:T(8,128)(2,1)S(1)} %pad_maximum_fusion.1.refs_0_), channel_id=1, source_target_pairs={{0,12},{1,5},{4,13},{5,8},{8,0},{9,9},{12,4},{13,1},{2,14},{3,7},{... | collective-permute-start | bytes 49160 | tf_op jit(solution)/shard_map/ppermute | solution.py:200
  17.2 0.7 %collective-permute-start.2 = (bf16[8,1024]{1,0:T(8,128)(2,1)S(1)}, bf16[8,1024]{1,0:T(8,128)(2,1)S(1)}, u32[]{:S(2)}, u32[]{:S(2)}) collective-permute-start(bf16[8,1024]{1,0:T(8,128)(2,1)S(1)} %pad_maximum_fusion.1.refs_0_), channel_id=1, source_target_pairs={{0,0},{1,9},{4,4},{5,1},{8,12},{9,5},{12,8},{13,13},{2,2},{3,11},{... | collective-permute-start | bytes 49160 | tf_op jit(solution)/shard_map/ppermute | solution.py:200
  17.8 0.0 copy-done
  17.9 0.4 %fusion.2 = f32[4,512]{1,0:T(4,128)S(1)} fusion(bf16[4,1024]{1,0:T(4,128)(2,1)S(1)} %collective-permute-done.1, bf16[512,1024]{1,0:T(8,128)(2,1)S(1)} %copy-done), kind=kOutput, calls=%fused_computation.7 | convolution fusion | flops 4194304 | bytes 1064960 | tf_op jit(solution)/shard_map/ep,qp->eq/dot_general | solution.py:206
  18.2 0.0 collective-permute-start.5
  18.2 0.4 %collective-permute-done.3 = bf16[8,1024]{1,0:T(8,128)(2,1)S(1)} collective-permute-done((bf16[8,1024]{1,0:T(8,128)(2,1)S(1)}, bf16[8,1024]{1,0:T(8,128)(2,1)S(1)}, u32[]{:S(2)}, u32[]{:S(2)}) %collective-permute-start.3) | collective-permute-done | bytes 16416 | tf_op jit(solution)/shard_map/ppermute | solution.py:200
  18.6 0.0 collective-permute-done.2
  18.6 1.0 %collective-permute-start.4 = (bf16[16,1024]{1,0:T(8,128)(2,1)S(1)}, bf16[16,1024]{1,0:T(8,128)(2,1)S(1)}, u32[]{:S(2)}, u32[]{:S(2)}) collective-permute-start(bf16[16,1024]{1,0:T(8,128)(2,1)S(1)} %pad_maximum_fusion.refs_1_), channel_id=1, source_target_pairs={{0,1},{1,0},{4,5},{5,4},{8,9},{9,8},{12,13},{13,12},{2,3},{3,2},{6... | collective-permute-start | bytes 98312 | tf_op jit(solution)/shard_map/ppermute | solution.py:204
  19.7 0.4 %fusion.1.refs_3_ = f32[4,512]{1,0:T(4,128)S(1)} fusion(bf16[4,1024]{1,0:T(4,128)(2,1)S(1)} %shard_map.78, bf16[512,1024]{1,0:T(8,128)(2,1)S(1)} %copy-done), kind=kOutput, calls=%fused_computation.6 | convolution fusion | flops 4194304 | bytes 1064960 | tf_op jit(solution)/shard_map/ep,qp->eq/dot_general | solution.py:205
  20.0 0.0 collective-permute-done.5.refs_4_
  20.1 0.5 %collective-permute-done.4.refs_2_ = bf16[16,1024]{1,0:T(8,128)(2,1)S(1)} collective-permute-done((bf16[16,1024]{1,0:T(8,128)(2,1)S(1)}, bf16[16,1024]{1,0:T(8,128)(2,1)S(1)}, u32[]{:S(2)}, u32[]{:S(2)}) %collective-permute-start.4) | collective-permute-done | bytes 32800 | tf_op jit(solution)/shard_map/ppermute | solution.py:204
  20.5 1.1 %shard_map.79 = (f32[128,1024]{1,0:T(8,128)}, f32[4,1024]{1,0:T(4,128)}) custom-call(bf16[8,1024]{1,0:T(8,128)(2,1)S(1)} %pad_maximum_fusion.1.refs_0_, bf16[16,1024]{1,0:T(8,128)(2,1)S(1)} %pad_maximum_fusion.refs_1_, bf16[16,1024]{1,0:T(8,128)(2,1)S(1)} %collective-permute-done.4.refs_2_, f32[4,512]{1,0:T(4,128)S(1)} %fusion.1.refs_3_, ...), custom_call_target="tpu_custom_call" | custom-call | tf_op jit(solution)/shard_map/pallas_call | solution.py:158
  (7 shorter events, 0.1 us)
Async XLA Ops:
  0.6 17.2 %copy-start = (bf16[512,1024]{1,0:T(8,128)(2,1)S(1)}, bf16[512,1024]{1,0:T(8,128)(2,1)}, u32[]{:S(2)}) copy-start(bf16[512,1024]{1,0:T(8,128)(2,1)} %param.11) | copy-start | bytes 3145732
  0.6 6.8 %copy-start.1 = (s32[4]{0:T(128)S(1)}, s32[4]{0:T(128)}, u32[]{:S(2)}) copy-start(s32[4]{0:T(128)} %param.8) | copy-start | bytes 52
  4.5 4.9 %collective-permute-start = (f16[64,256]{1,0:T(8,128)(2,1)S(1)}, f16[64,256]{1,0:T(8,128)(2,1)S(1)}, u32[]{:S(2)}, u32[]{:S(2)}) collective-permute-start(f16[64,256]{1,0:T(8,128)(2,1)S(1)} %convert_element_type.27), channel_id=1, source_target_pairs={{0,2},{2,0},{1,3},{3,1},{4,6},{6,4},{5,7},{7,5},{8,10},{10,8},{9,1... | collective-permute-start | bytes 98312 | tf_op jit(solution)/shard_map/ppermute | solution.py:184
  9.9 1.2 %collective-permute-start.1 = (bf16[4,1024]{1,0:T(4,128)(2,1)S(1)}, bf16[4,1024]{1,0:T(4,128)(2,1)S(1)}, u32[]{:S(2)}, u32[]{:S(2)}) collective-permute-start(bf16[4,1024]{1,0:T(4,128)(2,1)S(1)} %shard_map.78), channel_id=1, source_target_pairs={{0,1},{1,0},{4,5},{5,4},{8,9},{9,8},{12,13},{13,12},{2,3},{3,2},{6... | collective-permute-start | bytes 24584 | tf_op jit(solution)/shard_map/ppermute | solution.py:195
  11.1 7.5 %collective-permute-start.3 = (bf16[8,1024]{1,0:T(8,128)(2,1)S(1)}, bf16[8,1024]{1,0:T(8,128)(2,1)S(1)}, u32[]{:S(2)}, u32[]{:S(2)}) collective-permute-start(bf16[8,1024]{1,0:T(8,128)(2,1)S(1)} %pad_maximum_fusion.1.refs_0_), channel_id=1, source_target_pairs={{0,12},{1,5},{4,13},{5,8},{8,0},{9,9},{12,4},{13,1},{2,14},{3,7},{... | collective-permute-start | bytes 49160 | tf_op jit(solution)/shard_map/ppermute | solution.py:200
  17.2 1.4 %collective-permute-start.2 = (bf16[8,1024]{1,0:T(8,128)(2,1)S(1)}, bf16[8,1024]{1,0:T(8,128)(2,1)S(1)}, u32[]{:S(2)}, u32[]{:S(2)}) collective-permute-start(bf16[8,1024]{1,0:T(8,128)(2,1)S(1)} %pad_maximum_fusion.1.refs_0_), channel_id=1, source_target_pairs={{0,0},{1,9},{4,4},{5,1},{8,12},{9,5},{12,8},{13,13},{2,2},{3,11},{... | collective-permute-start | bytes 49160 | tf_op jit(solution)/shard_map/ppermute | solution.py:200
  18.2 1.8 %collective-permute-start.5 = (f32[4,512]{1,0:T(4,128)S(1)}, f32[4,512]{1,0:T(4,128)S(1)}, u32[]{:S(2)}, u32[]{:S(2)}) collective-permute-start(f32[4,512]{1,0:T(4,128)S(1)} %fusion.2), channel_id=1, source_target_pairs={{0,1},{1,0},{4,5},{5,4},{8,9},{9,8},{12,13},{13,12},{2,3},{3,2},{6... | collective-permute-start | bytes 24584 | tf_op jit(solution)/shard_map/ppermute | solution.py:207
  18.6 1.9 %collective-permute-start.4 = (bf16[16,1024]{1,0:T(8,128)(2,1)S(1)}, bf16[16,1024]{1,0:T(8,128)(2,1)S(1)}, u32[]{:S(2)}, u32[]{:S(2)}) collective-permute-start(bf16[16,1024]{1,0:T(8,128)(2,1)S(1)} %pad_maximum_fusion.refs_1_), channel_id=1, source_target_pairs={{0,1},{1,0},{4,5},{5,4},{8,9},{9,8},{12,13},{13,12},{2,3},{3,2},{6... | collective-permute-start | bytes 98312 | tf_op jit(solution)/shard_map/ppermute | solution.py:204
where the time goes:
time: 21.8 us; the launch traced here: 21.6 us
  starting transfers between devices  10.8 us (50%)
  Pallas kernels  5.41 us (25%)
  waiting for transfers between devices  3.78 us (17%)
  matrix products  0.74 us (3%)
  between operations  0.71 us (3%)
    ppermute x2, starting transfers between devices, per_device(): block = lax.ppermute(held, group, list(enumerate(targets)))  6.7 us
    pallas_call x1, Pallas kernels, project(): pl.pallas_call(functools.partial(project_kernel, scales), out_shape=jax.S...  3.78 us
    ppermute x1, starting transfers between devices, per_device(): came = lax.ppermute(sent, 'mp', [(0, 1), (1, 0)])  3 us
    ppermute x1, waiting for transfers between devices, per_device(): came = lax.ppermute(sent, 'mp', [(0, 1), (1, 0)])  1.73 us
    ppermute x1, waiting for transfers between devices, per_device(): came = lax.ppermute(grads, group, swap)  1.19 us
    pallas_call x1, Pallas kernels, finish(): pl.pallas_call(functools.partial(finish_kernel, examples, len(pieces), le...  1.07 us
    ppermute x1, starting transfers between devices, per_device(): gathered = [held, fetched, lax.ppermute(fetched, group, swap)]  1.05 us
    pallas_call x1, Pallas kernels, example_grads(): pl.pallas_call(functools.partial(grads_kernel, k_in, scales), out_shape=j...  0.57 us
  transfers between devices with their start and end apart: 6, of which 4 were waited for; matrix products, arithmetic and copies ran while one was open for 4% of the time, Pallas kernels for 0%

commit v1 on v0

--- a/solution.py
+++ b/solution.py
@@ -9,7 +9,7 @@
 
 SEQ = 64
 DEPTH = 256
-SENDS = ((6, 3, 7, 4, 0, 5, 2, 1), (0, 5, 2, 1, 6, 3, 4, 7))
+SENDS = ((7, 2, 3, 5, 0, 4, 1, 6), (5, 0, 7, 1, 3, 6, 2, 4))
 CONTRACT_LAST = (((1,), (1,)), ((), ()))
 CONTRACT_FIRST = (((0,), (0,)), ((), ()))
 
@@ -167,6 +167,20 @@
     )(*pieces, *raw)
 
 
+def first_arrivals(sends):
+    seen = [{chip} for chip in range(len(sends[0]) // 2)]
+    flags = []
+    for targets in sends:
+        bits = 0
+        for node, target in enumerate(targets):
+            if node // 2 not in seen[target // 2]:
+                seen[target // 2].add(node // 2)
+                bits |= 1 << target
+        flags.append(bits)
+    assert all(len(chips) == len(seen) for chips in seen)
+    return flags
+
+
 def per_device(hidden, out_grad, lengths, proj_in, proj_out, test_proj):
     k_in, k_out = proj_in.shape[1], proj_out.shape[1]
     flat = k_in * k_out
@@ -195,11 +209,8 @@
         came = lax.ppermute(grads, group, swap)
         held = jnp.concatenate([grads, came], axis=0)
         place = lax.axis_index(group)
-        fetched = []
-        for targets in reversed(SENDS):
-            block = lax.ppermute(held, group, list(enumerate(targets)))
-            kept = sum(1 << i for i, target in enumerate(targets) if i != target)
-            fetched.append(jnp.where(((kept >> place) & 1) == 1, block, 0))
+        blocks = [lax.ppermute(held, group, list(enumerate(targets))) for targets in reversed(SENDS)][::-1]
+        fetched = [jnp.where(((kept >> place) & 1) == 1, b, 0) for b, kept in zip(blocks, first_arrivals(SENDS))]
         fetched = jnp.concatenate(fetched, axis=0)
         gathered = [held, fetched, lax.ppermute(fetched, group, swap)]
         near = jnp.einsum("ep,qp->eq", grads, test_proj, preferred_element_type=jnp.float32)

time: 21.8 us -> 21.2 us (0.972)
  starting transfers between devices: 10.8 us -> 7.73 us
  waiting for transfers between devices: 3.78 us -> 6.29 us
    ppermute x2, starting transfers between devices: 6.7 us -> 4.36 us  [per_device(): lax.ppermute(held, group, list(enumerate(targets)))]
    ppermute x2, waiting for transfers between devices: 0.37 us -> 2.55 us  [per_device(): lax.ppermute(held, group, list(enumerate(targets)))]
    ppermute x1, starting transfers between devices: 1.05 us -> 0.07 us  [per_device(): gathered = [held, fetched, lax.ppermute(fetched, group, swap)]]
    ppermute x1, waiting for transfers between devices: 0.49 us -> 0.82 us  [per_device(): gathered = [held, fetched, lax.ppermute(fetched, group, swap)]]
    ppermute x1, starting transfers between devices: 0.01 us -> 0.29 us  [per_device(): raw = [near, lax.ppermute(for_other, group, swap)]]
where the time goes in v1:
time: 21.2 us; the launch traced here: 21.1 us
  starting transfers between devices  7.73 us (36%)
  waiting for transfers between devices  6.29 us (30%)
  Pallas kernels  5.41 us (26%)
  matrix products  0.74 us (3%)
  between operations  0.69 us (3%)
    ppermute x2, starting transfers between devices, per_device(): lax.ppermute(held, group, list(enumerate(targets)))  4.36 us
    pallas_call x1, Pallas kernels, project(): pl.pallas_call(functools.partial(project_kernel, scales), out_shape=jax.S...  3.78 us
    ppermute x1, starting transfers between devices, per_device(): came = lax.ppermute(sent, 'mp', [(0, 1), (1, 0)])  3 us
    ppermute x2, waiting for transfers between devices, per_device(): lax.ppermute(held, group, list(enumerate(targets)))  2.55 us
    ppermute x1, waiting for transfers between devices, per_device(): came = lax.ppermute(sent, 'mp', [(0, 1), (1, 0)])  1.73 us
    ppermute x1, waiting for transfers between devices, per_device(): came = lax.ppermute(grads, group, swap)  1.19 us
    pallas_call x1, Pallas kernels, finish(): pl.pallas_call(functools.partial(finish_kernel, examples, len(pieces), le...  1.07 us
    ppermute x1, waiting for transfers between devices, per_device(): gathered = [held, fetched, lax.ppermute(fetched, group, swap)]  0.82 us
  transfers between devices with their start and end apart: 6, of which 4 were waited for; matrix products, arithmetic and copies ran while one was open for 4% of the time, Pallas kernels for 0%

profile of v1, /device:TPU:0, one launch (start us, length us, event | category | flops | bytes accessed | tf_op | source)
XLA Modules:
  0.0 21.1 jit_solution(4736807181145824675)
XLA Ops:
  0.6 0.0 copy-start
  0.6 0.0 copy-start.1
  0.7 3.8 %shard_map.77 = f32[64,256]{1,0:T(8,128)S(1)} custom-call(bf16[256,7168]{1,0:T(8,128)(2,1)} %hidden.1, bf16[256,2048]{1,0:T(8,128)(2,1)} %out_grad.1, bf16[32,7168]{1,0:T(8,128)(2,1)} %bitcast.6, bf16[32,2048]{1,0:T(8,128)(2,1)} %bitcast.7), custom_call_target="tpu_custom_call" | custom-call | flops 150994944 | bytes 5308416 | tf_op jit(solution)/shard_map/pallas_call | solution.py:72
  4.5 3.0 %collective-permute-start = (f16[64,256]{1,0:T(8,128)(2,1)S(1)}, f16[64,256]{1,0:T(8,128)(2,1)S(1)}, u32[]{:S(2)}, u32[]{:S(2)}) collective-permute-start(f16[64,256]{1,0:T(8,128)(2,1)S(1)} %convert_element_type.27), channel_id=1, source_target_pairs={{0,2},{2,0},{1,3},{3,1},{4,6},{6,4},{5,7},{7,5},{8,10},{10,8},{9,1... | collective-permute-start | bytes 98312 | tf_op jit(solution)/shard_map/ppermute | solution.py:198
  7.5 0.0 copy-done.1
  7.5 0.1 fusion
  7.5 0.1 reshape.33.mask
  7.6 1.7 %collective-permute-done = f16[64,256]{1,0:T(8,128)(2,1)S(1)} collective-permute-done((f16[64,256]{1,0:T(8,128)(2,1)S(1)}, f16[64,256]{1,0:T(8,128)(2,1)S(1)}, u32[]{:S(2)}, u32[]{:S(2)}) %collective-permute-start) | collective-permute-done | bytes 32800 | tf_op jit(solution)/shard_map/ppermute | solution.py:198
  9.4 0.6 %shard_map.78 = bf16[4,1024]{1,0:T(4,128)(2,1)S(1)} custom-call(f32[1,256]{1,0:T(1,128)S(1)} %reshape.33.mask, f32[64,256]{1,0:T(8,128)S(1)} %convert_element_type.28.refs_0_, f32[64,256]{1,0:T(8,128)S(1)} %convert_element_type.29.refs_1_), custom_call_target="tpu_custom_call" | custom-call | flops 8589934592 | tf_op jit(solution)/shard_map/pallas_call | solution.py:119
  9.9 0.0 collective-permute-start.1
  9.9 1.2 %collective-permute-done.1 = bf16[4,1024]{1,0:T(4,128)(2,1)S(1)} collective-permute-done((bf16[4,1024]{1,0:T(4,128)(2,1)S(1)}, bf16[4,1024]{1,0:T(4,128)(2,1)S(1)}, u32[]{:S(2)}, u32[]{:S(2)}) %collective-permute-start.1) | collective-permute-done | bytes 8224 | tf_op jit(solution)/shard_map/ppermute | solution.py:209
  11.1 3.0 %collective-permute-start.3 = (bf16[8,1024]{1,0:T(8,128)(2,1)S(1)}, bf16[8,1024]{1,0:T(8,128)(2,1)S(1)}, u32[]{:S(2)}, u32[]{:S(2)}) collective-permute-start(bf16[8,1024]{1,0:T(8,128)(2,1)S(1)} %pad_maximum_fusion.1.refs_0_), channel_id=1, source_target_pairs={{0,9},{1,0},{4,13},{5,1},{8,5},{9,12},{12,4},{13,8},{2,11},{3,2},{... | collective-permute-start | bytes 49160 | tf_op jit(solution)/shard_map/ppermute | solution.py:212
  14.1 1.4 %collective-permute-start.2 = (bf16[8,1024]{1,0:T(8,128)(2,1)S(1)}, bf16[8,1024]{1,0:T(8,128)(2,1)S(1)}, u32[]{:S(2)}, u32[]{:S(2)}) collective-permute-start(bf16[8,1024]{1,0:T(8,128)(2,1)S(1)} %pad_maximum_fusion.1.refs_0_), channel_id=1, source_target_pairs={{0,13},{1,4},{4,5},{5,9},{8,0},{9,8},{12,1},{13,12},{2,15},{3,6},{... | collective-permute-start | bytes 49160 | tf_op jit(solution)/shard_map/ppermute | solution.py:212
  15.5 0.0 copy-done
  15.5 0.4 %fusion.2 = f32[4,512]{1,0:T(4,128)S(1)} fusion(bf16[4,1024]{1,0:T(4,128)(2,1)S(1)} %collective-permute-done.1, bf16[512,1024]{1,0:T(8,128)(2,1)S(1)} %copy-done), kind=kOutput, calls=%fused_computation.7 | convolution fusion | flops 4194304 | bytes 1064960 | tf_op jit(solution)/shard_map/ep,qp->eq/dot_general | solution.py:217
  15.9 0.3 %collective-permute-start.5 = (f32[4,512]{1,0:T(4,128)S(1)}, f32[4,512]{1,0:T(4,128)S(1)}, u32[]{:S(2)}, u32[]{:S(2)}) collective-permute-start(f32[4,512]{1,0:T(4,128)S(1)} %fusion.2), channel_id=1, source_target_pairs={{0,1},{1,0},{4,5},{5,4},{8,9},{9,8},{12,13},{13,12},{2,3},{3,2},{6... | collective-permute-start | bytes 24584 | tf_op jit(solution)/shard_map/ppermute | solution.py:218
  16.2 0.0 collective-permute-done.3
  16.2 2.6 %collective-permute-done.2 = bf16[8,1024]{1,0:T(8,128)(2,1)S(1)} collective-permute-done((bf16[8,1024]{1,0:T(8,128)(2,1)S(1)}, bf16[8,1024]{1,0:T(8,128)(2,1)S(1)}, u32[]{:S(2)}, u32[]{:S(2)}) %collective-permute-start.2) | collective-permute-done | bytes 16416 | tf_op jit(solution)/shard_map/ppermute | solution.py:212
  18.7 0.1 collective-permute-start.4
  18.8 0.4 %fusion.1.refs_3_ = f32[4,512]{1,0:T(4,128)S(1)} fusion(bf16[4,1024]{1,0:T(4,128)(2,1)S(1)} %shard_map.78, bf16[512,1024]{1,0:T(8,128)(2,1)S(1)} %copy-done), kind=kOutput, calls=%fused_computation.6 | convolution fusion | flops 4194304 | bytes 1064960 | tf_op jit(solution)/shard_map/ep,qp->eq/dot_general | solution.py:216
  19.2 0.0 collective-permute-done.5.refs_4_
  19.2 0.8 %collective-permute-done.4.refs_2_ = bf16[16,1024]{1,0:T(8,128)(2,1)S(1)} collective-permute-done((bf16[16,1024]{1,0:T(8,128)(2,1)S(1)}, bf16[16,1024]{1,0:T(8,128)(2,1)S(1)}, u32[]{:S(2)}, u32[]{:S(2)}) %collective-permute-start.4) | collective-permute-done | bytes 32800 | tf_op jit(solution)/shard_map/ppermute | solution.py:215
  20.0 1.1 %shard_map.79 = (f32[128,1024]{1,0:T(8,128)}, f32[4,1024]{1,0:T(4,128)}) custom-call(bf16[8,1024]{1,0:T(8,128)(2,1)S(1)} %pad_maximum_fusion.1.refs_0_, bf16[16,1024]{1,0:T(8,128)(2,1)S(1)} %pad_maximum_fusion.refs_1_, bf16[16,1024]{1,0:T(8,128)(2,1)S(1)} %collective-permute-done.4.refs_2_, f32[4,512]{1,0:T(4,128)S(1)} %fusion.1.refs_3_, ...), custom_call_target="tpu_custom_call" | custom-call | tf_op jit(solution)/shard_map/pallas_call | solution.py:158
  (7 shorter events, 0.1 us)
Async XLA Ops:
  0.6 14.9 %copy-start = (bf16[512,1024]{1,0:T(8,128)(2,1)S(1)}, bf16[512,1024]{1,0:T(8,128)(2,1)}, u32[]{:S(2)}) copy-start(bf16[512,1024]{1,0:T(8,128)(2,1)} %param.11) | copy-start | bytes 3145732
  0.6 6.8 %copy-start.1 = (s32[4]{0:T(128)S(1)}, s32[4]{0:T(128)}, u32[]{:S(2)}) copy-start(s32[4]{0:T(128)} %param.8) | copy-start | bytes 52
  4.5 4.9 %collective-permute-start = (f16[64,256]{1,0:T(8,128)(2,1)S(1)}, f16[64,256]{1,0:T(8,128)(2,1)S(1)}, u32[]{:S(2)}, u32[]{:S(2)}) collective-permute-start(f16[64,256]{1,0:T(8,128)(2,1)S(1)} %convert_element_type.27), channel_id=1, source_target_pairs={{0,2},{2,0},{1,3},{3,1},{4,6},{6,4},{5,7},{7,5},{8,10},{10,8},{9,1... | collective-permute-start | bytes 98312 | tf_op jit(solution)/shard_map/ppermute | solution.py:198
  9.9 1.2 %collective-permute-start.1 = (bf16[4,1024]{1,0:T(4,128)(2,1)S(1)}, bf16[4,1024]{1,0:T(4,128)(2,1)S(1)}, u32[]{:S(2)}, u32[]{:S(2)}) collective-permute-start(bf16[4,1024]{1,0:T(4,128)(2,1)S(1)} %shard_map.78), channel_id=1, source_target_pairs={{0,1},{1,0},{4,5},{5,4},{8,9},{9,8},{12,13},{13,12},{2,3},{3,2},{6... | collective-permute-start | bytes 24584 | tf_op jit(solution)/shard_map/ppermute | solution.py:209
  11.1 5.0 %collective-permute-start.3 = (bf16[8,1024]{1,0:T(8,128)(2,1)S(1)}, bf16[8,1024]{1,0:T(8,128)(2,1)S(1)}, u32[]{:S(2)}, u32[]{:S(2)}) collective-permute-start(bf16[8,1024]{1,0:T(8,128)(2,1)S(1)} %pad_maximum_fusion.1.refs_0_), channel_id=1, source_target_pairs={{0,9},{1,0},{4,13},{5,1},{8,5},{9,12},{12,4},{13,8},{2,11},{3,2},{... | collective-permute-start | bytes 49160 | tf_op jit(solution)/shard_map/ppermute | solution.py:212
  14.1 4.6 %collective-permute-start.2 = (bf16[8,1024]{1,0:T(8,128)(2,1)S(1)}, bf16[8,1024]{1,0:T(8,128)(2,1)S(1)}, u32[]{:S(2)}, u32[]{:S(2)}) collective-permute-start(bf16[8,1024]{1,0:T(8,128)(2,1)S(1)} %pad_maximum_fusion.1.refs_0_), channel_id=1, source_target_pairs={{0,13},{1,4},{4,5},{5,9},{8,0},{9,8},{12,1},{13,12},{2,15},{3,6},{... | collective-permute-start | bytes 49160 | tf_op jit(solution)/shard_map/ppermute | solution.py:212
  15.9 3.3 %collective-permute-start.5 = (f32[4,512]{1,0:T(4,128)S(1)}, f32[4,512]{1,0:T(4,128)S(1)}, u32[]{:S(2)}, u32[]{:S(2)}) collective-permute-start(f32[4,512]{1,0:T(4,128)S(1)} %fusion.2), channel_id=1, source_target_pairs={{0,1},{1,0},{4,5},{5,4},{8,9},{9,8},{12,13},{13,12},{2,3},{3,2},{6... | collective-permute-start | bytes 24584 | tf_op jit(solution)/shard_map/ppermute | solution.py:218
  18.7 1.3 %collective-permute-start.4 = (bf16[16,1024]{1,0:T(8,128)(2,1)S(1)}, bf16[16,1024]{1,0:T(8,128)(2,1)S(1)}, u32[]{:S(2)}, u32[]{:S(2)}) collective-permute-start(bf16[16,1024]{1,0:T(8,128)(2,1)S(1)} %pad_maximum_fusion.refs_1_), channel_id=1, source_target_pairs={{0,1},{1,0},{4,5},{5,4},{8,9},{9,8},{12,13},{13,12},{2,3},{3,2},{6... | collective-permute-start | bytes 98312 | tf_op jit(solution)/shard_map/ppermute | solution.py:215

commit v2 on v1

--- a/solution.py
+++ b/solution.py
@@ -209,8 +209,10 @@
         came = lax.ppermute(grads, group, swap)
         held = jnp.concatenate([grads, came], axis=0)
         place = lax.axis_index(group)
-        blocks = [lax.ppermute(held, group, list(enumerate(targets))) for targets in reversed(SENDS)][::-1]
-        fetched = [jnp.where(((kept >> place) & 1) == 1, b, 0) for b, kept in zip(blocks, first_arrivals(SENDS))]
+        fetched = []
+        for targets, kept in reversed(list(zip(SENDS, first_arrivals(SENDS)))):
+            block = lax.ppermute(held, group, list(enumerate(targets)))
+            fetched.append(jnp.where(((kept >> place) & 1) == 1, block, 0))
         fetched = jnp.concatenate(fetched, axis=0)
         gathered = [held, fetched, lax.ppermute(fetched, group, swap)]
         near = jnp.einsum("ep,qp->eq", grads, test_proj, preferred_element_type=jnp.float32)

time: 21.2 us -> 19.2 us (0.906)
  waiting for transfers between devices: 6.29 us -> 4.12 us
    ppermute x2, waiting for transfers between devices: 2.55 us -> 0.69 us  [per_device(): block = lax.ppermute(held, group, list(enumerate(targets)))]
    ppermute x2, starting transfers between devices: 4.36 us -> 3.96 us  [per_device(): block = lax.ppermute(held, group, list(enumerate(targets)))]
    ppermute x1, starting transfers between devices: 0.07 us -> 0.39 us  [per_device(): gathered = [held, fetched, lax.ppermute(fetched, group, swap)]]
    ppermute x1, waiting for transfers between devices: 0.82 us -> 0.51 us  [per_device(): gathered = [held, fetched, lax.ppermute(fetched, group, swap)]]
    ppermute x1, starting transfers between devices: 0.29 us -> 0.52 us  [per_device(): raw = [near, lax.ppermute(for_other, group, swap)]]
  transfers between devices with their start and end apart: 6 -> 6, of which waited for: 4 -> 5; matrix products, arithmetic and copies ran while one was open for 4% -> 5% of each run, Pallas kernels for 0% -> 0%
where the time goes in v2:
time: 19.2 us; the launch traced here: 19 us
  starting transfers between devices  7.87 us (41%)
  Pallas kernels  5.41 us (28%)
  waiting for transfers between devices  4.12 us (21%)
  matrix products  0.74 us (4%)
  between operations  0.68 us (4%)
    ppermute x2, starting transfers between devices, per_device(): block = lax.ppermute(held, group, list(enumerate(targets)))  3.96 us
    pallas_call x1, Pallas kernels, project(): pl.pallas_call(functools.partial(project_kernel, scales), out_shape=jax.S...  3.78 us
    ppermute x1, starting transfers between devices, per_device(): came = lax.ppermute(sent, 'mp', [(0, 1), (1, 0)])  3 us
    ppermute x1, waiting for transfers between devices, per_device(): came = lax.ppermute(sent, 'mp', [(0, 1), (1, 0)])  1.73 us
    ppermute x1, waiting for transfers between devices, per_device(): came = lax.ppermute(grads, group, swap)  1.19 us
    pallas_call x1, Pallas kernels, finish(): pl.pallas_call(functools.partial(finish_kernel, examples, len(pieces), le...  1.07 us
    ppermute x2, waiting for transfers between devices, per_device(): block = lax.ppermute(held, group, list(enumerate(targets)))  0.69 us
    pallas_call x1, Pallas kernels, example_grads(): pl.pallas_call(functools.partial(grads_kernel, k_in, scales), out_shape=j...  0.57 us
  transfers between devices with their start and end apart: 6, of which 5 were waited for; matrix products, arithmetic and copies ran while one was open for 5% of the time, Pallas kernels for 0%

profile of v2, /device:TPU:0, one launch (start us, length us, event | category | flops | bytes accessed | tf_op | source)
XLA Modules:
  0.0 19.0 jit_solution(8968528730393968685)
XLA Ops:
  0.6 0.0 copy-start
  0.6 0.0 copy-start.1
  0.7 3.8 %shard_map.77 = f32[64,256]{1,0:T(8,128)S(1)} custom-call(bf16[256,7168]{1,0:T(8,128)(2,1)} %hidden.1, bf16[256,2048]{1,0:T(8,128)(2,1)} %out_grad.1, bf16[32,7168]{1,0:T(8,128)(2,1)} %bitcast.6, bf16[32,2048]{1,0:T(8,128)(2,1)} %bitcast.7), custom_call_target="tpu_custom_call" | custom-call | flops 150994944 | bytes 5308416 | tf_op jit(solution)/shard_map/pallas_call | solution.py:72
  4.5 3.0 %collective-permute-start = (f16[64,256]{1,0:T(8,128)(2,1)S(1)}, f16[64,256]{1,0:T(8,128)(2,1)S(1)}, u32[]{:S(2)}, u32[]{:S(2)}) collective-permute-start(f16[64,256]{1,0:T(8,128)(2,1)S(1)} %convert_element_type.27), channel_id=1, source_target_pairs={{0,2},{2,0},{1,3},{3,1},{4,6},{6,4},{5,7},{7,5},{8,10},{10,8},{9,1... | collective-permute-start | bytes 98312 | tf_op jit(solution)/shard_map/ppermute | solution.py:198
  7.5 0.0 copy-done.1
  7.5 0.1 fusion
  7.5 0.1 reshape.33.mask
  7.6 1.7 %collective-permute-done = f16[64,256]{1,0:T(8,128)(2,1)S(1)} collective-permute-done((f16[64,256]{1,0:T(8,128)(2,1)S(1)}, f16[64,256]{1,0:T(8,128)(2,1)S(1)}, u32[]{:S(2)}, u32[]{:S(2)}) %collective-permute-start) | collective-permute-done | bytes 32800 | tf_op jit(solution)/shard_map/ppermute | solution.py:198
  9.4 0.6 %shard_map.78 = bf16[4,1024]{1,0:T(4,128)(2,1)S(1)} custom-call(f32[1,256]{1,0:T(1,128)S(1)} %reshape.33.mask, f32[64,256]{1,0:T(8,128)S(1)} %convert_element_type.28.refs_0_, f32[64,256]{1,0:T(8,128)S(1)} %convert_element_type.29.refs_1_), custom_call_target="tpu_custom_call" | custom-call | flops 8589934592 | tf_op jit(solution)/shard_map/pallas_call | solution.py:119
  9.9 0.0 collective-permute-start.1
  9.9 1.2 %collective-permute-done.1 = bf16[4,1024]{1,0:T(4,128)(2,1)S(1)} collective-permute-done((bf16[4,1024]{1,0:T(4,128)(2,1)S(1)}, bf16[4,1024]{1,0:T(4,128)(2,1)S(1)}, u32[]{:S(2)}, u32[]{:S(2)}) %collective-permute-start.1) | collective-permute-done | bytes 8224 | tf_op jit(solution)/shard_map/ppermute | solution.py:209
  11.1 4.0 %collective-permute-start.3 = (bf16[8,1024]{1,0:T(8,128)(2,1)S(1)}, bf16[8,1024]{1,0:T(8,128)(2,1)S(1)}, u32[]{:S(2)}, u32[]{:S(2)}) collective-permute-start(bf16[8,1024]{1,0:T(8,128)(2,1)S(1)} %pad_maximum_fusion.1.refs_0_), channel_id=1, source_target_pairs={{0,13},{1,4},{4,5},{5,9},{8,0},{9,8},{12,1},{13,12},{2,15},{3,6},{... | collective-permute-start | bytes 49160 | tf_op jit(solution)/shard_map/ppermute | solution.py:214
  15.1 0.0 collective-permute-start.2
  15.1 0.0 copy-done
  15.1 0.4 %fusion.2 = f32[4,512]{1,0:T(4,128)S(1)} fusion(bf16[4,1024]{1,0:T(4,128)(2,1)S(1)} %collective-permute-done.1, bf16[512,1024]{1,0:T(8,128)(2,1)S(1)} %copy-done), kind=kOutput, calls=%fused_computation.7 | convolution fusion | flops 4194304 | bytes 1064960 | tf_op jit(solution)/shard_map/ep,qp->eq/dot_general | solution.py:219
  15.5 0.5 %collective-permute-start.5 = (f32[4,512]{1,0:T(4,128)S(1)}, f32[4,512]{1,0:T(4,128)S(1)}, u32[]{:S(2)}, u32[]{:S(2)}) collective-permute-start(f32[4,512]{1,0:T(4,128)S(1)} %fusion.2), channel_id=1, source_target_pairs={{0,1},{1,0},{4,5},{5,4},{8,9},{9,8},{12,13},{13,12},{2,3},{3,2},{6... | collective-permute-start | bytes 24584 | tf_op jit(solution)/shard_map/ppermute | solution.py:220
  16.0 0.5 %collective-permute-done.3 = bf16[8,1024]{1,0:T(8,128)(2,1)S(1)} collective-permute-done((bf16[8,1024]{1,0:T(8,128)(2,1)S(1)}, bf16[8,1024]{1,0:T(8,128)(2,1)S(1)}, u32[]{:S(2)}, u32[]{:S(2)}) %collective-permute-start.3) | collective-permute-done | bytes 16416 | tf_op jit(solution)/shard_map/ppermute | solution.py:214
  16.5 0.1 collective-permute-done.2
  16.7 0.4 %collective-permute-start.4 = (bf16[16,1024]{1,0:T(8,128)(2,1)S(1)}, bf16[16,1024]{1,0:T(8,128)(2,1)S(1)}, u32[]{:S(2)}, u32[]{:S(2)}) collective-permute-start(bf16[16,1024]{1,0:T(8,128)(2,1)S(1)} %pad_maximum_fusion.refs_1_), channel_id=1, source_target_pairs={{0,1},{1,0},{4,5},{5,4},{8,9},{9,8},{12,13},{13,12},{2,3},{3,2},{6... | collective-permute-start | bytes 98312 | tf_op jit(solution)/shard_map/ppermute | solution.py:217
  17.1 0.4 %fusion.1.refs_3_ = f32[4,512]{1,0:T(4,128)S(1)} fusion(bf16[4,1024]{1,0:T(4,128)(2,1)S(1)} %shard_map.78, bf16[512,1024]{1,0:T(8,128)(2,1)S(1)} %copy-done), kind=kOutput, calls=%fused_computation.6 | convolution fusion | flops 4194304 | bytes 1064960 | tf_op jit(solution)/shard_map/ep,qp->eq/dot_general | solution.py:218
  17.5 0.0 collective-permute-done.5.refs_4_
  17.5 0.5 %collective-permute-done.4.refs_2_ = bf16[16,1024]{1,0:T(8,128)(2,1)S(1)} collective-permute-done((bf16[16,1024]{1,0:T(8,128)(2,1)S(1)}, bf16[16,1024]{1,0:T(8,128)(2,1)S(1)}, u32[]{:S(2)}, u32[]{:S(2)}) %collective-permute-start.4) | collective-permute-done | bytes 32800 | tf_op jit(solution)/shard_map/ppermute | solution.py:217
  18.0 1.1 %shard_map.79 = (f32[128,1024]{1,0:T(8,128)}, f32[4,1024]{1,0:T(4,128)}) custom-call(bf16[8,1024]{1,0:T(8,128)(2,1)S(1)} %pad_maximum_fusion.1.refs_0_, bf16[16,1024]{1,0:T(8,128)(2,1)S(1)} %pad_maximum_fusion.refs_1_, bf16[16,1024]{1,0:T(8,128)(2,1)S(1)} %collective-permute-done.4.refs_2_, f32[4,512]{1,0:T(4,128)S(1)} %fusion.1.refs_3_, ...), custom_call_target="tpu_custom_call" | custom-call | tf_op jit(solution)/shard_map/pallas_call | solution.py:158
  (7 shorter events, 0.1 us)
Async XLA Ops:
  0.6 14.5 %copy-start = (bf16[512,1024]{1,0:T(8,128)(2,1)S(1)}, bf16[512,1024]{1,0:T(8,128)(2,1)}, u32[]{:S(2)}) copy-start(bf16[512,1024]{1,0:T(8,128)(2,1)} %param.11) | copy-start | bytes 3145732
  0.6 6.8 %copy-start.1 = (s32[4]{0:T(128)S(1)}, s32[4]{0:T(128)}, u32[]{:S(2)}) copy-start(s32[4]{0:T(128)} %param.8) | copy-start | bytes 52
  4.5 4.9 %collective-permute-start = (f16[64,256]{1,0:T(8,128)(2,1)S(1)}, f16[64,256]{1,0:T(8,128)(2,1)S(1)}, u32[]{:S(2)}, u32[]{:S(2)}) collective-permute-start(f16[64,256]{1,0:T(8,128)(2,1)S(1)} %convert_element_type.27), channel_id=1, source_target_pairs={{0,2},{2,0},{1,3},{3,1},{4,6},{6,4},{5,7},{7,5},{8,10},{10,8},{9,1... | collective-permute-start | bytes 98312 | tf_op jit(solution)/shard_map/ppermute | solution.py:198
  9.9 1.2 %collective-permute-start.1 = (bf16[4,1024]{1,0:T(4,128)(2,1)S(1)}, bf16[4,1024]{1,0:T(4,128)(2,1)S(1)}, u32[]{:S(2)}, u32[]{:S(2)}) collective-permute-start(bf16[4,1024]{1,0:T(4,128)(2,1)S(1)} %shard_map.78), channel_id=1, source_target_pairs={{0,1},{1,0},{4,5},{5,4},{8,9},{9,8},{12,13},{13,12},{2,3},{3,2},{6... | collective-permute-start | bytes 24584 | tf_op jit(solution)/shard_map/ppermute | solution.py:209
  11.1 5.4 %collective-permute-start.3 = (bf16[8,1024]{1,0:T(8,128)(2,1)S(1)}, bf16[8,1024]{1,0:T(8,128)(2,1)S(1)}, u32[]{:S(2)}, u32[]{:S(2)}) collective-permute-start(bf16[8,1024]{1,0:T(8,128)(2,1)S(1)} %pad_maximum_fusion.1.refs_0_), channel_id=1, source_target_pairs={{0,13},{1,4},{4,5},{5,9},{8,0},{9,8},{12,1},{13,12},{2,15},{3,6},{... | collective-permute-start | bytes 49160 | tf_op jit(solution)/shard_map/ppermute | solution.py:214
  15.1 1.6 %collective-permute-start.2 = (bf16[8,1024]{1,0:T(8,128)(2,1)S(1)}, bf16[8,1024]{1,0:T(8,128)(2,1)S(1)}, u32[]{:S(2)}, u32[]{:S(2)}) collective-permute-start(bf16[8,1024]{1,0:T(8,128)(2,1)S(1)} %pad_maximum_fusion.1.refs_0_), channel_id=1, source_target_pairs={{0,9},{1,0},{4,13},{5,1},{8,5},{9,12},{12,4},{13,8},{2,11},{3,2},{... | collective-permute-start | bytes 49160 | tf_op jit(solution)/shard_map/ppermute | solution.py:214
  15.5 2.0 %collective-permute-start.5 = (f32[4,512]{1,0:T(4,128)S(1)}, f32[4,512]{1,0:T(4,128)S(1)}, u32[]{:S(2)}, u32[]{:S(2)}) collective-permute-start(f32[4,512]{1,0:T(4,128)S(1)} %fusion.2), channel_id=1, source_target_pairs={{0,1},{1,0},{4,5},{5,4},{8,9},{9,8},{12,13},{13,12},{2,3},{3,2},{6... | collective-permute-start | bytes 24584 | tf_op jit(solution)/shard_map/ppermute | solution.py:220
  16.7 1.3 %collective-permute-start.4 = (bf16[16,1024]{1,0:T(8,128)(2,1)S(1)}, bf16[16,1024]{1,0:T(8,128)(2,1)S(1)}, u32[]{:S(2)}, u32[]{:S(2)}) collective-permute-start(bf16[16,1024]{1,0:T(8,128)(2,1)S(1)} %pad_maximum_fusion.refs_1_), channel_id=1, source_target_pairs={{0,1},{1,0},{4,5},{5,4},{8,9},{9,8},{12,13},{13,12},{2,3},{3,2},{6... | collective-permute-start | bytes 98312 | tf_op jit(solution)/shard_map/ppermute | solution.py:217

commit v3 on v2

--- a/solution.py
+++ b/solution.py
@@ -14,72 +14,53 @@
 CONTRACT_FIRST = (((0,), (0,)), ((), ()))
 
 
-def chunk_of(width):
-    return next(size for size in (1024, 512, 256, 128) if width % size == 0)
-
-
-def tree_sum(terms):
-    while len(terms) > 1:
-        terms = [a + b for a, b in zip(terms[::2], terms[1::2])] + terms[len(terms) // 2 * 2:]
-    return terms[0]
-
-
-def project_kernel(scales, hidden, out_grad, proj_in, proj_out, out, hid, og, pin, pout, sems):
-    k_in = pin.shape[0]
-    sides = ((out_grad, proj_out, og, pout), (hidden, proj_in, hid, pin))
-
-    def part_copy(which, n):
-        src, _, dst, _ = sides[which]
-        size = chunk_of(src.shape[1])
-        lanes = pl.ds(n * size if isinstance(n, int) else pl.multiple_of(n * size, size), size)
-        return pltpu.make_async_copy(src.at[:, lanes], dst.at[:, lanes], sems.at[which, 1 + n])
-
-    def weight_copy(which):
-        return pltpu.make_async_copy(sides[which][1], sides[which][3], sems.at[which, 0])
-
-    counts = [side[0].shape[1] // chunk_of(side[0].shape[1]) for side in sides]
-    for which in (0, 1):
-        weight_copy(which).start()
-        for n in range(counts[which]):
-            part_copy(which, n).start()
-    for which in (0, 1):
-        _, _, dst, dst_w = sides[which]
-        size = chunk_of(dst.shape[1])
-        depth = min(size, DEPTH)
-        weight_copy(which).wait()
-
-        def step(n, total):
-            part_copy(which, n).wait()
-            terms = []
-            for k in range(0, size, depth):
-                lanes = pl.ds(pl.multiple_of(n * size + k, depth), depth)
-                terms.append(lax.dot_general(dst_w[:, lanes], dst[:, lanes], CONTRACT_LAST,
-                                             preferred_element_type=jnp.float32))
-            return total + tree_sum(terms)
-
-        zero = jnp.zeros((dst_w.shape[0], dst.shape[0]), jnp.float32)
-        total = lax.fori_loop(0, counts[which], step, zero)
-        if which == 0:
-            out[k_in:] = total * scales[1]
-        else:
-            out[:k_in] = total * scales[0]
+def project_kernel(scales, size, hidden, out_grad, proj_in, proj_out, out, data, weights, sums, sems):
+    narrow, width = out_grad.shape[1], hidden.shape[1]
+    before = narrow // size
+    first_weights = pltpu.make_async_copy(proj_out, weights.at[:, pl.ds(0, narrow)], sems.at[0])
+    other_weights = pltpu.make_async_copy(proj_in, weights.at[:, pl.ds(narrow, width)], sems.at[1])
+    first_weights.start()
+    for n in range(before + width // size):
+        src, at = (out_grad, n * size) if n < before else (hidden, n * size - narrow)
+        pltpu.make_async_copy(src.at[:, pl.ds(at, size)], data.at[:, pl.ds(n * size, size)], sems.at[2 + n]).start()
+        if n == 0:
+            other_weights.start()
+    sums[...] = jnp.zeros_like(sums)
+    first_weights.wait()
+
+    def step(n, carry):
+        @pl.when(n == before)
+        def _():
+            other_weights.wait()
+
+        lanes = pl.ds(pl.multiple_of(n * size, size), size)
+        pltpu.make_async_copy(hidden.at[:, pl.ds(0, size)], data.at[:, lanes], sems.at[2 + n]).wait()
+        which = (n < before).astype(jnp.int32)
+        sums[which] += lax.dot_general(data[:, lanes], weights[:, lanes], CONTRACT_LAST,
+                                       preferred_element_type=jnp.float32)
+        return carry
+
+    lax.fori_loop(0, before + width // size, step, 0)
+    k_in = proj_in.shape[0]
+    out[:k_in] = sums[0].T * scales[0]
+    out[k_in:] = sums[1].T * scales[1]
 
 
 def project(hidden, out_grad, proj_in, proj_out, scales):
     rows, width = hidden.shape
     narrow = out_grad.shape[1]
     k_in, k_out = proj_in.shape[1], proj_out.shape[1]
+    size = next(size for size in (1024, 512, 256, 128) if width % size == 0 and narrow % size == 0)
     return pl.pallas_call(
-        functools.partial(project_kernel, scales),
+        functools.partial(project_kernel, scales, size),
         out_shape=jax.ShapeDtypeStruct((k_in + k_out, rows), jnp.float32),
         in_specs=[pl.BlockSpec(memory_space=pltpu.HBM)] * 4,
         out_specs=pl.BlockSpec(memory_space=pltpu.VMEM),
         scratch_shapes=[
-            pltpu.VMEM((rows, width), jnp.bfloat16),
-            pltpu.VMEM((rows, narrow), jnp.bfloat16),
-            pltpu.VMEM((k_in, width), jnp.bfloat16),
-            pltpu.VMEM((k_out, narrow), jnp.bfloat16),
-            pltpu.SemaphoreType.DMA((2, 1 + max(width // chunk_of(width), narrow // chunk_of(narrow)))),
+            pltpu.VMEM((rows, narrow + width), jnp.bfloat16),
+            pltpu.VMEM((k_in, narrow + width), jnp.bfloat16),
+            pltpu.VMEM((2, rows, k_in), jnp.float32),
+            pltpu.SemaphoreType.DMA((2 + (narrow + width) // size,)),
         ],
         compiler_params=pltpu.CompilerParams(vmem_limit_bytes=24 << 20),
         cost_estimate=pl.CostEstimate(
@@ -106,7 +87,7 @@
     for at in range(0, k_in, per):
         rest = jnp.concatenate([act[i:i + 1] * grad for i in range(at, at + per)], axis=0)
         total = None
-        for _ in range(3):
+        for _ in range(2):
             high = rest.astype(jnp.bfloat16)
             rest = rest - high.astype(jnp.float32)
             part = lax.dot_general(pick, high, CONTRACT_LAST, preferred_element_type=jnp.float32)
@@ -128,8 +109,8 @@
 
 def finish_kernel(examples, n_pieces, n_raw, *refs):
     pieces, raw = refs[:n_pieces], refs[n_pieces:n_pieces + n_raw]
-    cov, scores = refs[n_pieces + n_raw:]
-    own_rows = cov.shape[0]
+    cov, scores, block, row, sems = refs[n_pieces + n_raw:]
+    own_rows, flat = cov.shape
     place = lax.axis_index(("dp", "sub"))
     every = jnp.concatenate([p[...] for p in pieces], axis=0)
     if own_rows % 128 == 0:
@@ -139,30 +120,41 @@
         at = pl.multiple_of((place * own_rows) // 128 * 128, 128)
         wider = jnp.concatenate([p[:, pl.ds(at, 128)] for p in pieces], axis=0)
         own = pltpu.roll(wider.astype(jnp.float32), at - place * own_rows + 128, 1)[:, :own_rows].astype(jnp.bfloat16)
+    copies = []
+    for n, at in enumerate(range(0, flat, flat // 4)):
+        lanes = pl.ds(at, flat // 4)
+        block[:, lanes] = lax.dot_general(own, every[:, at:at + flat // 4], CONTRACT_FIRST,
+                                          preferred_element_type=jnp.float32) * (1.0 / examples)
+        copies.append(pltpu.make_async_copy(block.at[:, lanes], cov.at[:, lanes], sems.at[n]))
+        copies[-1].start()
     wide = every.astype(jnp.float32)
     factor = lax.rsqrt(jnp.sum(wide * wide) / examples + 1e-06)
     if n_raw == 2:
         near, far = raw[0][...], raw[1][...]
         first = lax.axis_index("sub") == 0
         half = near.shape[1]
-        scores[:, :half] = jnp.where(first, near, far) * factor
-        scores[:, half:] = jnp.where(first, far, near) * factor
-    else:
-        scores[...] = raw[0][...] * factor
-    cov[...] = lax.dot_general(own, every, CONTRACT_FIRST, preferred_element_type=jnp.float32) * (1.0 / examples)
+        row[:, :half] = jnp.where(first, near, far) * factor
+        row[:, half:] = jnp.where(first, far, near) * factor
+    else:
+        row[...] = raw[0][...] * factor
+    copies.append(pltpu.make_async_copy(row, scores, sems.at[4]))
+    copies[-1].start()
+    for copy in copies:
+        copy.wait()
 
 
 def finish(examples, own_rows, pieces, raw):
     flat = pieces[0].shape[1]
     vmem = pl.BlockSpec(memory_space=pltpu.VMEM)
+    hbm = pl.BlockSpec(memory_space=pltpu.HBM)
+    cov = (own_rows, flat)
+    scores = (raw[0].shape[0], sum(r.shape[1] for r in raw))
     return pl.pallas_call(
         functools.partial(finish_kernel, examples, len(pieces), len(raw)),
-        out_shape=(
-            jax.ShapeDtypeStruct((own_rows, flat), jnp.float32),
-            jax.ShapeDtypeStruct((raw[0].shape[0], sum(r.shape[1] for r in raw)), jnp.float32),
-        ),
+        out_shape=(jax.ShapeDtypeStruct(cov, jnp.float32), jax.ShapeDtypeStruct(scores, jnp.float32)),
         in_specs=[vmem] * (len(pieces) + len(raw)),
-        out_specs=(vmem, vmem),
+        out_specs=(hbm, hbm),
+        scratch_shapes=[pltpu.VMEM(cov, jnp.float32), pltpu.VMEM(scores, jnp.float32), pltpu.SemaphoreType.DMA((5,))],
         compiler_params=pltpu.CompilerParams(vmem_limit_bytes=8 << 20),
     )(*pieces, *raw)
 

time: 19.2 us -> 19.1 us (level)
  no operation moved by 1% of the time
where the time goes in v3:
time: 19.1 us; the launch traced here: 19 us
  starting transfers between devices  7.9 us (41%)
  Pallas kernels  5.36 us (28%)
  waiting for transfers between devices  4.1 us (21%)
  matrix products  0.74 us (4%)
  between operations  0.68 us (4%)
    ppermute x2, starting transfers between devices, per_device(): block = lax.ppermute(held, group, list(enumerate(targets)))  3.95 us
    pallas_call x1, Pallas kernels, project(): pl.pallas_call(functools.partial(project_kernel, scales, size), out_shape...  3.88 us
    ppermute x1, starting transfers between devices, per_device(): came = lax.ppermute(sent, 'mp', [(0, 1), (1, 0)])  3 us
    ppermute x1, waiting for transfers between devices, per_device(): came = lax.ppermute(sent, 'mp', [(0, 1), (1, 0)])  1.73 us
    ppermute x1, waiting for transfers between devices, per_device(): came = lax.ppermute(grads, group, swap)  1.19 us
    pallas_call x1, Pallas kernels, finish(): pl.pallas_call(functools.partial(finish_kernel, examples, len(pieces), le...  1.06 us
    ppermute x2, waiting for transfers between devices, per_device(): block = lax.ppermute(held, group, list(enumerate(targets)))  0.69 us
    ppermute x1, starting transfers between devices, per_device(): raw = [near, lax.ppermute(for_other, group, swap)]  0.52 us
  transfers between devices with their start and end apart: 6, of which 5 were waited for; matrix products, arithmetic and copies ran while one was open for 5% of the time, Pallas kernels for 0%

profile of v3, /device:TPU:0, one launch (start us, length us, event | category | flops | bytes accessed | tf_op | source)
XLA Modules:
  0.0 19.0 jit_solution(18092261444110968118)
XLA Ops:
  0.6 0.0 copy-start
  0.6 0.0 copy-start.1
  0.7 3.9 %shard_map.77 = f32[64,256]{1,0:T(8,128)S(1)} custom-call(bf16[256,7168]{1,0:T(8,128)(2,1)} %hidden.1, bf16[256,2048]{1,0:T(8,128)(2,1)} %out_grad.1, bf16[32,7168]{1,0:T(8,128)(2,1)} %bitcast.6, bf16[32,2048]{1,0:T(8,128)(2,1)} %bitcast.7), custom_call_target="tpu_custom_call" | custom-call | flops 150994944 | bytes 5308416 | tf_op jit(solution)/shard_map/pallas_call | solution.py:54
  4.6 3.0 %collective-permute-start = (f16[64,256]{1,0:T(8,128)(2,1)S(1)}, f16[64,256]{1,0:T(8,128)(2,1)S(1)}, u32[]{:S(2)}, u32[]{:S(2)}) collective-permute-start(f16[64,256]{1,0:T(8,128)(2,1)S(1)} %convert_element_type.27), channel_id=1, source_target_pairs={{0,2},{2,0},{1,3},{3,1},{4,6},{6,4},{5,7},{7,5},{8,10},{10,8},{9,1... | collective-permute-start | bytes 98312 | tf_op jit(solution)/shard_map/ppermute | solution.py:190
  7.6 0.0 copy-done.1
  7.6 0.1 fusion
  7.6 0.1 reshape.33.mask
  7.7 1.7 %collective-permute-done = f16[64,256]{1,0:T(8,128)(2,1)S(1)} collective-permute-done((f16[64,256]{1,0:T(8,128)(2,1)S(1)}, f16[64,256]{1,0:T(8,128)(2,1)S(1)}, u32[]{:S(2)}, u32[]{:S(2)}) %collective-permute-start) | collective-permute-done | bytes 32800 | tf_op jit(solution)/shard_map/ppermute | solution.py:190
  9.5 0.4 %shard_map.78 = bf16[4,1024]{1,0:T(4,128)(2,1)S(1)} custom-call(f32[1,256]{1,0:T(1,128)S(1)} %reshape.33.mask, f32[64,256]{1,0:T(8,128)S(1)} %convert_element_type.28.refs_0_, f32[64,256]{1,0:T(8,128)S(1)} %convert_element_type.29.refs_1_), custom_call_target="tpu_custom_call" | custom-call | flops 8589934592 | tf_op jit(solution)/shard_map/pallas_call | solution.py:100
  9.9 0.0 collective-permute-start.1
  9.9 1.2 %collective-permute-done.1 = bf16[4,1024]{1,0:T(4,128)(2,1)S(1)} collective-permute-done((bf16[4,1024]{1,0:T(4,128)(2,1)S(1)}, bf16[4,1024]{1,0:T(4,128)(2,1)S(1)}, u32[]{:S(2)}, u32[]{:S(2)}) %collective-permute-start.1) | collective-permute-done | bytes 8224 | tf_op jit(solution)/shard_map/ppermute | solution.py:201
  11.1 3.9 %collective-permute-start.3 = (bf16[8,1024]{1,0:T(8,128)(2,1)S(1)}, bf16[8,1024]{1,0:T(8,128)(2,1)S(1)}, u32[]{:S(2)}, u32[]{:S(2)}) collective-permute-start(bf16[8,1024]{1,0:T(8,128)(2,1)S(1)} %pad_maximum_fusion.1.refs_0_), channel_id=1, source_target_pairs={{0,13},{1,4},{4,5},{5,9},{8,0},{9,8},{12,1},{13,12},{2,15},{3,6},{... | collective-permute-start | bytes 49160 | tf_op jit(solution)/shard_map/ppermute | solution.py:206
  15.0 0.0 collective-permute-start.2
  15.0 0.0 copy-done
  15.0 0.4 %fusion.2 = f32[4,512]{1,0:T(4,128)S(1)} fusion(bf16[4,1024]{1,0:T(4,128)(2,1)S(1)} %collective-permute-done.1, bf16[512,1024]{1,0:T(8,128)(2,1)S(1)} %copy-done), kind=kOutput, calls=%fused_computation.7 | convolution fusion | flops 4194304 | bytes 1064960 | tf_op jit(solution)/shard_map/ep,qp->eq/dot_general | solution.py:211
  15.4 0.5 %collective-permute-start.5 = (f32[4,512]{1,0:T(4,128)S(1)}, f32[4,512]{1,0:T(4,128)S(1)}, u32[]{:S(2)}, u32[]{:S(2)}) collective-permute-start(f32[4,512]{1,0:T(4,128)S(1)} %fusion.2), channel_id=1, source_target_pairs={{0,1},{1,0},{4,5},{5,4},{8,9},{9,8},{12,13},{13,12},{2,3},{3,2},{6... | collective-permute-start | bytes 24584 | tf_op jit(solution)/shard_map/ppermute | solution.py:212
  15.9 0.5 %collective-permute-done.3 = bf16[8,1024]{1,0:T(8,128)(2,1)S(1)} collective-permute-done((bf16[8,1024]{1,0:T(8,128)(2,1)S(1)}, bf16[8,1024]{1,0:T(8,128)(2,1)S(1)}, u32[]{:S(2)}, u32[]{:S(2)}) %collective-permute-start.3) | collective-permute-done | bytes 16416 | tf_op jit(solution)/shard_map/ppermute | solution.py:206
  16.5 0.1 collective-permute-done.2
  16.6 0.4 %collective-permute-start.4 = (bf16[16,1024]{1,0:T(8,128)(2,1)S(1)}, bf16[16,1024]{1,0:T(8,128)(2,1)S(1)}, u32[]{:S(2)}, u32[]{:S(2)}) collective-permute-start(bf16[16,1024]{1,0:T(8,128)(2,1)S(1)} %pad_maximum_fusion.refs_1_), channel_id=1, source_target_pairs={{0,1},{1,0},{4,5},{5,4},{8,9},{9,8},{12,13},{13,12},{2,3},{3,2},{6... | collective-permute-start | bytes 98312 | tf_op jit(solution)/shard_map/ppermute | solution.py:209
  17.1 0.4 %fusion.1.refs_3_ = f32[4,512]{1,0:T(4,128)S(1)} fusion(bf16[4,1024]{1,0:T(4,128)(2,1)S(1)} %shard_map.78, bf16[512,1024]{1,0:T(8,128)(2,1)S(1)} %copy-done), kind=kOutput, calls=%fused_computation.6 | convolution fusion | flops 4194304 | bytes 1064960 | tf_op jit(solution)/shard_map/ep,qp->eq/dot_general | solution.py:210
  17.4 0.0 collective-permute-done.5.refs_4_
  17.4 0.5 %collective-permute-done.4.refs_2_ = bf16[16,1024]{1,0:T(8,128)(2,1)S(1)} collective-permute-done((bf16[16,1024]{1,0:T(8,128)(2,1)S(1)}, bf16[16,1024]{1,0:T(8,128)(2,1)S(1)}, u32[]{:S(2)}, u32[]{:S(2)}) %collective-permute-start.4) | collective-permute-done | bytes 32800 | tf_op jit(solution)/shard_map/ppermute | solution.py:209
  17.9 1.1 %shard_map.79 = (f32[128,1024]{1,0:T(8,128)}, f32[4,1024]{1,0:T(4,128)}) custom-call(bf16[8,1024]{1,0:T(8,128)(2,1)S(1)} %pad_maximum_fusion.1.refs_0_, bf16[16,1024]{1,0:T(8,128)(2,1)S(1)} %pad_maximum_fusion.refs_1_, bf16[16,1024]{1,0:T(8,128)(2,1)S(1)} %collective-permute-done.4.refs_2_, f32[4,512]{1,0:T(4,128)S(1)} %fusion.1.refs_3_, ...), custom_call_target="tpu_custom_call" | custom-call | tf_op jit(solution)/shard_map/pallas_call | solution.py:152
  (7 shorter events, 0.1 us)
Async XLA Ops:
  0.6 14.4 %copy-start = (bf16[512,1024]{1,0:T(8,128)(2,1)S(1)}, bf16[512,1024]{1,0:T(8,128)(2,1)}, u32[]{:S(2)}) copy-start(bf16[512,1024]{1,0:T(8,128)(2,1)} %param.11) | copy-start | bytes 3145732
  0.6 6.9 %copy-start.1 = (s32[4]{0:T(128)S(1)}, s32[4]{0:T(128)}, u32[]{:S(2)}) copy-start(s32[4]{0:T(128)} %param.8) | copy-start | bytes 52
  4.6 4.9 %collective-permute-start = (f16[64,256]{1,0:T(8,128)(2,1)S(1)}, f16[64,256]{1,0:T(8,128)(2,1)S(1)}, u32[]{:S(2)}, u32[]{:S(2)}) collective-permute-start(f16[64,256]{1,0:T(8,128)(2,1)S(1)} %convert_element_type.27), channel_id=1, source_target_pairs={{0,2},{2,0},{1,3},{3,1},{4,6},{6,4},{5,7},{7,5},{8,10},{10,8},{9,1... | collective-permute-start | bytes 98312 | tf_op jit(solution)/shard_map/ppermute | solution.py:190
  9.9 1.2 %collective-permute-start.1 = (bf16[4,1024]{1,0:T(4,128)(2,1)S(1)}, bf16[4,1024]{1,0:T(4,128)(2,1)S(1)}, u32[]{:S(2)}, u32[]{:S(2)}) collective-permute-start(bf16[4,1024]{1,0:T(4,128)(2,1)S(1)} %shard_map.78), channel_id=1, source_target_pairs={{0,1},{1,0},{4,5},{5,4},{8,9},{9,8},{12,13},{13,12},{2,3},{3,2},{6... | collective-permute-start | bytes 24584 | tf_op jit(solution)/shard_map/ppermute | solution.py:201
  11.1 5.4 %collective-permute-start.3 = (bf16[8,1024]{1,0:T(8,128)(2,1)S(1)}, bf16[8,1024]{1,0:T(8,128)(2,1)S(1)}, u32[]{:S(2)}, u32[]{:S(2)}) collective-permute-start(bf16[8,1024]{1,0:T(8,128)(2,1)S(1)} %pad_maximum_fusion.1.refs_0_), channel_id=1, source_target_pairs={{0,13},{1,4},{4,5},{5,9},{8,0},{9,8},{12,1},{13,12},{2,15},{3,6},{... | collective-permute-start | bytes 49160 | tf_op jit(solution)/shard_map/ppermute | solution.py:206
  15.0 1.6 %collective-permute-start.2 = (bf16[8,1024]{1,0:T(8,128)(2,1)S(1)}, bf16[8,1024]{1,0:T(8,128)(2,1)S(1)}, u32[]{:S(2)}, u32[]{:S(2)}) collective-permute-start(bf16[8,1024]{1,0:T(8,128)(2,1)S(1)} %pad_maximum_fusion.1.refs_0_), channel_id=1, source_target_pairs={{0,9},{1,0},{4,13},{5,1},{8,5},{9,12},{12,4},{13,8},{2,11},{3,2},{... | collective-permute-start | bytes 49160 | tf_op jit(solution)/shard_map/ppermute | solution.py:206
  15.4 2.0 %collective-permute-start.5 = (f32[4,512]{1,0:T(4,128)S(1)}, f32[4,512]{1,0:T(4,128)S(1)}, u32[]{:S(2)}, u32[]{:S(2)}) collective-permute-start(f32[4,512]{1,0:T(4,128)S(1)} %fusion.2), channel_id=1, source_target_pairs={{0,1},{1,0},{4,5},{5,4},{8,9},{9,8},{12,13},{13,12},{2,3},{3,2},{6... | collective-permute-start | bytes 24584 | tf_op jit(solution)/shard_map/ppermute | solution.py:212
  16.6 1.3 %collective-permute-start.4 = (bf16[16,1024]{1,0:T(8,128)(2,1)S(1)}, bf16[16,1024]{1,0:T(8,128)(2,1)S(1)}, u32[]{:S(2)}, u32[]{:S(2)}) collective-permute-start(bf16[16,1024]{1,0:T(8,128)(2,1)S(1)} %pad_maximum_fusion.refs_1_), channel_id=1, source_target_pairs={{0,1},{1,0},{4,5},{5,4},{8,9},{9,8},{12,13},{13,12},{2,3},{3,2},{6... | collective-permute-start | bytes 98312 | tf_op jit(solution)/shard_map/ppermute | solution.py:209

commit v4 on v3

--- a/solution.py
+++ b/solution.py
@@ -15,32 +15,42 @@
 
 
 def project_kernel(scales, size, hidden, out_grad, proj_in, proj_out, out, data, weights, sums, sems):
-    narrow, width = out_grad.shape[1], hidden.shape[1]
-    before = narrow // size
-    first_weights = pltpu.make_async_copy(proj_out, weights.at[:, pl.ds(0, narrow)], sems.at[0])
-    other_weights = pltpu.make_async_copy(proj_in, weights.at[:, pl.ds(narrow, width)], sems.at[1])
-    first_weights.start()
-    for n in range(before + width // size):
-        src, at = (out_grad, n * size) if n < before else (hidden, n * size - narrow)
-        pltpu.make_async_copy(src.at[:, pl.ds(at, size)], data.at[:, pl.ds(n * size, size)], sems.at[2 + n]).start()
-        if n == 0:
-            other_weights.start()
+    rows, width = hidden.shape
+    narrow = out_grad.shape[1]
+    half = rows // 2
+    wide_lanes, narrow_lanes = pl.ds(0, width), pl.ds(width, narrow)
+    copies = [
+        pltpu.make_async_copy(proj_in, weights.at[:, wide_lanes], sems.at[0]),
+        pltpu.make_async_copy(hidden.at[pl.ds(0, half)], data.at[pl.ds(0, half), wide_lanes], sems.at[1]),
+        pltpu.make_async_copy(hidden.at[pl.ds(half, half)], data.at[pl.ds(half, half), wide_lanes], sems.at[2]),
+        pltpu.make_async_copy(proj_out, weights.at[:, narrow_lanes], sems.at[3]),
+        pltpu.make_async_copy(out_grad, data.at[:, narrow_lanes], sems.at[4]),
+    ]
+    for copy in copies:
+        copy.start()
     sums[...] = jnp.zeros_like(sums)
-    first_weights.wait()
+    many, few = width // size, narrow // size
+    copies[0].wait()
 
     def step(n, carry):
-        @pl.when(n == before)
-        def _():
-            other_weights.wait()
-
-        lanes = pl.ds(pl.multiple_of(n * size, size), size)
-        pltpu.make_async_copy(hidden.at[:, pl.ds(0, size)], data.at[:, lanes], sems.at[2 + n]).wait()
-        which = (n < before).astype(jnp.int32)
-        sums[which] += lax.dot_general(data[:, lanes], weights[:, lanes], CONTRACT_LAST,
-                                       preferred_element_type=jnp.float32)
+        for first, needed in ((0, copies[1:2]), (many, copies[2:3]), (2 * many, copies[3:])):
+            @pl.when(n == first)
+            def _():
+                for copy in needed:
+                    copy.wait()
+
+        late = n >= 2 * many
+        n = n - jnp.where(late, 2 * many, 0)
+        lower = n >= jnp.where(late, few, many)
+        chunk = n - jnp.where(lower, jnp.where(late, few, many), 0) + jnp.where(late, many, 0)
+        lanes = pl.ds(pl.multiple_of(chunk * size, size), size)
+        part = pl.ds(pl.multiple_of(jnp.where(lower, half, 0), half), half)
+        which = late.astype(jnp.int32)
+        sums[which, part] += lax.dot_general(data[part, lanes], weights[:, lanes], CONTRACT_LAST,
+                                             preferred_element_type=jnp.float32)
         return carry
 
-    lax.fori_loop(0, before + width // size, step, 0)
+    lax.fori_loop(0, 2 * (many + few), step, 0)
     k_in = proj_in.shape[0]
     out[:k_in] = sums[0].T * scales[0]
     out[k_in:] = sums[1].T * scales[1]
@@ -60,7 +70,7 @@
             pltpu.VMEM((rows, narrow + width), jnp.bfloat16),
             pltpu.VMEM((k_in, narrow + width), jnp.bfloat16),
             pltpu.VMEM((2, rows, k_in), jnp.float32),
-            pltpu.SemaphoreType.DMA((2 + (narrow + width) // size,)),
+            pltpu.SemaphoreType.DMA((5,)),
         ],
         compiler_params=pltpu.CompilerParams(vmem_limit_bytes=24 << 20),
         cost_estimate=pl.CostEstimate(

time: 19.1 us -> 21 us (1.099)
  Pallas kernels: 5.36 us -> 7.19 us
    pallas_call x1, Pallas kernels: 3.88 us -> 5.72 us  [project(): pl.pallas_call(functools.partial(project_kernel, scales, size), out_shape...]
  transfers between devices with their start and end apart: 6 -> 6, of which waited for: 5 -> 5; matrix products, arithmetic and copies ran while one was open for 5% -> 4% of each run, Pallas kernels for 0% -> 0%
where the time goes in v4:
time: 21 us; the launch traced here: 20.8 us
  starting transfers between devices  7.87 us (37%)
  Pallas kernels  7.19 us (34%)
  waiting for transfers between devices  4.13 us (20%)
  matrix products  0.74 us (4%)
  between operations  0.68 us (3%)
    pallas_call x1, Pallas kernels, project(): pl.pallas_call(functools.partial(project_kernel, scales, size), out_shape...  5.72 us
    ppermute x2, starting transfers between devices, per_device(): block = lax.ppermute(held, group, list(enumerate(targets)))  3.97 us
    ppermute x1, starting transfers between devices, per_device(): came = lax.ppermute(sent, 'mp', [(0, 1), (1, 0)])  3 us
    ppermute x1, waiting for transfers between devices, per_device(): came = lax.ppermute(sent, 'mp', [(0, 1), (1, 0)])  1.73 us
    ppermute x1, waiting for transfers between devices, per_device(): came = lax.ppermute(grads, group, swap)  1.19 us
    pallas_call x1, Pallas kernels, finish(): pl.pallas_call(functools.partial(finish_kernel, examples, len(pieces), le...  1.07 us
    ppermute x2, waiting for transfers between devices, per_device(): block = lax.ppermute(held, group, list(enumerate(targets)))  0.69 us
    ppermute x1, starting transfers between devices, per_device(): raw = [near, lax.ppermute(for_other, group, swap)]  0.52 us
  transfers between devices with their start and end apart: 6, of which 5 were waited for; matrix products, arithmetic and copies ran while one was open for 4% of the time, Pallas kernels for 0%

profile of v4, /device:TPU:0, one launch (start us, length us, event | category | flops | bytes accessed | tf_op | source)
XLA Modules:
  0.0 20.8 jit_solution(4509737061225396340)
XLA Ops:
  0.6 0.0 copy-start
  0.6 0.0 copy-start.1
  0.7 5.7 %shard_map.77 = f32[64,256]{1,0:T(8,128)S(1)} custom-call(bf16[256,7168]{1,0:T(8,128)(2,1)} %hidden.1, bf16[256,2048]{1,0:T(8,128)(2,1)} %out_grad.1, bf16[32,7168]{1,0:T(8,128)(2,1)} %bitcast.6, bf16[32,2048]{1,0:T(8,128)(2,1)} %bitcast.7), custom_call_target="tpu_custom_call" | custom-call | flops 150994944 | bytes 5308416 | tf_op jit(solution)/shard_map/pallas_call | solution.py:64
  6.4 3.0 %collective-permute-start = (f16[64,256]{1,0:T(8,128)(2,1)S(1)}, f16[64,256]{1,0:T(8,128)(2,1)S(1)}, u32[]{:S(2)}, u32[]{:S(2)}) collective-permute-start(f16[64,256]{1,0:T(8,128)(2,1)S(1)} %convert_element_type.27), channel_id=1, source_target_pairs={{0,2},{2,0},{1,3},{3,1},{4,6},{6,4},{5,7},{7,5},{8,10},{10,8},{9,1... | collective-permute-start | bytes 98312 | tf_op jit(solution)/shard_map/ppermute | solution.py:200
  9.4 0.0 copy-done.1
  9.4 0.1 fusion
  9.5 0.1 reshape.33.mask
  9.6 1.7 %collective-permute-done = f16[64,256]{1,0:T(8,128)(2,1)S(1)} collective-permute-done((f16[64,256]{1,0:T(8,128)(2,1)S(1)}, f16[64,256]{1,0:T(8,128)(2,1)S(1)}, u32[]{:S(2)}, u32[]{:S(2)}) %collective-permute-start) | collective-permute-done | bytes 32800 | tf_op jit(solution)/shard_map/ppermute | solution.py:200
  11.3 0.4 %shard_map.78 = bf16[4,1024]{1,0:T(4,128)(2,1)S(1)} custom-call(f32[1,256]{1,0:T(1,128)S(1)} %reshape.33.mask, f32[64,256]{1,0:T(8,128)S(1)} %convert_element_type.28.refs_0_, f32[64,256]{1,0:T(8,128)S(1)} %convert_element_type.29.refs_1_), custom_call_target="tpu_custom_call" | custom-call | flops 8589934592 | tf_op jit(solution)/shard_map/pallas_call | solution.py:110
  11.7 0.0 collective-permute-start.1
  11.7 1.2 %collective-permute-done.1 = bf16[4,1024]{1,0:T(4,128)(2,1)S(1)} collective-permute-done((bf16[4,1024]{1,0:T(4,128)(2,1)S(1)}, bf16[4,1024]{1,0:T(4,128)(2,1)S(1)}, u32[]{:S(2)}, u32[]{:S(2)}) %collective-permute-start.1) | collective-permute-done | bytes 8224 | tf_op jit(solution)/shard_map/ppermute | solution.py:211
  12.9 4.0 %collective-permute-start.3 = (bf16[8,1024]{1,0:T(8,128)(2,1)S(1)}, bf16[8,1024]{1,0:T(8,128)(2,1)S(1)}, u32[]{:S(2)}, u32[]{:S(2)}) collective-permute-start(bf16[8,1024]{1,0:T(8,128)(2,1)S(1)} %pad_maximum_fusion.1.refs_0_), channel_id=1, source_target_pairs={{0,13},{1,4},{4,5},{5,9},{8,0},{9,8},{12,1},{13,12},{2,15},{3,6},{... | collective-permute-start | bytes 49160 | tf_op jit(solution)/shard_map/ppermute | solution.py:216
  16.9 0.0 collective-permute-start.2
  16.9 0.0 copy-done
  16.9 0.4 %fusion.2 = f32[4,512]{1,0:T(4,128)S(1)} fusion(bf16[4,1024]{1,0:T(4,128)(2,1)S(1)} %collective-permute-done.1, bf16[512,1024]{1,0:T(8,128)(2,1)S(1)} %copy-done), kind=kOutput, calls=%fused_computation.7 | convolution fusion | flops 4194304 | bytes 1064960 | tf_op jit(solution)/shard_map/ep,qp->eq/dot_general | solution.py:221
  17.3 0.5 %collective-permute-start.5 = (f32[4,512]{1,0:T(4,128)S(1)}, f32[4,512]{1,0:T(4,128)S(1)}, u32[]{:S(2)}, u32[]{:S(2)}) collective-permute-start(f32[4,512]{1,0:T(4,128)S(1)} %fusion.2), channel_id=1, source_target_pairs={{0,1},{1,0},{4,5},{5,4},{8,9},{9,8},{12,13},{13,12},{2,3},{3,2},{6... | collective-permute-start | bytes 24584 | tf_op jit(solution)/shard_map/ppermute | solution.py:222
  17.8 0.5 %collective-permute-done.3 = bf16[8,1024]{1,0:T(8,128)(2,1)S(1)} collective-permute-done((bf16[8,1024]{1,0:T(8,128)(2,1)S(1)}, bf16[8,1024]{1,0:T(8,128)(2,1)S(1)}, u32[]{:S(2)}, u32[]{:S(2)}) %collective-permute-start.3) | collective-permute-done | bytes 16416 | tf_op jit(solution)/shard_map/ppermute | solution.py:216
  18.3 0.1 collective-permute-done.2
  18.5 0.4 %collective-permute-start.4 = (bf16[16,1024]{1,0:T(8,128)(2,1)S(1)}, bf16[16,1024]{1,0:T(8,128)(2,1)S(1)}, u32[]{:S(2)}, u32[]{:S(2)}) collective-permute-start(bf16[16,1024]{1,0:T(8,128)(2,1)S(1)} %pad_maximum_fusion.refs_1_), channel_id=1, source_target_pairs={{0,1},{1,0},{4,5},{5,4},{8,9},{9,8},{12,13},{13,12},{2,3},{3,2},{6... | collective-permute-start | bytes 98312 | tf_op jit(solution)/shard_map/ppermute | solution.py:219
  18.9 0.4 %fusion.1.refs_3_ = f32[4,512]{1,0:T(4,128)S(1)} fusion(bf16[4,1024]{1,0:T(4,128)(2,1)S(1)} %shard_map.78, bf16[512,1024]{1,0:T(8,128)(2,1)S(1)} %copy-done), kind=kOutput, calls=%fused_computation.6 | convolution fusion | flops 4194304 | bytes 1064960 | tf_op jit(solution)/shard_map/ep,qp->eq/dot_general | solution.py:220
  19.2 0.0 collective-permute-done.5.refs_4_
  19.2 0.5 %collective-permute-done.4.refs_2_ = bf16[16,1024]{1,0:T(8,128)(2,1)S(1)} collective-permute-done((bf16[16,1024]{1,0:T(8,128)(2,1)S(1)}, bf16[16,1024]{1,0:T(8,128)(2,1)S(1)}, u32[]{:S(2)}, u32[]{:S(2)}) %collective-permute-start.4) | collective-permute-done | bytes 32800 | tf_op jit(solution)/shard_map/ppermute | solution.py:219
  19.8 1.1 %shard_map.79 = (f32[128,1024]{1,0:T(8,128)}, f32[4,1024]{1,0:T(4,128)}) custom-call(bf16[8,1024]{1,0:T(8,128)(2,1)S(1)} %pad_maximum_fusion.1.refs_0_, bf16[16,1024]{1,0:T(8,128)(2,1)S(1)} %pad_maximum_fusion.refs_1_, bf16[16,1024]{1,0:T(8,128)(2,1)S(1)} %collective-permute-done.4.refs_2_, f32[4,512]{1,0:T(4,128)S(1)} %fusion.1.refs_3_, ...), custom_call_target="tpu_custom_call" | custom-call | tf_op jit(solution)/shard_map/pallas_call | solution.py:162
  (7 shorter events, 0.1 us)
Async XLA Ops:
  0.6 16.3 %copy-start = (bf16[512,1024]{1,0:T(8,128)(2,1)S(1)}, bf16[512,1024]{1,0:T(8,128)(2,1)}, u32[]{:S(2)}) copy-start(bf16[512,1024]{1,0:T(8,128)(2,1)} %param.11) | copy-start | bytes 3145732
  0.6 8.8 %copy-start.1 = (s32[4]{0:T(128)S(1)}, s32[4]{0:T(128)}, u32[]{:S(2)}) copy-start(s32[4]{0:T(128)} %param.8) | copy-start | bytes 52
  6.4 4.9 %collective-permute-start = (f16[64,256]{1,0:T(8,128)(2,1)S(1)}, f16[64,256]{1,0:T(8,128)(2,1)S(1)}, u32[]{:S(2)}, u32[]{:S(2)}) collective-permute-start(f16[64,256]{1,0:T(8,128)(2,1)S(1)} %convert_element_type.27), channel_id=1, source_target_pairs={{0,2},{2,0},{1,3},{3,1},{4,6},{6,4},{5,7},{7,5},{8,10},{10,8},{9,1... | collective-permute-start | bytes 98312 | tf_op jit(solution)/shard_map/ppermute | solution.py:200
  11.7 1.2 %collective-permute-start.1 = (bf16[4,1024]{1,0:T(4,128)(2,1)S(1)}, bf16[4,1024]{1,0:T(4,128)(2,1)S(1)}, u32[]{:S(2)}, u32[]{:S(2)}) collective-permute-start(bf16[4,1024]{1,0:T(4,128)(2,1)S(1)} %shard_map.78), channel_id=1, source_target_pairs={{0,1},{1,0},{4,5},{5,4},{8,9},{9,8},{12,13},{13,12},{2,3},{3,2},{6... | collective-permute-start | bytes 24584 | tf_op jit(solution)/shard_map/ppermute | solution.py:211
  12.9 5.4 %collective-permute-start.3 = (bf16[8,1024]{1,0:T(8,128)(2,1)S(1)}, bf16[8,1024]{1,0:T(8,128)(2,1)S(1)}, u32[]{:S(2)}, u32[]{:S(2)}) collective-permute-start(bf16[8,1024]{1,0:T(8,128)(2,1)S(1)} %pad_maximum_fusion.1.refs_0_), channel_id=1, source_target_pairs={{0,13},{1,4},{4,5},{5,9},{8,0},{9,8},{12,1},{13,12},{2,15},{3,6},{... | collective-permute-start | bytes 49160 | tf_op jit(solution)/shard_map/ppermute | solution.py:216
  16.9 1.6 %collective-permute-start.2 = (bf16[8,1024]{1,0:T(8,128)(2,1)S(1)}, bf16[8,1024]{1,0:T(8,128)(2,1)S(1)}, u32[]{:S(2)}, u32[]{:S(2)}) collective-permute-start(bf16[8,1024]{1,0:T(8,128)(2,1)S(1)} %pad_maximum_fusion.1.refs_0_), channel_id=1, source_target_pairs={{0,9},{1,0},{4,13},{5,1},{8,5},{9,12},{12,4},{13,8},{2,11},{3,2},{... | collective-permute-start | bytes 49160 | tf_op jit(solution)/shard_map/ppermute | solution.py:216
  17.3 2.0 %collective-permute-start.5 = (f32[4,512]{1,0:T(4,128)S(1)}, f32[4,512]{1,0:T(4,128)S(1)}, u32[]{:S(2)}, u32[]{:S(2)}) collective-permute-start(f32[4,512]{1,0:T(4,128)S(1)} %fusion.2), channel_id=1, source_target_pairs={{0,1},{1,0},{4,5},{5,4},{8,9},{9,8},{12,13},{13,12},{2,3},{3,2},{6... | collective-permute-start | bytes 24584 | tf_op jit(solution)/shard_map/ppermute | solution.py:222
  18.5 1.3 %collective-permute-start.4 = (bf16[16,1024]{1,0:T(8,128)(2,1)S(1)}, bf16[16,1024]{1,0:T(8,128)(2,1)S(1)}, u32[]{:S(2)}, u32[]{:S(2)}) collective-permute-start(bf16[16,1024]{1,0:T(8,128)(2,1)S(1)} %pad_maximum_fusion.refs_1_), channel_id=1, source_target_pairs={{0,1},{1,0},{4,5},{5,4},{8,9},{9,8},{12,13},{13,12},{2,3},{3,2},{6... | collective-permute-start | bytes 98312 | tf_op jit(solution)/shard_map/ppermute | solution.py:219

commit v5 on v2

--- a/solution.py
+++ b/solution.py
@@ -15,7 +15,7 @@
 
 
 def chunk_of(width):
-    return next(size for size in (1024, 512, 256, 128) if width % size == 0)
+    return width if width <= 2048 else next(size for size in (1792, 2048, 1024, 512, 256, 128) if width % size == 0)
 
 
 def tree_sum(terms):
@@ -106,7 +106,7 @@
     for at in range(0, k_in, per):
         rest = jnp.concatenate([act[i:i + 1] * grad for i in range(at, at + per)], axis=0)
         total = None
-        for _ in range(3):
+        for _ in range(2):
             high = rest.astype(jnp.bfloat16)
             rest = rest - high.astype(jnp.float32)
             part = lax.dot_general(pick, high, CONTRACT_LAST, preferred_element_type=jnp.float32)
@@ -128,8 +128,8 @@
 
 def finish_kernel(examples, n_pieces, n_raw, *refs):
     pieces, raw = refs[:n_pieces], refs[n_pieces:n_pieces + n_raw]
-    cov, scores = refs[n_pieces + n_raw:]
-    own_rows = cov.shape[0]
+    cov, scores, block, row, sems = refs[n_pieces + n_raw:]
+    own_rows, flat = cov.shape
     place = lax.axis_index(("dp", "sub"))
     every = jnp.concatenate([p[...] for p in pieces], axis=0)
     if own_rows % 128 == 0:
@@ -139,30 +139,41 @@
         at = pl.multiple_of((place * own_rows) // 128 * 128, 128)
         wider = jnp.concatenate([p[:, pl.ds(at, 128)] for p in pieces], axis=0)
         own = pltpu.roll(wider.astype(jnp.float32), at - place * own_rows + 128, 1)[:, :own_rows].astype(jnp.bfloat16)
+    copies = []
+    for n, at in enumerate(range(0, flat, flat // 4)):
+        lanes = pl.ds(at, flat // 4)
+        block[:, lanes] = lax.dot_general(own, every[:, at:at + flat // 4], CONTRACT_FIRST,
+                                          preferred_element_type=jnp.float32) * (1.0 / examples)
+        copies.append(pltpu.make_async_copy(block.at[:, lanes], cov.at[:, lanes], sems.at[n]))
+        copies[-1].start()
     wide = every.astype(jnp.float32)
     factor = lax.rsqrt(jnp.sum(wide * wide) / examples + 1e-06)
     if n_raw == 2:
         near, far = raw[0][...], raw[1][...]
         first = lax.axis_index("sub") == 0
         half = near.shape[1]
-        scores[:, :half] = jnp.where(first, near, far) * factor
-        scores[:, half:] = jnp.where(first, far, near) * factor
-    else:
-        scores[...] = raw[0][...] * factor
-    cov[...] = lax.dot_general(own, every, CONTRACT_FIRST, preferred_element_type=jnp.float32) * (1.0 / examples)
+        row[:, :half] = jnp.where(first, near, far) * factor
+        row[:, half:] = jnp.where(first, far, near) * factor
+    else:
+        row[...] = raw[0][...] * factor
+    copies.append(pltpu.make_async_copy(row, scores, sems.at[4]))
+    copies[-1].start()
+    for copy in copies:
+        copy.wait()
 
 
 def finish(examples, own_rows, pieces, raw):
     flat = pieces[0].shape[1]
     vmem = pl.BlockSpec(memory_space=pltpu.VMEM)
+    hbm = pl.BlockSpec(memory_space=pltpu.HBM)
+    cov = (own_rows, flat)
+    scores = (raw[0].shape[0], sum(r.shape[1] for r in raw))
     return pl.pallas_call(
         functools.partial(finish_kernel, examples, len(pieces), len(raw)),
-        out_shape=(
-            jax.ShapeDtypeStruct((own_rows, flat), jnp.float32),
-            jax.ShapeDtypeStruct((raw[0].shape[0], sum(r.shape[1] for r in raw)), jnp.float32),
-        ),
+        out_shape=(jax.ShapeDtypeStruct(cov, jnp.float32), jax.ShapeDtypeStruct(scores, jnp.float32)),
         in_specs=[vmem] * (len(pieces) + len(raw)),
-        out_specs=(vmem, vmem),
+        out_specs=(hbm, hbm),
+        scratch_shapes=[pltpu.VMEM(cov, jnp.float32), pltpu.VMEM(scores, jnp.float32), pltpu.SemaphoreType.DMA((5,))],
         compiler_params=pltpu.CompilerParams(vmem_limit_bytes=8 << 20),
     )(*pieces, *raw)
 

time: 19.2 us -> 18.8 us (0.979)
  Pallas kernels: 5.41 us -> 5.04 us
    pallas_call x1, Pallas kernels: 3.78 us -> 3.57 us  [project(): pl.pallas_call(functools.partial(project_kernel, scales), out_shape=jax.S...]
where the time goes in v5:
time: 18.8 us; the launch traced here: 18.7 us
  starting transfers between devices  7.87 us (42%)
  Pallas kernels  5.04 us (27%)
  waiting for transfers between devices  4.13 us (22%)
  matrix products  0.74 us (4%)
  between operations  0.68 us (4%)
    ppermute x2, starting transfers between devices, per_device(): block = lax.ppermute(held, group, list(enumerate(targets)))  3.96 us
    pallas_call x1, Pallas kernels, project(): pl.pallas_call(functools.partial(project_kernel, scales), out_shape=jax.S...  3.57 us
    ppermute x1, starting transfers between devices, per_device(): came = lax.ppermute(sent, 'mp', [(0, 1), (1, 0)])  3.01 us
    ppermute x1, waiting for transfers between devices, per_device(): came = lax.ppermute(sent, 'mp', [(0, 1), (1, 0)])  1.73 us
    ppermute x1, waiting for transfers between devices, per_device(): came = lax.ppermute(grads, group, swap)  1.19 us
    pallas_call x1, Pallas kernels, finish(): pl.pallas_call(functools.partial(finish_kernel, examples, len(pieces), le...  1.06 us
    ppermute x2, waiting for transfers between devices, per_device(): block = lax.ppermute(held, group, list(enumerate(targets)))  0.69 us
    ppermute x1, starting transfers between devices, per_device(): raw = [near, lax.ppermute(for_other, group, swap)]  0.52 us
  transfers between devices with their start and end apart: 6, of which 5 were waited for; matrix products, arithmetic and copies ran while one was open for 5% of the time, Pallas kernels for 0%

profile of v5, /device:TPU:0, one launch (start us, length us, event | category | flops | bytes accessed | tf_op | source)
XLA Modules:
  0.0 18.7 jit_solution(7612390786730232195)
XLA Ops:
  0.6 0.0 copy-start
  0.6 0.0 copy-start.1
  0.7 3.6 %shard_map.77 = f32[64,256]{1,0:T(8,128)S(1)} custom-call(bf16[256,7168]{1,0:T(8,128)(2,1)} %hidden.1, bf16[256,2048]{1,0:T(8,128)(2,1)} %out_grad.1, bf16[32,7168]{1,0:T(8,128)(2,1)} %bitcast.6, bf16[32,2048]{1,0:T(8,128)(2,1)} %bitcast.7), custom_call_target="tpu_custom_call" | custom-call | flops 150994944 | bytes 5308416 | tf_op jit(solution)/shard_map/pallas_call | solution.py:72
  4.2 3.0 %collective-permute-start = (f16[64,256]{1,0:T(8,128)(2,1)S(1)}, f16[64,256]{1,0:T(8,128)(2,1)S(1)}, u32[]{:S(2)}, u32[]{:S(2)}) collective-permute-start(f16[64,256]{1,0:T(8,128)(2,1)S(1)} %convert_element_type.27), channel_id=1, source_target_pairs={{0,2},{2,0},{1,3},{3,1},{4,6},{6,4},{5,7},{7,5},{8,10},{10,8},{9,1... | collective-permute-start | bytes 98312 | tf_op jit(solution)/shard_map/ppermute | solution.py:209
  7.3 0.0 copy-done.1
  7.3 0.1 fusion
  7.3 0.1 reshape.33.mask
  7.4 1.7 %collective-permute-done = f16[64,256]{1,0:T(8,128)(2,1)S(1)} collective-permute-done((f16[64,256]{1,0:T(8,128)(2,1)S(1)}, f16[64,256]{1,0:T(8,128)(2,1)S(1)}, u32[]{:S(2)}, u32[]{:S(2)}) %collective-permute-start) | collective-permute-done | bytes 32800 | tf_op jit(solution)/shard_map/ppermute | solution.py:209
  9.2 0.4 %shard_map.78 = bf16[4,1024]{1,0:T(4,128)(2,1)S(1)} custom-call(f32[1,256]{1,0:T(1,128)S(1)} %reshape.33.mask, f32[64,256]{1,0:T(8,128)S(1)} %convert_element_type.28.refs_0_, f32[64,256]{1,0:T(8,128)S(1)} %convert_element_type.29.refs_1_), custom_call_target="tpu_custom_call" | custom-call | flops 8589934592 | tf_op jit(solution)/shard_map/pallas_call | solution.py:119
  9.6 0.0 collective-permute-start.1
  9.6 1.2 %collective-permute-done.1 = bf16[4,1024]{1,0:T(4,128)(2,1)S(1)} collective-permute-done((bf16[4,1024]{1,0:T(4,128)(2,1)S(1)}, bf16[4,1024]{1,0:T(4,128)(2,1)S(1)}, u32[]{:S(2)}, u32[]{:S(2)}) %collective-permute-start.1) | collective-permute-done | bytes 8224 | tf_op jit(solution)/shard_map/ppermute | solution.py:220
  10.8 4.0 %collective-permute-start.3 = (bf16[8,1024]{1,0:T(8,128)(2,1)S(1)}, bf16[8,1024]{1,0:T(8,128)(2,1)S(1)}, u32[]{:S(2)}, u32[]{:S(2)}) collective-permute-start(bf16[8,1024]{1,0:T(8,128)(2,1)S(1)} %pad_maximum_fusion.1.refs_0_), channel_id=1, source_target_pairs={{0,13},{1,4},{4,5},{5,9},{8,0},{9,8},{12,1},{13,12},{2,15},{3,6},{... | collective-permute-start | bytes 49160 | tf_op jit(solution)/shard_map/ppermute | solution.py:225
  14.7 0.0 collective-permute-start.2
  14.7 0.0 copy-done
  14.7 0.4 %fusion.2 = f32[4,512]{1,0:T(4,128)S(1)} fusion(bf16[4,1024]{1,0:T(4,128)(2,1)S(1)} %collective-permute-done.1, bf16[512,1024]{1,0:T(8,128)(2,1)S(1)} %copy-done), kind=kOutput, calls=%fused_computation.7 | convolution fusion | flops 4194304 | bytes 1064960 | tf_op jit(solution)/shard_map/ep,qp->eq/dot_general | solution.py:230
  15.1 0.5 %collective-permute-start.5 = (f32[4,512]{1,0:T(4,128)S(1)}, f32[4,512]{1,0:T(4,128)S(1)}, u32[]{:S(2)}, u32[]{:S(2)}) collective-permute-start(f32[4,512]{1,0:T(4,128)S(1)} %fusion.2), channel_id=1, source_target_pairs={{0,1},{1,0},{4,5},{5,4},{8,9},{9,8},{12,13},{13,12},{2,3},{3,2},{6... | collective-permute-start | bytes 24584 | tf_op jit(solution)/shard_map/ppermute | solution.py:231
  15.6 0.5 %collective-permute-done.3 = bf16[8,1024]{1,0:T(8,128)(2,1)S(1)} collective-permute-done((bf16[8,1024]{1,0:T(8,128)(2,1)S(1)}, bf16[8,1024]{1,0:T(8,128)(2,1)S(1)}, u32[]{:S(2)}, u32[]{:S(2)}) %collective-permute-start.3) | collective-permute-done | bytes 16416 | tf_op jit(solution)/shard_map/ppermute | solution.py:225
  16.2 0.1 collective-permute-done.2
  16.3 0.4 %collective-permute-start.4 = (bf16[16,1024]{1,0:T(8,128)(2,1)S(1)}, bf16[16,1024]{1,0:T(8,128)(2,1)S(1)}, u32[]{:S(2)}, u32[]{:S(2)}) collective-permute-start(bf16[16,1024]{1,0:T(8,128)(2,1)S(1)} %pad_maximum_fusion.refs_1_), channel_id=1, source_target_pairs={{0,1},{1,0},{4,5},{5,4},{8,9},{9,8},{12,13},{13,12},{2,3},{3,2},{6... | collective-permute-start | bytes 98312 | tf_op jit(solution)/shard_map/ppermute | solution.py:228
  16.7 0.4 %fusion.1.refs_3_ = f32[4,512]{1,0:T(4,128)S(1)} fusion(bf16[4,1024]{1,0:T(4,128)(2,1)S(1)} %shard_map.78, bf16[512,1024]{1,0:T(8,128)(2,1)S(1)} %copy-done), kind=kOutput, calls=%fused_computation.6 | convolution fusion | flops 4194304 | bytes 1064960 | tf_op jit(solution)/shard_map/ep,qp->eq/dot_general | solution.py:229
  17.1 0.0 collective-permute-done.5.refs_4_
  17.1 0.5 %collective-permute-done.4.refs_2_ = bf16[16,1024]{1,0:T(8,128)(2,1)S(1)} collective-permute-done((bf16[16,1024]{1,0:T(8,128)(2,1)S(1)}, bf16[16,1024]{1,0:T(8,128)(2,1)S(1)}, u32[]{:S(2)}, u32[]{:S(2)}) %collective-permute-start.4) | collective-permute-done | bytes 32800 | tf_op jit(solution)/shard_map/ppermute | solution.py:228
  17.6 1.1 %shard_map.79 = (f32[128,1024]{1,0:T(8,128)}, f32[4,1024]{1,0:T(4,128)}) custom-call(bf16[8,1024]{1,0:T(8,128)(2,1)S(1)} %pad_maximum_fusion.1.refs_0_, bf16[16,1024]{1,0:T(8,128)(2,1)S(1)} %pad_maximum_fusion.refs_1_, bf16[16,1024]{1,0:T(8,128)(2,1)S(1)} %collective-permute-done.4.refs_2_, f32[4,512]{1,0:T(4,128)S(1)} %fusion.1.refs_3_, ...), custom_call_target="tpu_custom_call" | custom-call | tf_op jit(solution)/shard_map/pallas_call | solution.py:171
  (7 shorter events, 0.1 us)
Async XLA Ops:
  0.6 14.1 %copy-start = (bf16[512,1024]{1,0:T(8,128)(2,1)S(1)}, bf16[512,1024]{1,0:T(8,128)(2,1)}, u32[]{:S(2)}) copy-start(bf16[512,1024]{1,0:T(8,128)(2,1)} %param.11) | copy-start | bytes 3145732
  0.6 6.6 %copy-start.1 = (s32[4]{0:T(128)S(1)}, s32[4]{0:T(128)}, u32[]{:S(2)}) copy-start(s32[4]{0:T(128)} %param.8) | copy-start | bytes 52
  4.2 4.9 %collective-permute-start = (f16[64,256]{1,0:T(8,128)(2,1)S(1)}, f16[64,256]{1,0:T(8,128)(2,1)S(1)}, u32[]{:S(2)}, u32[]{:S(2)}) collective-permute-start(f16[64,256]{1,0:T(8,128)(2,1)S(1)} %convert_element_type.27), channel_id=1, source_target_pairs={{0,2},{2,0},{1,3},{3,1},{4,6},{6,4},{5,7},{7,5},{8,10},{10,8},{9,1... | collective-permute-start | bytes 98312 | tf_op jit(solution)/shard_map/ppermute | solution.py:209
  9.6 1.2 %collective-permute-start.1 = (bf16[4,1024]{1,0:T(4,128)(2,1)S(1)}, bf16[4,1024]{1,0:T(4,128)(2,1)S(1)}, u32[]{:S(2)}, u32[]{:S(2)}) collective-permute-start(bf16[4,1024]{1,0:T(4,128)(2,1)S(1)} %shard_map.78), channel_id=1, source_target_pairs={{0,1},{1,0},{4,5},{5,4},{8,9},{9,8},{12,13},{13,12},{2,3},{3,2},{6... | collective-permute-start | bytes 24584 | tf_op jit(solution)/shard_map/ppermute | solution.py:220
  10.8 5.4 %collective-permute-start.3 = (bf16[8,1024]{1,0:T(8,128)(2,1)S(1)}, bf16[8,1024]{1,0:T(8,128)(2,1)S(1)}, u32[]{:S(2)}, u32[]{:S(2)}) collective-permute-start(bf16[8,1024]{1,0:T(8,128)(2,1)S(1)} %pad_maximum_fusion.1.refs_0_), channel_id=1, source_target_pairs={{0,13},{1,4},{4,5},{5,9},{8,0},{9,8},{12,1},{13,12},{2,15},{3,6},{... | collective-permute-start | bytes 49160 | tf_op jit(solution)/shard_map/ppermute | solution.py:225
  14.7 1.6 %collective-permute-start.2 = (bf16[8,1024]{1,0:T(8,128)(2,1)S(1)}, bf16[8,1024]{1,0:T(8,128)(2,1)S(1)}, u32[]{:S(2)}, u32[]{:S(2)}) collective-permute-start(bf16[8,1024]{1,0:T(8,128)(2,1)S(1)} %pad_maximum_fusion.1.refs_0_), channel_id=1, source_target_pairs={{0,9},{1,0},{4,13},{5,1},{8,5},{9,12},{12,4},{13,8},{2,11},{3,2},{... | collective-permute-start | bytes 49160 | tf_op jit(solution)/shard_map/ppermute | solution.py:225
  15.1 2.0 %collective-permute-start.5 = (f32[4,512]{1,0:T(4,128)S(1)}, f32[4,512]{1,0:T(4,128)S(1)}, u32[]{:S(2)}, u32[]{:S(2)}) collective-permute-start(f32[4,512]{1,0:T(4,128)S(1)} %fusion.2), channel_id=1, source_target_pairs={{0,1},{1,0},{4,5},{5,4},{8,9},{9,8},{12,13},{13,12},{2,3},{3,2},{6... | collective-permute-start | bytes 24584 | tf_op jit(solution)/shard_map/ppermute | solution.py:231
  16.3 1.3 %collective-permute-start.4 = (bf16[16,1024]{1,0:T(8,128)(2,1)S(1)}, bf16[16,1024]{1,0:T(8,128)(2,1)S(1)}, u32[]{:S(2)}, u32[]{:S(2)}) collective-permute-start(bf16[16,1024]{1,0:T(8,128)(2,1)S(1)} %pad_maximum_fusion.refs_1_), channel_id=1, source_target_pairs={{0,1},{1,0},{4,5},{5,4},{8,9},{9,8},{12,13},{13,12},{2,3},{3,2},{6... | collective-permute-start | bytes 98312 | tf_op jit(solution)/shard_map/ppermute | solution.py:228

commit v6 on v5

--- a/solution.py
+++ b/solution.py
@@ -9,7 +9,8 @@
 
 SEQ = 64
 DEPTH = 256
-SENDS = ((7, 2, 3, 5, 0, 4, 1, 6), (5, 0, 7, 1, 3, 6, 2, 4))
+SWAPPED_SEND = (2, 5, 4, 7, 6, 0, 3, 1)
+DIRECT_SEND = (7, 6, 1, 0, 2, 3, 5, 4)
 CONTRACT_LAST = (((1,), (1,)), ((), ()))
 CONTRACT_FIRST = (((0,), (0,)), ((), ()))
 
@@ -178,20 +179,6 @@
     )(*pieces, *raw)
 
 
-def first_arrivals(sends):
-    seen = [{chip} for chip in range(len(sends[0]) // 2)]
-    flags = []
-    for targets in sends:
-        bits = 0
-        for node, target in enumerate(targets):
-            if node // 2 not in seen[target // 2]:
-                seen[target // 2].add(node // 2)
-                bits |= 1 << target
-        flags.append(bits)
-    assert all(len(chips) == len(seen) for chips in seen)
-    return flags
-
-
 def per_device(hidden, out_grad, lengths, proj_in, proj_out, test_proj):
     k_in, k_out = proj_in.shape[1], proj_out.shape[1]
     flat = k_in * k_out
@@ -219,13 +206,9 @@
         swap = [(i, i ^ 1) for i in range(sharers)]
         came = lax.ppermute(grads, group, swap)
         held = jnp.concatenate([grads, came], axis=0)
-        place = lax.axis_index(group)
-        fetched = []
-        for targets, kept in reversed(list(zip(SENDS, first_arrivals(SENDS)))):
-            block = lax.ppermute(held, group, list(enumerate(targets)))
-            fetched.append(jnp.where(((kept >> place) & 1) == 1, block, 0))
-        fetched = jnp.concatenate(fetched, axis=0)
-        gathered = [held, fetched, lax.ppermute(fetched, group, swap)]
+        direct = lax.ppermute(held, group, list(enumerate(DIRECT_SEND)))
+        fetched = lax.ppermute(held, group, list(enumerate(SWAPPED_SEND)))
+        gathered = [held, direct, fetched, lax.ppermute(fetched, group, swap)]
         near = jnp.einsum("ep,qp->eq", grads, test_proj, preferred_element_type=jnp.float32)
         for_other = jnp.einsum("ep,qp->eq", came, test_proj, preferred_element_type=jnp.float32)
         raw = [near, lax.ppermute(for_other, group, swap)]

time: 18.8 us -> 18 us (0.957)
  waiting for transfers between devices: 4.13 us -> 3.39 us
    ppermute x3, waiting for transfers between devices: 1.21 us -> 0.42 us  [the longest x1 0.38 us: per_device(): gathered = [held, direct, fetched, lax.ppermute(fetched, group, swap)]]
  transfers between devices with their start and end apart: 6 -> 6, of which waited for: 5 -> 4; matrix products, arithmetic and copies ran while one was open for 5% -> 5% of each run, Pallas kernels for 0% -> 0%
where the time goes in v6:
time: 18 us; the launch traced here: 17.9 us
  starting transfers between devices  7.84 us (44%)
  Pallas kernels  5.04 us (28%)
  waiting for transfers between devices  3.39 us (19%)
  matrix products  0.74 us (4%)
  between operations  0.68 us (4%)
    pallas_call x1, Pallas kernels, project(): pl.pallas_call(functools.partial(project_kernel, scales), out_shape=jax.S...  3.57 us
    ppermute x1, starting transfers between devices, per_device(): came = lax.ppermute(sent, 'mp', [(0, 1), (1, 0)])  3.01 us
    ppermute x1, starting transfers between devices, per_device(): fetched = lax.ppermute(held, group, list(enumerate(SWAPPED_SEND)))  2.16 us
    ppermute x1, starting transfers between devices, per_device(): direct = lax.ppermute(held, group, list(enumerate(DIRECT_SEND)))  1.87 us
    ppermute x1, waiting for transfers between devices, per_device(): came = lax.ppermute(sent, 'mp', [(0, 1), (1, 0)])  1.73 us
    ppermute x1, waiting for transfers between devices, per_device(): came = lax.ppermute(grads, group, swap)  1.19 us
    pallas_call x1, Pallas kernels, finish(): pl.pallas_call(functools.partial(finish_kernel, examples, len(pieces), le...  1.07 us
    pallas_call x1, Pallas kernels, example_grads(): pl.pallas_call(functools.partial(grads_kernel, k_in, scales), out_shape=j...  0.41 us
  transfers between devices with their start and end apart: 6, of which 4 were waited for; matrix products, arithmetic and copies ran while one was open for 5% of the time, Pallas kernels for 0%

profile of v6, /device:TPU:0, one launch (start us, length us, event | category | flops | bytes accessed | tf_op | source)
XLA Modules:
  0.0 17.9 jit_solution(9978670451680014679)
XLA Ops:
  0.6 0.0 copy-start
  0.6 0.0 copy-start.1
  0.7 3.6 %shard_map.77 = f32[64,256]{1,0:T(8,128)S(1)} custom-call(bf16[256,7168]{1,0:T(8,128)(2,1)} %hidden.1, bf16[256,2048]{1,0:T(8,128)(2,1)} %out_grad.1, bf16[32,7168]{1,0:T(8,128)(2,1)} %bitcast.6, bf16[32,2048]{1,0:T(8,128)(2,1)} %bitcast.7), custom_call_target="tpu_custom_call" | custom-call | flops 150994944 | bytes 5308416 | tf_op jit(solution)/shard_map/pallas_call | solution.py:73
  4.2 3.0 %collective-permute-start = (f16[64,256]{1,0:T(8,128)(2,1)S(1)}, f16[64,256]{1,0:T(8,128)(2,1)S(1)}, u32[]{:S(2)}, u32[]{:S(2)}) collective-permute-start(f16[64,256]{1,0:T(8,128)(2,1)S(1)} %convert_element_type.24), channel_id=1, source_target_pairs={{0,2},{2,0},{1,3},{3,1},{4,6},{6,4},{5,7},{7,5},{8,10},{10,8},{9,1... | collective-permute-start | bytes 98312 | tf_op jit(solution)/shard_map/ppermute | solution.py:196
  7.3 0.0 copy-done.1
  7.3 0.1 fusion
  7.3 0.1 reshape.33.mask
  7.4 1.7 %collective-permute-done = f16[64,256]{1,0:T(8,128)(2,1)S(1)} collective-permute-done((f16[64,256]{1,0:T(8,128)(2,1)S(1)}, f16[64,256]{1,0:T(8,128)(2,1)S(1)}, u32[]{:S(2)}, u32[]{:S(2)}) %collective-permute-start) | collective-permute-done | bytes 32800 | tf_op jit(solution)/shard_map/ppermute | solution.py:196
  9.2 0.4 %shard_map.78 = bf16[4,1024]{1,0:T(4,128)(2,1)S(1)} custom-call(f32[1,256]{1,0:T(1,128)S(1)} %reshape.33.mask, f32[64,256]{1,0:T(8,128)S(1)} %convert_element_type.25.refs_0_, f32[64,256]{1,0:T(8,128)S(1)} %convert_element_type.26.refs_1_), custom_call_target="tpu_custom_call" | custom-call | flops 8589934592 | tf_op jit(solution)/shard_map/pallas_call | solution.py:120
  9.6 0.0 collective-permute-start.1
  9.6 1.2 %collective-permute-done.1 = bf16[4,1024]{1,0:T(4,128)(2,1)S(1)} collective-permute-done((bf16[4,1024]{1,0:T(4,128)(2,1)S(1)}, bf16[4,1024]{1,0:T(4,128)(2,1)S(1)}, u32[]{:S(2)}, u32[]{:S(2)}) %collective-permute-start.1) | collective-permute-done | bytes 8224 | tf_op jit(solution)/shard_map/ppermute | solution.py:207
  10.8 2.2 %collective-permute-start.3 = (bf16[8,1024]{1,0:T(8,128)(2,1)S(1)}, bf16[8,1024]{1,0:T(8,128)(2,1)S(1)}, u32[]{:S(2)}, u32[]{:S(2)}) collective-permute-start(bf16[8,1024]{1,0:T(8,128)(2,1)S(1)} %pad_maximum_fusion.refs_0_), channel_id=1, source_target_pairs={{0,4},{1,9},{4,8},{5,13},{8,12},{9,0},{12,5},{13,1},{2,6},{3,11},{... | collective-permute-start | bytes 49160 | tf_op jit(solution)/shard_map/ppermute | solution.py:210
  12.9 1.9 %collective-permute-start.2 = (bf16[8,1024]{1,0:T(8,128)(2,1)S(1)}, bf16[8,1024]{1,0:T(8,128)(2,1)S(1)}, u32[]{:S(2)}, u32[]{:S(2)}) collective-permute-start(bf16[8,1024]{1,0:T(8,128)(2,1)S(1)} %pad_maximum_fusion.refs_0_), channel_id=1, source_target_pairs={{0,13},{1,12},{4,1},{5,0},{8,4},{9,5},{12,9},{13,8},{2,15},{3,14},... | collective-permute-start | bytes 49160 | tf_op jit(solution)/shard_map/ppermute | solution.py:209
  14.8 0.0 copy-done
  14.8 0.4 %fusion.2 = f32[4,512]{1,0:T(4,128)S(1)} fusion(bf16[4,1024]{1,0:T(4,128)(2,1)S(1)} %collective-permute-done.1, bf16[512,1024]{1,0:T(8,128)(2,1)S(1)} %copy-done), kind=kOutput, calls=%fused_computation.4 | convolution fusion | flops 4194304 | bytes 1064960 | tf_op jit(solution)/shard_map/ep,qp->eq/dot_general | solution.py:213
  15.2 0.4 %collective-permute-start.5 = (f32[4,512]{1,0:T(4,128)S(1)}, f32[4,512]{1,0:T(4,128)S(1)}, u32[]{:S(2)}, u32[]{:S(2)}) collective-permute-start(f32[4,512]{1,0:T(4,128)S(1)} %fusion.2), channel_id=1, source_target_pairs={{0,1},{1,0},{4,5},{5,4},{8,9},{9,8},{12,13},{13,12},{2,3},{3,2},{6... | collective-permute-start | bytes 24584 | tf_op jit(solution)/shard_map/ppermute | solution.py:214
  15.6 0.0 collective-permute-done.3.refs_2_
  15.6 0.4 %collective-permute-start.4 = (bf16[8,1024]{1,0:T(8,128)(2,1)S(1)}, bf16[8,1024]{1,0:T(8,128)(2,1)S(1)}, u32[]{:S(2)}, u32[]{:S(2)}) collective-permute-start(bf16[8,1024]{1,0:T(8,128)(2,1)S(1)} %collective-permute-done.3.refs_2_), channel_id=1, source_target_pairs={{0,1},{1,0},{4,5},{5,4},{8,9},{9,8},{12,13},{13,12},{2,3},{3,2},{6... | collective-permute-start | bytes 49160 | tf_op jit(solution)/shard_map/ppermute | solution.py:211
  16.0 0.4 %fusion.1.refs_4_ = f32[4,512]{1,0:T(4,128)S(1)} fusion(bf16[4,1024]{1,0:T(4,128)(2,1)S(1)} %shard_map.78, bf16[512,1024]{1,0:T(8,128)(2,1)S(1)} %copy-done), kind=kOutput, calls=%fused_computation.3 | convolution fusion | flops 4194304 | bytes 1064960 | tf_op jit(solution)/shard_map/ep,qp->eq/dot_general | solution.py:212
  16.3 0.1 collective-permute-done.5.refs_5_
  16.4 0.0 collective-permute-done.2.refs_1_
  16.4 0.4 %collective-permute-done.4.refs_3_ = bf16[8,1024]{1,0:T(8,128)(2,1)S(1)} collective-permute-done((bf16[8,1024]{1,0:T(8,128)(2,1)S(1)}, bf16[8,1024]{1,0:T(8,128)(2,1)S(1)}, u32[]{:S(2)}, u32[]{:S(2)}) %collective-permute-start.4) | collective-permute-done | bytes 16416 | tf_op jit(solution)/shard_map/ppermute | solution.py:211
  16.8 1.1 %shard_map.79 = (f32[128,1024]{1,0:T(8,128)}, f32[4,1024]{1,0:T(4,128)}) custom-call(bf16[8,1024]{1,0:T(8,128)(2,1)S(1)} %pad_maximum_fusion.refs_0_, bf16[8,1024]{1,0:T(8,128)(2,1)S(1)} %collective-permute-done.2.refs_1_, bf16[8,1024]{1,0:T(8,128)(2,1)S(1)} %collective-permute-done.3.refs_2_, bf16[8,1024]{1,0:T(8,128)(2,1)S(1)} %collective-permute-done.4.refs_3_, ...), custom_call_target="tpu_custom_call" | custom-call | tf_op jit(solution)/shard_map/pallas_call | solution.py:172
  (4 shorter events, 0.0 us)
Async XLA Ops:
  0.6 14.2 %copy-start = (bf16[512,1024]{1,0:T(8,128)(2,1)S(1)}, bf16[512,1024]{1,0:T(8,128)(2,1)}, u32[]{:S(2)}) copy-start(bf16[512,1024]{1,0:T(8,128)(2,1)} %param.11) | copy-start | bytes 3145732
  0.6 6.6 %copy-start.1 = (s32[4]{0:T(128)S(1)}, s32[4]{0:T(128)}, u32[]{:S(2)}) copy-start(s32[4]{0:T(128)} %param.8) | copy-start | bytes 52
  4.2 4.9 %collective-permute-start = (f16[64,256]{1,0:T(8,128)(2,1)S(1)}, f16[64,256]{1,0:T(8,128)(2,1)S(1)}, u32[]{:S(2)}, u32[]{:S(2)}) collective-permute-start(f16[64,256]{1,0:T(8,128)(2,1)S(1)} %convert_element_type.24), channel_id=1, source_target_pairs={{0,2},{2,0},{1,3},{3,1},{4,6},{6,4},{5,7},{7,5},{8,10},{10,8},{9,1... | collective-permute-start | bytes 98312 | tf_op jit(solution)/shard_map/ppermute | solution.py:196
  9.6 1.2 %collective-permute-start.1 = (bf16[4,1024]{1,0:T(4,128)(2,1)S(1)}, bf16[4,1024]{1,0:T(4,128)(2,1)S(1)}, u32[]{:S(2)}, u32[]{:S(2)}) collective-permute-start(bf16[4,1024]{1,0:T(4,128)(2,1)S(1)} %shard_map.78), channel_id=1, source_target_pairs={{0,1},{1,0},{4,5},{5,4},{8,9},{9,8},{12,13},{13,12},{2,3},{3,2},{6... | collective-permute-start | bytes 24584 | tf_op jit(solution)/shard_map/ppermute | solution.py:207
  10.8 4.8 %collective-permute-start.3 = (bf16[8,1024]{1,0:T(8,128)(2,1)S(1)}, bf16[8,1024]{1,0:T(8,128)(2,1)S(1)}, u32[]{:S(2)}, u32[]{:S(2)}) collective-permute-start(bf16[8,1024]{1,0:T(8,128)(2,1)S(1)} %pad_maximum_fusion.refs_0_), channel_id=1, source_target_pairs={{0,4},{1,9},{4,8},{5,13},{8,12},{9,0},{12,5},{13,1},{2,6},{3,11},{... | collective-permute-start | bytes 49160 | tf_op jit(solution)/shard_map/ppermute | solution.py:210
  12.9 3.5 %collective-permute-start.2 = (bf16[8,1024]{1,0:T(8,128)(2,1)S(1)}, bf16[8,1024]{1,0:T(8,128)(2,1)S(1)}, u32[]{:S(2)}, u32[]{:S(2)}) collective-permute-start(bf16[8,1024]{1,0:T(8,128)(2,1)S(1)} %pad_maximum_fusion.refs_0_), channel_id=1, source_target_pairs={{0,13},{1,12},{4,1},{5,0},{8,4},{9,5},{12,9},{13,8},{2,15},{3,14},... | collective-permute-start | bytes 49160 | tf_op jit(solution)/shard_map/ppermute | solution.py:209
  15.2 1.2 %collective-permute-start.5 = (f32[4,512]{1,0:T(4,128)S(1)}, f32[4,512]{1,0:T(4,128)S(1)}, u32[]{:S(2)}, u32[]{:S(2)}) collective-permute-start(f32[4,512]{1,0:T(4,128)S(1)} %fusion.2), channel_id=1, source_target_pairs={{0,1},{1,0},{4,5},{5,4},{8,9},{9,8},{12,13},{13,12},{2,3},{3,2},{6... | collective-permute-start | bytes 24584 | tf_op jit(solution)/shard_map/ppermute | solution.py:214
  15.6 1.2 %collective-permute-start.4 = (bf16[8,1024]{1,0:T(8,128)(2,1)S(1)}, bf16[8,1024]{1,0:T(8,128)(2,1)S(1)}, u32[]{:S(2)}, u32[]{:S(2)}) collective-permute-start(bf16[8,1024]{1,0:T(8,128)(2,1)S(1)} %collective-permute-done.3.refs_2_), channel_id=1, source_target_pairs={{0,1},{1,0},{4,5},{5,4},{8,9},{9,8},{12,13},{13,12},{2,3},{3,2},{6... | collective-permute-start | bytes 49160 | tf_op jit(solution)/shard_map/ppermute | solution.py:211

commit v7 on v6

--- a/solution.py
+++ b/solution.py
@@ -15,8 +15,9 @@
 CONTRACT_FIRST = (((0,), (0,)), ((), ()))
 
 
-def chunk_of(width):
-    return width if width <= 2048 else next(size for size in (1792, 2048, 1024, 512, 256, 128) if width % size == 0)
+def first_chunk(width):
+    small = width // 7
+    return small if width % 7 == 0 and small % 128 == 0 else 0
 
 
 def tree_sum(terms):
@@ -25,62 +26,79 @@
     return terms[0]
 
 
-def project_kernel(scales, hidden, out_grad, proj_in, proj_out, out, hid, og, pin, pout, sems):
+def project_kernel(scales, hidden, out_grad, lengths, proj_in, proj_out, out, hid, og, pin, pout, limits, sems):
+    rows, width = hidden.shape
     k_in = pin.shape[0]
-    sides = ((out_grad, proj_out, og, pout), (hidden, proj_in, hid, pin))
-
-    def part_copy(which, n):
-        src, _, dst, _ = sides[which]
-        size = chunk_of(src.shape[1])
-        lanes = pl.ds(n * size if isinstance(n, int) else pl.multiple_of(n * size, size), size)
-        return pltpu.make_async_copy(src.at[:, lanes], dst.at[:, lanes], sems.at[which, 1 + n])
-
-    def weight_copy(which):
-        return pltpu.make_async_copy(sides[which][1], sides[which][3], sems.at[which, 0])
-
-    counts = [side[0].shape[1] // chunk_of(side[0].shape[1]) for side in sides]
-    for which in (0, 1):
-        weight_copy(which).start()
-        for n in range(counts[which]):
-            part_copy(which, n).start()
-    for which in (0, 1):
-        _, _, dst, dst_w = sides[which]
-        size = chunk_of(dst.shape[1])
+    small = first_chunk(width)
+    half = (width - small) // 2
+
+    def copies_of(n):
+        if isinstance(n, int) and n == 0:
+            lanes = pl.ds(0, small)
+        elif isinstance(n, int) and n == 1:
+            return [pltpu.make_async_copy(proj_out, pout, sems.at[0, 1]), pltpu.make_async_copy(out_grad, og, sems.at[1, 1])]
+        else:
+            lanes = pl.ds(small + (n - 2) * half, half)
+        return [
+            pltpu.make_async_copy(proj_in.at[:, lanes], pin.at[:, lanes], sems.at[0, n]),
+            pltpu.make_async_copy(hidden.at[:, lanes], hid.at[:, lanes], sems.at[1, n]),
+        ]
+
+    def partial(weights, data, at, size):
         depth = min(size, DEPTH)
-        weight_copy(which).wait()
-
-        def step(n, total):
-            part_copy(which, n).wait()
-            terms = []
-            for k in range(0, size, depth):
-                lanes = pl.ds(pl.multiple_of(n * size + k, depth), depth)
-                terms.append(lax.dot_general(dst_w[:, lanes], dst[:, lanes], CONTRACT_LAST,
-                                             preferred_element_type=jnp.float32))
-            return total + tree_sum(terms)
-
-        zero = jnp.zeros((dst_w.shape[0], dst.shape[0]), jnp.float32)
-        total = lax.fori_loop(0, counts[which], step, zero)
-        if which == 0:
-            out[k_in:] = total * scales[1]
-        else:
-            out[:k_in] = total * scales[0]
-
-
-def project(hidden, out_grad, proj_in, proj_out, scales):
+        terms = []
+        for k in range(0, size, depth):
+            lanes = pl.ds(at + k if isinstance(at, int) else pl.multiple_of(at + k, 128), depth)
+            terms.append(lax.dot_general(weights[:, lanes], data[:, lanes], CONTRACT_LAST,
+                                         preferred_element_type=jnp.float32))
+        return tree_sum(terms)
+
+    steps = range(0 if small else 1, 4)
+    for n in steps:
+        for copy in copies_of(n):
+            copy.start()
+    bounds = pltpu.make_async_copy(lengths, limits, sems.at[0, 4])
+    bounds.start()
+    total = jnp.zeros((k_in, rows), jnp.float32)
+    if small:
+        for copy in copies_of(0):
+            copy.wait()
+        total = partial(pin, hid, 0, small)
+    for copy in copies_of(1):
+        copy.wait()
+    out[k_in:] = partial(pout, og, 0, og.shape[1]) * scales[1]
+
+    def step(n, total):
+        for copy in copies_of(n):
+            copy.wait()
+        return total + partial(pin, hid, small + (n - 2) * half, half)
+
+    total = lax.fori_loop(2, 4, step, total)
+    bounds.wait()
+    slot = lax.broadcasted_iota(jnp.int32, (1, rows), 1)
+    limit = jnp.zeros((1, rows), jnp.int32)
+    for e in range(lengths.shape[0]):
+        limit = jnp.where(slot >= e * SEQ, e * SEQ + limits[e], limit)
+    out[:k_in] = jnp.where(slot < limit, total * scales[0], 0.0)
+
+
+def project(hidden, out_grad, lengths, proj_in, proj_out, scales):
     rows, width = hidden.shape
     narrow = out_grad.shape[1]
     k_in, k_out = proj_in.shape[1], proj_out.shape[1]
+    operands = (hidden, out_grad, lengths, proj_in.T, proj_out.T)
     return pl.pallas_call(
         functools.partial(project_kernel, scales),
         out_shape=jax.ShapeDtypeStruct((k_in + k_out, rows), jnp.float32),
-        in_specs=[pl.BlockSpec(memory_space=pltpu.HBM)] * 4,
+        in_specs=[pl.BlockSpec(memory_space=pltpu.HBM)] * 5,
         out_specs=pl.BlockSpec(memory_space=pltpu.VMEM),
         scratch_shapes=[
             pltpu.VMEM((rows, width), jnp.bfloat16),
             pltpu.VMEM((rows, narrow), jnp.bfloat16),
             pltpu.VMEM((k_in, width), jnp.bfloat16),
             pltpu.VMEM((k_out, narrow), jnp.bfloat16),
-            pltpu.SemaphoreType.DMA((2, 1 + max(width // chunk_of(width), narrow // chunk_of(narrow)))),
+            pltpu.SMEM(lengths.shape, jnp.int32),
+            pltpu.SemaphoreType.DMA((2, 5)),
         ],
         compiler_params=pltpu.CompilerParams(vmem_limit_bytes=24 << 20),
         cost_estimate=pl.CostEstimate(
@@ -88,16 +106,16 @@
             bytes_accessed=2 * rows * (width + narrow) + 2 * (width * k_in + narrow * k_out),
             transcendentals=0,
         ),
-    )(*(pltpu.with_memory_space_constraint(x, pltpu.HBM) for x in (hidden, out_grad, proj_in.T, proj_out.T)))
-
-
-def grads_kernel(k_in, scales, mask, *refs):
+    )(*(pltpu.with_memory_space_constraint(x, pltpu.HBM) for x in operands))
+
+
+def grads_kernel(k_in, scales, *refs):
     *pieces, out = refs
     both = pieces[0][...]
     for piece in pieces[1:]:
         both = both + piece[...]
     rows = both.shape[1]
-    act = both[:k_in] * (mask[...] * (1.0 / scales[0]))
+    act = both[:k_in] * (1.0 / scales[0])
     grad = both[k_in:] * (1.0 / scales[1])
     row = lax.broadcasted_iota(jnp.int32, (16, rows), 0)
     col = lax.broadcasted_iota(jnp.int32, (16, rows), 1)
@@ -115,16 +133,16 @@
         out[:, at * k_out:(at + per) * k_out] = total[:out.shape[0]].astype(jnp.bfloat16)
 
 
-def example_grads(mask, pieces, k_in, k_out, scales):
+def example_grads(pieces, k_in, k_out, scales):
     vmem = pl.BlockSpec(memory_space=pltpu.VMEM)
     return pl.pallas_call(
         functools.partial(grads_kernel, k_in, scales),
-        out_shape=jax.ShapeDtypeStruct((mask.shape[1] // SEQ, k_in * k_out), jnp.bfloat16),
-        in_specs=[vmem] * (1 + len(pieces)),
+        out_shape=jax.ShapeDtypeStruct((pieces[0].shape[1] // SEQ, k_in * k_out), jnp.bfloat16),
+        in_specs=[vmem] * len(pieces),
         out_specs=vmem,
         compiler_params=pltpu.CompilerParams(vmem_limit_bytes=6 << 20),
         cost_estimate=pl.CostEstimate(flops=1 << 33, bytes_accessed=0, transcendentals=0),
-    )(mask, *pieces)
+    )(*pieces)
 
 
 def finish_kernel(examples, n_pieces, n_raw, *refs):
@@ -182,36 +200,31 @@
 def per_device(hidden, out_grad, lengths, proj_in, proj_out, test_proj):
     k_in, k_out = proj_in.shape[1], proj_out.shape[1]
     flat = k_in * k_out
-    rows = hidden.shape[0]
     group = ("dp", "sub")
     sharers = lax.axis_size(group)
     examples = lengths.shape[0] * sharers
-    n_sub = lax.axis_size("sub")
-
-    paired = lax.axis_size("mp") == 2
-    scales = (128.0, 4.0) if paired else (1.0, 1.0)
-    both = project(hidden, out_grad, proj_in, proj_out, scales)
-    if paired:
+    crossed = lax.axis_size("mp") == 2 and lax.axis_size("sub") == 2
+    scales = (128.0, 4.0) if crossed else (1.0, 1.0)
+    both = project(hidden, out_grad, lengths, proj_in, proj_out, scales)
+    if crossed:
         sent = lax.optimization_barrier(both.astype(jnp.float16))
-        came = lax.ppermute(sent, "mp", [(0, 1), (1, 0)])
-        pieces = [sent.astype(jnp.float32), came.astype(jnp.float32)]
-    else:
-        pieces = [lax.psum(both, "mp")]
-    lengths, _ = lax.optimization_barrier((lengths, both))
-    slots = jnp.arange(SEQ, dtype=jnp.int32)
-    mask = (slots[None, :] < lengths[:, None]).astype(jnp.float32).reshape(1, rows)
-    grads = example_grads(mask, pieces, k_in, k_out, scales)
-
-    if n_sub == 2 and lax.axis_size("dp") == 4:
+        far = lax.ppermute(sent, ("mp", "sub"), [(0, 3), (1, 2), (2, 1), (3, 0)])
+        near = lax.ppermute(sent, "sub", [(0, 1), (1, 0)])
+        made = example_grads([near.astype(jnp.float32), far.astype(jnp.float32)], k_in, k_out, scales)
+        grads = lax.ppermute(made, "sub", [(0, 1), (1, 0)])
+    else:
+        grads = example_grads([lax.psum(both, "mp")], k_in, k_out, scales)
+
+    if crossed and lax.axis_size("dp") == 4:
         swap = [(i, i ^ 1) for i in range(sharers)]
-        came = lax.ppermute(grads, group, swap)
-        held = jnp.concatenate([grads, came], axis=0)
+        for_other = jnp.einsum("ep,qp->eq", made, test_proj, preferred_element_type=jnp.float32)
+        grads, for_other = lax.optimization_barrier((grads, for_other))
+        held = jnp.concatenate([made, grads], axis=0)
+        fetched = lax.ppermute(held, group, list(enumerate(SWAPPED_SEND)))
         direct = lax.ppermute(held, group, list(enumerate(DIRECT_SEND)))
-        fetched = lax.ppermute(held, group, list(enumerate(SWAPPED_SEND)))
         gathered = [held, direct, fetched, lax.ppermute(fetched, group, swap)]
-        near = jnp.einsum("ep,qp->eq", grads, test_proj, preferred_element_type=jnp.float32)
-        for_other = jnp.einsum("ep,qp->eq", came, test_proj, preferred_element_type=jnp.float32)
-        raw = [near, lax.ppermute(for_other, group, swap)]
+        own = jnp.einsum("ep,qp->eq", grads, test_proj, preferred_element_type=jnp.float32)
+        raw = [own, lax.ppermute(for_other, group, swap)]
     else:
         tests = lax.all_gather(test_proj, "sub", axis=0, tiled=True)
         raw = [jnp.einsum("ep,qp->eq", grads, tests, preferred_element_type=jnp.float32)]

time: 18 us -> 17.6 us (0.978)
  waiting for transfers between devices: 3.39 us -> 2.03 us
  starting transfers between devices: 7.84 us -> 9.09 us
  Pallas kernels: 5.04 us -> 4.85 us
    ppermute x3 -> x4, waiting for transfers between devices: 2.97 us -> 1.56 us  [the longest x1 1.1 us: per_device(): far = lax.ppermute(sent, ('mp', 'sub'), [(0, 3), (1, 2), (2, 1), (3, 0)])]
    ppermute x3 -> x4, starting transfers between devices: 3.4 us -> 4.01 us  [the longest x1 2.44 us: per_device(): far = lax.ppermute(sent, ('mp', 'sub'), [(0, 3), (1, 2), (2, 1), (3, 0)])]
    ppermute x1, starting transfers between devices: 0.4 us -> 0.79 us  [per_device(): gathered = [held, direct, fetched, lax.ppermute(fetched, group, swap)]]
    ppermute x1, starting transfers between devices: 2.16 us -> 2.43 us  [per_device(): fetched = lax.ppermute(held, group, list(enumerate(SWAPPED_SEND)))]
    pallas_call x1, Pallas kernels: 3.57 us -> 3.37 us  [project(): pl.pallas_call(functools.partial(project_kernel, scales), out_shape=jax.S...]
  transfers between devices with their start and end apart: 6 -> 7, of which waited for: 4 -> 4; matrix products, arithmetic and copies ran while one was open for 5% -> 4% of each run, Pallas kernels for 0% -> 0%
where the time goes in v7:
time: 17.6 us; the launch traced here: 17.4 us
  starting transfers between devices  9.09 us (52%)
  Pallas kernels  4.85 us (28%)
  waiting for transfers between devices  2.03 us (12%)
  matrix products  0.74 us (4%)
  between operations  0.68 us (4%)
    pallas_call x1, Pallas kernels, project(): pl.pallas_call(functools.partial(project_kernel, scales), out_shape=jax.S...  3.37 us
    ppermute x1, starting transfers between devices, per_device(): far = lax.ppermute(sent, ('mp', 'sub'), [(0, 3), (1, 2), (2, 1), (3, 0)])  2.44 us
    ppermute x1, starting transfers between devices, per_device(): fetched = lax.ppermute(held, group, list(enumerate(SWAPPED_SEND)))  2.43 us
    ppermute x1, starting transfers between devices, per_device(): direct = lax.ppermute(held, group, list(enumerate(DIRECT_SEND)))  1.87 us
    ppermute x1, waiting for transfers between devices, per_device(): far = lax.ppermute(sent, ('mp', 'sub'), [(0, 3), (1, 2), (2, 1), (3, 0)])  1.1 us
    pallas_call x1, Pallas kernels, finish(): pl.pallas_call(functools.partial(finish_kernel, examples, len(pieces), le...  1.07 us
    ppermute x1, starting transfers between devices, per_device(): gathered = [held, direct, fetched, lax.ppermute(fetched, group, swap)]  0.79 us
    ppermute x1, starting transfers between devices, per_device(): near = lax.ppermute(sent, 'sub', [(0, 1), (1, 0)])  0.67 us
  transfers between devices with their start and end apart: 7, of which 4 were waited for; matrix products, arithmetic and copies ran while one was open for 4% of the time, Pallas kernels for 0%

profile of v7, /device:TPU:0, one launch (start us, length us, event | category | flops | bytes accessed | tf_op | source)
XLA Modules:
  0.0 17.4 jit_solution(2667749561136147578)
XLA Ops:
  0.6 0.0 copy-start
  0.6 3.4 %shard_map.77 = f32[64,256]{1,0:T(8,128)S(1)} custom-call(bf16[256,7168]{1,0:T(8,128)(2,1)} %hidden.1, bf16[256,2048]{1,0:T(8,128)(2,1)} %out_grad.1, s32[4]{0:T(128)} %lengths.1, bf16[32,7168]{1,0:T(8,128)(2,1)} %bitcast.6, bf16[32,2048]{1,0:T(8,128)(2,1)} %bitcast.7), custom_call_target="tpu_custom_call" | custom-call | flops 150994944 | bytes 5308416 | tf_op jit(solution)/shard_map/pallas_call | solution.py:90
  4.0 2.4 %collective-permute-start.1 = (f16[64,256]{1,0:T(8,128)(2,1)S(1)}, f16[64,256]{1,0:T(8,128)(2,1)S(1)}, u32[]{:S(2)}, u32[]{:S(2)}) collective-permute-start(f16[64,256]{1,0:T(8,128)(2,1)S(1)} %convert_element_type.9), channel_id=1, source_target_pairs={{0,3},{1,2},{2,1},{3,0},{4,7},{5,6},{6,5},{7,4},{8,11},{9,10},{10,... | collective-permute-start | bytes 98312 | tf_op jit(solution)/shard_map/ppermute | solution.py:211
  6.5 0.7 %collective-permute-start = (f16[64,256]{1,0:T(8,128)(2,1)S(1)}, f16[64,256]{1,0:T(8,128)(2,1)S(1)}, u32[]{:S(2)}, u32[]{:S(2)}) collective-permute-start(f16[64,256]{1,0:T(8,128)(2,1)S(1)} %convert_element_type.9), channel_id=1, source_target_pairs={{0,1},{1,0},{2,3},{3,2},{4,5},{5,4},{6,7},{7,6},{8,9},{9,8},{10,11... | collective-permute-start | bytes 98312 | tf_op jit(solution)/shard_map/ppermute | solution.py:212
  7.2 1.1 %collective-permute-done.1 = f16[64,256]{1,0:T(8,128)(2,1)S(1)} collective-permute-done((f16[64,256]{1,0:T(8,128)(2,1)S(1)}, f16[64,256]{1,0:T(8,128)(2,1)S(1)}, u32[]{:S(2)}, u32[]{:S(2)}) %collective-permute-start.1) | collective-permute-done | bytes 32800 | tf_op jit(solution)/shard_map/ppermute | solution.py:211
  8.3 0.0 collective-permute-done
  8.3 0.4 %shard_map.78 = bf16[4,1024]{1,0:T(4,128)(2,1)S(1)} custom-call(f32[64,256]{1,0:T(8,128)S(1)} %convert_element_type.10.refs_0_, f32[64,256]{1,0:T(8,128)S(1)} %convert_element_type.11.refs_1_), custom_call_target="tpu_custom_call" | custom-call | flops 8589934592 | tf_op jit(solution)/shard_map/pallas_call | solution.py:138
  8.7 0.5 %collective-permute-start.2 = (bf16[4,1024]{1,0:T(4,128)(2,1)S(1)}, bf16[4,1024]{1,0:T(4,128)(2,1)S(1)}, u32[]{:S(2)}, u32[]{:S(2)}) collective-permute-start(bf16[4,1024]{1,0:T(4,128)(2,1)S(1)} %shard_map.78), channel_id=1, source_target_pairs={{0,1},{1,0},{2,3},{3,2},{4,5},{5,4},{6,7},{7,6},{8,9},{9,8},{10,11... | collective-permute-start | bytes 24584 | tf_op jit(solution)/shard_map/ppermute | solution.py:214
  9.2 0.0 copy-done
  9.2 0.4 %fusion = f32[4,512]{1,0:T(4,128)S(1)} fusion(bf16[4,1024]{1,0:T(4,128)(2,1)S(1)} %shard_map.78, bf16[512,1024]{1,0:T(8,128)(2,1)S(1)} %copy-done), kind=kOutput, calls=%fused_computation.1 | convolution fusion | flops 4194304 | bytes 1064960 | tf_op jit(solution)/shard_map/ep,qp->eq/dot_general | solution.py:220
  9.6 0.5 %collective-permute-done.2 = bf16[4,1024]{1,0:T(4,128)(2,1)S(1)} collective-permute-done((bf16[4,1024]{1,0:T(4,128)(2,1)S(1)}, bf16[4,1024]{1,0:T(4,128)(2,1)S(1)}, u32[]{:S(2)}, u32[]{:S(2)}) %collective-permute-start.2) | collective-permute-done | bytes 8224 | tf_op jit(solution)/shard_map/ppermute | solution.py:214
  10.1 2.4 %collective-permute-start.4 = (bf16[8,1024]{1,0:T(8,128)(2,1)S(1)}, bf16[8,1024]{1,0:T(8,128)(2,1)S(1)}, u32[]{:S(2)}, u32[]{:S(2)}) collective-permute-start(bf16[8,1024]{1,0:T(8,128)(2,1)S(1)} %pad_maximum_fusion.refs_0_), channel_id=1, source_target_pairs={{0,4},{1,9},{4,8},{5,13},{8,12},{9,0},{12,5},{13,1},{2,6},{3,11},{... | collective-permute-start | bytes 49160 | tf_op jit(solution)/shard_map/ppermute | solution.py:223
  12.5 1.9 %collective-permute-start.3 = (bf16[8,1024]{1,0:T(8,128)(2,1)S(1)}, bf16[8,1024]{1,0:T(8,128)(2,1)S(1)}, u32[]{:S(2)}, u32[]{:S(2)}) collective-permute-start(bf16[8,1024]{1,0:T(8,128)(2,1)S(1)} %pad_maximum_fusion.refs_0_), channel_id=1, source_target_pairs={{0,13},{1,12},{4,1},{5,0},{8,4},{9,5},{12,9},{13,8},{2,15},{3,14},... | collective-permute-start | bytes 49160 | tf_op jit(solution)/shard_map/ppermute | solution.py:224
  14.4 0.4 %collective-permute-start.6 = (f32[4,512]{1,0:T(4,128)S(1)}, f32[4,512]{1,0:T(4,128)S(1)}, u32[]{:S(2)}, u32[]{:S(2)}) collective-permute-start(f32[4,512]{1,0:T(4,128)S(1)} %fusion), channel_id=1, source_target_pairs={{0,1},{1,0},{4,5},{5,4},{8,9},{9,8},{12,13},{13,12},{2,3},{3,2},{6... | collective-permute-start | bytes 24584 | tf_op jit(solution)/shard_map/ppermute | solution.py:227
  14.7 0.0 collective-permute-done.4.refs_2_
  14.7 0.8 %collective-permute-start.5 = (bf16[8,1024]{1,0:T(8,128)(2,1)S(1)}, bf16[8,1024]{1,0:T(8,128)(2,1)S(1)}, u32[]{:S(2)}, u32[]{:S(2)}) collective-permute-start(bf16[8,1024]{1,0:T(8,128)(2,1)S(1)} %collective-permute-done.4.refs_2_), channel_id=1, source_target_pairs={{0,1},{1,0},{4,5},{5,4},{8,9},{9,8},{12,13},{13,12},{2,3},{3,2},{6... | collective-permute-start | bytes 49160 | tf_op jit(solution)/shard_map/ppermute | solution.py:225
  15.5 0.4 %fusion.1.refs_4_ = f32[4,512]{1,0:T(4,128)S(1)} fusion(bf16[4,1024]{1,0:T(4,128)(2,1)S(1)} %collective-permute-done.2, bf16[512,1024]{1,0:T(8,128)(2,1)S(1)} %copy-done), kind=kOutput, calls=%fused_computation.2 | convolution fusion | flops 4194304 | bytes 1064960 | tf_op jit(solution)/shard_map/ep,qp->eq/dot_general | solution.py:226
  15.9 0.0 collective-permute-done.6.refs_5_
  15.9 0.1 collective-permute-done.3.refs_1_
  16.0 0.4 %collective-permute-done.5.refs_3_ = bf16[8,1024]{1,0:T(8,128)(2,1)S(1)} collective-permute-done((bf16[8,1024]{1,0:T(8,128)(2,1)S(1)}, bf16[8,1024]{1,0:T(8,128)(2,1)S(1)}, u32[]{:S(2)}, u32[]{:S(2)}) %collective-permute-start.5) | collective-permute-done | bytes 16416 | tf_op jit(solution)/shard_map/ppermute | solution.py:225
  16.4 1.1 %shard_map.79 = (f32[128,1024]{1,0:T(8,128)}, f32[4,1024]{1,0:T(4,128)}) custom-call(bf16[8,1024]{1,0:T(8,128)(2,1)S(1)} %pad_maximum_fusion.refs_0_, bf16[8,1024]{1,0:T(8,128)(2,1)S(1)} %collective-permute-done.3.refs_1_, bf16[8,1024]{1,0:T(8,128)(2,1)S(1)} %collective-permute-done.4.refs_2_, bf16[8,1024]{1,0:T(8,128)(2,1)S(1)} %collective-permute-done.5.refs_3_, ...), custom_call_target="tpu_custom_call" | custom-call | tf_op jit(solution)/shard_map/pallas_call | solution.py:190
  (4 shorter events, 0.0 us)
Async XLA Ops:
  0.6 8.6 %copy-start = (bf16[512,1024]{1,0:T(8,128)(2,1)S(1)}, bf16[512,1024]{1,0:T(8,128)(2,1)}, u32[]{:S(2)}) copy-start(bf16[512,1024]{1,0:T(8,128)(2,1)} %param.11) | copy-start | bytes 3145732
  4.0 4.2 %collective-permute-start.1 = (f16[64,256]{1,0:T(8,128)(2,1)S(1)}, f16[64,256]{1,0:T(8,128)(2,1)S(1)}, u32[]{:S(2)}, u32[]{:S(2)}) collective-permute-start(f16[64,256]{1,0:T(8,128)(2,1)S(1)} %convert_element_type.9), channel_id=1, source_target_pairs={{0,3},{1,2},{2,1},{3,0},{4,7},{5,6},{6,5},{7,4},{8,11},{9,10},{10,... | collective-permute-start | bytes 98312 | tf_op jit(solution)/shard_map/ppermute | solution.py:211
  6.5 1.8 %collective-permute-start = (f16[64,256]{1,0:T(8,128)(2,1)S(1)}, f16[64,256]{1,0:T(8,128)(2,1)S(1)}, u32[]{:S(2)}, u32[]{:S(2)}) collective-permute-start(f16[64,256]{1,0:T(8,128)(2,1)S(1)} %convert_element_type.9), channel_id=1, source_target_pairs={{0,1},{1,0},{2,3},{3,2},{4,5},{5,4},{6,7},{7,6},{8,9},{9,8},{10,11... | collective-permute-start | bytes 98312 | tf_op jit(solution)/shard_map/ppermute | solution.py:212
  8.7 1.3 %collective-permute-start.2 = (bf16[4,1024]{1,0:T(4,128)(2,1)S(1)}, bf16[4,1024]{1,0:T(4,128)(2,1)S(1)}, u32[]{:S(2)}, u32[]{:S(2)}) collective-permute-start(bf16[4,1024]{1,0:T(4,128)(2,1)S(1)} %shard_map.78), channel_id=1, source_target_pairs={{0,1},{1,0},{2,3},{3,2},{4,5},{5,4},{6,7},{7,6},{8,9},{9,8},{10,11... | collective-permute-start | bytes 24584 | tf_op jit(solution)/shard_map/ppermute | solution.py:214
  10.1 4.7 %collective-permute-start.4 = (bf16[8,1024]{1,0:T(8,128)(2,1)S(1)}, bf16[8,1024]{1,0:T(8,128)(2,1)S(1)}, u32[]{:S(2)}, u32[]{:S(2)}) collective-permute-start(bf16[8,1024]{1,0:T(8,128)(2,1)S(1)} %pad_maximum_fusion.refs_0_), channel_id=1, source_target_pairs={{0,4},{1,9},{4,8},{5,13},{8,12},{9,0},{12,5},{13,1},{2,6},{3,11},{... | collective-permute-start | bytes 49160 | tf_op jit(solution)/shard_map/ppermute | solution.py:223
  12.5 3.5 %collective-permute-start.3 = (bf16[8,1024]{1,0:T(8,128)(2,1)S(1)}, bf16[8,1024]{1,0:T(8,128)(2,1)S(1)}, u32[]{:S(2)}, u32[]{:S(2)}) collective-permute-start(bf16[8,1024]{1,0:T(8,128)(2,1)S(1)} %pad_maximum_fusion.refs_0_), channel_id=1, source_target_pairs={{0,13},{1,12},{4,1},{5,0},{8,4},{9,5},{12,9},{13,8},{2,15},{3,14},... | collective-permute-start | bytes 49160 | tf_op jit(solution)/shard_map/ppermute | solution.py:224
  14.4 1.5 %collective-permute-start.6 = (f32[4,512]{1,0:T(4,128)S(1)}, f32[4,512]{1,0:T(4,128)S(1)}, u32[]{:S(2)}, u32[]{:S(2)}) collective-permute-start(f32[4,512]{1,0:T(4,128)S(1)} %fusion), channel_id=1, source_target_pairs={{0,1},{1,0},{4,5},{5,4},{8,9},{9,8},{12,13},{13,12},{2,3},{3,2},{6... | collective-permute-start | bytes 24584 | tf_op jit(solution)/shard_map/ppermute | solution.py:227
  14.7 1.6 %collective-permute-start.5 = (bf16[8,1024]{1,0:T(8,128)(2,1)S(1)}, bf16[8,1024]{1,0:T(8,128)(2,1)S(1)}, u32[]{:S(2)}, u32[]{:S(2)}) collective-permute-start(bf16[8,1024]{1,0:T(8,128)(2,1)S(1)} %collective-permute-done.4.refs_2_), channel_id=1, source_target_pairs={{0,1},{1,0},{4,5},{5,4},{8,9},{9,8},{12,13},{13,12},{2,3},{3,2},{6... | collective-permute-start | bytes 49160 | tf_op jit(solution)/shard_map/ppermute | solution.py:225

commit v8 on v7

--- a/solution.py
+++ b/solution.py
@@ -46,12 +46,13 @@
 
     def partial(weights, data, at, size):
         depth = min(size, DEPTH)
-        terms = []
-        for k in range(0, size, depth):
+        terms = [], []
+        for n, k in enumerate(range(0, size, depth)):
             lanes = pl.ds(at + k if isinstance(at, int) else pl.multiple_of(at + k, 128), depth)
-            terms.append(lax.dot_general(weights[:, lanes], data[:, lanes], CONTRACT_LAST,
-                                         preferred_element_type=jnp.float32))
-        return tree_sum(terms)
+            left, right = (weights, data) if n % 2 == 0 else (data, weights)
+            terms[n % 2].append(lax.dot_general(left[:, lanes], right[:, lanes], CONTRACT_LAST,
+                                                preferred_element_type=jnp.float32))
+        return tree_sum(terms[0]), tree_sum(terms[1])
 
     steps = range(0 if small else 1, 4)
     for n in steps:
@@ -59,21 +60,25 @@
             copy.start()
     bounds = pltpu.make_async_copy(lengths, limits, sems.at[0, 4])
     bounds.start()
-    total = jnp.zeros((k_in, rows), jnp.float32)
+    act = jnp.zeros((k_in, rows), jnp.float32), jnp.zeros((rows, k_in), jnp.float32)
     if small:
         for copy in copies_of(0):
             copy.wait()
-        total = partial(pin, hid, 0, small)
+        act = partial(pin, hid, 0, small)
     for copy in copies_of(1):
         copy.wait()
-    out[k_in:] = partial(pout, og, 0, og.shape[1]) * scales[1]
-
-    def step(n, total):
+    grad = partial(pout, og, 0, og.shape[1])
+
+    def step(n, act):
         for copy in copies_of(n):
             copy.wait()
-        return total + partial(pin, hid, small + (n - 2) * half, half)
-
-    total = lax.fori_loop(2, 4, step, total)
+        more = partial(pin, hid, small + (n - 2) * half, half)
+        return act[0] + more[0], act[1] + more[1]
+
+    act = lax.fori_loop(2, 4, step, act)
+    turned = jnp.concatenate([act[1], grad[1]], axis=1).T
+    total = act[0] + turned[:k_in]
+    out[k_in:] = (grad[0] + turned[k_in:]) * scales[1]
     bounds.wait()
     slot = lax.broadcasted_iota(jnp.int32, (1, rows), 1)
     limit = jnp.zeros((1, rows), jnp.int32)

time: 17.6 us -> 17.7 us (level)
  no operation moved by 1% of the time
where the time goes in v8:
time: 17.7 us; the launch traced here: 17.5 us
  starting transfers between devices  9.08 us (51%)
  Pallas kernels  4.94 us (28%)
  waiting for transfers between devices  2.03 us (11%)
  matrix products  0.74 us (4%)
  between operations  0.68 us (4%)
    pallas_call x1, Pallas kernels, project(): pl.pallas_call(functools.partial(project_kernel, scales), out_shape=jax.S...  3.46 us
    ppermute x1, starting transfers between devices, per_device(): far = lax.ppermute(sent, ('mp', 'sub'), [(0, 3), (1, 2), (2, 1), (3, 0)])  2.44 us
    ppermute x1, starting transfers between devices, per_device(): fetched = lax.ppermute(held, group, list(enumerate(SWAPPED_SEND)))  2.42 us
    ppermute x1, starting transfers between devices, per_device(): direct = lax.ppermute(held, group, list(enumerate(DIRECT_SEND)))  1.87 us
    ppermute x1, waiting for transfers between devices, per_device(): far = lax.ppermute(sent, ('mp', 'sub'), [(0, 3), (1, 2), (2, 1), (3, 0)])  1.1 us
    pallas_call x1, Pallas kernels, finish(): pl.pallas_call(functools.partial(finish_kernel, examples, len(pieces), le...  1.06 us
    ppermute x1, starting transfers between devices, per_device(): gathered = [held, direct, fetched, lax.ppermute(fetched, group, swap)]  0.79 us
    ppermute x1, starting transfers between devices, per_device(): near = lax.ppermute(sent, 'sub', [(0, 1), (1, 0)])  0.68 us
  transfers between devices with their start and end apart: 7, of which 4 were waited for; matrix products, arithmetic and copies ran while one was open for 4% of the time, Pallas kernels for 0%

profile of v8, /device:TPU:0, one launch (start us, length us, event | category | flops | bytes accessed | tf_op | source)
XLA Modules:
  0.0 17.5 jit_solution(7609020632731571711)
XLA Ops:
  0.6 0.0 copy-start
  0.6 3.5 %shard_map.77 = f32[64,256]{1,0:T(8,128)S(1)} custom-call(bf16[256,7168]{1,0:T(8,128)(2,1)} %hidden.1, bf16[256,2048]{1,0:T(8,128)(2,1)} %out_grad.1, s32[4]{0:T(128)} %lengths.1, bf16[32,7168]{1,0:T(8,128)(2,1)} %bitcast.6, bf16[32,2048]{1,0:T(8,128)(2,1)} %bitcast.7), custom_call_target="tpu_custom_call" | custom-call | flops 150994944 | bytes 5308416 | tf_op jit(solution)/shard_map/pallas_call | solution.py:95
  4.1 2.4 %collective-permute-start.1 = (f16[64,256]{1,0:T(8,128)(2,1)S(1)}, f16[64,256]{1,0:T(8,128)(2,1)S(1)}, u32[]{:S(2)}, u32[]{:S(2)}) collective-permute-start(f16[64,256]{1,0:T(8,128)(2,1)S(1)} %convert_element_type.9), channel_id=1, source_target_pairs={{0,3},{1,2},{2,1},{3,0},{4,7},{5,6},{6,5},{7,4},{8,11},{9,10},{10,... | collective-permute-start | bytes 98312 | tf_op jit(solution)/shard_map/ppermute | solution.py:216
  6.6 0.7 %collective-permute-start = (f16[64,256]{1,0:T(8,128)(2,1)S(1)}, f16[64,256]{1,0:T(8,128)(2,1)S(1)}, u32[]{:S(2)}, u32[]{:S(2)}) collective-permute-start(f16[64,256]{1,0:T(8,128)(2,1)S(1)} %convert_element_type.9), channel_id=1, source_target_pairs={{0,1},{1,0},{2,3},{3,2},{4,5},{5,4},{6,7},{7,6},{8,9},{9,8},{10,11... | collective-permute-start | bytes 98312 | tf_op jit(solution)/shard_map/ppermute | solution.py:217
  7.2 1.1 %collective-permute-done.1 = f16[64,256]{1,0:T(8,128)(2,1)S(1)} collective-permute-done((f16[64,256]{1,0:T(8,128)(2,1)S(1)}, f16[64,256]{1,0:T(8,128)(2,1)S(1)}, u32[]{:S(2)}, u32[]{:S(2)}) %collective-permute-start.1) | collective-permute-done | bytes 32800 | tf_op jit(solution)/shard_map/ppermute | solution.py:216
  8.4 0.0 collective-permute-done
  8.4 0.4 %shard_map.78 = bf16[4,1024]{1,0:T(4,128)(2,1)S(1)} custom-call(f32[64,256]{1,0:T(8,128)S(1)} %convert_element_type.10.refs_0_, f32[64,256]{1,0:T(8,128)S(1)} %convert_element_type.11.refs_1_), custom_call_target="tpu_custom_call" | custom-call | flops 8589934592 | tf_op jit(solution)/shard_map/pallas_call | solution.py:143
  8.8 0.5 %collective-permute-start.2 = (bf16[4,1024]{1,0:T(4,128)(2,1)S(1)}, bf16[4,1024]{1,0:T(4,128)(2,1)S(1)}, u32[]{:S(2)}, u32[]{:S(2)}) collective-permute-start(bf16[4,1024]{1,0:T(4,128)(2,1)S(1)} %shard_map.78), channel_id=1, source_target_pairs={{0,1},{1,0},{2,3},{3,2},{4,5},{5,4},{6,7},{7,6},{8,9},{9,8},{10,11... | collective-permute-start | bytes 24584 | tf_op jit(solution)/shard_map/ppermute | solution.py:219
  9.3 0.0 copy-done
  9.3 0.4 %fusion = f32[4,512]{1,0:T(4,128)S(1)} fusion(bf16[4,1024]{1,0:T(4,128)(2,1)S(1)} %shard_map.78, bf16[512,1024]{1,0:T(8,128)(2,1)S(1)} %copy-done), kind=kOutput, calls=%fused_computation.1 | convolution fusion | flops 4194304 | bytes 1064960 | tf_op jit(solution)/shard_map/ep,qp->eq/dot_general | solution.py:225
  9.7 0.5 %collective-permute-done.2 = bf16[4,1024]{1,0:T(4,128)(2,1)S(1)} collective-permute-done((bf16[4,1024]{1,0:T(4,128)(2,1)S(1)}, bf16[4,1024]{1,0:T(4,128)(2,1)S(1)}, u32[]{:S(2)}, u32[]{:S(2)}) %collective-permute-start.2) | collective-permute-done | bytes 8224 | tf_op jit(solution)/shard_map/ppermute | solution.py:219
  10.2 2.4 %collective-permute-start.4 = (bf16[8,1024]{1,0:T(8,128)(2,1)S(1)}, bf16[8,1024]{1,0:T(8,128)(2,1)S(1)}, u32[]{:S(2)}, u32[]{:S(2)}) collective-permute-start(bf16[8,1024]{1,0:T(8,128)(2,1)S(1)} %pad_maximum_fusion.refs_0_), channel_id=1, source_target_pairs={{0,4},{1,9},{4,8},{5,13},{8,12},{9,0},{12,5},{13,1},{2,6},{3,11},{... | collective-permute-start | bytes 49160 | tf_op jit(solution)/shard_map/ppermute | solution.py:228
  12.6 1.9 %collective-permute-start.3 = (bf16[8,1024]{1,0:T(8,128)(2,1)S(1)}, bf16[8,1024]{1,0:T(8,128)(2,1)S(1)}, u32[]{:S(2)}, u32[]{:S(2)}) collective-permute-start(bf16[8,1024]{1,0:T(8,128)(2,1)S(1)} %pad_maximum_fusion.refs_0_), channel_id=1, source_target_pairs={{0,13},{1,12},{4,1},{5,0},{8,4},{9,5},{12,9},{13,8},{2,15},{3,14},... | collective-permute-start | bytes 49160 | tf_op jit(solution)/shard_map/ppermute | solution.py:229
  14.4 0.4 %collective-permute-start.6 = (f32[4,512]{1,0:T(4,128)S(1)}, f32[4,512]{1,0:T(4,128)S(1)}, u32[]{:S(2)}, u32[]{:S(2)}) collective-permute-start(f32[4,512]{1,0:T(4,128)S(1)} %fusion), channel_id=1, source_target_pairs={{0,1},{1,0},{4,5},{5,4},{8,9},{9,8},{12,13},{13,12},{2,3},{3,2},{6... | collective-permute-start | bytes 24584 | tf_op jit(solution)/shard_map/ppermute | solution.py:232
  14.8 0.0 collective-permute-done.4.refs_2_
  14.8 0.8 %collective-permute-start.5 = (bf16[8,1024]{1,0:T(8,128)(2,1)S(1)}, bf16[8,1024]{1,0:T(8,128)(2,1)S(1)}, u32[]{:S(2)}, u32[]{:S(2)}) collective-permute-start(bf16[8,1024]{1,0:T(8,128)(2,1)S(1)} %collective-permute-done.4.refs_2_), channel_id=1, source_target_pairs={{0,1},{1,0},{4,5},{5,4},{8,9},{9,8},{12,13},{13,12},{2,3},{3,2},{6... | collective-permute-start | bytes 49160 | tf_op jit(solution)/shard_map/ppermute | solution.py:230
  15.6 0.4 %fusion.1.refs_4_ = f32[4,512]{1,0:T(4,128)S(1)} fusion(bf16[4,1024]{1,0:T(4,128)(2,1)S(1)} %collective-permute-done.2, bf16[512,1024]{1,0:T(8,128)(2,1)S(1)} %copy-done), kind=kOutput, calls=%fused_computation.2 | convolution fusion | flops 4194304 | bytes 1064960 | tf_op jit(solution)/shard_map/ep,qp->eq/dot_general | solution.py:231
  16.0 0.0 collective-permute-done.6.refs_5_
  16.0 0.1 collective-permute-done.3.refs_1_
  16.1 0.4 %collective-permute-done.5.refs_3_ = bf16[8,1024]{1,0:T(8,128)(2,1)S(1)} collective-permute-done((bf16[8,1024]{1,0:T(8,128)(2,1)S(1)}, bf16[8,1024]{1,0:T(8,128)(2,1)S(1)}, u32[]{:S(2)}, u32[]{:S(2)}) %collective-permute-start.5) | collective-permute-done | bytes 16416 | tf_op jit(solution)/shard_map/ppermute | solution.py:230
  16.5 1.1 %shard_map.79 = (f32[128,1024]{1,0:T(8,128)}, f32[4,1024]{1,0:T(4,128)}) custom-call(bf16[8,1024]{1,0:T(8,128)(2,1)S(1)} %pad_maximum_fusion.refs_0_, bf16[8,1024]{1,0:T(8,128)(2,1)S(1)} %collective-permute-done.3.refs_1_, bf16[8,1024]{1,0:T(8,128)(2,1)S(1)} %collective-permute-done.4.refs_2_, bf16[8,1024]{1,0:T(8,128)(2,1)S(1)} %collective-permute-done.5.refs_3_, ...), custom_call_target="tpu_custom_call" | custom-call | tf_op jit(solution)/shard_map/pallas_call | solution.py:195
  (4 shorter events, 0.0 us)
Async XLA Ops:
  0.6 8.7 %copy-start = (bf16[512,1024]{1,0:T(8,128)(2,1)S(1)}, bf16[512,1024]{1,0:T(8,128)(2,1)}, u32[]{:S(2)}) copy-start(bf16[512,1024]{1,0:T(8,128)(2,1)} %param.11) | copy-start | bytes 3145732
  4.1 4.2 %collective-permute-start.1 = (f16[64,256]{1,0:T(8,128)(2,1)S(1)}, f16[64,256]{1,0:T(8,128)(2,1)S(1)}, u32[]{:S(2)}, u32[]{:S(2)}) collective-permute-start(f16[64,256]{1,0:T(8,128)(2,1)S(1)} %convert_element_type.9), channel_id=1, source_target_pairs={{0,3},{1,2},{2,1},{3,0},{4,7},{5,6},{6,5},{7,4},{8,11},{9,10},{10,... | collective-permute-start | bytes 98312 | tf_op jit(solution)/shard_map/ppermute | solution.py:216
  6.6 1.8 %collective-permute-start = (f16[64,256]{1,0:T(8,128)(2,1)S(1)}, f16[64,256]{1,0:T(8,128)(2,1)S(1)}, u32[]{:S(2)}, u32[]{:S(2)}) collective-permute-start(f16[64,256]{1,0:T(8,128)(2,1)S(1)} %convert_element_type.9), channel_id=1, source_target_pairs={{0,1},{1,0},{2,3},{3,2},{4,5},{5,4},{6,7},{7,6},{8,9},{9,8},{10,11... | collective-permute-start | bytes 98312 | tf_op jit(solution)/shard_map/ppermute | solution.py:217
  8.8 1.3 %collective-permute-start.2 = (bf16[4,1024]{1,0:T(4,128)(2,1)S(1)}, bf16[4,1024]{1,0:T(4,128)(2,1)S(1)}, u32[]{:S(2)}, u32[]{:S(2)}) collective-permute-start(bf16[4,1024]{1,0:T(4,128)(2,1)S(1)} %shard_map.78), channel_id=1, source_target_pairs={{0,1},{1,0},{2,3},{3,2},{4,5},{5,4},{6,7},{7,6},{8,9},{9,8},{10,11... | collective-permute-start | bytes 24584 | tf_op jit(solution)/shard_map/ppermute | solution.py:219
  10.2 4.7 %collective-permute-start.4 = (bf16[8,1024]{1,0:T(8,128)(2,1)S(1)}, bf16[8,1024]{1,0:T(8,128)(2,1)S(1)}, u32[]{:S(2)}, u32[]{:S(2)}) collective-permute-start(bf16[8,1024]{1,0:T(8,128)(2,1)S(1)} %pad_maximum_fusion.refs_0_), channel_id=1, source_target_pairs={{0,4},{1,9},{4,8},{5,13},{8,12},{9,0},{12,5},{13,1},{2,6},{3,11},{... | collective-permute-start | bytes 49160 | tf_op jit(solution)/shard_map/ppermute | solution.py:228
  12.6 3.5 %collective-permute-start.3 = (bf16[8,1024]{1,0:T(8,128)(2,1)S(1)}, bf16[8,1024]{1,0:T(8,128)(2,1)S(1)}, u32[]{:S(2)}, u32[]{:S(2)}) collective-permute-start(bf16[8,1024]{1,0:T(8,128)(2,1)S(1)} %pad_maximum_fusion.refs_0_), channel_id=1, source_target_pairs={{0,13},{1,12},{4,1},{5,0},{8,4},{9,5},{12,9},{13,8},{2,15},{3,14},... | collective-permute-start | bytes 49160 | tf_op jit(solution)/shard_map/ppermute | solution.py:229
  14.4 1.5 %collective-permute-start.6 = (f32[4,512]{1,0:T(4,128)S(1)}, f32[4,512]{1,0:T(4,128)S(1)}, u32[]{:S(2)}, u32[]{:S(2)}) collective-permute-start(f32[4,512]{1,0:T(4,128)S(1)} %fusion), channel_id=1, source_target_pairs={{0,1},{1,0},{4,5},{5,4},{8,9},{9,8},{12,13},{13,12},{2,3},{3,2},{6... | collective-permute-start | bytes 24584 | tf_op jit(solution)/shard_map/ppermute | solution.py:232
  14.8 1.6 %collective-permute-start.5 = (bf16[8,1024]{1,0:T(8,128)(2,1)S(1)}, bf16[8,1024]{1,0:T(8,128)(2,1)S(1)}, u32[]{:S(2)}, u32[]{:S(2)}) collective-permute-start(bf16[8,1024]{1,0:T(8,128)(2,1)S(1)} %collective-permute-done.4.refs_2_), channel_id=1, source_target_pairs={{0,1},{1,0},{4,5},{5,4},{8,9},{9,8},{12,13},{13,12},{2,3},{3,2},{6... | collective-permute-start | bytes 49160 | tf_op jit(solution)/shard_map/ppermute | solution.py:230

commit v9 on v7

--- a/solution.py
+++ b/solution.py
@@ -109,28 +109,47 @@
     )(*(pltpu.with_memory_space_constraint(x, pltpu.HBM) for x in operands))
 
 
+def halves(x):
+    high = x.astype(jnp.bfloat16)
+    return high, (x - high.astype(jnp.float32)).astype(jnp.bfloat16)
+
+
 def grads_kernel(k_in, scales, *refs):
     *pieces, out = refs
     both = pieces[0][...]
     for piece in pieces[1:]:
         both = both + piece[...]
-    rows = both.shape[1]
-    act = both[:k_in] * (1.0 / scales[0])
-    grad = both[k_in:] * (1.0 / scales[1])
-    row = lax.broadcasted_iota(jnp.int32, (16, rows), 0)
-    col = lax.broadcasted_iota(jnp.int32, (16, rows), 1)
-    pick = jnp.where((col >= row * SEQ) & (col < (row + 1) * SEQ), 1.0, 0.0).astype(jnp.bfloat16)
-    per = 8
-    k_out = grad.shape[0]
-    for at in range(0, k_in, per):
-        rest = jnp.concatenate([act[i:i + 1] * grad for i in range(at, at + per)], axis=0)
-        total = None
-        for _ in range(2):
-            high = rest.astype(jnp.bfloat16)
-            rest = rest - high.astype(jnp.float32)
-            part = lax.dot_general(pick, high, CONTRACT_LAST, preferred_element_type=jnp.float32)
-            total = part if total is None else total + part
-        out[:, at * k_out:(at + per) * k_out] = total[:out.shape[0]].astype(jnp.bfloat16)
+    k_out, rows = both.shape[0] - k_in, both.shape[1]
+    count = rows // SEQ
+    across = 128 // k_out
+    act_high, act_low = halves(both[:k_in])
+    grad_high, grad_low = halves(both[k_in:])
+    slot = lax.broadcasted_iota(jnp.int32, (1, rows), 1)
+
+    def by_example(act):
+        return jnp.concatenate(
+            [jnp.where((slot >= e * SEQ) & (slot < (e + 1) * SEQ), act, jnp.zeros_like(act)) for e in range(count)], axis=0)
+
+    def tiled(grad):
+        return jnp.concatenate([grad] * across, axis=0)
+
+    high = by_example(act_high)
+    left = jnp.concatenate([high, high, by_example(act_low)], axis=1)
+    high = tiled(grad_high)
+    right = jnp.concatenate([high, tiled(grad_low), high], axis=1)
+    product = lax.dot_general(left, right, CONTRACT_LAST, preferred_element_type=jnp.float32)
+    product = (product * (1.0 / (scales[0] * scales[1]))).astype(jnp.bfloat16).astype(jnp.float32)
+    row = lax.broadcasted_iota(jnp.int32, product.shape, 0)
+    lane = lax.broadcasted_iota(jnp.int32, product.shape, 1)
+    product = jnp.where(row % across == lane // k_out, product, 0.0).astype(jnp.bfloat16)
+    groups = k_in // across
+    shape = (groups * count, count * k_in)
+    to = lax.broadcasted_iota(jnp.int32, shape, 0)
+    source = lax.broadcasted_iota(jnp.int32, shape, 1)
+    pick = (source // k_in == to % count) & (source % k_in // across == to // count)
+    picked = jnp.dot(jnp.where(pick, 1.0, 0.0).astype(jnp.bfloat16), product, preferred_element_type=jnp.float32)
+    for group in range(groups):
+        out[:, group * 128:(group + 1) * 128] = picked[group * count:(group + 1) * count].astype(jnp.bfloat16)
 
 
 def example_grads(pieces, k_in, k_out, scales):
@@ -159,11 +178,12 @@
         wider = jnp.concatenate([p[:, pl.ds(at, 128)] for p in pieces], axis=0)
         own = pltpu.roll(wider.astype(jnp.float32), at - place * own_rows + 128, 1)[:, :own_rows].astype(jnp.bfloat16)
     copies = []
-    for n, at in enumerate(range(0, flat, flat // 4)):
-        lanes = pl.ds(at, flat // 4)
-        block[:, lanes] = lax.dot_general(own, every[:, at:at + flat // 4], CONTRACT_FIRST,
-                                          preferred_element_type=jnp.float32) * (1.0 / examples)
-        copies.append(pltpu.make_async_copy(block.at[:, lanes], cov.at[:, lanes], sems.at[n]))
+    step = max(own_rows // 4, 8)
+    for n, at in enumerate(range(0, own_rows, step)):
+        part = pl.ds(at, step)
+        block[part] = lax.dot_general(own[:, at:at + step], every, CONTRACT_FIRST,
+                                      preferred_element_type=jnp.float32) * (1.0 / examples)
+        copies.append(pltpu.make_async_copy(block.at[part], cov.at[part], sems.at[n]))
         copies[-1].start()
     wide = every.astype(jnp.float32)
     factor = lax.rsqrt(jnp.sum(wide * wide) / examples + 1e-06)

time: 17.6 us -> 17.5 us (level)
  no operation moved by 1% of the time
where the time goes in v9:
time: 17.5 us; the launch traced here: 17.4 us
  starting transfers between devices  9.08 us (52%)
  Pallas kernels  4.78 us (27%)
  waiting for transfers between devices  2.03 us (12%)
  matrix products  0.74 us (4%)
  between operations  0.68 us (4%)
    pallas_call x1, Pallas kernels, project(): pl.pallas_call(functools.partial(project_kernel, scales), out_shape=jax.S...  3.37 us
    ppermute x1, starting transfers between devices, per_device(): far = lax.ppermute(sent, ('mp', 'sub'), [(0, 3), (1, 2), (2, 1), (3, 0)])  2.44 us
    ppermute x1, starting transfers between devices, per_device(): fetched = lax.ppermute(held, group, list(enumerate(SWAPPED_SEND)))  2.43 us
    ppermute x1, starting transfers between devices, per_device(): direct = lax.ppermute(held, group, list(enumerate(DIRECT_SEND)))  1.87 us
    ppermute x1, waiting for transfers between devices, per_device(): far = lax.ppermute(sent, ('mp', 'sub'), [(0, 3), (1, 2), (2, 1), (3, 0)])  1.1 us
    pallas_call x1, Pallas kernels, finish(): pl.pallas_call(functools.partial(finish_kernel, examples, len(pieces), le...  1.06 us
    ppermute x1, starting transfers between devices, per_device(): gathered = [held, direct, fetched, lax.ppermute(fetched, group, swap)]  0.79 us
    ppermute x1, starting transfers between devices, per_device(): near = lax.ppermute(sent, 'sub', [(0, 1), (1, 0)])  0.67 us
  transfers between devices with their start and end apart: 7, of which 4 were waited for; matrix products, arithmetic and copies ran while one was open for 4% of the time, Pallas kernels for 0%

profile of v9, /device:TPU:0, one launch (start us, length us, event | category | flops | bytes accessed | tf_op | source)
XLA Modules:
  0.0 17.4 jit_solution(1130261398001081940)
XLA Ops:
  0.6 0.0 copy-start
  0.6 3.4 %shard_map.77 = f32[64,256]{1,0:T(8,128)S(1)} custom-call(bf16[256,7168]{1,0:T(8,128)(2,1)} %hidden.1, bf16[256,2048]{1,0:T(8,128)(2,1)} %out_grad.1, s32[4]{0:T(128)} %lengths.1, bf16[32,7168]{1,0:T(8,128)(2,1)} %bitcast.6, bf16[32,2048]{1,0:T(8,128)(2,1)} %bitcast.7), custom_call_target="tpu_custom_call" | custom-call | flops 150994944 | bytes 5308416 | tf_op jit(solution)/shard_map/pallas_call | solution.py:90
  4.0 2.4 %collective-permute-start.1 = (f16[64,256]{1,0:T(8,128)(2,1)S(1)}, f16[64,256]{1,0:T(8,128)(2,1)S(1)}, u32[]{:S(2)}, u32[]{:S(2)}) collective-permute-start(f16[64,256]{1,0:T(8,128)(2,1)S(1)} %convert_element_type.9), channel_id=1, source_target_pairs={{0,3},{1,2},{2,1},{3,0},{4,7},{5,6},{6,5},{7,4},{8,11},{9,10},{10,... | collective-permute-start | bytes 98312 | tf_op jit(solution)/shard_map/ppermute | solution.py:231
  6.5 0.7 %collective-permute-start = (f16[64,256]{1,0:T(8,128)(2,1)S(1)}, f16[64,256]{1,0:T(8,128)(2,1)S(1)}, u32[]{:S(2)}, u32[]{:S(2)}) collective-permute-start(f16[64,256]{1,0:T(8,128)(2,1)S(1)} %convert_element_type.9), channel_id=1, source_target_pairs={{0,1},{1,0},{2,3},{3,2},{4,5},{5,4},{6,7},{7,6},{8,9},{9,8},{10,11... | collective-permute-start | bytes 98312 | tf_op jit(solution)/shard_map/ppermute | solution.py:232
  7.2 1.1 %collective-permute-done.1 = f16[64,256]{1,0:T(8,128)(2,1)S(1)} collective-permute-done((f16[64,256]{1,0:T(8,128)(2,1)S(1)}, f16[64,256]{1,0:T(8,128)(2,1)S(1)}, u32[]{:S(2)}, u32[]{:S(2)}) %collective-permute-start.1) | collective-permute-done | bytes 32800 | tf_op jit(solution)/shard_map/ppermute | solution.py:231
  8.3 0.0 collective-permute-done
  8.3 0.3 %shard_map.78 = bf16[4,1024]{1,0:T(4,128)(2,1)S(1)} custom-call(f32[64,256]{1,0:T(8,128)S(1)} %convert_element_type.10.refs_0_, f32[64,256]{1,0:T(8,128)S(1)} %convert_element_type.11.refs_1_), custom_call_target="tpu_custom_call" | custom-call | flops 8589934592 | tf_op jit(solution)/shard_map/pallas_call | solution.py:157
  8.6 0.5 %collective-permute-start.2 = (bf16[4,1024]{1,0:T(4,128)(2,1)S(1)}, bf16[4,1024]{1,0:T(4,128)(2,1)S(1)}, u32[]{:S(2)}, u32[]{:S(2)}) collective-permute-start(bf16[4,1024]{1,0:T(4,128)(2,1)S(1)} %shard_map.78), channel_id=1, source_target_pairs={{0,1},{1,0},{2,3},{3,2},{4,5},{5,4},{6,7},{7,6},{8,9},{9,8},{10,11... | collective-permute-start | bytes 24584 | tf_op jit(solution)/shard_map/ppermute | solution.py:234
  9.1 0.0 copy-done
  9.1 0.4 %fusion = f32[4,512]{1,0:T(4,128)S(1)} fusion(bf16[4,1024]{1,0:T(4,128)(2,1)S(1)} %shard_map.78, bf16[512,1024]{1,0:T(8,128)(2,1)S(1)} %copy-done), kind=kOutput, calls=%fused_computation.1 | convolution fusion | flops 4194304 | bytes 1064960 | tf_op jit(solution)/shard_map/ep,qp->eq/dot_general | solution.py:240
  9.5 0.5 %collective-permute-done.2 = bf16[4,1024]{1,0:T(4,128)(2,1)S(1)} collective-permute-done((bf16[4,1024]{1,0:T(4,128)(2,1)S(1)}, bf16[4,1024]{1,0:T(4,128)(2,1)S(1)}, u32[]{:S(2)}, u32[]{:S(2)}) %collective-permute-start.2) | collective-permute-done | bytes 8224 | tf_op jit(solution)/shard_map/ppermute | solution.py:234
  10.0 2.4 %collective-permute-start.4 = (bf16[8,1024]{1,0:T(8,128)(2,1)S(1)}, bf16[8,1024]{1,0:T(8,128)(2,1)S(1)}, u32[]{:S(2)}, u32[]{:S(2)}) collective-permute-start(bf16[8,1024]{1,0:T(8,128)(2,1)S(1)} %pad_maximum_fusion.refs_0_), channel_id=1, source_target_pairs={{0,4},{1,9},{4,8},{5,13},{8,12},{9,0},{12,5},{13,1},{2,6},{3,11},{... | collective-permute-start | bytes 49160 | tf_op jit(solution)/shard_map/ppermute | solution.py:243
  12.4 1.9 %collective-permute-start.3 = (bf16[8,1024]{1,0:T(8,128)(2,1)S(1)}, bf16[8,1024]{1,0:T(8,128)(2,1)S(1)}, u32[]{:S(2)}, u32[]{:S(2)}) collective-permute-start(bf16[8,1024]{1,0:T(8,128)(2,1)S(1)} %pad_maximum_fusion.refs_0_), channel_id=1, source_target_pairs={{0,13},{1,12},{4,1},{5,0},{8,4},{9,5},{12,9},{13,8},{2,15},{3,14},... | collective-permute-start | bytes 49160 | tf_op jit(solution)/shard_map/ppermute | solution.py:244
  14.3 0.4 %collective-permute-start.6 = (f32[4,512]{1,0:T(4,128)S(1)}, f32[4,512]{1,0:T(4,128)S(1)}, u32[]{:S(2)}, u32[]{:S(2)}) collective-permute-start(f32[4,512]{1,0:T(4,128)S(1)} %fusion), channel_id=1, source_target_pairs={{0,1},{1,0},{4,5},{5,4},{8,9},{9,8},{12,13},{13,12},{2,3},{3,2},{6... | collective-permute-start | bytes 24584 | tf_op jit(solution)/shard_map/ppermute | solution.py:247
  14.7 0.0 collective-permute-done.4.refs_2_
  14.7 0.8 %collective-permute-start.5 = (bf16[8,1024]{1,0:T(8,128)(2,1)S(1)}, bf16[8,1024]{1,0:T(8,128)(2,1)S(1)}, u32[]{:S(2)}, u32[]{:S(2)}) collective-permute-start(bf16[8,1024]{1,0:T(8,128)(2,1)S(1)} %collective-permute-done.4.refs_2_), channel_id=1, source_target_pairs={{0,1},{1,0},{4,5},{5,4},{8,9},{9,8},{12,13},{13,12},{2,3},{3,2},{6... | collective-permute-start | bytes 49160 | tf_op jit(solution)/shard_map/ppermute | solution.py:245
  15.5 0.4 %fusion.1.refs_4_ = f32[4,512]{1,0:T(4,128)S(1)} fusion(bf16[4,1024]{1,0:T(4,128)(2,1)S(1)} %collective-permute-done.2, bf16[512,1024]{1,0:T(8,128)(2,1)S(1)} %copy-done), kind=kOutput, calls=%fused_computation.2 | convolution fusion | flops 4194304 | bytes 1064960 | tf_op jit(solution)/shard_map/ep,qp->eq/dot_general | solution.py:246
  15.8 0.0 collective-permute-done.6.refs_5_
  15.8 0.1 collective-permute-done.3.refs_1_
  15.9 0.4 %collective-permute-done.5.refs_3_ = bf16[8,1024]{1,0:T(8,128)(2,1)S(1)} collective-permute-done((bf16[8,1024]{1,0:T(8,128)(2,1)S(1)}, bf16[8,1024]{1,0:T(8,128)(2,1)S(1)}, u32[]{:S(2)}, u32[]{:S(2)}) %collective-permute-start.5) | collective-permute-done | bytes 16416 | tf_op jit(solution)/shard_map/ppermute | solution.py:245
  16.3 1.1 %shard_map.79 = (f32[128,1024]{1,0:T(8,128)}, f32[4,1024]{1,0:T(4,128)}) custom-call(bf16[8,1024]{1,0:T(8,128)(2,1)S(1)} %pad_maximum_fusion.refs_0_, bf16[8,1024]{1,0:T(8,128)(2,1)S(1)} %collective-permute-done.3.refs_1_, bf16[8,1024]{1,0:T(8,128)(2,1)S(1)} %collective-permute-done.4.refs_2_, bf16[8,1024]{1,0:T(8,128)(2,1)S(1)} %collective-permute-done.5.refs_3_, ...), custom_call_target="tpu_custom_call" | custom-call | tf_op jit(solution)/shard_map/pallas_call | solution.py:210
  (4 shorter events, 0.0 us)
Async XLA Ops:
  0.6 8.5 %copy-start = (bf16[512,1024]{1,0:T(8,128)(2,1)S(1)}, bf16[512,1024]{1,0:T(8,128)(2,1)}, u32[]{:S(2)}) copy-start(bf16[512,1024]{1,0:T(8,128)(2,1)} %param.11) | copy-start | bytes 3145732
  4.0 4.2 %collective-permute-start.1 = (f16[64,256]{1,0:T(8,128)(2,1)S(1)}, f16[64,256]{1,0:T(8,128)(2,1)S(1)}, u32[]{:S(2)}, u32[]{:S(2)}) collective-permute-start(f16[64,256]{1,0:T(8,128)(2,1)S(1)} %convert_element_type.9), channel_id=1, source_target_pairs={{0,3},{1,2},{2,1},{3,0},{4,7},{5,6},{6,5},{7,4},{8,11},{9,10},{10,... | collective-permute-start | bytes 98312 | tf_op jit(solution)/shard_map/ppermute | solution.py:231
  6.5 1.8 %collective-permute-start = (f16[64,256]{1,0:T(8,128)(2,1)S(1)}, f16[64,256]{1,0:T(8,128)(2,1)S(1)}, u32[]{:S(2)}, u32[]{:S(2)}) collective-permute-start(f16[64,256]{1,0:T(8,128)(2,1)S(1)} %convert_element_type.9), channel_id=1, source_target_pairs={{0,1},{1,0},{2,3},{3,2},{4,5},{5,4},{6,7},{7,6},{8,9},{9,8},{10,11... | collective-permute-start | bytes 98312 | tf_op jit(solution)/shard_map/ppermute | solution.py:232
  8.6 1.3 %collective-permute-start.2 = (bf16[4,1024]{1,0:T(4,128)(2,1)S(1)}, bf16[4,1024]{1,0:T(4,128)(2,1)S(1)}, u32[]{:S(2)}, u32[]{:S(2)}) collective-permute-start(bf16[4,1024]{1,0:T(4,128)(2,1)S(1)} %shard_map.78), channel_id=1, source_target_pairs={{0,1},{1,0},{2,3},{3,2},{4,5},{5,4},{6,7},{7,6},{8,9},{9,8},{10,11... | collective-permute-start | bytes 24584 | tf_op jit(solution)/shard_map/ppermute | solution.py:234
  10.0 4.7 %collective-permute-start.4 = (bf16[8,1024]{1,0:T(8,128)(2,1)S(1)}, bf16[8,1024]{1,0:T(8,128)(2,1)S(1)}, u32[]{:S(2)}, u32[]{:S(2)}) collective-permute-start(bf16[8,1024]{1,0:T(8,128)(2,1)S(1)} %pad_maximum_fusion.refs_0_), channel_id=1, source_target_pairs={{0,4},{1,9},{4,8},{5,13},{8,12},{9,0},{12,5},{13,1},{2,6},{3,11},{... | collective-permute-start | bytes 49160 | tf_op jit(solution)/shard_map/ppermute | solution.py:243
  12.4 3.5 %collective-permute-start.3 = (bf16[8,1024]{1,0:T(8,128)(2,1)S(1)}, bf16[8,1024]{1,0:T(8,128)(2,1)S(1)}, u32[]{:S(2)}, u32[]{:S(2)}) collective-permute-start(bf16[8,1024]{1,0:T(8,128)(2,1)S(1)} %pad_maximum_fusion.refs_0_), channel_id=1, source_target_pairs={{0,13},{1,12},{4,1},{5,0},{8,4},{9,5},{12,9},{13,8},{2,15},{3,14},... | collective-permute-start | bytes 49160 | tf_op jit(solution)/shard_map/ppermute | solution.py:244
  14.3 1.5 %collective-permute-start.6 = (f32[4,512]{1,0:T(4,128)S(1)}, f32[4,512]{1,0:T(4,128)S(1)}, u32[]{:S(2)}, u32[]{:S(2)}) collective-permute-start(f32[4,512]{1,0:T(4,128)S(1)} %fusion), channel_id=1, source_target_pairs={{0,1},{1,0},{4,5},{5,4},{8,9},{9,8},{12,13},{13,12},{2,3},{3,2},{6... | collective-permute-start | bytes 24584 | tf_op jit(solution)/shard_map/ppermute | solution.py:247
  14.7 1.6 %collective-permute-start.5 = (bf16[8,1024]{1,0:T(8,128)(2,1)S(1)}, bf16[8,1024]{1,0:T(8,128)(2,1)S(1)}, u32[]{:S(2)}, u32[]{:S(2)}) collective-permute-start(bf16[8,1024]{1,0:T(8,128)(2,1)S(1)} %collective-permute-done.4.refs_2_), channel_id=1, source_target_pairs={{0,1},{1,0},{4,5},{5,4},{8,9},{9,8},{12,13},{13,12},{2,3},{3,2},{6... | collective-permute-start | bytes 49160 | tf_op jit(solution)/shard_map/ppermute | solution.py:245

commit v10 on v9

--- a/solution.py
+++ b/solution.py
@@ -26,7 +26,7 @@
     return terms[0]
 
 
-def project_kernel(scales, hidden, out_grad, lengths, proj_in, proj_out, out, hid, og, pin, pout, limits, sems):
+def project_kernel(scales, hidden, out_grad, lengths, proj_in, proj_out, tests, out, near_tests, hid, og, pin, pout, limits, sems):
     rows, width = hidden.shape
     k_in = pin.shape[0]
     small = first_chunk(width)
@@ -59,6 +59,8 @@
             copy.start()
     bounds = pltpu.make_async_copy(lengths, limits, sems.at[0, 4])
     bounds.start()
+    fetch = pltpu.make_async_copy(tests, near_tests, sems.at[1, 4])
+    fetch.start()
     total = jnp.zeros((k_in, rows), jnp.float32)
     if small:
         for copy in copies_of(0):
@@ -80,18 +82,22 @@
     for e in range(lengths.shape[0]):
         limit = jnp.where(slot >= e * SEQ, e * SEQ + limits[e], limit)
     out[:k_in] = jnp.where(slot < limit, total * scales[0], 0.0)
-
-
-def project(hidden, out_grad, lengths, proj_in, proj_out, scales):
+    fetch.wait()
+
+
+def project(hidden, out_grad, lengths, proj_in, proj_out, test_proj, scales):
     rows, width = hidden.shape
     narrow = out_grad.shape[1]
     k_in, k_out = proj_in.shape[1], proj_out.shape[1]
-    operands = (hidden, out_grad, lengths, proj_in.T, proj_out.T)
+    operands = (hidden, out_grad, lengths, proj_in.T, proj_out.T, test_proj)
     return pl.pallas_call(
         functools.partial(project_kernel, scales),
-        out_shape=jax.ShapeDtypeStruct((k_in + k_out, rows), jnp.float32),
-        in_specs=[pl.BlockSpec(memory_space=pltpu.HBM)] * 5,
-        out_specs=pl.BlockSpec(memory_space=pltpu.VMEM),
+        out_shape=(
+            jax.ShapeDtypeStruct((k_in + k_out, rows), jnp.float32),
+            jax.ShapeDtypeStruct(test_proj.shape, test_proj.dtype),
+        ),
+        in_specs=[pl.BlockSpec(memory_space=pltpu.HBM)] * 6,
+        out_specs=(pl.BlockSpec(memory_space=pltpu.VMEM),) * 2,
         scratch_shapes=[
             pltpu.VMEM((rows, width), jnp.bfloat16),
             pltpu.VMEM((rows, narrow), jnp.bfloat16),
@@ -225,7 +231,7 @@
     examples = lengths.shape[0] * sharers
     crossed = lax.axis_size("mp") == 2 and lax.axis_size("sub") == 2
     scales = (128.0, 4.0) if crossed else (1.0, 1.0)
-    both = project(hidden, out_grad, lengths, proj_in, proj_out, scales)
+    both, test_proj = project(hidden, out_grad, lengths, proj_in, proj_out, test_proj, scales)
     if crossed:
         sent = lax.optimization_barrier(both.astype(jnp.float16))
         far = lax.ppermute(sent, ("mp", "sub"), [(0, 3), (1, 2), (2, 1), (3, 0)])

time: 17.5 us -> 17.4 us (level)
  no operation moved by 1% of the time
where the time goes in v10:
time: 17.4 us; the launch traced here: 17.3 us
  starting transfers between devices  9.08 us (52%)
  Pallas kernels  4.7 us (27%)
  waiting for transfers between devices  2.03 us (12%)
  matrix products  0.74 us (4%)
  between operations  0.67 us (4%)
    pallas_call x1, Pallas kernels, project(): pl.pallas_call(functools.partial(project_kernel, scales), out_shape=(jax....  3.29 us
    ppermute x1, starting transfers between devices, per_device(): far = lax.ppermute(sent, ('mp', 'sub'), [(0, 3), (1, 2), (2, 1), (3, 0)])  2.44 us
    ppermute x1, starting transfers between devices, per_device(): fetched = lax.ppermute(held, group, list(enumerate(SWAPPED_SEND)))  2.41 us
    ppermute x1, starting transfers between devices, per_device(): direct = lax.ppermute(held, group, list(enumerate(DIRECT_SEND)))  1.88 us
    ppermute x1, waiting for transfers between devices, per_device(): far = lax.ppermute(sent, ('mp', 'sub'), [(0, 3), (1, 2), (2, 1), (3, 0)])  1.1 us
    pallas_call x1, Pallas kernels, finish(): pl.pallas_call(functools.partial(finish_kernel, examples, len(pieces), le...  1.06 us
    ppermute x1, starting transfers between devices, per_device(): gathered = [held, direct, fetched, lax.ppermute(fetched, group, swap)]  0.8 us
    ppermute x1, starting transfers between devices, per_device(): near = lax.ppermute(sent, 'sub', [(0, 1), (1, 0)])  0.68 us
  transfers between devices with their start and end apart: 7, of which 4 were waited for; matrix products, arithmetic and copies ran while one was open for 4% of the time, Pallas kernels for 0%

profile of v10, /device:TPU:0, one launch (start us, length us, event | category | flops | bytes accessed | tf_op | source)
XLA Modules:
  0.0 17.3 jit_solution(10366494643259117150)
XLA Ops:
  0.6 3.3 %shard_map.77 = (f32[64,256]{1,0:T(8,128)S(1)}, bf16[512,1024]{1,0:T(8,128)(2,1)S(1)}) custom-call(bf16[256,7168]{1,0:T(8,128)(2,1)} %hidden.1, bf16[256,2048]{1,0:T(8,128)(2,1)} %out_grad.1, s32[4]{0:T(128)} %lengths.1, bf16[32,7168]{1,0:T(8,128)(2,1)} %bitcast.6, bf16[32,2048]{1,0:T(8,128)(2,1)} %bitcast.7, bf16[512,1024]{1,0:T(8,128)(2,1)} %tests.1), custom_call_target="tpu_custom_call" | custom-call | flops 150994944 | bytes 5308416 | tf_op jit(solution)/shard_map/pallas_call | solution.py:93
  3.9 2.4 %collective-permute-start.1 = (f16[64,256]{1,0:T(8,128)(2,1)S(1)}, f16[64,256]{1,0:T(8,128)(2,1)S(1)}, u32[]{:S(2)}, u32[]{:S(2)}) collective-permute-start(f16[64,256]{1,0:T(8,128)(2,1)S(1)} %convert_element_type.9), channel_id=1, source_target_pairs={{0,3},{1,2},{2,1},{3,0},{4,7},{5,6},{6,5},{7,4},{8,11},{9,10},{10,... | collective-permute-start | bytes 98312 | tf_op jit(solution)/shard_map/ppermute | solution.py:237
  6.4 0.7 %collective-permute-start = (f16[64,256]{1,0:T(8,128)(2,1)S(1)}, f16[64,256]{1,0:T(8,128)(2,1)S(1)}, u32[]{:S(2)}, u32[]{:S(2)}) collective-permute-start(f16[64,256]{1,0:T(8,128)(2,1)S(1)} %convert_element_type.9), channel_id=1, source_target_pairs={{0,1},{1,0},{2,3},{3,2},{4,5},{5,4},{6,7},{7,6},{8,9},{9,8},{10,11... | collective-permute-start | bytes 98312 | tf_op jit(solution)/shard_map/ppermute | solution.py:238
  7.1 1.1 %collective-permute-done.1 = f16[64,256]{1,0:T(8,128)(2,1)S(1)} collective-permute-done((f16[64,256]{1,0:T(8,128)(2,1)S(1)}, f16[64,256]{1,0:T(8,128)(2,1)S(1)}, u32[]{:S(2)}, u32[]{:S(2)}) %collective-permute-start.1) | collective-permute-done | bytes 32800 | tf_op jit(solution)/shard_map/ppermute | solution.py:237
  8.2 0.0 collective-permute-done
  8.2 0.3 %shard_map.78 = bf16[4,1024]{1,0:T(4,128)(2,1)S(1)} custom-call(f32[64,256]{1,0:T(8,128)S(1)} %convert_element_type.10.refs_0_, f32[64,256]{1,0:T(8,128)S(1)} %convert_element_type.11.refs_1_), custom_call_target="tpu_custom_call" | custom-call | flops 8589934592 | tf_op jit(solution)/shard_map/pallas_call | solution.py:163
  8.5 0.5 %collective-permute-start.2 = (bf16[4,1024]{1,0:T(4,128)(2,1)S(1)}, bf16[4,1024]{1,0:T(4,128)(2,1)S(1)}, u32[]{:S(2)}, u32[]{:S(2)}) collective-permute-start(bf16[4,1024]{1,0:T(4,128)(2,1)S(1)} %shard_map.78), channel_id=1, source_target_pairs={{0,1},{1,0},{2,3},{3,2},{4,5},{5,4},{6,7},{7,6},{8,9},{9,8},{10,11... | collective-permute-start | bytes 24584 | tf_op jit(solution)/shard_map/ppermute | solution.py:240
  9.1 0.4 %fusion = f32[4,512]{1,0:T(4,128)S(1)} fusion(bf16[4,1024]{1,0:T(4,128)(2,1)S(1)} %shard_map.78, bf16[512,1024]{1,0:T(8,128)(2,1)S(1)} %get-tuple-element.7), kind=kOutput, calls=%fused_computation.1 | convolution fusion | flops 4194304 | bytes 1064960 | tf_op jit(solution)/shard_map/ep,qp->eq/dot_general | solution.py:246
  9.4 0.5 %collective-permute-done.2 = bf16[4,1024]{1,0:T(4,128)(2,1)S(1)} collective-permute-done((bf16[4,1024]{1,0:T(4,128)(2,1)S(1)}, bf16[4,1024]{1,0:T(4,128)(2,1)S(1)}, u32[]{:S(2)}, u32[]{:S(2)}) %collective-permute-start.2) | collective-permute-done | bytes 8224 | tf_op jit(solution)/shard_map/ppermute | solution.py:240
  9.9 2.4 %collective-permute-start.4 = (bf16[8,1024]{1,0:T(8,128)(2,1)S(1)}, bf16[8,1024]{1,0:T(8,128)(2,1)S(1)}, u32[]{:S(2)}, u32[]{:S(2)}) collective-permute-start(bf16[8,1024]{1,0:T(8,128)(2,1)S(1)} %pad_maximum_fusion.refs_0_), channel_id=1, source_target_pairs={{0,4},{1,9},{4,8},{5,13},{8,12},{9,0},{12,5},{13,1},{2,6},{3,11},{... | collective-permute-start | bytes 49160 | tf_op jit(solution)/shard_map/ppermute | solution.py:249
  12.3 1.9 %collective-permute-start.3 = (bf16[8,1024]{1,0:T(8,128)(2,1)S(1)}, bf16[8,1024]{1,0:T(8,128)(2,1)S(1)}, u32[]{:S(2)}, u32[]{:S(2)}) collective-permute-start(bf16[8,1024]{1,0:T(8,128)(2,1)S(1)} %pad_maximum_fusion.refs_0_), channel_id=1, source_target_pairs={{0,13},{1,12},{4,1},{5,0},{8,4},{9,5},{12,9},{13,8},{2,15},{3,14},... | collective-permute-start | bytes 49160 | tf_op jit(solution)/shard_map/ppermute | solution.py:250
  14.2 0.4 %collective-permute-start.6 = (f32[4,512]{1,0:T(4,128)S(1)}, f32[4,512]{1,0:T(4,128)S(1)}, u32[]{:S(2)}, u32[]{:S(2)}) collective-permute-start(f32[4,512]{1,0:T(4,128)S(1)} %fusion), channel_id=1, source_target_pairs={{0,1},{1,0},{4,5},{5,4},{8,9},{9,8},{12,13},{13,12},{2,3},{3,2},{6... | collective-permute-start | bytes 24584 | tf_op jit(solution)/shard_map/ppermute | solution.py:253
  14.5 0.0 collective-permute-done.4.refs_2_
  14.6 0.8 %collective-permute-start.5 = (bf16[8,1024]{1,0:T(8,128)(2,1)S(1)}, bf16[8,1024]{1,0:T(8,128)(2,1)S(1)}, u32[]{:S(2)}, u32[]{:S(2)}) collective-permute-start(bf16[8,1024]{1,0:T(8,128)(2,1)S(1)} %collective-permute-done.4.refs_2_), channel_id=1, source_target_pairs={{0,1},{1,0},{4,5},{5,4},{8,9},{9,8},{12,13},{13,12},{2,3},{3,2},{6... | collective-permute-start | bytes 49160 | tf_op jit(solution)/shard_map/ppermute | solution.py:251
  15.4 0.4 %fusion.1.refs_4_ = f32[4,512]{1,0:T(4,128)S(1)} fusion(bf16[4,1024]{1,0:T(4,128)(2,1)S(1)} %collective-permute-done.2, bf16[512,1024]{1,0:T(8,128)(2,1)S(1)} %get-tuple-element.7), kind=kOutput, calls=%fused_computation.2 | convolution fusion | flops 4194304 | bytes 1064960 | tf_op jit(solution)/shard_map/ep,qp->eq/dot_general | solution.py:252
  15.7 0.0 collective-permute-done.6.refs_5_
  15.7 0.1 collective-permute-done.3.refs_1_
  15.8 0.4 %collective-permute-done.5.refs_3_ = bf16[8,1024]{1,0:T(8,128)(2,1)S(1)} collective-permute-done((bf16[8,1024]{1,0:T(8,128)(2,1)S(1)}, bf16[8,1024]{1,0:T(8,128)(2,1)S(1)}, u32[]{:S(2)}, u32[]{:S(2)}) %collective-permute-start.5) | collective-permute-done | bytes 16416 | tf_op jit(solution)/shard_map/ppermute | solution.py:251
  16.2 1.1 %shard_map.79 = (f32[128,1024]{1,0:T(8,128)}, f32[4,1024]{1,0:T(4,128)}) custom-call(bf16[8,1024]{1,0:T(8,128)(2,1)S(1)} %pad_maximum_fusion.refs_0_, bf16[8,1024]{1,0:T(8,128)(2,1)S(1)} %collective-permute-done.3.refs_1_, bf16[8,1024]{1,0:T(8,128)(2,1)S(1)} %collective-permute-done.4.refs_2_, bf16[8,1024]{1,0:T(8,128)(2,1)S(1)} %collective-permute-done.5.refs_3_, ...), custom_call_target="tpu_custom_call" | custom-call | tf_op jit(solution)/shard_map/pallas_call | solution.py:216
  (4 shorter events, 0.0 us)
Async XLA Ops:
  3.9 4.2 %collective-permute-start.1 = (f16[64,256]{1,0:T(8,128)(2,1)S(1)}, f16[64,256]{1,0:T(8,128)(2,1)S(1)}, u32[]{:S(2)}, u32[]{:S(2)}) collective-permute-start(f16[64,256]{1,0:T(8,128)(2,1)S(1)} %convert_element_type.9), channel_id=1, source_target_pairs={{0,3},{1,2},{2,1},{3,0},{4,7},{5,6},{6,5},{7,4},{8,11},{9,10},{10,... | collective-permute-start | bytes 98312 | tf_op jit(solution)/shard_map/ppermute | solution.py:237
  6.4 1.8 %collective-permute-start = (f16[64,256]{1,0:T(8,128)(2,1)S(1)}, f16[64,256]{1,0:T(8,128)(2,1)S(1)}, u32[]{:S(2)}, u32[]{:S(2)}) collective-permute-start(f16[64,256]{1,0:T(8,128)(2,1)S(1)} %convert_element_type.9), channel_id=1, source_target_pairs={{0,1},{1,0},{2,3},{3,2},{4,5},{5,4},{6,7},{7,6},{8,9},{9,8},{10,11... | collective-permute-start | bytes 98312 | tf_op jit(solution)/shard_map/ppermute | solution.py:238
  8.5 1.3 %collective-permute-start.2 = (bf16[4,1024]{1,0:T(4,128)(2,1)S(1)}, bf16[4,1024]{1,0:T(4,128)(2,1)S(1)}, u32[]{:S(2)}, u32[]{:S(2)}) collective-permute-start(bf16[4,1024]{1,0:T(4,128)(2,1)S(1)} %shard_map.78), channel_id=1, source_target_pairs={{0,1},{1,0},{2,3},{3,2},{4,5},{5,4},{6,7},{7,6},{8,9},{9,8},{10,11... | collective-permute-start | bytes 24584 | tf_op jit(solution)/shard_map/ppermute | solution.py:240
  9.9 4.7 %collective-permute-start.4 = (bf16[8,1024]{1,0:T(8,128)(2,1)S(1)}, bf16[8,1024]{1,0:T(8,128)(2,1)S(1)}, u32[]{:S(2)}, u32[]{:S(2)}) collective-permute-start(bf16[8,1024]{1,0:T(8,128)(2,1)S(1)} %pad_maximum_fusion.refs_0_), channel_id=1, source_target_pairs={{0,4},{1,9},{4,8},{5,13},{8,12},{9,0},{12,5},{13,1},{2,6},{3,11},{... | collective-permute-start | bytes 49160 | tf_op jit(solution)/shard_map/ppermute | solution.py:249
  12.3 3.5 %collective-permute-start.3 = (bf16[8,1024]{1,0:T(8,128)(2,1)S(1)}, bf16[8,1024]{1,0:T(8,128)(2,1)S(1)}, u32[]{:S(2)}, u32[]{:S(2)}) collective-permute-start(bf16[8,1024]{1,0:T(8,128)(2,1)S(1)} %pad_maximum_fusion.refs_0_), channel_id=1, source_target_pairs={{0,13},{1,12},{4,1},{5,0},{8,4},{9,5},{12,9},{13,8},{2,15},{3,14},... | collective-permute-start | bytes 49160 | tf_op jit(solution)/shard_map/ppermute | solution.py:250
  14.2 1.5 %collective-permute-start.6 = (f32[4,512]{1,0:T(4,128)S(1)}, f32[4,512]{1,0:T(4,128)S(1)}, u32[]{:S(2)}, u32[]{:S(2)}) collective-permute-start(f32[4,512]{1,0:T(4,128)S(1)} %fusion), channel_id=1, source_target_pairs={{0,1},{1,0},{4,5},{5,4},{8,9},{9,8},{12,13},{13,12},{2,3},{3,2},{6... | collective-permute-start | bytes 24584 | tf_op jit(solution)/shard_map/ppermute | solution.py:253
  14.6 1.6 %collective-permute-start.5 = (bf16[8,1024]{1,0:T(8,128)(2,1)S(1)}, bf16[8,1024]{1,0:T(8,128)(2,1)S(1)}, u32[]{:S(2)}, u32[]{:S(2)}) collective-permute-start(bf16[8,1024]{1,0:T(8,128)(2,1)S(1)} %collective-permute-done.4.refs_2_), channel_id=1, source_target_pairs={{0,1},{1,0},{4,5},{5,4},{8,9},{9,8},{12,13},{13,12},{2,3},{3,2},{6... | collective-permute-start | bytes 49160 | tf_op jit(solution)/shard_map/ppermute | solution.py:251

commit v11 on v10

--- a/solution.py
+++ b/solution.py
@@ -183,7 +183,19 @@
         at = pl.multiple_of((place * own_rows) // 128 * 128, 128)
         wider = jnp.concatenate([p[:, pl.ds(at, 128)] for p in pieces], axis=0)
         own = pltpu.roll(wider.astype(jnp.float32), at - place * own_rows + 128, 1)[:, :own_rows].astype(jnp.bfloat16)
-    copies = []
+    wide = every.astype(jnp.float32)
+    total = jnp.sum(jnp.sum(wide * wide, axis=0, keepdims=True), axis=1, keepdims=True)
+    factor = lax.rsqrt(total * (1.0 / examples) + 1e-06)
+    if n_raw == 2:
+        near, far = raw[0][...] * factor, raw[1][...] * factor
+        first = lax.axis_index("sub") == 0
+        half = near.shape[1]
+        row[:, :half] = jnp.where(first, near, far)
+        row[:, half:] = jnp.where(first, far, near)
+    else:
+        row[...] = raw[0][...] * factor
+    copies = [pltpu.make_async_copy(row, scores, sems.at[4])]
+    copies[0].start()
     step = max(own_rows // 4, 8)
     for n, at in enumerate(range(0, own_rows, step)):
         part = pl.ds(at, step)
@@ -191,18 +203,6 @@
                                       preferred_element_type=jnp.float32) * (1.0 / examples)
         copies.append(pltpu.make_async_copy(block.at[part], cov.at[part], sems.at[n]))
         copies[-1].start()
-    wide = every.astype(jnp.float32)
-    factor = lax.rsqrt(jnp.sum(wide * wide) / examples + 1e-06)
-    if n_raw == 2:
-        near, far = raw[0][...], raw[1][...]
-        first = lax.axis_index("sub") == 0
-        half = near.shape[1]
-        row[:, :half] = jnp.where(first, near, far) * factor
-        row[:, half:] = jnp.where(first, far, near) * factor
-    else:
-        row[...] = raw[0][...] * factor
-    copies.append(pltpu.make_async_copy(row, scores, sems.at[4]))
-    copies[-1].start()
     for copy in copies:
         copy.wait()
 

time: 17.4 us -> 17.4 us (level)
  no operation moved by 1% of the time
where the time goes in v11:
time: 17.4 us; the launch traced here: 17.2 us
  starting transfers between devices  9.08 us (52%)
  Pallas kernels  4.69 us (27%)
  waiting for transfers between devices  2.03 us (12%)
  matrix products  0.74 us (4%)
  between operations  0.67 us (4%)
    pallas_call x1, Pallas kernels, project(): pl.pallas_call(functools.partial(project_kernel, scales), out_shape=(jax....  3.29 us
    ppermute x1, starting transfers between devices, per_device(): far = lax.ppermute(sent, ('mp', 'sub'), [(0, 3), (1, 2), (2, 1), (3, 0)])  2.44 us
    ppermute x1, starting transfers between devices, per_device(): fetched = lax.ppermute(held, group, list(enumerate(SWAPPED_SEND)))  2.41 us
    ppermute x1, starting transfers between devices, per_device(): direct = lax.ppermute(held, group, list(enumerate(DIRECT_SEND)))  1.88 us
    ppermute x1, waiting for transfers between devices, per_device(): far = lax.ppermute(sent, ('mp', 'sub'), [(0, 3), (1, 2), (2, 1), (3, 0)])  1.1 us
    pallas_call x1, Pallas kernels, finish(): pl.pallas_call(functools.partial(finish_kernel, examples, len(pieces), le...  1.05 us
    ppermute x1, starting transfers between devices, per_device(): gathered = [held, direct, fetched, lax.ppermute(fetched, group, swap)]  0.8 us
    ppermute x1, starting transfers between devices, per_device(): near = lax.ppermute(sent, 'sub', [(0, 1), (1, 0)])  0.68 us
  transfers between devices with their start and end apart: 7, of which 4 were waited for; matrix products, arithmetic and copies ran while one was open for 4% of the time, Pallas kernels for 0%

profile of v11, /device:TPU:0, one launch (start us, length us, event | category | flops | bytes accessed | tf_op | source)
XLA Modules:
  0.0 17.2 jit_solution(247205416494636449)
XLA Ops:
  0.6 3.3 %shard_map.77 = (f32[64,256]{1,0:T(8,128)S(1)}, bf16[512,1024]{1,0:T(8,128)(2,1)S(1)}) custom-call(bf16[256,7168]{1,0:T(8,128)(2,1)} %hidden.1, bf16[256,2048]{1,0:T(8,128)(2,1)} %out_grad.1, s32[4]{0:T(128)} %lengths.1, bf16[32,7168]{1,0:T(8,128)(2,1)} %bitcast.6, bf16[32,2048]{1,0:T(8,128)(2,1)} %bitcast.7, bf16[512,1024]{1,0:T(8,128)(2,1)} %tests.1), custom_call_target="tpu_custom_call" | custom-call | flops 150994944 | bytes 5308416 | tf_op jit(solution)/shard_map/pallas_call | solution.py:93
  3.9 2.4 %collective-permute-start.1 = (f16[64,256]{1,0:T(8,128)(2,1)S(1)}, f16[64,256]{1,0:T(8,128)(2,1)S(1)}, u32[]{:S(2)}, u32[]{:S(2)}) collective-permute-start(f16[64,256]{1,0:T(8,128)(2,1)S(1)} %convert_element_type.9), channel_id=1, source_target_pairs={{0,3},{1,2},{2,1},{3,0},{4,7},{5,6},{6,5},{7,4},{8,11},{9,10},{10,... | collective-permute-start | bytes 98312 | tf_op jit(solution)/shard_map/ppermute | solution.py:237
  6.4 0.7 %collective-permute-start = (f16[64,256]{1,0:T(8,128)(2,1)S(1)}, f16[64,256]{1,0:T(8,128)(2,1)S(1)}, u32[]{:S(2)}, u32[]{:S(2)}) collective-permute-start(f16[64,256]{1,0:T(8,128)(2,1)S(1)} %convert_element_type.9), channel_id=1, source_target_pairs={{0,1},{1,0},{2,3},{3,2},{4,5},{5,4},{6,7},{7,6},{8,9},{9,8},{10,11... | collective-permute-start | bytes 98312 | tf_op jit(solution)/shard_map/ppermute | solution.py:238
  7.1 1.1 %collective-permute-done.1 = f16[64,256]{1,0:T(8,128)(2,1)S(1)} collective-permute-done((f16[64,256]{1,0:T(8,128)(2,1)S(1)}, f16[64,256]{1,0:T(8,128)(2,1)S(1)}, u32[]{:S(2)}, u32[]{:S(2)}) %collective-permute-start.1) | collective-permute-done | bytes 32800 | tf_op jit(solution)/shard_map/ppermute | solution.py:237
  8.2 0.0 collective-permute-done
  8.2 0.3 %shard_map.78 = bf16[4,1024]{1,0:T(4,128)(2,1)S(1)} custom-call(f32[64,256]{1,0:T(8,128)S(1)} %convert_element_type.10.refs_0_, f32[64,256]{1,0:T(8,128)S(1)} %convert_element_type.11.refs_1_), custom_call_target="tpu_custom_call" | custom-call | flops 8589934592 | tf_op jit(solution)/shard_map/pallas_call | solution.py:163
  8.5 0.5 %collective-permute-start.2 = (bf16[4,1024]{1,0:T(4,128)(2,1)S(1)}, bf16[4,1024]{1,0:T(4,128)(2,1)S(1)}, u32[]{:S(2)}, u32[]{:S(2)}) collective-permute-start(bf16[4,1024]{1,0:T(4,128)(2,1)S(1)} %shard_map.78), channel_id=1, source_target_pairs={{0,1},{1,0},{2,3},{3,2},{4,5},{5,4},{6,7},{7,6},{8,9},{9,8},{10,11... | collective-permute-start | bytes 24584 | tf_op jit(solution)/shard_map/ppermute | solution.py:240
  9.1 0.4 %fusion = f32[4,512]{1,0:T(4,128)S(1)} fusion(bf16[4,1024]{1,0:T(4,128)(2,1)S(1)} %shard_map.78, bf16[512,1024]{1,0:T(8,128)(2,1)S(1)} %get-tuple-element.7), kind=kOutput, calls=%fused_computation.1 | convolution fusion | flops 4194304 | bytes 1064960 | tf_op jit(solution)/shard_map/ep,qp->eq/dot_general | solution.py:246
  9.4 0.5 %collective-permute-done.2 = bf16[4,1024]{1,0:T(4,128)(2,1)S(1)} collective-permute-done((bf16[4,1024]{1,0:T(4,128)(2,1)S(1)}, bf16[4,1024]{1,0:T(4,128)(2,1)S(1)}, u32[]{:S(2)}, u32[]{:S(2)}) %collective-permute-start.2) | collective-permute-done | bytes 8224 | tf_op jit(solution)/shard_map/ppermute | solution.py:240
  9.9 2.4 %collective-permute-start.4 = (bf16[8,1024]{1,0:T(8,128)(2,1)S(1)}, bf16[8,1024]{1,0:T(8,128)(2,1)S(1)}, u32[]{:S(2)}, u32[]{:S(2)}) collective-permute-start(bf16[8,1024]{1,0:T(8,128)(2,1)S(1)} %pad_maximum_fusion.refs_0_), channel_id=1, source_target_pairs={{0,4},{1,9},{4,8},{5,13},{8,12},{9,0},{12,5},{13,1},{2,6},{3,11},{... | collective-permute-start | bytes 49160 | tf_op jit(solution)/shard_map/ppermute | solution.py:249
  12.3 1.9 %collective-permute-start.3 = (bf16[8,1024]{1,0:T(8,128)(2,1)S(1)}, bf16[8,1024]{1,0:T(8,128)(2,1)S(1)}, u32[]{:S(2)}, u32[]{:S(2)}) collective-permute-start(bf16[8,1024]{1,0:T(8,128)(2,1)S(1)} %pad_maximum_fusion.refs_0_), channel_id=1, source_target_pairs={{0,13},{1,12},{4,1},{5,0},{8,4},{9,5},{12,9},{13,8},{2,15},{3,14},... | collective-permute-start | bytes 49160 | tf_op jit(solution)/shard_map/ppermute | solution.py:250
  14.2 0.4 %collective-permute-start.6 = (f32[4,512]{1,0:T(4,128)S(1)}, f32[4,512]{1,0:T(4,128)S(1)}, u32[]{:S(2)}, u32[]{:S(2)}) collective-permute-start(f32[4,512]{1,0:T(4,128)S(1)} %fusion), channel_id=1, source_target_pairs={{0,1},{1,0},{4,5},{5,4},{8,9},{9,8},{12,13},{13,12},{2,3},{3,2},{6... | collective-permute-start | bytes 24584 | tf_op jit(solution)/shard_map/ppermute | solution.py:253
  14.5 0.0 collective-permute-done.4.refs_2_
  14.6 0.8 %collective-permute-start.5 = (bf16[8,1024]{1,0:T(8,128)(2,1)S(1)}, bf16[8,1024]{1,0:T(8,128)(2,1)S(1)}, u32[]{:S(2)}, u32[]{:S(2)}) collective-permute-start(bf16[8,1024]{1,0:T(8,128)(2,1)S(1)} %collective-permute-done.4.refs_2_), channel_id=1, source_target_pairs={{0,1},{1,0},{4,5},{5,4},{8,9},{9,8},{12,13},{13,12},{2,3},{3,2},{6... | collective-permute-start | bytes 49160 | tf_op jit(solution)/shard_map/ppermute | solution.py:251
  15.4 0.4 %fusion.1.refs_4_ = f32[4,512]{1,0:T(4,128)S(1)} fusion(bf16[4,1024]{1,0:T(4,128)(2,1)S(1)} %collective-permute-done.2, bf16[512,1024]{1,0:T(8,128)(2,1)S(1)} %get-tuple-element.7), kind=kOutput, calls=%fused_computation.2 | convolution fusion | flops 4194304 | bytes 1064960 | tf_op jit(solution)/shard_map/ep,qp->eq/dot_general | solution.py:252
  15.7 0.0 collective-permute-done.6.refs_5_
  15.7 0.1 collective-permute-done.3.refs_1_
  15.8 0.4 %collective-permute-done.5.refs_3_ = bf16[8,1024]{1,0:T(8,128)(2,1)S(1)} collective-permute-done((bf16[8,1024]{1,0:T(8,128)(2,1)S(1)}, bf16[8,1024]{1,0:T(8,128)(2,1)S(1)}, u32[]{:S(2)}, u32[]{:S(2)}) %collective-permute-start.5) | collective-permute-done | bytes 16416 | tf_op jit(solution)/shard_map/ppermute | solution.py:251
  16.2 1.1 %shard_map.79 = (f32[128,1024]{1,0:T(8,128)}, f32[4,1024]{1,0:T(4,128)}) custom-call(bf16[8,1024]{1,0:T(8,128)(2,1)S(1)} %pad_maximum_fusion.refs_0_, bf16[8,1024]{1,0:T(8,128)(2,1)S(1)} %collective-permute-done.3.refs_1_, bf16[8,1024]{1,0:T(8,128)(2,1)S(1)} %collective-permute-done.4.refs_2_, bf16[8,1024]{1,0:T(8,128)(2,1)S(1)} %collective-permute-done.5.refs_3_, ...), custom_call_target="tpu_custom_call" | custom-call | tf_op jit(solution)/shard_map/pallas_call | solution.py:216
  (4 shorter events, 0.0 us)
Async XLA Ops:
  3.9 4.2 %collective-permute-start.1 = (f16[64,256]{1,0:T(8,128)(2,1)S(1)}, f16[64,256]{1,0:T(8,128)(2,1)S(1)}, u32[]{:S(2)}, u32[]{:S(2)}) collective-permute-start(f16[64,256]{1,0:T(8,128)(2,1)S(1)} %convert_element_type.9), channel_id=1, source_target_pairs={{0,3},{1,2},{2,1},{3,0},{4,7},{5,6},{6,5},{7,4},{8,11},{9,10},{10,... | collective-permute-start | bytes 98312 | tf_op jit(solution)/shard_map/ppermute | solution.py:237
  6.4 1.8 %collective-permute-start = (f16[64,256]{1,0:T(8,128)(2,1)S(1)}, f16[64,256]{1,0:T(8,128)(2,1)S(1)}, u32[]{:S(2)}, u32[]{:S(2)}) collective-permute-start(f16[64,256]{1,0:T(8,128)(2,1)S(1)} %convert_element_type.9), channel_id=1, source_target_pairs={{0,1},{1,0},{2,3},{3,2},{4,5},{5,4},{6,7},{7,6},{8,9},{9,8},{10,11... | collective-permute-start | bytes 98312 | tf_op jit(solution)/shard_map/ppermute | solution.py:238
  8.5 1.3 %collective-permute-start.2 = (bf16[4,1024]{1,0:T(4,128)(2,1)S(1)}, bf16[4,1024]{1,0:T(4,128)(2,1)S(1)}, u32[]{:S(2)}, u32[]{:S(2)}) collective-permute-start(bf16[4,1024]{1,0:T(4,128)(2,1)S(1)} %shard_map.78), channel_id=1, source_target_pairs={{0,1},{1,0},{2,3},{3,2},{4,5},{5,4},{6,7},{7,6},{8,9},{9,8},{10,11... | collective-permute-start | bytes 24584 | tf_op jit(solution)/shard_map/ppermute | solution.py:240
  9.9 4.7 %collective-permute-start.4 = (bf16[8,1024]{1,0:T(8,128)(2,1)S(1)}, bf16[8,1024]{1,0:T(8,128)(2,1)S(1)}, u32[]{:S(2)}, u32[]{:S(2)}) collective-permute-start(bf16[8,1024]{1,0:T(8,128)(2,1)S(1)} %pad_maximum_fusion.refs_0_), channel_id=1, source_target_pairs={{0,4},{1,9},{4,8},{5,13},{8,12},{9,0},{12,5},{13,1},{2,6},{3,11},{... | collective-permute-start | bytes 49160 | tf_op jit(solution)/shard_map/ppermute | solution.py:249
  12.3 3.5 %collective-permute-start.3 = (bf16[8,1024]{1,0:T(8,128)(2,1)S(1)}, bf16[8,1024]{1,0:T(8,128)(2,1)S(1)}, u32[]{:S(2)}, u32[]{:S(2)}) collective-permute-start(bf16[8,1024]{1,0:T(8,128)(2,1)S(1)} %pad_maximum_fusion.refs_0_), channel_id=1, source_target_pairs={{0,13},{1,12},{4,1},{5,0},{8,4},{9,5},{12,9},{13,8},{2,15},{3,14},... | collective-permute-start | bytes 49160 | tf_op jit(solution)/shard_map/ppermute | solution.py:250
  14.2 1.5 %collective-permute-start.6 = (f32[4,512]{1,0:T(4,128)S(1)}, f32[4,512]{1,0:T(4,128)S(1)}, u32[]{:S(2)}, u32[]{:S(2)}) collective-permute-start(f32[4,512]{1,0:T(4,128)S(1)} %fusion), channel_id=1, source_target_pairs={{0,1},{1,0},{4,5},{5,4},{8,9},{9,8},{12,13},{13,12},{2,3},{3,2},{6... | collective-permute-start | bytes 24584 | tf_op jit(solution)/shard_map/ppermute | solution.py:253
  14.6 1.6 %collective-permute-start.5 = (bf16[8,1024]{1,0:T(8,128)(2,1)S(1)}, bf16[8,1024]{1,0:T(8,128)(2,1)S(1)}, u32[]{:S(2)}, u32[]{:S(2)}) collective-permute-start(bf16[8,1024]{1,0:T(8,128)(2,1)S(1)} %collective-permute-done.4.refs_2_), channel_id=1, source_target_pairs={{0,1},{1,0},{4,5},{5,4},{8,9},{9,8},{12,13},{13,12},{2,3},{3,2},{6... | collective-permute-start | bytes 49160 | tf_op jit(solution)/shard_map/ppermute | solution.py:251

commit v12 on v11

--- a/solution.py
+++ b/solution.py
@@ -8,9 +8,9 @@
 from jax.sharding import PartitionSpec as P
 
 SEQ = 64
-DEPTH = 256
-SWAPPED_SEND = (2, 5, 4, 7, 6, 0, 3, 1)
-DIRECT_SEND = (7, 6, 1, 0, 2, 3, 5, 4)
+DEPTHS = (1024, 512, 256, 128)
+SWAPPED_SEND = (3, 5, 4, 7, 6, 0, 2, 1)
+DIRECT_SEND = (7, 6, 0, 1, 2, 3, 5, 4)
 CONTRACT_LAST = (((1,), (1,)), ((), ()))
 CONTRACT_FIRST = (((0,), (0,)), ((), ()))
 
@@ -45,7 +45,7 @@
         ]
 
     def partial(weights, data, at, size):
-        depth = min(size, DEPTH)
+        depth = next(depth for depth in DEPTHS if size % depth == 0)
         terms = []
         for k in range(0, size, depth):
             lanes = pl.ds(at + k if isinstance(at, int) else pl.multiple_of(at + k, 128), depth)

time: 17.4 us -> 17.4 us (level)
    ppermute x1, starting transfers between devices: 0.37 us -> 0.61 us  [per_device(): raw = [own, lax.ppermute(for_other, group, swap)]]
    ppermute x1, starting transfers between devices: 0.8 us -> 0.56 us  [per_device(): gathered = [held, direct, fetched, lax.ppermute(fetched, group, swap)]]
    ppermute x1, starting transfers between devices: 2.41 us -> 2.18 us  [per_device(): fetched = lax.ppermute(held, group, list(enumerate(SWAPPED_SEND)))]
    ppermute x1, starting transfers between devices: 1.88 us -> 2.1 us  [per_device(): direct = lax.ppermute(held, group, list(enumerate(DIRECT_SEND)))]
where the time goes in v12:
time: 17.4 us; the launch traced here: 17.2 us
  starting transfers between devices  9.07 us (52%)
  Pallas kernels  4.67 us (27%)
  waiting for transfers between devices  2.04 us (12%)
  matrix products  0.74 us (4%)
  between operations  0.67 us (4%)
    pallas_call x1, Pallas kernels, project(): pl.pallas_call(functools.partial(project_kernel, scales), out_shape=(jax....  3.26 us
    ppermute x1, starting transfers between devices, per_device(): far = lax.ppermute(sent, ('mp', 'sub'), [(0, 3), (1, 2), (2, 1), (3, 0)])  2.44 us
    ppermute x1, starting transfers between devices, per_device(): fetched = lax.ppermute(held, group, list(enumerate(SWAPPED_SEND)))  2.18 us
    ppermute x1, starting transfers between devices, per_device(): direct = lax.ppermute(held, group, list(enumerate(DIRECT_SEND)))  2.1 us
    ppermute x1, waiting for transfers between devices, per_device(): far = lax.ppermute(sent, ('mp', 'sub'), [(0, 3), (1, 2), (2, 1), (3, 0)])  1.1 us
    pallas_call x1, Pallas kernels, finish(): pl.pallas_call(functools.partial(finish_kernel, examples, len(pieces), le...  1.05 us
    ppermute x1, starting transfers between devices, per_device(): near = lax.ppermute(sent, 'sub', [(0, 1), (1, 0)])  0.68 us
    ppermute x1, starting transfers between devices, per_device(): raw = [own, lax.ppermute(for_other, group, swap)]  0.61 us
  transfers between devices with their start and end apart: 7, of which 4 were waited for; matrix products, arithmetic and copies ran while one was open for 4% of the time, Pallas kernels for 0%

profile of v12, /device:TPU:0, one launch (start us, length us, event | category | flops | bytes accessed | tf_op | source)
XLA Modules:
  0.0 17.2 jit_solution(4267116887685139942)
XLA Ops:
  0.6 3.3 %shard_map.77 = (f32[64,256]{1,0:T(8,128)S(1)}, bf16[512,1024]{1,0:T(8,128)(2,1)S(1)}) custom-call(bf16[256,7168]{1,0:T(8,128)(2,1)} %hidden.1, bf16[256,2048]{1,0:T(8,128)(2,1)} %out_grad.1, s32[4]{0:T(128)} %lengths.1, bf16[32,7168]{1,0:T(8,128)(2,1)} %bitcast.6, bf16[32,2048]{1,0:T(8,128)(2,1)} %bitcast.7, bf16[512,1024]{1,0:T(8,128)(2,1)} %tests.1), custom_call_target="tpu_custom_call" | custom-call | flops 150994944 | bytes 5308416 | tf_op jit(solution)/shard_map/pallas_call | solution.py:93
  3.9 2.4 %collective-permute-start.1 = (f16[64,256]{1,0:T(8,128)(2,1)S(1)}, f16[64,256]{1,0:T(8,128)(2,1)S(1)}, u32[]{:S(2)}, u32[]{:S(2)}) collective-permute-start(f16[64,256]{1,0:T(8,128)(2,1)S(1)} %convert_element_type.9), channel_id=1, source_target_pairs={{0,3},{1,2},{2,1},{3,0},{4,7},{5,6},{6,5},{7,4},{8,11},{9,10},{10,... | collective-permute-start | bytes 98312 | tf_op jit(solution)/shard_map/ppermute | solution.py:237
  6.4 0.7 %collective-permute-start = (f16[64,256]{1,0:T(8,128)(2,1)S(1)}, f16[64,256]{1,0:T(8,128)(2,1)S(1)}, u32[]{:S(2)}, u32[]{:S(2)}) collective-permute-start(f16[64,256]{1,0:T(8,128)(2,1)S(1)} %convert_element_type.9), channel_id=1, source_target_pairs={{0,1},{1,0},{2,3},{3,2},{4,5},{5,4},{6,7},{7,6},{8,9},{9,8},{10,11... | collective-permute-start | bytes 98312 | tf_op jit(solution)/shard_map/ppermute | solution.py:238
  7.0 1.1 %collective-permute-done.1 = f16[64,256]{1,0:T(8,128)(2,1)S(1)} collective-permute-done((f16[64,256]{1,0:T(8,128)(2,1)S(1)}, f16[64,256]{1,0:T(8,128)(2,1)S(1)}, u32[]{:S(2)}, u32[]{:S(2)}) %collective-permute-start.1) | collective-permute-done | bytes 32800 | tf_op jit(solution)/shard_map/ppermute | solution.py:237
  8.2 0.0 collective-permute-done
  8.2 0.3 %shard_map.78 = bf16[4,1024]{1,0:T(4,128)(2,1)S(1)} custom-call(f32[64,256]{1,0:T(8,128)S(1)} %convert_element_type.10.refs_0_, f32[64,256]{1,0:T(8,128)S(1)} %convert_element_type.11.refs_1_), custom_call_target="tpu_custom_call" | custom-call | flops 8589934592 | tf_op jit(solution)/shard_map/pallas_call | solution.py:163
  8.5 0.5 %collective-permute-start.2 = (bf16[4,1024]{1,0:T(4,128)(2,1)S(1)}, bf16[4,1024]{1,0:T(4,128)(2,1)S(1)}, u32[]{:S(2)}, u32[]{:S(2)}) collective-permute-start(bf16[4,1024]{1,0:T(4,128)(2,1)S(1)} %shard_map.78), channel_id=1, source_target_pairs={{0,1},{1,0},{2,3},{3,2},{4,5},{5,4},{6,7},{7,6},{8,9},{9,8},{10,11... | collective-permute-start | bytes 24584 | tf_op jit(solution)/shard_map/ppermute | solution.py:240
  9.0 0.4 %fusion = f32[4,512]{1,0:T(4,128)S(1)} fusion(bf16[4,1024]{1,0:T(4,128)(2,1)S(1)} %shard_map.78, bf16[512,1024]{1,0:T(8,128)(2,1)S(1)} %get-tuple-element.7), kind=kOutput, calls=%fused_computation.1 | convolution fusion | flops 4194304 | bytes 1064960 | tf_op jit(solution)/shard_map/ep,qp->eq/dot_general | solution.py:246
  9.4 0.5 %collective-permute-done.2 = bf16[4,1024]{1,0:T(4,128)(2,1)S(1)} collective-permute-done((bf16[4,1024]{1,0:T(4,128)(2,1)S(1)}, bf16[4,1024]{1,0:T(4,128)(2,1)S(1)}, u32[]{:S(2)}, u32[]{:S(2)}) %collective-permute-start.2) | collective-permute-done | bytes 8224 | tf_op jit(solution)/shard_map/ppermute | solution.py:240
  9.9 2.2 %collective-permute-start.4 = (bf16[8,1024]{1,0:T(8,128)(2,1)S(1)}, bf16[8,1024]{1,0:T(8,128)(2,1)S(1)}, u32[]{:S(2)}, u32[]{:S(2)}) collective-permute-start(bf16[8,1024]{1,0:T(8,128)(2,1)S(1)} %pad_maximum_fusion.refs_0_), channel_id=1, source_target_pairs={{0,5},{1,9},{4,8},{5,13},{8,12},{9,0},{12,4},{13,1},{2,7},{3,11},{... | collective-permute-start | bytes 49160 | tf_op jit(solution)/shard_map/ppermute | solution.py:249
  12.1 2.1 %collective-permute-start.3 = (bf16[8,1024]{1,0:T(8,128)(2,1)S(1)}, bf16[8,1024]{1,0:T(8,128)(2,1)S(1)}, u32[]{:S(2)}, u32[]{:S(2)}) collective-permute-start(bf16[8,1024]{1,0:T(8,128)(2,1)S(1)} %pad_maximum_fusion.refs_0_), channel_id=1, source_target_pairs={{0,13},{1,12},{4,0},{5,1},{8,4},{9,5},{12,9},{13,8},{2,15},{3,14},... | collective-permute-start | bytes 49160 | tf_op jit(solution)/shard_map/ppermute | solution.py:250
  14.1 0.6 %collective-permute-start.6 = (f32[4,512]{1,0:T(4,128)S(1)}, f32[4,512]{1,0:T(4,128)S(1)}, u32[]{:S(2)}, u32[]{:S(2)}) collective-permute-start(f32[4,512]{1,0:T(4,128)S(1)} %fusion), channel_id=1, source_target_pairs={{0,1},{1,0},{4,5},{5,4},{8,9},{9,8},{12,13},{13,12},{2,3},{3,2},{6... | collective-permute-start | bytes 24584 | tf_op jit(solution)/shard_map/ppermute | solution.py:253
  14.8 0.0 collective-permute-done.4.refs_2_
  14.8 0.6 %collective-permute-start.5 = (bf16[8,1024]{1,0:T(8,128)(2,1)S(1)}, bf16[8,1024]{1,0:T(8,128)(2,1)S(1)}, u32[]{:S(2)}, u32[]{:S(2)}) collective-permute-start(bf16[8,1024]{1,0:T(8,128)(2,1)S(1)} %collective-permute-done.4.refs_2_), channel_id=1, source_target_pairs={{0,1},{1,0},{4,5},{5,4},{8,9},{9,8},{12,13},{13,12},{2,3},{3,2},{6... | collective-permute-start | bytes 49160 | tf_op jit(solution)/shard_map/ppermute | solution.py:251
  15.3 0.4 %fusion.1.refs_4_ = f32[4,512]{1,0:T(4,128)S(1)} fusion(bf16[4,1024]{1,0:T(4,128)(2,1)S(1)} %collective-permute-done.2, bf16[512,1024]{1,0:T(8,128)(2,1)S(1)} %get-tuple-element.7), kind=kOutput, calls=%fused_computation.2 | convolution fusion | flops 4194304 | bytes 1064960 | tf_op jit(solution)/shard_map/ep,qp->eq/dot_general | solution.py:252
  15.7 0.0 collective-permute-done.6.refs_5_
  15.7 0.1 collective-permute-done.3.refs_1_
  15.8 0.4 %collective-permute-done.5.refs_3_ = bf16[8,1024]{1,0:T(8,128)(2,1)S(1)} collective-permute-done((bf16[8,1024]{1,0:T(8,128)(2,1)S(1)}, bf16[8,1024]{1,0:T(8,128)(2,1)S(1)}, u32[]{:S(2)}, u32[]{:S(2)}) %collective-permute-start.5) | collective-permute-done | bytes 16416 | tf_op jit(solution)/shard_map/ppermute | solution.py:251
  16.2 1.1 %shard_map.79 = (f32[128,1024]{1,0:T(8,128)}, f32[4,1024]{1,0:T(4,128)}) custom-call(bf16[8,1024]{1,0:T(8,128)(2,1)S(1)} %pad_maximum_fusion.refs_0_, bf16[8,1024]{1,0:T(8,128)(2,1)S(1)} %collective-permute-done.3.refs_1_, bf16[8,1024]{1,0:T(8,128)(2,1)S(1)} %collective-permute-done.4.refs_2_, bf16[8,1024]{1,0:T(8,128)(2,1)S(1)} %collective-permute-done.5.refs_3_, ...), custom_call_target="tpu_custom_call" | custom-call | tf_op jit(solution)/shard_map/pallas_call | solution.py:216
  (4 shorter events, 0.0 us)
Async XLA Ops:
  3.9 4.2 %collective-permute-start.1 = (f16[64,256]{1,0:T(8,128)(2,1)S(1)}, f16[64,256]{1,0:T(8,128)(2,1)S(1)}, u32[]{:S(2)}, u32[]{:S(2)}) collective-permute-start(f16[64,256]{1,0:T(8,128)(2,1)S(1)} %convert_element_type.9), channel_id=1, source_target_pairs={{0,3},{1,2},{2,1},{3,0},{4,7},{5,6},{6,5},{7,4},{8,11},{9,10},{10,... | collective-permute-start | bytes 98312 | tf_op jit(solution)/shard_map/ppermute | solution.py:237
  6.4 1.8 %collective-permute-start = (f16[64,256]{1,0:T(8,128)(2,1)S(1)}, f16[64,256]{1,0:T(8,128)(2,1)S(1)}, u32[]{:S(2)}, u32[]{:S(2)}) collective-permute-start(f16[64,256]{1,0:T(8,128)(2,1)S(1)} %convert_element_type.9), channel_id=1, source_target_pairs={{0,1},{1,0},{2,3},{3,2},{4,5},{5,4},{6,7},{7,6},{8,9},{9,8},{10,11... | collective-permute-start | bytes 98312 | tf_op jit(solution)/shard_map/ppermute | solution.py:238
  8.5 1.3 %collective-permute-start.2 = (bf16[4,1024]{1,0:T(4,128)(2,1)S(1)}, bf16[4,1024]{1,0:T(4,128)(2,1)S(1)}, u32[]{:S(2)}, u32[]{:S(2)}) collective-permute-start(bf16[4,1024]{1,0:T(4,128)(2,1)S(1)} %shard_map.78), channel_id=1, source_target_pairs={{0,1},{1,0},{2,3},{3,2},{4,5},{5,4},{6,7},{7,6},{8,9},{9,8},{10,11... | collective-permute-start | bytes 24584 | tf_op jit(solution)/shard_map/ppermute | solution.py:240
  9.9 4.9 %collective-permute-start.4 = (bf16[8,1024]{1,0:T(8,128)(2,1)S(1)}, bf16[8,1024]{1,0:T(8,128)(2,1)S(1)}, u32[]{:S(2)}, u32[]{:S(2)}) collective-permute-start(bf16[8,1024]{1,0:T(8,128)(2,1)S(1)} %pad_maximum_fusion.refs_0_), channel_id=1, source_target_pairs={{0,5},{1,9},{4,8},{5,13},{8,12},{9,0},{12,4},{13,1},{2,7},{3,11},{... | collective-permute-start | bytes 49160 | tf_op jit(solution)/shard_map/ppermute | solution.py:249
  12.1 3.8 %collective-permute-start.3 = (bf16[8,1024]{1,0:T(8,128)(2,1)S(1)}, bf16[8,1024]{1,0:T(8,128)(2,1)S(1)}, u32[]{:S(2)}, u32[]{:S(2)}) collective-permute-start(bf16[8,1024]{1,0:T(8,128)(2,1)S(1)} %pad_maximum_fusion.refs_0_), channel_id=1, source_target_pairs={{0,13},{1,12},{4,0},{5,1},{8,4},{9,5},{12,9},{13,8},{2,15},{3,14},... | collective-permute-start | bytes 49160 | tf_op jit(solution)/shard_map/ppermute | solution.py:250
  14.1 1.5 %collective-permute-start.6 = (f32[4,512]{1,0:T(4,128)S(1)}, f32[4,512]{1,0:T(4,128)S(1)}, u32[]{:S(2)}, u32[]{:S(2)}) collective-permute-start(f32[4,512]{1,0:T(4,128)S(1)} %fusion), channel_id=1, source_target_pairs={{0,1},{1,0},{4,5},{5,4},{8,9},{9,8},{12,13},{13,12},{2,3},{3,2},{6... | collective-permute-start | bytes 24584 | tf_op jit(solution)/shard_map/ppermute | solution.py:253
  14.8 1.4 %collective-permute-start.5 = (bf16[8,1024]{1,0:T(8,128)(2,1)S(1)}, bf16[8,1024]{1,0:T(8,128)(2,1)S(1)}, u32[]{:S(2)}, u32[]{:S(2)}) collective-permute-start(bf16[8,1024]{1,0:T(8,128)(2,1)S(1)} %collective-permute-done.4.refs_2_), channel_id=1, source_target_pairs={{0,1},{1,0},{4,5},{5,4},{8,9},{9,8},{12,13},{13,12},{2,3},{3,2},{6... | collective-permute-start | bytes 49160 | tf_op jit(solution)/shard_map/ppermute | solution.py:251

commit v13 on v12

--- a/solution.py
+++ b/solution.py
@@ -236,7 +236,7 @@
         sent = lax.optimization_barrier(both.astype(jnp.float16))
         far = lax.ppermute(sent, ("mp", "sub"), [(0, 3), (1, 2), (2, 1), (3, 0)])
         near = lax.ppermute(sent, "sub", [(0, 1), (1, 0)])
-        made = example_grads([near.astype(jnp.float32), far.astype(jnp.float32)], k_in, k_out, scales)
+        made = example_grads([far.astype(jnp.float32), near.astype(jnp.float32)], k_in, k_out, scales)
         grads = lax.ppermute(made, "sub", [(0, 1), (1, 0)])
     else:
         grads = example_grads([lax.psum(both, "mp")], k_in, k_out, scales)

time: 17.4 us -> 17.4 us (level)
  waiting for transfers between devices: 2.04 us -> 2.82 us
  starting transfers between devices: 9.07 us -> 8.33 us
    ppermute x1, waiting for transfers between devices: 1.1 us -> 1.66 us  [per_device(): far = lax.ppermute(sent, ('mp', 'sub'), [(0, 3), (1, 2), (2, 1), (3, 0)])]
    ppermute x1, starting transfers between devices: 0.5 us -> 0.12 us  [per_device(): grads = lax.ppermute(made, 'sub', [(0, 1), (1, 0)])]
    ppermute x1, starting transfers between devices: 2.18 us -> 1.81 us  [per_device(): fetched = lax.ppermute(held, group, list(enumerate(SWAPPED_SEND)))]
    ppermute x1, waiting for transfers between devices: 0.46 us -> 0.69 us  [per_device(): grads = lax.ppermute(made, 'sub', [(0, 1), (1, 0)])]
    ppermute x1, starting transfers between devices: 0.56 us -> 0.74 us  [per_device(): gathered = [held, direct, fetched, lax.ppermute(fetched, group, swap)]]
    ppermute x1, starting transfers between devices: 0.61 us -> 0.43 us  [per_device(): raw = [own, lax.ppermute(for_other, group, swap)]]
where the time goes in v13:
time: 17.4 us; the launch traced here: 17.3 us
  starting transfers between devices  8.33 us (48%)
  Pallas kernels  4.67 us (27%)
  waiting for transfers between devices  2.82 us (16%)
  matrix products  0.74 us (4%)
  between operations  0.66 us (4%)
    pallas_call x1, Pallas kernels, project(): pl.pallas_call(functools.partial(project_kernel, scales), out_shape=(jax....  3.26 us
    ppermute x1, starting transfers between devices, per_device(): far = lax.ppermute(sent, ('mp', 'sub'), [(0, 3), (1, 2), (2, 1), (3, 0)])  2.61 us
    ppermute x1, starting transfers between devices, per_device(): direct = lax.ppermute(held, group, list(enumerate(DIRECT_SEND)))  2.1 us
    ppermute x1, starting transfers between devices, per_device(): fetched = lax.ppermute(held, group, list(enumerate(SWAPPED_SEND)))  1.81 us
    ppermute x1, waiting for transfers between devices, per_device(): far = lax.ppermute(sent, ('mp', 'sub'), [(0, 3), (1, 2), (2, 1), (3, 0)])  1.66 us
    pallas_call x1, Pallas kernels, finish(): pl.pallas_call(functools.partial(finish_kernel, examples, len(pieces), le...  1.05 us
    ppermute x1, starting transfers between devices, per_device(): gathered = [held, direct, fetched, lax.ppermute(fetched, group, swap)]  0.74 us
    ppermute x1, waiting for transfers between devices, per_device(): grads = lax.ppermute(made, 'sub', [(0, 1), (1, 0)])  0.69 us
  transfers between devices with their start and end apart: 7, of which 4 were waited for; matrix products, arithmetic and copies ran while one was open for 4% of the time, Pallas kernels for 0%

profile of v13, /device:TPU:0, one launch (start us, length us, event | category | flops | bytes accessed | tf_op | source)
XLA Modules:
  0.0 17.3 jit_solution(9656185535628402539)
XLA Ops:
  0.6 3.3 %shard_map.77 = (f32[64,256]{1,0:T(8,128)S(1)}, bf16[512,1024]{1,0:T(8,128)(2,1)S(1)}) custom-call(bf16[256,7168]{1,0:T(8,128)(2,1)} %hidden.1, bf16[256,2048]{1,0:T(8,128)(2,1)} %out_grad.1, s32[4]{0:T(128)} %lengths.1, bf16[32,7168]{1,0:T(8,128)(2,1)} %bitcast.6, bf16[32,2048]{1,0:T(8,128)(2,1)} %bitcast.7, bf16[512,1024]{1,0:T(8,128)(2,1)} %tests.1), custom_call_target="tpu_custom_call" | custom-call | flops 150994944 | bytes 5308416 | tf_op jit(solution)/shard_map/pallas_call | solution.py:93
  3.9 0.5 %collective-permute-start.1 = (f16[64,256]{1,0:T(8,128)(2,1)S(1)}, f16[64,256]{1,0:T(8,128)(2,1)S(1)}, u32[]{:S(2)}, u32[]{:S(2)}) collective-permute-start(f16[64,256]{1,0:T(8,128)(2,1)S(1)} %convert_element_type.9), channel_id=1, source_target_pairs={{0,1},{1,0},{2,3},{3,2},{4,5},{5,4},{6,7},{7,6},{8,9},{9,8},{10,11... | collective-permute-start | bytes 98312 | tf_op jit(solution)/shard_map/ppermute | solution.py:238
  4.4 2.6 %collective-permute-start = (f16[64,256]{1,0:T(8,128)(2,1)S(1)}, f16[64,256]{1,0:T(8,128)(2,1)S(1)}, u32[]{:S(2)}, u32[]{:S(2)}) collective-permute-start(f16[64,256]{1,0:T(8,128)(2,1)S(1)} %convert_element_type.9), channel_id=1, source_target_pairs={{0,3},{1,2},{2,1},{3,0},{4,7},{5,6},{6,5},{7,4},{8,11},{9,10},{10,... | collective-permute-start | bytes 98312 | tf_op jit(solution)/shard_map/ppermute | solution.py:237
  7.1 0.0 collective-permute-done.1
  7.1 1.7 %collective-permute-done = f16[64,256]{1,0:T(8,128)(2,1)S(1)} collective-permute-done((f16[64,256]{1,0:T(8,128)(2,1)S(1)}, f16[64,256]{1,0:T(8,128)(2,1)S(1)}, u32[]{:S(2)}, u32[]{:S(2)}) %collective-permute-start) | collective-permute-done | bytes 32800 | tf_op jit(solution)/shard_map/ppermute | solution.py:237
  8.7 0.4 %shard_map.78 = bf16[4,1024]{1,0:T(4,128)(2,1)S(1)} custom-call(f32[64,256]{1,0:T(8,128)S(1)} %convert_element_type.10.refs_0_, f32[64,256]{1,0:T(8,128)S(1)} %convert_element_type.11.refs_1_), custom_call_target="tpu_custom_call" | custom-call | flops 8589934592 | tf_op jit(solution)/shard_map/pallas_call | solution.py:163
  9.1 0.1 collective-permute-start.2
  9.2 0.4 %fusion = f32[4,512]{1,0:T(4,128)S(1)} fusion(bf16[4,1024]{1,0:T(4,128)(2,1)S(1)} %shard_map.78, bf16[512,1024]{1,0:T(8,128)(2,1)S(1)} %get-tuple-element.7), kind=kOutput, calls=%fused_computation.1 | convolution fusion | flops 4194304 | bytes 1064960 | tf_op jit(solution)/shard_map/ep,qp->eq/dot_general | solution.py:246
  9.6 0.7 %collective-permute-done.2 = bf16[4,1024]{1,0:T(4,128)(2,1)S(1)} collective-permute-done((bf16[4,1024]{1,0:T(4,128)(2,1)S(1)}, bf16[4,1024]{1,0:T(4,128)(2,1)S(1)}, u32[]{:S(2)}, u32[]{:S(2)}) %collective-permute-start.2) | collective-permute-done | bytes 8224 | tf_op jit(solution)/shard_map/ppermute | solution.py:240
  10.3 1.8 %collective-permute-start.4 = (bf16[8,1024]{1,0:T(8,128)(2,1)S(1)}, bf16[8,1024]{1,0:T(8,128)(2,1)S(1)}, u32[]{:S(2)}, u32[]{:S(2)}) collective-permute-start(bf16[8,1024]{1,0:T(8,128)(2,1)S(1)} %pad_maximum_fusion.refs_0_), channel_id=1, source_target_pairs={{0,5},{1,9},{4,8},{5,13},{8,12},{9,0},{12,4},{13,1},{2,7},{3,11},{... | collective-permute-start | bytes 49160 | tf_op jit(solution)/shard_map/ppermute | solution.py:249
  12.1 2.1 %collective-permute-start.3 = (bf16[8,1024]{1,0:T(8,128)(2,1)S(1)}, bf16[8,1024]{1,0:T(8,128)(2,1)S(1)}, u32[]{:S(2)}, u32[]{:S(2)}) collective-permute-start(bf16[8,1024]{1,0:T(8,128)(2,1)S(1)} %pad_maximum_fusion.refs_0_), channel_id=1, source_target_pairs={{0,13},{1,12},{4,0},{5,1},{8,4},{9,5},{12,9},{13,8},{2,15},{3,14},... | collective-permute-start | bytes 49160 | tf_op jit(solution)/shard_map/ppermute | solution.py:250
  14.2 0.4 %collective-permute-start.6 = (f32[4,512]{1,0:T(4,128)S(1)}, f32[4,512]{1,0:T(4,128)S(1)}, u32[]{:S(2)}, u32[]{:S(2)}) collective-permute-start(f32[4,512]{1,0:T(4,128)S(1)} %fusion), channel_id=1, source_target_pairs={{0,1},{1,0},{4,5},{5,4},{8,9},{9,8},{12,13},{13,12},{2,3},{3,2},{6... | collective-permute-start | bytes 24584 | tf_op jit(solution)/shard_map/ppermute | solution.py:253
  14.6 0.0 collective-permute-done.4.refs_2_
  14.6 0.7 %collective-permute-start.5 = (bf16[8,1024]{1,0:T(8,128)(2,1)S(1)}, bf16[8,1024]{1,0:T(8,128)(2,1)S(1)}, u32[]{:S(2)}, u32[]{:S(2)}) collective-permute-start(bf16[8,1024]{1,0:T(8,128)(2,1)S(1)} %collective-permute-done.4.refs_2_), channel_id=1, source_target_pairs={{0,1},{1,0},{4,5},{5,4},{8,9},{9,8},{12,13},{13,12},{2,3},{3,2},{6... | collective-permute-start | bytes 49160 | tf_op jit(solution)/shard_map/ppermute | solution.py:251
  15.4 0.4 %fusion.1.refs_4_ = f32[4,512]{1,0:T(4,128)S(1)} fusion(bf16[4,1024]{1,0:T(4,128)(2,1)S(1)} %collective-permute-done.2, bf16[512,1024]{1,0:T(8,128)(2,1)S(1)} %get-tuple-element.7), kind=kOutput, calls=%fused_computation.2 | convolution fusion | flops 4194304 | bytes 1064960 | tf_op jit(solution)/shard_map/ep,qp->eq/dot_general | solution.py:252
  15.7 0.0 collective-permute-done.6.refs_5_
  15.7 0.1 collective-permute-done.3.refs_1_
  15.8 0.4 %collective-permute-done.5.refs_3_ = bf16[8,1024]{1,0:T(8,128)(2,1)S(1)} collective-permute-done((bf16[8,1024]{1,0:T(8,128)(2,1)S(1)}, bf16[8,1024]{1,0:T(8,128)(2,1)S(1)}, u32[]{:S(2)}, u32[]{:S(2)}) %collective-permute-start.5) | collective-permute-done | bytes 16416 | tf_op jit(solution)/shard_map/ppermute | solution.py:251
  16.2 1.1 %shard_map.79 = (f32[128,1024]{1,0:T(8,128)}, f32[4,1024]{1,0:T(4,128)}) custom-call(bf16[8,1024]{1,0:T(8,128)(2,1)S(1)} %pad_maximum_fusion.refs_0_, bf16[8,1024]{1,0:T(8,128)(2,1)S(1)} %collective-permute-done.3.refs_1_, bf16[8,1024]{1,0:T(8,128)(2,1)S(1)} %collective-permute-done.4.refs_2_, bf16[8,1024]{1,0:T(8,128)(2,1)S(1)} %collective-permute-done.5.refs_3_, ...), custom_call_target="tpu_custom_call" | custom-call | tf_op jit(solution)/shard_map/pallas_call | solution.py:216
  (4 shorter events, 0.0 us)
Async XLA Ops:
  3.9 3.1 %collective-permute-start.1 = (f16[64,256]{1,0:T(8,128)(2,1)S(1)}, f16[64,256]{1,0:T(8,128)(2,1)S(1)}, u32[]{:S(2)}, u32[]{:S(2)}) collective-permute-start(f16[64,256]{1,0:T(8,128)(2,1)S(1)} %convert_element_type.9), channel_id=1, source_target_pairs={{0,1},{1,0},{2,3},{3,2},{4,5},{5,4},{6,7},{7,6},{8,9},{9,8},{10,11... | collective-permute-start | bytes 98312 | tf_op jit(solution)/shard_map/ppermute | solution.py:238
  4.4 4.3 %collective-permute-start = (f16[64,256]{1,0:T(8,128)(2,1)S(1)}, f16[64,256]{1,0:T(8,128)(2,1)S(1)}, u32[]{:S(2)}, u32[]{:S(2)}) collective-permute-start(f16[64,256]{1,0:T(8,128)(2,1)S(1)} %convert_element_type.9), channel_id=1, source_target_pairs={{0,3},{1,2},{2,1},{3,0},{4,7},{5,6},{6,5},{7,4},{8,11},{9,10},{10,... | collective-permute-start | bytes 98312 | tf_op jit(solution)/shard_map/ppermute | solution.py:237
  9.1 1.2 %collective-permute-start.2 = (bf16[4,1024]{1,0:T(4,128)(2,1)S(1)}, bf16[4,1024]{1,0:T(4,128)(2,1)S(1)}, u32[]{:S(2)}, u32[]{:S(2)}) collective-permute-start(bf16[4,1024]{1,0:T(4,128)(2,1)S(1)} %shard_map.78), channel_id=1, source_target_pairs={{0,1},{1,0},{2,3},{3,2},{4,5},{5,4},{6,7},{7,6},{8,9},{9,8},{10,11... | collective-permute-start | bytes 24584 | tf_op jit(solution)/shard_map/ppermute | solution.py:240
  10.3 4.3 %collective-permute-start.4 = (bf16[8,1024]{1,0:T(8,128)(2,1)S(1)}, bf16[8,1024]{1,0:T(8,128)(2,1)S(1)}, u32[]{:S(2)}, u32[]{:S(2)}) collective-permute-start(bf16[8,1024]{1,0:T(8,128)(2,1)S(1)} %pad_maximum_fusion.refs_0_), channel_id=1, source_target_pairs={{0,5},{1,9},{4,8},{5,13},{8,12},{9,0},{12,4},{13,1},{2,7},{3,11},{... | collective-permute-start | bytes 49160 | tf_op jit(solution)/shard_map/ppermute | solution.py:249
  12.1 3.8 %collective-permute-start.3 = (bf16[8,1024]{1,0:T(8,128)(2,1)S(1)}, bf16[8,1024]{1,0:T(8,128)(2,1)S(1)}, u32[]{:S(2)}, u32[]{:S(2)}) collective-permute-start(bf16[8,1024]{1,0:T(8,128)(2,1)S(1)} %pad_maximum_fusion.refs_0_), channel_id=1, source_target_pairs={{0,13},{1,12},{4,0},{5,1},{8,4},{9,5},{12,9},{13,8},{2,15},{3,14},... | collective-permute-start | bytes 49160 | tf_op jit(solution)/shard_map/ppermute | solution.py:250
  14.2 1.5 %collective-permute-start.6 = (f32[4,512]{1,0:T(4,128)S(1)}, f32[4,512]{1,0:T(4,128)S(1)}, u32[]{:S(2)}, u32[]{:S(2)}) collective-permute-start(f32[4,512]{1,0:T(4,128)S(1)} %fusion), channel_id=1, source_target_pairs={{0,1},{1,0},{4,5},{5,4},{8,9},{9,8},{12,13},{13,12},{2,3},{3,2},{6... | collective-permute-start | bytes 24584 | tf_op jit(solution)/shard_map/ppermute | solution.py:253
  14.6 1.6 %collective-permute-start.5 = (bf16[8,1024]{1,0:T(8,128)(2,1)S(1)}, bf16[8,1024]{1,0:T(8,128)(2,1)S(1)}, u32[]{:S(2)}, u32[]{:S(2)}) collective-permute-start(bf16[8,1024]{1,0:T(8,128)(2,1)S(1)} %collective-permute-done.4.refs_2_), channel_id=1, source_target_pairs={{0,1},{1,0},{4,5},{5,4},{8,9},{9,8},{12,13},{13,12},{2,3},{3,2},{6... | collective-permute-start | bytes 49160 | tf_op jit(solution)/shard_map/ppermute | solution.py:251

commit v14 on v13

--- a/solution.py
+++ b/solution.py
@@ -55,8 +55,8 @@
 
     steps = range(0 if small else 1, 4)
     for n in steps:
-        for copy in copies_of(n):
-            copy.start()
+        for priority, copy in enumerate(copies_of(n)):
+            copy.start(priority=(priority + n) % 2)
     bounds = pltpu.make_async_copy(lengths, limits, sems.at[0, 4])
     bounds.start()
     fetch = pltpu.make_async_copy(tests, near_tests, sems.at[1, 4])
@@ -202,7 +202,7 @@
         block[part] = lax.dot_general(own[:, at:at + step], every, CONTRACT_FIRST,
                                       preferred_element_type=jnp.float32) * (1.0 / examples)
         copies.append(pltpu.make_async_copy(block.at[part], cov.at[part], sems.at[n]))
-        copies[-1].start()
+        copies[-1].start(priority=n % 2)
     for copy in copies:
         copy.wait()
 

time: 17.4 us -> 18.5 us (1.063)
  Pallas kernels: 4.67 us -> 5.8 us
    pallas_call x1, Pallas kernels: 3.26 us -> 4.4 us  [project(): pl.pallas_call(functools.partial(project_kernel, scales), out_shape=(jax....]
where the time goes in v14:
time: 18.5 us; the launch traced here: 18.4 us
  starting transfers between devices  8.33 us (45%)
  Pallas kernels  5.8 us (31%)
  waiting for transfers between devices  2.82 us (15%)
  matrix products  0.74 us (4%)
  between operations  0.66 us (4%)
    pallas_call x1, Pallas kernels, project(): pl.pallas_call(functools.partial(project_kernel, scales), out_shape=(jax....  4.4 us
    ppermute x1, starting transfers between devices, per_device(): far = lax.ppermute(sent, ('mp', 'sub'), [(0, 3), (1, 2), (2, 1), (3, 0)])  2.62 us
    ppermute x1, starting transfers between devices, per_device(): direct = lax.ppermute(held, group, list(enumerate(DIRECT_SEND)))  2.1 us
    ppermute x1, starting transfers between devices, per_device(): fetched = lax.ppermute(held, group, list(enumerate(SWAPPED_SEND)))  1.81 us
    ppermute x1, waiting for transfers between devices, per_device(): far = lax.ppermute(sent, ('mp', 'sub'), [(0, 3), (1, 2), (2, 1), (3, 0)])  1.66 us
    pallas_call x1, Pallas kernels, finish(): pl.pallas_call(functools.partial(finish_kernel, examples, len(pieces), le...  1.05 us
    ppermute x1, starting transfers between devices, per_device(): gathered = [held, direct, fetched, lax.ppermute(fetched, group, swap)]  0.74 us
    ppermute x1, waiting for transfers between devices, per_device(): grads = lax.ppermute(made, 'sub', [(0, 1), (1, 0)])  0.69 us
  transfers between devices with their start and end apart: 7, of which 4 were waited for; matrix products, arithmetic and copies ran while one was open for 4% of the time, Pallas kernels for 0%

profile of v14, /device:TPU:0, one launch (start us, length us, event | category | flops | bytes accessed | tf_op | source)
XLA Modules:
  0.0 18.4 jit_solution(903055406171566608)
XLA Ops:
  0.6 4.4 %shard_map.77 = (f32[64,256]{1,0:T(8,128)S(1)}, bf16[512,1024]{1,0:T(8,128)(2,1)S(1)}) custom-call(bf16[256,7168]{1,0:T(8,128)(2,1)} %hidden.1, bf16[256,2048]{1,0:T(8,128)(2,1)} %out_grad.1, s32[4]{0:T(128)} %lengths.1, bf16[32,7168]{1,0:T(8,128)(2,1)} %bitcast.6, bf16[32,2048]{1,0:T(8,128)(2,1)} %bitcast.7, bf16[512,1024]{1,0:T(8,128)(2,1)} %tests.1), custom_call_target="tpu_custom_call" | custom-call | flops 150994944 | bytes 5308416 | tf_op jit(solution)/shard_map/pallas_call | solution.py:93
  5.1 0.5 %collective-permute-start.1 = (f16[64,256]{1,0:T(8,128)(2,1)S(1)}, f16[64,256]{1,0:T(8,128)(2,1)S(1)}, u32[]{:S(2)}, u32[]{:S(2)}) collective-permute-start(f16[64,256]{1,0:T(8,128)(2,1)S(1)} %convert_element_type.9), channel_id=1, source_target_pairs={{0,1},{1,0},{2,3},{3,2},{4,5},{5,4},{6,7},{7,6},{8,9},{9,8},{10,11... | collective-permute-start | bytes 98312 | tf_op jit(solution)/shard_map/ppermute | solution.py:238
  5.6 2.6 %collective-permute-start = (f16[64,256]{1,0:T(8,128)(2,1)S(1)}, f16[64,256]{1,0:T(8,128)(2,1)S(1)}, u32[]{:S(2)}, u32[]{:S(2)}) collective-permute-start(f16[64,256]{1,0:T(8,128)(2,1)S(1)} %convert_element_type.9), channel_id=1, source_target_pairs={{0,3},{1,2},{2,1},{3,0},{4,7},{5,6},{6,5},{7,4},{8,11},{9,10},{10,... | collective-permute-start | bytes 98312 | tf_op jit(solution)/shard_map/ppermute | solution.py:237
  8.2 0.0 collective-permute-done.1
  8.2 1.7 %collective-permute-done = f16[64,256]{1,0:T(8,128)(2,1)S(1)} collective-permute-done((f16[64,256]{1,0:T(8,128)(2,1)S(1)}, f16[64,256]{1,0:T(8,128)(2,1)S(1)}, u32[]{:S(2)}, u32[]{:S(2)}) %collective-permute-start) | collective-permute-done | bytes 32800 | tf_op jit(solution)/shard_map/ppermute | solution.py:237
  9.9 0.4 %shard_map.78 = bf16[4,1024]{1,0:T(4,128)(2,1)S(1)} custom-call(f32[64,256]{1,0:T(8,128)S(1)} %convert_element_type.10.refs_0_, f32[64,256]{1,0:T(8,128)S(1)} %convert_element_type.11.refs_1_), custom_call_target="tpu_custom_call" | custom-call | flops 8589934592 | tf_op jit(solution)/shard_map/pallas_call | solution.py:163
  10.2 0.1 collective-permute-start.2
  10.3 0.4 %fusion = f32[4,512]{1,0:T(4,128)S(1)} fusion(bf16[4,1024]{1,0:T(4,128)(2,1)S(1)} %shard_map.78, bf16[512,1024]{1,0:T(8,128)(2,1)S(1)} %get-tuple-element.7), kind=kOutput, calls=%fused_computation.1 | convolution fusion | flops 4194304 | bytes 1064960 | tf_op jit(solution)/shard_map/ep,qp->eq/dot_general | solution.py:246
  10.7 0.7 %collective-permute-done.2 = bf16[4,1024]{1,0:T(4,128)(2,1)S(1)} collective-permute-done((bf16[4,1024]{1,0:T(4,128)(2,1)S(1)}, bf16[4,1024]{1,0:T(4,128)(2,1)S(1)}, u32[]{:S(2)}, u32[]{:S(2)}) %collective-permute-start.2) | collective-permute-done | bytes 8224 | tf_op jit(solution)/shard_map/ppermute | solution.py:240
  11.4 1.8 %collective-permute-start.4 = (bf16[8,1024]{1,0:T(8,128)(2,1)S(1)}, bf16[8,1024]{1,0:T(8,128)(2,1)S(1)}, u32[]{:S(2)}, u32[]{:S(2)}) collective-permute-start(bf16[8,1024]{1,0:T(8,128)(2,1)S(1)} %pad_maximum_fusion.refs_0_), channel_id=1, source_target_pairs={{0,5},{1,9},{4,8},{5,13},{8,12},{9,0},{12,4},{13,1},{2,7},{3,11},{... | collective-permute-start | bytes 49160 | tf_op jit(solution)/shard_map/ppermute | solution.py:249
  13.2 2.1 %collective-permute-start.3 = (bf16[8,1024]{1,0:T(8,128)(2,1)S(1)}, bf16[8,1024]{1,0:T(8,128)(2,1)S(1)}, u32[]{:S(2)}, u32[]{:S(2)}) collective-permute-start(bf16[8,1024]{1,0:T(8,128)(2,1)S(1)} %pad_maximum_fusion.refs_0_), channel_id=1, source_target_pairs={{0,13},{1,12},{4,0},{5,1},{8,4},{9,5},{12,9},{13,8},{2,15},{3,14},... | collective-permute-start | bytes 49160 | tf_op jit(solution)/shard_map/ppermute | solution.py:250
  15.3 0.4 %collective-permute-start.6 = (f32[4,512]{1,0:T(4,128)S(1)}, f32[4,512]{1,0:T(4,128)S(1)}, u32[]{:S(2)}, u32[]{:S(2)}) collective-permute-start(f32[4,512]{1,0:T(4,128)S(1)} %fusion), channel_id=1, source_target_pairs={{0,1},{1,0},{4,5},{5,4},{8,9},{9,8},{12,13},{13,12},{2,3},{3,2},{6... | collective-permute-start | bytes 24584 | tf_op jit(solution)/shard_map/ppermute | solution.py:253
  15.8 0.0 collective-permute-done.4.refs_2_
  15.8 0.7 %collective-permute-start.5 = (bf16[8,1024]{1,0:T(8,128)(2,1)S(1)}, bf16[8,1024]{1,0:T(8,128)(2,1)S(1)}, u32[]{:S(2)}, u32[]{:S(2)}) collective-permute-start(bf16[8,1024]{1,0:T(8,128)(2,1)S(1)} %collective-permute-done.4.refs_2_), channel_id=1, source_target_pairs={{0,1},{1,0},{4,5},{5,4},{8,9},{9,8},{12,13},{13,12},{2,3},{3,2},{6... | collective-permute-start | bytes 49160 | tf_op jit(solution)/shard_map/ppermute | solution.py:251
  16.5 0.4 %fusion.1.refs_4_ = f32[4,512]{1,0:T(4,128)S(1)} fusion(bf16[4,1024]{1,0:T(4,128)(2,1)S(1)} %collective-permute-done.2, bf16[512,1024]{1,0:T(8,128)(2,1)S(1)} %get-tuple-element.7), kind=kOutput, calls=%fused_computation.2 | convolution fusion | flops 4194304 | bytes 1064960 | tf_op jit(solution)/shard_map/ep,qp->eq/dot_general | solution.py:252
  16.9 0.0 collective-permute-done.6.refs_5_
  16.9 0.1 collective-permute-done.3.refs_1_
  17.0 0.4 %collective-permute-done.5.refs_3_ = bf16[8,1024]{1,0:T(8,128)(2,1)S(1)} collective-permute-done((bf16[8,1024]{1,0:T(8,128)(2,1)S(1)}, bf16[8,1024]{1,0:T(8,128)(2,1)S(1)}, u32[]{:S(2)}, u32[]{:S(2)}) %collective-permute-start.5) | collective-permute-done | bytes 16416 | tf_op jit(solution)/shard_map/ppermute | solution.py:251
  17.3 1.1 %shard_map.79 = (f32[128,1024]{1,0:T(8,128)}, f32[4,1024]{1,0:T(4,128)}) custom-call(bf16[8,1024]{1,0:T(8,128)(2,1)S(1)} %pad_maximum_fusion.refs_0_, bf16[8,1024]{1,0:T(8,128)(2,1)S(1)} %collective-permute-done.3.refs_1_, bf16[8,1024]{1,0:T(8,128)(2,1)S(1)} %collective-permute-done.4.refs_2_, bf16[8,1024]{1,0:T(8,128)(2,1)S(1)} %collective-permute-done.5.refs_3_, ...), custom_call_target="tpu_custom_call" | custom-call | tf_op jit(solution)/shard_map/pallas_call | solution.py:216
  (4 shorter events, 0.0 us)
Async XLA Ops:
  5.1 3.1 %collective-permute-start.1 = (f16[64,256]{1,0:T(8,128)(2,1)S(1)}, f16[64,256]{1,0:T(8,128)(2,1)S(1)}, u32[]{:S(2)}, u32[]{:S(2)}) collective-permute-start(f16[64,256]{1,0:T(8,128)(2,1)S(1)} %convert_element_type.9), channel_id=1, source_target_pairs={{0,1},{1,0},{2,3},{3,2},{4,5},{5,4},{6,7},{7,6},{8,9},{9,8},{10,11... | collective-permute-start | bytes 98312 | tf_op jit(solution)/shard_map/ppermute | solution.py:238
  5.6 4.3 %collective-permute-start = (f16[64,256]{1,0:T(8,128)(2,1)S(1)}, f16[64,256]{1,0:T(8,128)(2,1)S(1)}, u32[]{:S(2)}, u32[]{:S(2)}) collective-permute-start(f16[64,256]{1,0:T(8,128)(2,1)S(1)} %convert_element_type.9), channel_id=1, source_target_pairs={{0,3},{1,2},{2,1},{3,0},{4,7},{5,6},{6,5},{7,4},{8,11},{9,10},{10,... | collective-permute-start | bytes 98312 | tf_op jit(solution)/shard_map/ppermute | solution.py:237
  10.2 1.2 %collective-permute-start.2 = (bf16[4,1024]{1,0:T(4,128)(2,1)S(1)}, bf16[4,1024]{1,0:T(4,128)(2,1)S(1)}, u32[]{:S(2)}, u32[]{:S(2)}) collective-permute-start(bf16[4,1024]{1,0:T(4,128)(2,1)S(1)} %shard_map.78), channel_id=1, source_target_pairs={{0,1},{1,0},{2,3},{3,2},{4,5},{5,4},{6,7},{7,6},{8,9},{9,8},{10,11... | collective-permute-start | bytes 24584 | tf_op jit(solution)/shard_map/ppermute | solution.py:240
  11.4 4.3 %collective-permute-start.4 = (bf16[8,1024]{1,0:T(8,128)(2,1)S(1)}, bf16[8,1024]{1,0:T(8,128)(2,1)S(1)}, u32[]{:S(2)}, u32[]{:S(2)}) collective-permute-start(bf16[8,1024]{1,0:T(8,128)(2,1)S(1)} %pad_maximum_fusion.refs_0_), channel_id=1, source_target_pairs={{0,5},{1,9},{4,8},{5,13},{8,12},{9,0},{12,4},{13,1},{2,7},{3,11},{... | collective-permute-start | bytes 49160 | tf_op jit(solution)/shard_map/ppermute | solution.py:249
  13.2 3.8 %collective-permute-start.3 = (bf16[8,1024]{1,0:T(8,128)(2,1)S(1)}, bf16[8,1024]{1,0:T(8,128)(2,1)S(1)}, u32[]{:S(2)}, u32[]{:S(2)}) collective-permute-start(bf16[8,1024]{1,0:T(8,128)(2,1)S(1)} %pad_maximum_fusion.refs_0_), channel_id=1, source_target_pairs={{0,13},{1,12},{4,0},{5,1},{8,4},{9,5},{12,9},{13,8},{2,15},{3,14},... | collective-permute-start | bytes 49160 | tf_op jit(solution)/shard_map/ppermute | solution.py:250
  15.3 1.5 %collective-permute-start.6 = (f32[4,512]{1,0:T(4,128)S(1)}, f32[4,512]{1,0:T(4,128)S(1)}, u32[]{:S(2)}, u32[]{:S(2)}) collective-permute-start(f32[4,512]{1,0:T(4,128)S(1)} %fusion), channel_id=1, source_target_pairs={{0,1},{1,0},{4,5},{5,4},{8,9},{9,8},{12,13},{13,12},{2,3},{3,2},{6... | collective-permute-start | bytes 24584 | tf_op jit(solution)/shard_map/ppermute | solution.py:253
  15.8 1.6 %collective-permute-start.5 = (bf16[8,1024]{1,0:T(8,128)(2,1)S(1)}, bf16[8,1024]{1,0:T(8,128)(2,1)S(1)}, u32[]{:S(2)}, u32[]{:S(2)}) collective-permute-start(bf16[8,1024]{1,0:T(8,128)(2,1)S(1)} %collective-permute-done.4.refs_2_), channel_id=1, source_target_pairs={{0,1},{1,0},{4,5},{5,4},{8,9},{9,8},{12,13},{13,12},{2,3},{3,2},{6... | collective-permute-start | bytes 49160 | tf_op jit(solution)/shard_map/ppermute | solution.py:251

commit v15 on v12

--- a/solution.py
+++ b/solution.py
@@ -26,7 +26,7 @@
     return terms[0]
 
 
-def project_kernel(scales, hidden, out_grad, lengths, proj_in, proj_out, tests, out, near_tests, hid, og, pin, pout, limits, sems):
+def project_kernel(scales, hidden, out_grad, lengths, proj_in, proj_out, out, hid, og, pin, pout, limits, sems):
     rows, width = hidden.shape
     k_in = pin.shape[0]
     small = first_chunk(width)
@@ -59,8 +59,6 @@
             copy.start()
     bounds = pltpu.make_async_copy(lengths, limits, sems.at[0, 4])
     bounds.start()
-    fetch = pltpu.make_async_copy(tests, near_tests, sems.at[1, 4])
-    fetch.start()
     total = jnp.zeros((k_in, rows), jnp.float32)
     if small:
         for copy in copies_of(0):
@@ -82,22 +80,18 @@
     for e in range(lengths.shape[0]):
         limit = jnp.where(slot >= e * SEQ, e * SEQ + limits[e], limit)
     out[:k_in] = jnp.where(slot < limit, total * scales[0], 0.0)
-    fetch.wait()
-
-
-def project(hidden, out_grad, lengths, proj_in, proj_out, test_proj, scales):
+
+
+def project(hidden, out_grad, lengths, proj_in, proj_out, scales):
     rows, width = hidden.shape
     narrow = out_grad.shape[1]
     k_in, k_out = proj_in.shape[1], proj_out.shape[1]
-    operands = (hidden, out_grad, lengths, proj_in.T, proj_out.T, test_proj)
+    operands = (hidden, out_grad, lengths, proj_in.T, proj_out.T)
     return pl.pallas_call(
         functools.partial(project_kernel, scales),
-        out_shape=(
-            jax.ShapeDtypeStruct((k_in + k_out, rows), jnp.float32),
-            jax.ShapeDtypeStruct(test_proj.shape, test_proj.dtype),
-        ),
-        in_specs=[pl.BlockSpec(memory_space=pltpu.HBM)] * 6,
-        out_specs=(pl.BlockSpec(memory_space=pltpu.VMEM),) * 2,
+        out_shape=jax.ShapeDtypeStruct((k_in + k_out, rows), jnp.float32),
+        in_specs=[pl.BlockSpec(memory_space=pltpu.HBM)] * 5,
+        out_specs=pl.BlockSpec(memory_space=pltpu.VMEM),
         scratch_shapes=[
             pltpu.VMEM((rows, width), jnp.bfloat16),
             pltpu.VMEM((rows, narrow), jnp.bfloat16),
@@ -113,6 +107,24 @@
             transcendentals=0,
         ),
     )(*(pltpu.with_memory_space_constraint(x, pltpu.HBM) for x in operands))
+
+
+def fetch_kernel(_, src, dst, sem):
+    copy = pltpu.make_async_copy(src, dst, sem)
+    copy.start()
+    copy.wait()
+
+
+def fetch(array, after):
+    return pl.pallas_call(
+        fetch_kernel,
+        out_shape=jax.ShapeDtypeStruct(array.shape, array.dtype),
+        in_specs=[pl.BlockSpec(memory_space=pl.ANY), pl.BlockSpec(memory_space=pltpu.HBM)],
+        out_specs=pl.BlockSpec(memory_space=pltpu.VMEM),
+        scratch_shapes=[pltpu.SemaphoreType.DMA(())],
+        compiler_params=pltpu.CompilerParams(vmem_limit_bytes=8 << 20),
+        cost_estimate=pl.CostEstimate(flops=0, bytes_accessed=4 << 20, transcendentals=0),
+    )(after, pltpu.with_memory_space_constraint(array, pltpu.HBM))
 
 
 def halves(x):
@@ -231,11 +243,13 @@
     examples = lengths.shape[0] * sharers
     crossed = lax.axis_size("mp") == 2 and lax.axis_size("sub") == 2
     scales = (128.0, 4.0) if crossed else (1.0, 1.0)
-    both, test_proj = project(hidden, out_grad, lengths, proj_in, proj_out, test_proj, scales)
+    both = project(hidden, out_grad, lengths, proj_in, proj_out, scales)
     if crossed:
         sent = lax.optimization_barrier(both.astype(jnp.float16))
         far = lax.ppermute(sent, ("mp", "sub"), [(0, 3), (1, 2), (2, 1), (3, 0)])
-        near = lax.ppermute(sent, "sub", [(0, 1), (1, 0)])
+        test_proj = fetch(test_proj, both)
+        swapped, test_proj = lax.optimization_barrier((sent, test_proj))
+        near = lax.ppermute(swapped, "sub", [(0, 1), (1, 0)])
         made = example_grads([near.astype(jnp.float32), far.astype(jnp.float32)], k_in, k_out, scales)
         grads = lax.ppermute(made, "sub", [(0, 1), (1, 0)])
     else:

time: 17.4 us -> 17.7 us (1.017)
  Pallas kernels: 4.67 us -> 5.9 us
  starting transfers between devices: 9.07 us -> 8.38 us
  waiting for transfers between devices: 2.04 us -> 1.78 us
    pallas_call x1 -> x2, Pallas kernels: 3.26 us -> 4.49 us  [the longest x1 3.26 us: project(): pl.pallas_call(functools.partial(project_kernel, scales), out_shape=jax.S...]
    ppermute x1, waiting for transfers between devices: 1.1 us -> 0.01 us  [per_device(): far = lax.ppermute(sent, ('mp', 'sub'), [(0, 3), (1, 2), (2, 1), (3, 0)])]
    ppermute x1, waiting for transfers between devices: 0.01 us -> 0.85 us  [per_device(): near = lax.ppermute(swapped, 'sub', [(0, 1), (1, 0)])]
    ppermute x1, starting transfers between devices: 2.18 us -> 1.58 us  [per_device(): fetched = lax.ppermute(held, group, list(enumerate(SWAPPED_SEND)))]
    ppermute x1, starting transfers between devices: 0.61 us -> 0.43 us  [per_device(): raw = [own, lax.ppermute(for_other, group, swap)]]
  transfers between devices with their start and end apart: 7 -> 7, of which waited for: 4 -> 4; matrix products, arithmetic and copies ran while one was open for 4% -> 4% of each run, Pallas kernels for 0% -> 7%
where the time goes in v15:
time: 17.7 us; the launch traced here: 17.5 us
  starting transfers between devices  8.38 us (47%)
  Pallas kernels  5.9 us (33%)
  waiting for transfers between devices  1.78 us (10%)
  matrix products  0.74 us (4%)
  between operations  0.67 us (4%)
    pallas_call x1, Pallas kernels, project(): pl.pallas_call(functools.partial(project_kernel, scales), out_shape=jax.S...  3.26 us
    ppermute x1, starting transfers between devices, per_device(): far = lax.ppermute(sent, ('mp', 'sub'), [(0, 3), (1, 2), (2, 1), (3, 0)])  2.44 us
    ppermute x1, starting transfers between devices, per_device(): direct = lax.ppermute(held, group, list(enumerate(DIRECT_SEND)))  2.1 us
    ppermute x1, starting transfers between devices, per_device(): fetched = lax.ppermute(held, group, list(enumerate(SWAPPED_SEND)))  1.58 us
    pallas_call x1, Pallas kernels, fetch(): pl.pallas_call(fetch_kernel, out_shape=jax.ShapeDtypeStruct(array.shape,...  1.23 us
    pallas_call x1, Pallas kernels, finish(): pl.pallas_call(functools.partial(finish_kernel, examples, len(pieces), le...  1.05 us
    ppermute x1, waiting for transfers between devices, per_device(): near = lax.ppermute(swapped, 'sub', [(0, 1), (1, 0)])  0.85 us
    ppermute x1, starting transfers between devices, per_device(): near = lax.ppermute(swapped, 'sub', [(0, 1), (1, 0)])  0.74 us
  transfers between devices with their start and end apart: 7, of which 4 were waited for; matrix products, arithmetic and copies ran while one was open for 4% of the time, Pallas kernels for 7%

profile of v15, /device:TPU:0, one launch (start us, length us, event | category | flops | bytes accessed | tf_op | source)
XLA Modules:
  0.0 17.5 jit_solution(17942522856642694164)
XLA Ops:
  0.6 3.3 %shard_map.77._ = f32[64,256]{1,0:T(8,128)S(1)} custom-call(bf16[256,7168]{1,0:T(8,128)(2,1)} %hidden.1, bf16[256,2048]{1,0:T(8,128)(2,1)} %out_grad.1, s32[4]{0:T(128)} %lengths.1, bf16[32,7168]{1,0:T(8,128)(2,1)} %bitcast.6, bf16[32,2048]{1,0:T(8,128)(2,1)} %bitcast.7), custom_call_target="tpu_custom_call" | custom-call | flops 150994944 | bytes 5308416 | tf_op jit(solution)/shard_map/pallas_call | solution.py:90
  3.9 2.4 %collective-permute-start.1 = (f16[64,256]{1,0:T(8,128)(2,1)S(1)}, f16[64,256]{1,0:T(8,128)(2,1)S(1)}, u32[]{:S(2)}, u32[]{:S(2)}) collective-permute-start(f16[64,256]{1,0:T(8,128)(2,1)S(1)} %convert_element_type.9), channel_id=1, source_target_pairs={{0,3},{1,2},{2,1},{3,0},{4,7},{5,6},{6,5},{7,4},{8,11},{9,10},{10,... | collective-permute-start | bytes 98312 | tf_op jit(solution)/shard_map/ppermute | solution.py:249
  6.4 1.2 %shard_map.78 = bf16[512,1024]{1,0:T(8,128)(2,1)S(1)} custom-call(f32[64,256]{1,0:T(8,128)S(1)} %shard_map.77._, bf16[512,1024]{1,0:T(8,128)(2,1)} %src.1), custom_call_target="tpu_custom_call" | custom-call | bytes 4194304 | tf_op jit(solution)/shard_map/pallas_call | solution.py:119
  7.6 0.7 %collective-permute-start = (f16[64,256]{1,0:T(8,128)(2,1)S(1)}, f16[64,256]{1,0:T(8,128)(2,1)S(1)}, u32[]{:S(2)}, u32[]{:S(2)}) collective-permute-start(f16[64,256]{1,0:T(8,128)(2,1)S(1)} %convert_element_type.9), channel_id=1, source_target_pairs={{0,1},{1,0},{2,3},{3,2},{4,5},{5,4},{6,7},{7,6},{8,9},{9,8},{10,11... | collective-permute-start | bytes 98312 | tf_op jit(solution)/shard_map/ppermute | solution.py:252
  8.3 0.0 collective-permute-done.1
  8.4 0.8 %collective-permute-done = f16[64,256]{1,0:T(8,128)(2,1)S(1)} collective-permute-done((f16[64,256]{1,0:T(8,128)(2,1)S(1)}, f16[64,256]{1,0:T(8,128)(2,1)S(1)}, u32[]{:S(2)}, u32[]{:S(2)}) %collective-permute-start) | collective-permute-done | bytes 32800 | tf_op jit(solution)/shard_map/ppermute | solution.py:252
  9.2 0.4 %shard_map.79 = bf16[4,1024]{1,0:T(4,128)(2,1)S(1)} custom-call(f32[64,256]{1,0:T(8,128)S(1)} %convert_element_type.10.refs_0_, f32[64,256]{1,0:T(8,128)S(1)} %convert_element_type.11.refs_1_), custom_call_target="tpu_custom_call" | custom-call | flops 8589934592 | tf_op jit(solution)/shard_map/pallas_call | solution.py:175
  9.6 0.4 %collective-permute-start.2 = (bf16[4,1024]{1,0:T(4,128)(2,1)S(1)}, bf16[4,1024]{1,0:T(4,128)(2,1)S(1)}, u32[]{:S(2)}, u32[]{:S(2)}) collective-permute-start(bf16[4,1024]{1,0:T(4,128)(2,1)S(1)} %shard_map.79), channel_id=1, source_target_pairs={{0,1},{1,0},{2,3},{3,2},{4,5},{5,4},{6,7},{7,6},{8,9},{9,8},{10,11... | collective-permute-start | bytes 24584 | tf_op jit(solution)/shard_map/ppermute | solution.py:254
  9.9 0.4 %fusion = f32[4,512]{1,0:T(4,128)S(1)} fusion(bf16[4,1024]{1,0:T(4,128)(2,1)S(1)} %shard_map.79, bf16[512,1024]{1,0:T(8,128)(2,1)S(1)} %shard_map.78), kind=kOutput, calls=%fused_computation.1 | convolution fusion | flops 4194304 | bytes 1064960 | tf_op jit(solution)/shard_map/ep,qp->eq/dot_general | solution.py:260
  10.3 0.5 %collective-permute-done.2 = bf16[4,1024]{1,0:T(4,128)(2,1)S(1)} collective-permute-done((bf16[4,1024]{1,0:T(4,128)(2,1)S(1)}, bf16[4,1024]{1,0:T(4,128)(2,1)S(1)}, u32[]{:S(2)}, u32[]{:S(2)}) %collective-permute-start.2) | collective-permute-done | bytes 8224 | tf_op jit(solution)/shard_map/ppermute | solution.py:254
  10.8 1.6 %collective-permute-start.4 = (bf16[8,1024]{1,0:T(8,128)(2,1)S(1)}, bf16[8,1024]{1,0:T(8,128)(2,1)S(1)}, u32[]{:S(2)}, u32[]{:S(2)}) collective-permute-start(bf16[8,1024]{1,0:T(8,128)(2,1)S(1)} %pad_maximum_fusion.refs_0_), channel_id=1, source_target_pairs={{0,5},{1,9},{4,8},{5,13},{8,12},{9,0},{12,4},{13,1},{2,7},{3,11},{... | collective-permute-start | bytes 49160 | tf_op jit(solution)/shard_map/ppermute | solution.py:263
  12.3 2.1 %collective-permute-start.3 = (bf16[8,1024]{1,0:T(8,128)(2,1)S(1)}, bf16[8,1024]{1,0:T(8,128)(2,1)S(1)}, u32[]{:S(2)}, u32[]{:S(2)}) collective-permute-start(bf16[8,1024]{1,0:T(8,128)(2,1)S(1)} %pad_maximum_fusion.refs_0_), channel_id=1, source_target_pairs={{0,13},{1,12},{4,0},{5,1},{8,4},{9,5},{12,9},{13,8},{2,15},{3,14},... | collective-permute-start | bytes 49160 | tf_op jit(solution)/shard_map/ppermute | solution.py:264
  14.4 0.4 %collective-permute-start.6 = (f32[4,512]{1,0:T(4,128)S(1)}, f32[4,512]{1,0:T(4,128)S(1)}, u32[]{:S(2)}, u32[]{:S(2)}) collective-permute-start(f32[4,512]{1,0:T(4,128)S(1)} %fusion), channel_id=1, source_target_pairs={{0,1},{1,0},{4,5},{5,4},{8,9},{9,8},{12,13},{13,12},{2,3},{3,2},{6... | collective-permute-start | bytes 24584 | tf_op jit(solution)/shard_map/ppermute | solution.py:267
  14.9 0.0 collective-permute-done.4.refs_2_
  14.9 0.7 %collective-permute-start.5 = (bf16[8,1024]{1,0:T(8,128)(2,1)S(1)}, bf16[8,1024]{1,0:T(8,128)(2,1)S(1)}, u32[]{:S(2)}, u32[]{:S(2)}) collective-permute-start(bf16[8,1024]{1,0:T(8,128)(2,1)S(1)} %collective-permute-done.4.refs_2_), channel_id=1, source_target_pairs={{0,1},{1,0},{4,5},{5,4},{8,9},{9,8},{12,13},{13,12},{2,3},{3,2},{6... | collective-permute-start | bytes 49160 | tf_op jit(solution)/shard_map/ppermute | solution.py:265
  15.6 0.4 %fusion.1.refs_4_ = f32[4,512]{1,0:T(4,128)S(1)} fusion(bf16[4,1024]{1,0:T(4,128)(2,1)S(1)} %collective-permute-done.2, bf16[512,1024]{1,0:T(8,128)(2,1)S(1)} %shard_map.78), kind=kOutput, calls=%fused_computation.2 | convolution fusion | flops 4194304 | bytes 1064960 | tf_op jit(solution)/shard_map/ep,qp->eq/dot_general | solution.py:266
  16.0 0.0 collective-permute-done.6.refs_5_
  16.0 0.1 collective-permute-done.3.refs_1_
  16.1 0.4 %collective-permute-done.5.refs_3_ = bf16[8,1024]{1,0:T(8,128)(2,1)S(1)} collective-permute-done((bf16[8,1024]{1,0:T(8,128)(2,1)S(1)}, bf16[8,1024]{1,0:T(8,128)(2,1)S(1)}, u32[]{:S(2)}, u32[]{:S(2)}) %collective-permute-start.5) | collective-permute-done | bytes 16416 | tf_op jit(solution)/shard_map/ppermute | solution.py:265
  16.5 1.1 %shard_map.80 = (f32[128,1024]{1,0:T(8,128)}, f32[4,1024]{1,0:T(4,128)}) custom-call(bf16[8,1024]{1,0:T(8,128)(2,1)S(1)} %pad_maximum_fusion.refs_0_, bf16[8,1024]{1,0:T(8,128)(2,1)S(1)} %collective-permute-done.3.refs_1_, bf16[8,1024]{1,0:T(8,128)(2,1)S(1)} %collective-permute-done.4.refs_2_, bf16[8,1024]{1,0:T(8,128)(2,1)S(1)} %collective-permute-done.5.refs_3_, ...), custom_call_target="tpu_custom_call" | custom-call | tf_op jit(solution)/shard_map/pallas_call | solution.py:228
  (4 shorter events, 0.0 us)
Async XLA Ops:
  3.9 4.4 %collective-permute-start.1 = (f16[64,256]{1,0:T(8,128)(2,1)S(1)}, f16[64,256]{1,0:T(8,128)(2,1)S(1)}, u32[]{:S(2)}, u32[]{:S(2)}) collective-permute-start(f16[64,256]{1,0:T(8,128)(2,1)S(1)} %convert_element_type.9), channel_id=1, source_target_pairs={{0,3},{1,2},{2,1},{3,0},{4,7},{5,6},{6,5},{7,4},{8,11},{9,10},{10,... | collective-permute-start | bytes 98312 | tf_op jit(solution)/shard_map/ppermute | solution.py:249
  7.6 1.6 %collective-permute-start = (f16[64,256]{1,0:T(8,128)(2,1)S(1)}, f16[64,256]{1,0:T(8,128)(2,1)S(1)}, u32[]{:S(2)}, u32[]{:S(2)}) collective-permute-start(f16[64,256]{1,0:T(8,128)(2,1)S(1)} %convert_element_type.9), channel_id=1, source_target_pairs={{0,1},{1,0},{2,3},{3,2},{4,5},{5,4},{6,7},{7,6},{8,9},{9,8},{10,11... | collective-permute-start | bytes 98312 | tf_op jit(solution)/shard_map/ppermute | solution.py:252
  9.6 1.2 %collective-permute-start.2 = (bf16[4,1024]{1,0:T(4,128)(2,1)S(1)}, bf16[4,1024]{1,0:T(4,128)(2,1)S(1)}, u32[]{:S(2)}, u32[]{:S(2)}) collective-permute-start(bf16[4,1024]{1,0:T(4,128)(2,1)S(1)} %shard_map.79), channel_id=1, source_target_pairs={{0,1},{1,0},{2,3},{3,2},{4,5},{5,4},{6,7},{7,6},{8,9},{9,8},{10,11... | collective-permute-start | bytes 24584 | tf_op jit(solution)/shard_map/ppermute | solution.py:254
  10.8 4.1 %collective-permute-start.4 = (bf16[8,1024]{1,0:T(8,128)(2,1)S(1)}, bf16[8,1024]{1,0:T(8,128)(2,1)S(1)}, u32[]{:S(2)}, u32[]{:S(2)}) collective-permute-start(bf16[8,1024]{1,0:T(8,128)(2,1)S(1)} %pad_maximum_fusion.refs_0_), channel_id=1, source_target_pairs={{0,5},{1,9},{4,8},{5,13},{8,12},{9,0},{12,4},{13,1},{2,7},{3,11},{... | collective-permute-start | bytes 49160 | tf_op jit(solution)/shard_map/ppermute | solution.py:263
  12.3 3.8 %collective-permute-start.3 = (bf16[8,1024]{1,0:T(8,128)(2,1)S(1)}, bf16[8,1024]{1,0:T(8,128)(2,1)S(1)}, u32[]{:S(2)}, u32[]{:S(2)}) collective-permute-start(bf16[8,1024]{1,0:T(8,128)(2,1)S(1)} %pad_maximum_fusion.refs_0_), channel_id=1, source_target_pairs={{0,13},{1,12},{4,0},{5,1},{8,4},{9,5},{12,9},{13,8},{2,15},{3,14},... | collective-permute-start | bytes 49160 | tf_op jit(solution)/shard_map/ppermute | solution.py:264
  14.4 1.5 %collective-permute-start.6 = (f32[4,512]{1,0:T(4,128)S(1)}, f32[4,512]{1,0:T(4,128)S(1)}, u32[]{:S(2)}, u32[]{:S(2)}) collective-permute-start(f32[4,512]{1,0:T(4,128)S(1)} %fusion), channel_id=1, source_target_pairs={{0,1},{1,0},{4,5},{5,4},{8,9},{9,8},{12,13},{13,12},{2,3},{3,2},{6... | collective-permute-start | bytes 24584 | tf_op jit(solution)/shard_map/ppermute | solution.py:267
  14.9 1.6 %collective-permute-start.5 = (bf16[8,1024]{1,0:T(8,128)(2,1)S(1)}, bf16[8,1024]{1,0:T(8,128)(2,1)S(1)}, u32[]{:S(2)}, u32[]{:S(2)}) collective-permute-start(bf16[8,1024]{1,0:T(8,128)(2,1)S(1)} %collective-permute-done.4.refs_2_), channel_id=1, source_target_pairs={{0,1},{1,0},{4,5},{5,4},{8,9},{9,8},{12,13},{13,12},{2,3},{3,2},{6... | collective-permute-start | bytes 49160 | tf_op jit(solution)/shard_map/ppermute | solution.py:265

commit v16 on v13

--- a/solution.py
+++ b/solution.py
@@ -121,41 +121,34 @@
 
 
 def grads_kernel(k_in, scales, *refs):
-    *pieces, out = refs
+    *pieces, out, summed, placed = refs
     both = pieces[0][...]
     for piece in pieces[1:]:
         both = both + piece[...]
-    k_out, rows = both.shape[0] - k_in, both.shape[1]
-    count = rows // SEQ
+    k_out, slots = both.shape[0] - k_in, both.shape[1]
+    for n in range(slots // 128):
+        summed[n] = both[:k_in, n * 128:(n + 1) * 128]
+    count = slots // SEQ
     across = 128 // k_out
-    act_high, act_low = halves(both[:k_in])
-    grad_high, grad_low = halves(both[k_in:])
-    slot = lax.broadcasted_iota(jnp.int32, (1, rows), 1)
-
-    def by_example(act):
-        return jnp.concatenate(
-            [jnp.where((slot >= e * SEQ) & (slot < (e + 1) * SEQ), act, jnp.zeros_like(act)) for e in range(count)], axis=0)
-
-    def tiled(grad):
-        return jnp.concatenate([grad] * across, axis=0)
-
-    high = by_example(act_high)
-    left = jnp.concatenate([high, high, by_example(act_low)], axis=1)
-    high = tiled(grad_high)
-    right = jnp.concatenate([high, tiled(grad_low), high], axis=1)
+    groups = k_in // across
+    slot = lax.broadcasted_iota(jnp.int32, (1, slots), 1)
+    left = []
+    for first in range(across):
+        act = jnp.concatenate([summed[n, pl.ds(first, groups, stride=across), :] for n in range(slots // 128)], axis=1)
+        left += [jnp.where((slot >= e * SEQ) & (slot < (e + 1) * SEQ), act, 0.0) for e in range(count)]
+    high, low = halves(jnp.concatenate(left, axis=0))
+    left = jnp.concatenate([high, high, low], axis=1)
+    high, low = (jnp.concatenate([part] * across, axis=0) for part in halves(both[k_in:]))
+    right = jnp.concatenate([high, low, high], axis=1)
     product = lax.dot_general(left, right, CONTRACT_LAST, preferred_element_type=jnp.float32)
-    product = (product * (1.0 / (scales[0] * scales[1]))).astype(jnp.bfloat16).astype(jnp.float32)
-    row = lax.broadcasted_iota(jnp.int32, product.shape, 0)
-    lane = lax.broadcasted_iota(jnp.int32, product.shape, 1)
-    product = jnp.where(row % across == lane // k_out, product, 0.0).astype(jnp.bfloat16)
-    groups = k_in // across
-    shape = (groups * count, count * k_in)
-    to = lax.broadcasted_iota(jnp.int32, shape, 0)
-    source = lax.broadcasted_iota(jnp.int32, shape, 1)
-    pick = (source // k_in == to % count) & (source % k_in // across == to // count)
-    picked = jnp.dot(jnp.where(pick, 1.0, 0.0).astype(jnp.bfloat16), product, preferred_element_type=jnp.float32)
+    size = count * groups
+    lane = lax.broadcasted_iota(jnp.int32, (size, 128), 1)
+    kept = product[:size]
+    for first in range(1, across):
+        kept = jnp.where(lane // k_out == first, product[first * size:(first + 1) * size], kept)
+    placed[...] = kept * (1.0 / (scales[0] * scales[1]))
     for group in range(groups):
-        out[:, group * 128:(group + 1) * 128] = picked[group * count:(group + 1) * count].astype(jnp.bfloat16)
+        out[:, group * 128:(group + 1) * 128] = placed[pl.ds(group, count, stride=groups), :].astype(jnp.bfloat16)
 
 
 def example_grads(pieces, k_in, k_out, scales):
@@ -165,6 +158,10 @@
         out_shape=jax.ShapeDtypeStruct((pieces[0].shape[1] // SEQ, k_in * k_out), jnp.bfloat16),
         in_specs=[vmem] * len(pieces),
         out_specs=vmem,
+        scratch_shapes=[
+            pltpu.VMEM((pieces[0].shape[1] // 128, k_in, 128), jnp.float32),
+            pltpu.VMEM((pieces[0].shape[1] // SEQ * k_in * k_out // 128, 128), jnp.float32),
+        ],
         compiler_params=pltpu.CompilerParams(vmem_limit_bytes=6 << 20),
         cost_estimate=pl.CostEstimate(flops=1 << 33, bytes_accessed=0, transcendentals=0),
     )(*pieces)
@@ -182,7 +179,7 @@
     else:
         at = pl.multiple_of((place * own_rows) // 128 * 128, 128)
         wider = jnp.concatenate([p[:, pl.ds(at, 128)] for p in pieces], axis=0)
-        own = pltpu.roll(wider.astype(jnp.float32), at - place * own_rows + 128, 1)[:, :own_rows].astype(jnp.bfloat16)
+        own = pltpu.roll(wider.astype(jnp.float32), (at - place * own_rows + 128) % 128, 1)[:, :own_rows].astype(jnp.bfloat16)
     wide = every.astype(jnp.float32)
     total = jnp.sum(jnp.sum(wide * wide, axis=0, keepdims=True), axis=1, keepdims=True)
     factor = lax.rsqrt(total * (1.0 / examples) + 1e-06)

time: 17.4 us -> 17.3 us (level)
  no operation moved by 1% of the time
where the time goes in v16:
time: 17.3 us; the launch traced here: 17.2 us
  starting transfers between devices  8.39 us (48%)
  Pallas kernels  4.54 us (26%)
  waiting for transfers between devices  2.82 us (16%)
  matrix products  0.74 us (4%)
  between operations  0.67 us (4%)
    pallas_call x1, Pallas kernels, project(): pl.pallas_call(functools.partial(project_kernel, scales), out_shape=(jax....  3.26 us
    ppermute x1, starting transfers between devices, per_device(): far = lax.ppermute(sent, ('mp', 'sub'), [(0, 3), (1, 2), (2, 1), (3, 0)])  2.61 us
    ppermute x1, starting transfers between devices, per_device(): direct = lax.ppermute(held, group, list(enumerate(DIRECT_SEND)))  2.1 us
    ppermute x1, starting transfers between devices, per_device(): fetched = lax.ppermute(held, group, list(enumerate(SWAPPED_SEND)))  1.81 us
    ppermute x1, waiting for transfers between devices, per_device(): far = lax.ppermute(sent, ('mp', 'sub'), [(0, 3), (1, 2), (2, 1), (3, 0)])  1.66 us
    pallas_call x1, Pallas kernels, finish(): pl.pallas_call(functools.partial(finish_kernel, examples, len(pieces), le...  1.05 us
    ppermute x1, starting transfers between devices, per_device(): gathered = [held, direct, fetched, lax.ppermute(fetched, group, swap)]  0.74 us
    ppermute x1, waiting for transfers between devices, per_device(): grads = lax.ppermute(made, 'sub', [(0, 1), (1, 0)])  0.69 us
  transfers between devices with their start and end apart: 7, of which 4 were waited for; matrix products, arithmetic and copies ran while one was open for 4% of the time, Pallas kernels for 0%

profile of v16, /device:TPU:0, one launch (start us, length us, event | category | flops | bytes accessed | tf_op | source)
XLA Modules:
  0.0 17.2 jit_solution(8344195929578669579)
XLA Ops:
  0.6 3.3 %shard_map.77 = (f32[64,256]{1,0:T(8,128)S(1)}, bf16[512,1024]{1,0:T(8,128)(2,1)S(1)}) custom-call(bf16[256,7168]{1,0:T(8,128)(2,1)} %hidden.1, bf16[256,2048]{1,0:T(8,128)(2,1)} %out_grad.1, s32[4]{0:T(128)} %lengths.1, bf16[32,7168]{1,0:T(8,128)(2,1)} %bitcast.6, bf16[32,2048]{1,0:T(8,128)(2,1)} %bitcast.7, bf16[512,1024]{1,0:T(8,128)(2,1)} %tests.1), custom_call_target="tpu_custom_call" | custom-call | flops 150994944 | bytes 5308416 | tf_op jit(solution)/shard_map/pallas_call | solution.py:93
  3.9 0.5 %collective-permute-start.1 = (f16[64,256]{1,0:T(8,128)(2,1)S(1)}, f16[64,256]{1,0:T(8,128)(2,1)S(1)}, u32[]{:S(2)}, u32[]{:S(2)}) collective-permute-start(f16[64,256]{1,0:T(8,128)(2,1)S(1)} %convert_element_type.9), channel_id=1, source_target_pairs={{0,1},{1,0},{2,3},{3,2},{4,5},{5,4},{6,7},{7,6},{8,9},{9,8},{10,11... | collective-permute-start | bytes 98312 | tf_op jit(solution)/shard_map/ppermute | solution.py:235
  4.4 2.6 %collective-permute-start = (f16[64,256]{1,0:T(8,128)(2,1)S(1)}, f16[64,256]{1,0:T(8,128)(2,1)S(1)}, u32[]{:S(2)}, u32[]{:S(2)}) collective-permute-start(f16[64,256]{1,0:T(8,128)(2,1)S(1)} %convert_element_type.9), channel_id=1, source_target_pairs={{0,3},{1,2},{2,1},{3,0},{4,7},{5,6},{6,5},{7,4},{8,11},{9,10},{10,... | collective-permute-start | bytes 98312 | tf_op jit(solution)/shard_map/ppermute | solution.py:234
  7.1 0.0 collective-permute-done.1
  7.1 1.7 %collective-permute-done = f16[64,256]{1,0:T(8,128)(2,1)S(1)} collective-permute-done((f16[64,256]{1,0:T(8,128)(2,1)S(1)}, f16[64,256]{1,0:T(8,128)(2,1)S(1)}, u32[]{:S(2)}, u32[]{:S(2)}) %collective-permute-start) | collective-permute-done | bytes 32800 | tf_op jit(solution)/shard_map/ppermute | solution.py:234
  8.7 0.2 %shard_map.78 = bf16[4,1024]{1,0:T(4,128)(2,1)S(1)} custom-call(f32[64,256]{1,0:T(8,128)S(1)} %convert_element_type.10.refs_0_, f32[64,256]{1,0:T(8,128)S(1)} %convert_element_type.11.refs_1_), custom_call_target="tpu_custom_call" | custom-call | flops 8589934592 | tf_op jit(solution)/shard_map/pallas_call | solution.py:156
  9.0 0.2 %collective-permute-start.2 = (bf16[4,1024]{1,0:T(4,128)(2,1)S(1)}, bf16[4,1024]{1,0:T(4,128)(2,1)S(1)}, u32[]{:S(2)}, u32[]{:S(2)}) collective-permute-start(bf16[4,1024]{1,0:T(4,128)(2,1)S(1)} %shard_map.78), channel_id=1, source_target_pairs={{0,1},{1,0},{2,3},{3,2},{4,5},{5,4},{6,7},{7,6},{8,9},{9,8},{10,11... | collective-permute-start | bytes 24584 | tf_op jit(solution)/shard_map/ppermute | solution.py:237
  9.1 0.4 %fusion = f32[4,512]{1,0:T(4,128)S(1)} fusion(bf16[4,1024]{1,0:T(4,128)(2,1)S(1)} %shard_map.78, bf16[512,1024]{1,0:T(8,128)(2,1)S(1)} %get-tuple-element.7), kind=kOutput, calls=%fused_computation.1 | convolution fusion | flops 4194304 | bytes 1064960 | tf_op jit(solution)/shard_map/ep,qp->eq/dot_general | solution.py:243
  9.5 0.7 %collective-permute-done.2 = bf16[4,1024]{1,0:T(4,128)(2,1)S(1)} collective-permute-done((bf16[4,1024]{1,0:T(4,128)(2,1)S(1)}, bf16[4,1024]{1,0:T(4,128)(2,1)S(1)}, u32[]{:S(2)}, u32[]{:S(2)}) %collective-permute-start.2) | collective-permute-done | bytes 8224 | tf_op jit(solution)/shard_map/ppermute | solution.py:237
  10.2 1.8 %collective-permute-start.4 = (bf16[8,1024]{1,0:T(8,128)(2,1)S(1)}, bf16[8,1024]{1,0:T(8,128)(2,1)S(1)}, u32[]{:S(2)}, u32[]{:S(2)}) collective-permute-start(bf16[8,1024]{1,0:T(8,128)(2,1)S(1)} %pad_maximum_fusion.refs_0_), channel_id=1, source_target_pairs={{0,5},{1,9},{4,8},{5,13},{8,12},{9,0},{12,4},{13,1},{2,7},{3,11},{... | collective-permute-start | bytes 49160 | tf_op jit(solution)/shard_map/ppermute | solution.py:246
  12.0 2.1 %collective-permute-start.3 = (bf16[8,1024]{1,0:T(8,128)(2,1)S(1)}, bf16[8,1024]{1,0:T(8,128)(2,1)S(1)}, u32[]{:S(2)}, u32[]{:S(2)}) collective-permute-start(bf16[8,1024]{1,0:T(8,128)(2,1)S(1)} %pad_maximum_fusion.refs_0_), channel_id=1, source_target_pairs={{0,13},{1,12},{4,0},{5,1},{8,4},{9,5},{12,9},{13,8},{2,15},{3,14},... | collective-permute-start | bytes 49160 | tf_op jit(solution)/shard_map/ppermute | solution.py:247
  14.1 0.4 %collective-permute-start.6 = (f32[4,512]{1,0:T(4,128)S(1)}, f32[4,512]{1,0:T(4,128)S(1)}, u32[]{:S(2)}, u32[]{:S(2)}) collective-permute-start(f32[4,512]{1,0:T(4,128)S(1)} %fusion), channel_id=1, source_target_pairs={{0,1},{1,0},{4,5},{5,4},{8,9},{9,8},{12,13},{13,12},{2,3},{3,2},{6... | collective-permute-start | bytes 24584 | tf_op jit(solution)/shard_map/ppermute | solution.py:250
  14.6 0.0 collective-permute-done.4.refs_2_
  14.6 0.7 %collective-permute-start.5 = (bf16[8,1024]{1,0:T(8,128)(2,1)S(1)}, bf16[8,1024]{1,0:T(8,128)(2,1)S(1)}, u32[]{:S(2)}, u32[]{:S(2)}) collective-permute-start(bf16[8,1024]{1,0:T(8,128)(2,1)S(1)} %collective-permute-done.4.refs_2_), channel_id=1, source_target_pairs={{0,1},{1,0},{4,5},{5,4},{8,9},{9,8},{12,13},{13,12},{2,3},{3,2},{6... | collective-permute-start | bytes 49160 | tf_op jit(solution)/shard_map/ppermute | solution.py:248
  15.3 0.4 %fusion.1.refs_4_ = f32[4,512]{1,0:T(4,128)S(1)} fusion(bf16[4,1024]{1,0:T(4,128)(2,1)S(1)} %collective-permute-done.2, bf16[512,1024]{1,0:T(8,128)(2,1)S(1)} %get-tuple-element.7), kind=kOutput, calls=%fused_computation.2 | convolution fusion | flops 4194304 | bytes 1064960 | tf_op jit(solution)/shard_map/ep,qp->eq/dot_general | solution.py:249
  15.7 0.0 collective-permute-done.6.refs_5_
  15.7 0.1 collective-permute-done.3.refs_1_
  15.8 0.4 %collective-permute-done.5.refs_3_ = bf16[8,1024]{1,0:T(8,128)(2,1)S(1)} collective-permute-done((bf16[8,1024]{1,0:T(8,128)(2,1)S(1)}, bf16[8,1024]{1,0:T(8,128)(2,1)S(1)}, u32[]{:S(2)}, u32[]{:S(2)}) %collective-permute-start.5) | collective-permute-done | bytes 16416 | tf_op jit(solution)/shard_map/ppermute | solution.py:248
  16.1 1.1 %shard_map.79 = (f32[128,1024]{1,0:T(8,128)}, f32[4,1024]{1,0:T(4,128)}) custom-call(bf16[8,1024]{1,0:T(8,128)(2,1)S(1)} %pad_maximum_fusion.refs_0_, bf16[8,1024]{1,0:T(8,128)(2,1)S(1)} %collective-permute-done.3.refs_1_, bf16[8,1024]{1,0:T(8,128)(2,1)S(1)} %collective-permute-done.4.refs_2_, bf16[8,1024]{1,0:T(8,128)(2,1)S(1)} %collective-permute-done.5.refs_3_, ...), custom_call_target="tpu_custom_call" | custom-call | tf_op jit(solution)/shard_map/pallas_call | solution.py:213
  (4 shorter events, 0.0 us)
Async XLA Ops:
  3.9 3.1 %collective-permute-start.1 = (f16[64,256]{1,0:T(8,128)(2,1)S(1)}, f16[64,256]{1,0:T(8,128)(2,1)S(1)}, u32[]{:S(2)}, u32[]{:S(2)}) collective-permute-start(f16[64,256]{1,0:T(8,128)(2,1)S(1)} %convert_element_type.9), channel_id=1, source_target_pairs={{0,1},{1,0},{2,3},{3,2},{4,5},{5,4},{6,7},{7,6},{8,9},{9,8},{10,11... | collective-permute-start | bytes 98312 | tf_op jit(solution)/shard_map/ppermute | solution.py:235
  4.4 4.3 %collective-permute-start = (f16[64,256]{1,0:T(8,128)(2,1)S(1)}, f16[64,256]{1,0:T(8,128)(2,1)S(1)}, u32[]{:S(2)}, u32[]{:S(2)}) collective-permute-start(f16[64,256]{1,0:T(8,128)(2,1)S(1)} %convert_element_type.9), channel_id=1, source_target_pairs={{0,3},{1,2},{2,1},{3,0},{4,7},{5,6},{6,5},{7,4},{8,11},{9,10},{10,... | collective-permute-start | bytes 98312 | tf_op jit(solution)/shard_map/ppermute | solution.py:234
  9.0 1.2 %collective-permute-start.2 = (bf16[4,1024]{1,0:T(4,128)(2,1)S(1)}, bf16[4,1024]{1,0:T(4,128)(2,1)S(1)}, u32[]{:S(2)}, u32[]{:S(2)}) collective-permute-start(bf16[4,1024]{1,0:T(4,128)(2,1)S(1)} %shard_map.78), channel_id=1, source_target_pairs={{0,1},{1,0},{2,3},{3,2},{4,5},{5,4},{6,7},{7,6},{8,9},{9,8},{10,11... | collective-permute-start | bytes 24584 | tf_op jit(solution)/shard_map/ppermute | solution.py:237
  10.2 4.3 %collective-permute-start.4 = (bf16[8,1024]{1,0:T(8,128)(2,1)S(1)}, bf16[8,1024]{1,0:T(8,128)(2,1)S(1)}, u32[]{:S(2)}, u32[]{:S(2)}) collective-permute-start(bf16[8,1024]{1,0:T(8,128)(2,1)S(1)} %pad_maximum_fusion.refs_0_), channel_id=1, source_target_pairs={{0,5},{1,9},{4,8},{5,13},{8,12},{9,0},{12,4},{13,1},{2,7},{3,11},{... | collective-permute-start | bytes 49160 | tf_op jit(solution)/shard_map/ppermute | solution.py:246
  12.0 3.8 %collective-permute-start.3 = (bf16[8,1024]{1,0:T(8,128)(2,1)S(1)}, bf16[8,1024]{1,0:T(8,128)(2,1)S(1)}, u32[]{:S(2)}, u32[]{:S(2)}) collective-permute-start(bf16[8,1024]{1,0:T(8,128)(2,1)S(1)} %pad_maximum_fusion.refs_0_), channel_id=1, source_target_pairs={{0,13},{1,12},{4,0},{5,1},{8,4},{9,5},{12,9},{13,8},{2,15},{3,14},... | collective-permute-start | bytes 49160 | tf_op jit(solution)/shard_map/ppermute | solution.py:247
  14.1 1.5 %collective-permute-start.6 = (f32[4,512]{1,0:T(4,128)S(1)}, f32[4,512]{1,0:T(4,128)S(1)}, u32[]{:S(2)}, u32[]{:S(2)}) collective-permute-start(f32[4,512]{1,0:T(4,128)S(1)} %fusion), channel_id=1, source_target_pairs={{0,1},{1,0},{4,5},{5,4},{8,9},{9,8},{12,13},{13,12},{2,3},{3,2},{6... | collective-permute-start | bytes 24584 | tf_op jit(solution)/shard_map/ppermute | solution.py:250
  14.6 1.6 %collective-permute-start.5 = (bf16[8,1024]{1,0:T(8,128)(2,1)S(1)}, bf16[8,1024]{1,0:T(8,128)(2,1)S(1)}, u32[]{:S(2)}, u32[]{:S(2)}) collective-permute-start(bf16[8,1024]{1,0:T(8,128)(2,1)S(1)} %collective-permute-done.4.refs_2_), channel_id=1, source_target_pairs={{0,1},{1,0},{4,5},{5,4},{8,9},{9,8},{12,13},{13,12},{2,3},{3,2},{6... | collective-permute-start | bytes 49160 | tf_op jit(solution)/shard_map/ppermute | solution.py:248

commit v17 on v16

--- a/solution.py
+++ b/solution.py
@@ -233,7 +233,7 @@
         sent = lax.optimization_barrier(both.astype(jnp.float16))
         far = lax.ppermute(sent, ("mp", "sub"), [(0, 3), (1, 2), (2, 1), (3, 0)])
         near = lax.ppermute(sent, "sub", [(0, 1), (1, 0)])
-        made = example_grads([far.astype(jnp.float32), near.astype(jnp.float32)], k_in, k_out, scales)
+        made = example_grads([near.astype(jnp.float32), far.astype(jnp.float32)], k_in, k_out, scales)
         grads = lax.ppermute(made, "sub", [(0, 1), (1, 0)])
     else:
         grads = example_grads([lax.psum(both, "mp")], k_in, k_out, scales)

time: 17.3 us -> 17.3 us (level)
  waiting for transfers between devices: 2.82 us -> 2.04 us
  starting transfers between devices: 8.39 us -> 9.13 us
    ppermute x1, waiting for transfers between devices: 1.66 us -> 1.1 us  [per_device(): far = lax.ppermute(sent, ('mp', 'sub'), [(0, 3), (1, 2), (2, 1), (3, 0)])]
    ppermute x1, starting transfers between devices: 0.18 us -> 0.56 us  [per_device(): grads = lax.ppermute(made, 'sub', [(0, 1), (1, 0)])]
    ppermute x1, starting transfers between devices: 1.81 us -> 2.18 us  [per_device(): fetched = lax.ppermute(held, group, list(enumerate(SWAPPED_SEND)))]
    ppermute x1, waiting for transfers between devices: 0.69 us -> 0.46 us  [per_device(): grads = lax.ppermute(made, 'sub', [(0, 1), (1, 0)])]
    ppermute x1, starting transfers between devices: 0.43 us -> 0.61 us  [per_device(): raw = [own, lax.ppermute(for_other, group, swap)]]
    ppermute x1, starting transfers between devices: 0.74 us -> 0.56 us  [per_device(): gathered = [held, direct, fetched, lax.ppermute(fetched, group, swap)]]
where the time goes in v17:
time: 17.3 us; the launch traced here: 17.2 us
  starting transfers between devices  9.13 us (53%)
  Pallas kernels  4.54 us (26%)
  waiting for transfers between devices  2.04 us (12%)
  matrix products  0.74 us (4%)
  between operations  0.67 us (4%)
    pallas_call x1, Pallas kernels, project(): pl.pallas_call(functools.partial(project_kernel, scales), out_shape=(jax....  3.26 us
    ppermute x1, starting transfers between devices, per_device(): far = lax.ppermute(sent, ('mp', 'sub'), [(0, 3), (1, 2), (2, 1), (3, 0)])  2.44 us
    ppermute x1, starting transfers between devices, per_device(): fetched = lax.ppermute(held, group, list(enumerate(SWAPPED_SEND)))  2.18 us
    ppermute x1, starting transfers between devices, per_device(): direct = lax.ppermute(held, group, list(enumerate(DIRECT_SEND)))  2.1 us
    ppermute x1, waiting for transfers between devices, per_device(): far = lax.ppermute(sent, ('mp', 'sub'), [(0, 3), (1, 2), (2, 1), (3, 0)])  1.1 us
    pallas_call x1, Pallas kernels, finish(): pl.pallas_call(functools.partial(finish_kernel, examples, len(pieces), le...  1.05 us
    ppermute x1, starting transfers between devices, per_device(): near = lax.ppermute(sent, 'sub', [(0, 1), (1, 0)])  0.68 us
    ppermute x1, starting transfers between devices, per_device(): raw = [own, lax.ppermute(for_other, group, swap)]  0.61 us
  transfers between devices with their start and end apart: 7, of which 4 were waited for; matrix products, arithmetic and copies ran while one was open for 4% of the time, Pallas kernels for 0%

profile of v17, /device:TPU:0, one launch (start us, length us, event | category | flops | bytes accessed | tf_op | source)
XLA Modules:
  0.0 17.2 jit_solution(13584877644760451582)
XLA Ops:
  0.6 3.3 %shard_map.77 = (f32[64,256]{1,0:T(8,128)S(1)}, bf16[512,1024]{1,0:T(8,128)(2,1)S(1)}) custom-call(bf16[256,7168]{1,0:T(8,128)(2,1)} %hidden.1, bf16[256,2048]{1,0:T(8,128)(2,1)} %out_grad.1, s32[4]{0:T(128)} %lengths.1, bf16[32,7168]{1,0:T(8,128)(2,1)} %bitcast.6, bf16[32,2048]{1,0:T(8,128)(2,1)} %bitcast.7, bf16[512,1024]{1,0:T(8,128)(2,1)} %tests.1), custom_call_target="tpu_custom_call" | custom-call | flops 150994944 | bytes 5308416 | tf_op jit(solution)/shard_map/pallas_call | solution.py:93
  3.9 2.4 %collective-permute-start.1 = (f16[64,256]{1,0:T(8,128)(2,1)S(1)}, f16[64,256]{1,0:T(8,128)(2,1)S(1)}, u32[]{:S(2)}, u32[]{:S(2)}) collective-permute-start(f16[64,256]{1,0:T(8,128)(2,1)S(1)} %convert_element_type.9), channel_id=1, source_target_pairs={{0,3},{1,2},{2,1},{3,0},{4,7},{5,6},{6,5},{7,4},{8,11},{9,10},{10,... | collective-permute-start | bytes 98312 | tf_op jit(solution)/shard_map/ppermute | solution.py:234
  6.4 0.7 %collective-permute-start = (f16[64,256]{1,0:T(8,128)(2,1)S(1)}, f16[64,256]{1,0:T(8,128)(2,1)S(1)}, u32[]{:S(2)}, u32[]{:S(2)}) collective-permute-start(f16[64,256]{1,0:T(8,128)(2,1)S(1)} %convert_element_type.9), channel_id=1, source_target_pairs={{0,1},{1,0},{2,3},{3,2},{4,5},{5,4},{6,7},{7,6},{8,9},{9,8},{10,11... | collective-permute-start | bytes 98312 | tf_op jit(solution)/shard_map/ppermute | solution.py:235
  7.0 1.1 %collective-permute-done.1 = f16[64,256]{1,0:T(8,128)(2,1)S(1)} collective-permute-done((f16[64,256]{1,0:T(8,128)(2,1)S(1)}, f16[64,256]{1,0:T(8,128)(2,1)S(1)}, u32[]{:S(2)}, u32[]{:S(2)}) %collective-permute-start.1) | collective-permute-done | bytes 32800 | tf_op jit(solution)/shard_map/ppermute | solution.py:234
  8.2 0.0 collective-permute-done
  8.2 0.2 %shard_map.78 = bf16[4,1024]{1,0:T(4,128)(2,1)S(1)} custom-call(f32[64,256]{1,0:T(8,128)S(1)} %convert_element_type.10.refs_0_, f32[64,256]{1,0:T(8,128)S(1)} %convert_element_type.11.refs_1_), custom_call_target="tpu_custom_call" | custom-call | flops 8589934592 | tf_op jit(solution)/shard_map/pallas_call | solution.py:156
  8.4 0.6 %collective-permute-start.2 = (bf16[4,1024]{1,0:T(4,128)(2,1)S(1)}, bf16[4,1024]{1,0:T(4,128)(2,1)S(1)}, u32[]{:S(2)}, u32[]{:S(2)}) collective-permute-start(bf16[4,1024]{1,0:T(4,128)(2,1)S(1)} %shard_map.78), channel_id=1, source_target_pairs={{0,1},{1,0},{2,3},{3,2},{4,5},{5,4},{6,7},{7,6},{8,9},{9,8},{10,11... | collective-permute-start | bytes 24584 | tf_op jit(solution)/shard_map/ppermute | solution.py:237
  9.0 0.4 %fusion = f32[4,512]{1,0:T(4,128)S(1)} fusion(bf16[4,1024]{1,0:T(4,128)(2,1)S(1)} %shard_map.78, bf16[512,1024]{1,0:T(8,128)(2,1)S(1)} %get-tuple-element.7), kind=kOutput, calls=%fused_computation.1 | convolution fusion | flops 4194304 | bytes 1064960 | tf_op jit(solution)/shard_map/ep,qp->eq/dot_general | solution.py:243
  9.3 0.5 %collective-permute-done.2 = bf16[4,1024]{1,0:T(4,128)(2,1)S(1)} collective-permute-done((bf16[4,1024]{1,0:T(4,128)(2,1)S(1)}, bf16[4,1024]{1,0:T(4,128)(2,1)S(1)}, u32[]{:S(2)}, u32[]{:S(2)}) %collective-permute-start.2) | collective-permute-done | bytes 8224 | tf_op jit(solution)/shard_map/ppermute | solution.py:237
  9.8 2.2 %collective-permute-start.4 = (bf16[8,1024]{1,0:T(8,128)(2,1)S(1)}, bf16[8,1024]{1,0:T(8,128)(2,1)S(1)}, u32[]{:S(2)}, u32[]{:S(2)}) collective-permute-start(bf16[8,1024]{1,0:T(8,128)(2,1)S(1)} %pad_maximum_fusion.refs_0_), channel_id=1, source_target_pairs={{0,5},{1,9},{4,8},{5,13},{8,12},{9,0},{12,4},{13,1},{2,7},{3,11},{... | collective-permute-start | bytes 49160 | tf_op jit(solution)/shard_map/ppermute | solution.py:246
  12.0 2.1 %collective-permute-start.3 = (bf16[8,1024]{1,0:T(8,128)(2,1)S(1)}, bf16[8,1024]{1,0:T(8,128)(2,1)S(1)}, u32[]{:S(2)}, u32[]{:S(2)}) collective-permute-start(bf16[8,1024]{1,0:T(8,128)(2,1)S(1)} %pad_maximum_fusion.refs_0_), channel_id=1, source_target_pairs={{0,13},{1,12},{4,0},{5,1},{8,4},{9,5},{12,9},{13,8},{2,15},{3,14},... | collective-permute-start | bytes 49160 | tf_op jit(solution)/shard_map/ppermute | solution.py:247
  14.1 0.6 %collective-permute-start.6 = (f32[4,512]{1,0:T(4,128)S(1)}, f32[4,512]{1,0:T(4,128)S(1)}, u32[]{:S(2)}, u32[]{:S(2)}) collective-permute-start(f32[4,512]{1,0:T(4,128)S(1)} %fusion), channel_id=1, source_target_pairs={{0,1},{1,0},{4,5},{5,4},{8,9},{9,8},{12,13},{13,12},{2,3},{3,2},{6... | collective-permute-start | bytes 24584 | tf_op jit(solution)/shard_map/ppermute | solution.py:250
  14.7 0.0 collective-permute-done.4.refs_2_
  14.7 0.6 %collective-permute-start.5 = (bf16[8,1024]{1,0:T(8,128)(2,1)S(1)}, bf16[8,1024]{1,0:T(8,128)(2,1)S(1)}, u32[]{:S(2)}, u32[]{:S(2)}) collective-permute-start(bf16[8,1024]{1,0:T(8,128)(2,1)S(1)} %collective-permute-done.4.refs_2_), channel_id=1, source_target_pairs={{0,1},{1,0},{4,5},{5,4},{8,9},{9,8},{12,13},{13,12},{2,3},{3,2},{6... | collective-permute-start | bytes 49160 | tf_op jit(solution)/shard_map/ppermute | solution.py:248
  15.3 0.4 %fusion.1.refs_4_ = f32[4,512]{1,0:T(4,128)S(1)} fusion(bf16[4,1024]{1,0:T(4,128)(2,1)S(1)} %collective-permute-done.2, bf16[512,1024]{1,0:T(8,128)(2,1)S(1)} %get-tuple-element.7), kind=kOutput, calls=%fused_computation.2 | convolution fusion | flops 4194304 | bytes 1064960 | tf_op jit(solution)/shard_map/ep,qp->eq/dot_general | solution.py:249
  15.6 0.0 collective-permute-done.6.refs_5_
  15.6 0.1 collective-permute-done.3.refs_1_
  15.7 0.4 %collective-permute-done.5.refs_3_ = bf16[8,1024]{1,0:T(8,128)(2,1)S(1)} collective-permute-done((bf16[8,1024]{1,0:T(8,128)(2,1)S(1)}, bf16[8,1024]{1,0:T(8,128)(2,1)S(1)}, u32[]{:S(2)}, u32[]{:S(2)}) %collective-permute-start.5) | collective-permute-done | bytes 16416 | tf_op jit(solution)/shard_map/ppermute | solution.py:248
  16.1 1.1 %shard_map.79 = (f32[128,1024]{1,0:T(8,128)}, f32[4,1024]{1,0:T(4,128)}) custom-call(bf16[8,1024]{1,0:T(8,128)(2,1)S(1)} %pad_maximum_fusion.refs_0_, bf16[8,1024]{1,0:T(8,128)(2,1)S(1)} %collective-permute-done.3.refs_1_, bf16[8,1024]{1,0:T(8,128)(2,1)S(1)} %collective-permute-done.4.refs_2_, bf16[8,1024]{1,0:T(8,128)(2,1)S(1)} %collective-permute-done.5.refs_3_, ...), custom_call_target="tpu_custom_call" | custom-call | tf_op jit(solution)/shard_map/pallas_call | solution.py:213
  (4 shorter events, 0.0 us)
Async XLA Ops:
  3.9 4.2 %collective-permute-start.1 = (f16[64,256]{1,0:T(8,128)(2,1)S(1)}, f16[64,256]{1,0:T(8,128)(2,1)S(1)}, u32[]{:S(2)}, u32[]{:S(2)}) collective-permute-start(f16[64,256]{1,0:T(8,128)(2,1)S(1)} %convert_element_type.9), channel_id=1, source_target_pairs={{0,3},{1,2},{2,1},{3,0},{4,7},{5,6},{6,5},{7,4},{8,11},{9,10},{10,... | collective-permute-start | bytes 98312 | tf_op jit(solution)/shard_map/ppermute | solution.py:234
  6.4 1.8 %collective-permute-start = (f16[64,256]{1,0:T(8,128)(2,1)S(1)}, f16[64,256]{1,0:T(8,128)(2,1)S(1)}, u32[]{:S(2)}, u32[]{:S(2)}) collective-permute-start(f16[64,256]{1,0:T(8,128)(2,1)S(1)} %convert_element_type.9), channel_id=1, source_target_pairs={{0,1},{1,0},{2,3},{3,2},{4,5},{5,4},{6,7},{7,6},{8,9},{9,8},{10,11... | collective-permute-start | bytes 98312 | tf_op jit(solution)/shard_map/ppermute | solution.py:235
  8.4 1.4 %collective-permute-start.2 = (bf16[4,1024]{1,0:T(4,128)(2,1)S(1)}, bf16[4,1024]{1,0:T(4,128)(2,1)S(1)}, u32[]{:S(2)}, u32[]{:S(2)}) collective-permute-start(bf16[4,1024]{1,0:T(4,128)(2,1)S(1)} %shard_map.78), channel_id=1, source_target_pairs={{0,1},{1,0},{2,3},{3,2},{4,5},{5,4},{6,7},{7,6},{8,9},{9,8},{10,11... | collective-permute-start | bytes 24584 | tf_op jit(solution)/shard_map/ppermute | solution.py:237
  9.8 4.9 %collective-permute-start.4 = (bf16[8,1024]{1,0:T(8,128)(2,1)S(1)}, bf16[8,1024]{1,0:T(8,128)(2,1)S(1)}, u32[]{:S(2)}, u32[]{:S(2)}) collective-permute-start(bf16[8,1024]{1,0:T(8,128)(2,1)S(1)} %pad_maximum_fusion.refs_0_), channel_id=1, source_target_pairs={{0,5},{1,9},{4,8},{5,13},{8,12},{9,0},{12,4},{13,1},{2,7},{3,11},{... | collective-permute-start | bytes 49160 | tf_op jit(solution)/shard_map/ppermute | solution.py:246
  12.0 3.8 %collective-permute-start.3 = (bf16[8,1024]{1,0:T(8,128)(2,1)S(1)}, bf16[8,1024]{1,0:T(8,128)(2,1)S(1)}, u32[]{:S(2)}, u32[]{:S(2)}) collective-permute-start(bf16[8,1024]{1,0:T(8,128)(2,1)S(1)} %pad_maximum_fusion.refs_0_), channel_id=1, source_target_pairs={{0,13},{1,12},{4,0},{5,1},{8,4},{9,5},{12,9},{13,8},{2,15},{3,14},... | collective-permute-start | bytes 49160 | tf_op jit(solution)/shard_map/ppermute | solution.py:247
  14.1 1.5 %collective-permute-start.6 = (f32[4,512]{1,0:T(4,128)S(1)}, f32[4,512]{1,0:T(4,128)S(1)}, u32[]{:S(2)}, u32[]{:S(2)}) collective-permute-start(f32[4,512]{1,0:T(4,128)S(1)} %fusion), channel_id=1, source_target_pairs={{0,1},{1,0},{4,5},{5,4},{8,9},{9,8},{12,13},{13,12},{2,3},{3,2},{6... | collective-permute-start | bytes 24584 | tf_op jit(solution)/shard_map/ppermute | solution.py:250
  14.7 1.4 %collective-permute-start.5 = (bf16[8,1024]{1,0:T(8,128)(2,1)S(1)}, bf16[8,1024]{1,0:T(8,128)(2,1)S(1)}, u32[]{:S(2)}, u32[]{:S(2)}) collective-permute-start(bf16[8,1024]{1,0:T(8,128)(2,1)S(1)} %collective-permute-done.4.refs_2_), channel_id=1, source_target_pairs={{0,1},{1,0},{4,5},{5,4},{8,9},{9,8},{12,13},{13,12},{2,3},{3,2},{6... | collective-permute-start | bytes 49160 | tf_op jit(solution)/shard_map/ppermute | solution.py:248

commit v18 on v17

--- a/solution.py
+++ b/solution.py
@@ -16,8 +16,8 @@
 
 
 def first_chunk(width):
-    small = width // 7
-    return small if width % 7 == 0 and small % 128 == 0 else 0
+    small = width // 14 * 3
+    return small if width % 14 == 0 and small % 128 == 0 and (width - small) % 256 == 0 else 0
 
 
 def tree_sum(terms):

time: 17.3 us -> 17.6 us (1.017)
  Pallas kernels: 4.54 us -> 4.86 us
    pallas_call x1, Pallas kernels: 3.26 us -> 3.58 us  [project(): pl.pallas_call(functools.partial(project_kernel, scales), out_shape=(jax....]
where the time goes in v18:
time: 17.6 us; the launch traced here: 17.5 us
  starting transfers between devices  9.13 us (52%)
  Pallas kernels  4.86 us (28%)
  waiting for transfers between devices  2.04 us (12%)
  matrix products  0.74 us (4%)
  between operations  0.67 us (4%)
    pallas_call x1, Pallas kernels, project(): pl.pallas_call(functools.partial(project_kernel, scales), out_shape=(jax....  3.58 us
    ppermute x1, starting transfers between devices, per_device(): far = lax.ppermute(sent, ('mp', 'sub'), [(0, 3), (1, 2), (2, 1), (3, 0)])  2.44 us
    ppermute x1, starting transfers between devices, per_device(): fetched = lax.ppermute(held, group, list(enumerate(SWAPPED_SEND)))  2.19 us
    ppermute x1, starting transfers between devices, per_device(): direct = lax.ppermute(held, group, list(enumerate(DIRECT_SEND)))  2.09 us
    ppermute x1, waiting for transfers between devices, per_device(): far = lax.ppermute(sent, ('mp', 'sub'), [(0, 3), (1, 2), (2, 1), (3, 0)])  1.1 us
    pallas_call x1, Pallas kernels, finish(): pl.pallas_call(functools.partial(finish_kernel, examples, len(pieces), le...  1.05 us
    ppermute x1, starting transfers between devices, per_device(): near = lax.ppermute(sent, 'sub', [(0, 1), (1, 0)])  0.67 us
    ppermute x1, starting transfers between devices, per_device(): raw = [own, lax.ppermute(for_other, group, swap)]  0.61 us
  transfers between devices with their start and end apart: 7, of which 4 were waited for; matrix products, arithmetic and copies ran while one was open for 4% of the time, Pallas kernels for 0%

profile of v18, /device:TPU:0, one launch (start us, length us, event | category | flops | bytes accessed | tf_op | source)
XLA Modules:
  0.0 17.5 jit_solution(10351954742519320984)
XLA Ops:
  0.6 3.6 %shard_map.77 = (f32[64,256]{1,0:T(8,128)S(1)}, bf16[512,1024]{1,0:T(8,128)(2,1)S(1)}) custom-call(bf16[256,7168]{1,0:T(8,128)(2,1)} %hidden.1, bf16[256,2048]{1,0:T(8,128)(2,1)} %out_grad.1, s32[4]{0:T(128)} %lengths.1, bf16[32,7168]{1,0:T(8,128)(2,1)} %bitcast.6, bf16[32,2048]{1,0:T(8,128)(2,1)} %bitcast.7, bf16[512,1024]{1,0:T(8,128)(2,1)} %tests.1), custom_call_target="tpu_custom_call" | custom-call | flops 150994944 | bytes 5308416 | tf_op jit(solution)/shard_map/pallas_call | solution.py:93
  4.2 2.4 %collective-permute-start.1 = (f16[64,256]{1,0:T(8,128)(2,1)S(1)}, f16[64,256]{1,0:T(8,128)(2,1)S(1)}, u32[]{:S(2)}, u32[]{:S(2)}) collective-permute-start(f16[64,256]{1,0:T(8,128)(2,1)S(1)} %convert_element_type.9), channel_id=1, source_target_pairs={{0,3},{1,2},{2,1},{3,0},{4,7},{5,6},{6,5},{7,4},{8,11},{9,10},{10,... | collective-permute-start | bytes 98312 | tf_op jit(solution)/shard_map/ppermute | solution.py:234
  6.7 0.7 %collective-permute-start = (f16[64,256]{1,0:T(8,128)(2,1)S(1)}, f16[64,256]{1,0:T(8,128)(2,1)S(1)}, u32[]{:S(2)}, u32[]{:S(2)}) collective-permute-start(f16[64,256]{1,0:T(8,128)(2,1)S(1)} %convert_element_type.9), channel_id=1, source_target_pairs={{0,1},{1,0},{2,3},{3,2},{4,5},{5,4},{6,7},{7,6},{8,9},{9,8},{10,11... | collective-permute-start | bytes 98312 | tf_op jit(solution)/shard_map/ppermute | solution.py:235
  7.4 1.1 %collective-permute-done.1 = f16[64,256]{1,0:T(8,128)(2,1)S(1)} collective-permute-done((f16[64,256]{1,0:T(8,128)(2,1)S(1)}, f16[64,256]{1,0:T(8,128)(2,1)S(1)}, u32[]{:S(2)}, u32[]{:S(2)}) %collective-permute-start.1) | collective-permute-done | bytes 32800 | tf_op jit(solution)/shard_map/ppermute | solution.py:234
  8.5 0.0 collective-permute-done
  8.5 0.2 %shard_map.78 = bf16[4,1024]{1,0:T(4,128)(2,1)S(1)} custom-call(f32[64,256]{1,0:T(8,128)S(1)} %convert_element_type.10.refs_0_, f32[64,256]{1,0:T(8,128)S(1)} %convert_element_type.11.refs_1_), custom_call_target="tpu_custom_call" | custom-call | flops 8589934592 | tf_op jit(solution)/shard_map/pallas_call | solution.py:156
  8.7 0.6 %collective-permute-start.2 = (bf16[4,1024]{1,0:T(4,128)(2,1)S(1)}, bf16[4,1024]{1,0:T(4,128)(2,1)S(1)}, u32[]{:S(2)}, u32[]{:S(2)}) collective-permute-start(bf16[4,1024]{1,0:T(4,128)(2,1)S(1)} %shard_map.78), channel_id=1, source_target_pairs={{0,1},{1,0},{2,3},{3,2},{4,5},{5,4},{6,7},{7,6},{8,9},{9,8},{10,11... | collective-permute-start | bytes 24584 | tf_op jit(solution)/shard_map/ppermute | solution.py:237
  9.3 0.4 %fusion = f32[4,512]{1,0:T(4,128)S(1)} fusion(bf16[4,1024]{1,0:T(4,128)(2,1)S(1)} %shard_map.78, bf16[512,1024]{1,0:T(8,128)(2,1)S(1)} %get-tuple-element.7), kind=kOutput, calls=%fused_computation.1 | convolution fusion | flops 4194304 | bytes 1064960 | tf_op jit(solution)/shard_map/ep,qp->eq/dot_general | solution.py:243
  9.6 0.5 %collective-permute-done.2 = bf16[4,1024]{1,0:T(4,128)(2,1)S(1)} collective-permute-done((bf16[4,1024]{1,0:T(4,128)(2,1)S(1)}, bf16[4,1024]{1,0:T(4,128)(2,1)S(1)}, u32[]{:S(2)}, u32[]{:S(2)}) %collective-permute-start.2) | collective-permute-done | bytes 8224 | tf_op jit(solution)/shard_map/ppermute | solution.py:237
  10.1 2.2 %collective-permute-start.4 = (bf16[8,1024]{1,0:T(8,128)(2,1)S(1)}, bf16[8,1024]{1,0:T(8,128)(2,1)S(1)}, u32[]{:S(2)}, u32[]{:S(2)}) collective-permute-start(bf16[8,1024]{1,0:T(8,128)(2,1)S(1)} %pad_maximum_fusion.refs_0_), channel_id=1, source_target_pairs={{0,5},{1,9},{4,8},{5,13},{8,12},{9,0},{12,4},{13,1},{2,7},{3,11},{... | collective-permute-start | bytes 49160 | tf_op jit(solution)/shard_map/ppermute | solution.py:246
  12.3 2.1 %collective-permute-start.3 = (bf16[8,1024]{1,0:T(8,128)(2,1)S(1)}, bf16[8,1024]{1,0:T(8,128)(2,1)S(1)}, u32[]{:S(2)}, u32[]{:S(2)}) collective-permute-start(bf16[8,1024]{1,0:T(8,128)(2,1)S(1)} %pad_maximum_fusion.refs_0_), channel_id=1, source_target_pairs={{0,13},{1,12},{4,0},{5,1},{8,4},{9,5},{12,9},{13,8},{2,15},{3,14},... | collective-permute-start | bytes 49160 | tf_op jit(solution)/shard_map/ppermute | solution.py:247
  14.4 0.6 %collective-permute-start.6 = (f32[4,512]{1,0:T(4,128)S(1)}, f32[4,512]{1,0:T(4,128)S(1)}, u32[]{:S(2)}, u32[]{:S(2)}) collective-permute-start(f32[4,512]{1,0:T(4,128)S(1)} %fusion), channel_id=1, source_target_pairs={{0,1},{1,0},{4,5},{5,4},{8,9},{9,8},{12,13},{13,12},{2,3},{3,2},{6... | collective-permute-start | bytes 24584 | tf_op jit(solution)/shard_map/ppermute | solution.py:250
  15.0 0.0 collective-permute-done.4.refs_2_
  15.0 0.6 %collective-permute-start.5 = (bf16[8,1024]{1,0:T(8,128)(2,1)S(1)}, bf16[8,1024]{1,0:T(8,128)(2,1)S(1)}, u32[]{:S(2)}, u32[]{:S(2)}) collective-permute-start(bf16[8,1024]{1,0:T(8,128)(2,1)S(1)} %collective-permute-done.4.refs_2_), channel_id=1, source_target_pairs={{0,1},{1,0},{4,5},{5,4},{8,9},{9,8},{12,13},{13,12},{2,3},{3,2},{6... | collective-permute-start | bytes 49160 | tf_op jit(solution)/shard_map/ppermute | solution.py:248
  15.6 0.4 %fusion.1.refs_4_ = f32[4,512]{1,0:T(4,128)S(1)} fusion(bf16[4,1024]{1,0:T(4,128)(2,1)S(1)} %collective-permute-done.2, bf16[512,1024]{1,0:T(8,128)(2,1)S(1)} %get-tuple-element.7), kind=kOutput, calls=%fused_computation.2 | convolution fusion | flops 4194304 | bytes 1064960 | tf_op jit(solution)/shard_map/ep,qp->eq/dot_general | solution.py:249
  15.9 0.0 collective-permute-done.6.refs_5_
  16.0 0.1 collective-permute-done.3.refs_1_
  16.1 0.3 %collective-permute-done.5.refs_3_ = bf16[8,1024]{1,0:T(8,128)(2,1)S(1)} collective-permute-done((bf16[8,1024]{1,0:T(8,128)(2,1)S(1)}, bf16[8,1024]{1,0:T(8,128)(2,1)S(1)}, u32[]{:S(2)}, u32[]{:S(2)}) %collective-permute-start.5) | collective-permute-done | bytes 16416 | tf_op jit(solution)/shard_map/ppermute | solution.py:248
  16.4 1.1 %shard_map.79 = (f32[128,1024]{1,0:T(8,128)}, f32[4,1024]{1,0:T(4,128)}) custom-call(bf16[8,1024]{1,0:T(8,128)(2,1)S(1)} %pad_maximum_fusion.refs_0_, bf16[8,1024]{1,0:T(8,128)(2,1)S(1)} %collective-permute-done.3.refs_1_, bf16[8,1024]{1,0:T(8,128)(2,1)S(1)} %collective-permute-done.4.refs_2_, bf16[8,1024]{1,0:T(8,128)(2,1)S(1)} %collective-permute-done.5.refs_3_, ...), custom_call_target="tpu_custom_call" | custom-call | tf_op jit(solution)/shard_map/pallas_call | solution.py:213
  (4 shorter events, 0.0 us)
Async XLA Ops:
  4.2 4.2 %collective-permute-start.1 = (f16[64,256]{1,0:T(8,128)(2,1)S(1)}, f16[64,256]{1,0:T(8,128)(2,1)S(1)}, u32[]{:S(2)}, u32[]{:S(2)}) collective-permute-start(f16[64,256]{1,0:T(8,128)(2,1)S(1)} %convert_element_type.9), channel_id=1, source_target_pairs={{0,3},{1,2},{2,1},{3,0},{4,7},{5,6},{6,5},{7,4},{8,11},{9,10},{10,... | collective-permute-start | bytes 98312 | tf_op jit(solution)/shard_map/ppermute | solution.py:234
  6.7 1.8 %collective-permute-start = (f16[64,256]{1,0:T(8,128)(2,1)S(1)}, f16[64,256]{1,0:T(8,128)(2,1)S(1)}, u32[]{:S(2)}, u32[]{:S(2)}) collective-permute-start(f16[64,256]{1,0:T(8,128)(2,1)S(1)} %convert_element_type.9), channel_id=1, source_target_pairs={{0,1},{1,0},{2,3},{3,2},{4,5},{5,4},{6,7},{7,6},{8,9},{9,8},{10,11... | collective-permute-start | bytes 98312 | tf_op jit(solution)/shard_map/ppermute | solution.py:235
  8.7 1.4 %collective-permute-start.2 = (bf16[4,1024]{1,0:T(4,128)(2,1)S(1)}, bf16[4,1024]{1,0:T(4,128)(2,1)S(1)}, u32[]{:S(2)}, u32[]{:S(2)}) collective-permute-start(bf16[4,1024]{1,0:T(4,128)(2,1)S(1)} %shard_map.78), channel_id=1, source_target_pairs={{0,1},{1,0},{2,3},{3,2},{4,5},{5,4},{6,7},{7,6},{8,9},{9,8},{10,11... | collective-permute-start | bytes 24584 | tf_op jit(solution)/shard_map/ppermute | solution.py:237
  10.1 4.9 %collective-permute-start.4 = (bf16[8,1024]{1,0:T(8,128)(2,1)S(1)}, bf16[8,1024]{1,0:T(8,128)(2,1)S(1)}, u32[]{:S(2)}, u32[]{:S(2)}) collective-permute-start(bf16[8,1024]{1,0:T(8,128)(2,1)S(1)} %pad_maximum_fusion.refs_0_), channel_id=1, source_target_pairs={{0,5},{1,9},{4,8},{5,13},{8,12},{9,0},{12,4},{13,1},{2,7},{3,11},{... | collective-permute-start | bytes 49160 | tf_op jit(solution)/shard_map/ppermute | solution.py:246
  12.3 3.8 %collective-permute-start.3 = (bf16[8,1024]{1,0:T(8,128)(2,1)S(1)}, bf16[8,1024]{1,0:T(8,128)(2,1)S(1)}, u32[]{:S(2)}, u32[]{:S(2)}) collective-permute-start(bf16[8,1024]{1,0:T(8,128)(2,1)S(1)} %pad_maximum_fusion.refs_0_), channel_id=1, source_target_pairs={{0,13},{1,12},{4,0},{5,1},{8,4},{9,5},{12,9},{13,8},{2,15},{3,14},... | collective-permute-start | bytes 49160 | tf_op jit(solution)/shard_map/ppermute | solution.py:247
  14.4 1.5 %collective-permute-start.6 = (f32[4,512]{1,0:T(4,128)S(1)}, f32[4,512]{1,0:T(4,128)S(1)}, u32[]{:S(2)}, u32[]{:S(2)}) collective-permute-start(f32[4,512]{1,0:T(4,128)S(1)} %fusion), channel_id=1, source_target_pairs={{0,1},{1,0},{4,5},{5,4},{8,9},{9,8},{12,13},{13,12},{2,3},{3,2},{6... | collective-permute-start | bytes 24584 | tf_op jit(solution)/shard_map/ppermute | solution.py:250
  15.0 1.4 %collective-permute-start.5 = (bf16[8,1024]{1,0:T(8,128)(2,1)S(1)}, bf16[8,1024]{1,0:T(8,128)(2,1)S(1)}, u32[]{:S(2)}, u32[]{:S(2)}) collective-permute-start(bf16[8,1024]{1,0:T(8,128)(2,1)S(1)} %collective-permute-done.4.refs_2_), channel_id=1, source_target_pairs={{0,1},{1,0},{4,5},{5,4},{8,9},{9,8},{12,13},{13,12},{2,3},{3,2},{6... | collective-permute-start | bytes 49160 | tf_op jit(solution)/shard_map/ppermute | solution.py:248

commit v19 on v18

--- a/solution.py
+++ b/solution.py
@@ -16,7 +16,7 @@
 
 
 def first_chunk(width):
-    small = width // 14 * 3
+    small = width // 14
     return small if width % 14 == 0 and small % 128 == 0 and (width - small) % 256 == 0 else 0
 
 

time: 17.6 us -> 17.5 us (level)
  no operation moved by 1% of the time
where the time goes in v19:
time: 17.5 us; the launch traced here: 17.3 us
  starting transfers between devices  9.13 us (52%)
  Pallas kernels  4.7 us (27%)
  waiting for transfers between devices  2.04 us (12%)
  matrix products  0.74 us (4%)
  between operations  0.67 us (4%)
    pallas_call x1, Pallas kernels, project(): pl.pallas_call(functools.partial(project_kernel, scales), out_shape=(jax....  3.42 us
    ppermute x1, starting transfers between devices, per_device(): far = lax.ppermute(sent, ('mp', 'sub'), [(0, 3), (1, 2), (2, 1), (3, 0)])  2.44 us
    ppermute x1, starting transfers between devices, per_device(): fetched = lax.ppermute(held, group, list(enumerate(SWAPPED_SEND)))  2.18 us
    ppermute x1, starting transfers between devices, per_device(): direct = lax.ppermute(held, group, list(enumerate(DIRECT_SEND)))  2.1 us
    ppermute x1, waiting for transfers between devices, per_device(): far = lax.ppermute(sent, ('mp', 'sub'), [(0, 3), (1, 2), (2, 1), (3, 0)])  1.1 us
    pallas_call x1, Pallas kernels, finish(): pl.pallas_call(functools.partial(finish_kernel, examples, len(pieces), le...  1.05 us
    ppermute x1, starting transfers between devices, per_device(): near = lax.ppermute(sent, 'sub', [(0, 1), (1, 0)])  0.68 us
    ppermute x1, starting transfers between devices, per_device(): raw = [own, lax.ppermute(for_other, group, swap)]  0.61 us
  transfers between devices with their start and end apart: 7, of which 4 were waited for; matrix products, arithmetic and copies ran while one was open for 4% of the time, Pallas kernels for 0%

profile of v19, /device:TPU:0, one launch (start us, length us, event | category | flops | bytes accessed | tf_op | source)
XLA Modules:
  0.0 17.3 jit_solution(17650874982716137301)
XLA Ops:
  0.6 3.4 %shard_map.77 = (f32[64,256]{1,0:T(8,128)S(1)}, bf16[512,1024]{1,0:T(8,128)(2,1)S(1)}) custom-call(bf16[256,7168]{1,0:T(8,128)(2,1)} %hidden.1, bf16[256,2048]{1,0:T(8,128)(2,1)} %out_grad.1, s32[4]{0:T(128)} %lengths.1, bf16[32,7168]{1,0:T(8,128)(2,1)} %bitcast.6, bf16[32,2048]{1,0:T(8,128)(2,1)} %bitcast.7, bf16[512,1024]{1,0:T(8,128)(2,1)} %tests.1), custom_call_target="tpu_custom_call" | custom-call | flops 150994944 | bytes 5308416 | tf_op jit(solution)/shard_map/pallas_call | solution.py:93
  4.1 2.4 %collective-permute-start.1 = (f16[64,256]{1,0:T(8,128)(2,1)S(1)}, f16[64,256]{1,0:T(8,128)(2,1)S(1)}, u32[]{:S(2)}, u32[]{:S(2)}) collective-permute-start(f16[64,256]{1,0:T(8,128)(2,1)S(1)} %convert_element_type.9), channel_id=1, source_target_pairs={{0,3},{1,2},{2,1},{3,0},{4,7},{5,6},{6,5},{7,4},{8,11},{9,10},{10,... | collective-permute-start | bytes 98312 | tf_op jit(solution)/shard_map/ppermute | solution.py:234
  6.5 0.7 %collective-permute-start = (f16[64,256]{1,0:T(8,128)(2,1)S(1)}, f16[64,256]{1,0:T(8,128)(2,1)S(1)}, u32[]{:S(2)}, u32[]{:S(2)}) collective-permute-start(f16[64,256]{1,0:T(8,128)(2,1)S(1)} %convert_element_type.9), channel_id=1, source_target_pairs={{0,1},{1,0},{2,3},{3,2},{4,5},{5,4},{6,7},{7,6},{8,9},{9,8},{10,11... | collective-permute-start | bytes 98312 | tf_op jit(solution)/shard_map/ppermute | solution.py:235
  7.2 1.1 %collective-permute-done.1 = f16[64,256]{1,0:T(8,128)(2,1)S(1)} collective-permute-done((f16[64,256]{1,0:T(8,128)(2,1)S(1)}, f16[64,256]{1,0:T(8,128)(2,1)S(1)}, u32[]{:S(2)}, u32[]{:S(2)}) %collective-permute-start.1) | collective-permute-done | bytes 32800 | tf_op jit(solution)/shard_map/ppermute | solution.py:234
  8.3 0.0 collective-permute-done
  8.3 0.2 %shard_map.78 = bf16[4,1024]{1,0:T(4,128)(2,1)S(1)} custom-call(f32[64,256]{1,0:T(8,128)S(1)} %convert_element_type.10.refs_0_, f32[64,256]{1,0:T(8,128)S(1)} %convert_element_type.11.refs_1_), custom_call_target="tpu_custom_call" | custom-call | flops 8589934592 | tf_op jit(solution)/shard_map/pallas_call | solution.py:156
  8.6 0.6 %collective-permute-start.2 = (bf16[4,1024]{1,0:T(4,128)(2,1)S(1)}, bf16[4,1024]{1,0:T(4,128)(2,1)S(1)}, u32[]{:S(2)}, u32[]{:S(2)}) collective-permute-start(bf16[4,1024]{1,0:T(4,128)(2,1)S(1)} %shard_map.78), channel_id=1, source_target_pairs={{0,1},{1,0},{2,3},{3,2},{4,5},{5,4},{6,7},{7,6},{8,9},{9,8},{10,11... | collective-permute-start | bytes 24584 | tf_op jit(solution)/shard_map/ppermute | solution.py:237
  9.1 0.4 %fusion = f32[4,512]{1,0:T(4,128)S(1)} fusion(bf16[4,1024]{1,0:T(4,128)(2,1)S(1)} %shard_map.78, bf16[512,1024]{1,0:T(8,128)(2,1)S(1)} %get-tuple-element.7), kind=kOutput, calls=%fused_computation.1 | convolution fusion | flops 4194304 | bytes 1064960 | tf_op jit(solution)/shard_map/ep,qp->eq/dot_general | solution.py:243
  9.5 0.5 %collective-permute-done.2 = bf16[4,1024]{1,0:T(4,128)(2,1)S(1)} collective-permute-done((bf16[4,1024]{1,0:T(4,128)(2,1)S(1)}, bf16[4,1024]{1,0:T(4,128)(2,1)S(1)}, u32[]{:S(2)}, u32[]{:S(2)}) %collective-permute-start.2) | collective-permute-done | bytes 8224 | tf_op jit(solution)/shard_map/ppermute | solution.py:237
  10.0 2.2 %collective-permute-start.4 = (bf16[8,1024]{1,0:T(8,128)(2,1)S(1)}, bf16[8,1024]{1,0:T(8,128)(2,1)S(1)}, u32[]{:S(2)}, u32[]{:S(2)}) collective-permute-start(bf16[8,1024]{1,0:T(8,128)(2,1)S(1)} %pad_maximum_fusion.refs_0_), channel_id=1, source_target_pairs={{0,5},{1,9},{4,8},{5,13},{8,12},{9,0},{12,4},{13,1},{2,7},{3,11},{... | collective-permute-start | bytes 49160 | tf_op jit(solution)/shard_map/ppermute | solution.py:246
  12.2 2.1 %collective-permute-start.3 = (bf16[8,1024]{1,0:T(8,128)(2,1)S(1)}, bf16[8,1024]{1,0:T(8,128)(2,1)S(1)}, u32[]{:S(2)}, u32[]{:S(2)}) collective-permute-start(bf16[8,1024]{1,0:T(8,128)(2,1)S(1)} %pad_maximum_fusion.refs_0_), channel_id=1, source_target_pairs={{0,13},{1,12},{4,0},{5,1},{8,4},{9,5},{12,9},{13,8},{2,15},{3,14},... | collective-permute-start | bytes 49160 | tf_op jit(solution)/shard_map/ppermute | solution.py:247
  14.2 0.6 %collective-permute-start.6 = (f32[4,512]{1,0:T(4,128)S(1)}, f32[4,512]{1,0:T(4,128)S(1)}, u32[]{:S(2)}, u32[]{:S(2)}) collective-permute-start(f32[4,512]{1,0:T(4,128)S(1)} %fusion), channel_id=1, source_target_pairs={{0,1},{1,0},{4,5},{5,4},{8,9},{9,8},{12,13},{13,12},{2,3},{3,2},{6... | collective-permute-start | bytes 24584 | tf_op jit(solution)/shard_map/ppermute | solution.py:250
  14.9 0.0 collective-permute-done.4.refs_2_
  14.9 0.6 %collective-permute-start.5 = (bf16[8,1024]{1,0:T(8,128)(2,1)S(1)}, bf16[8,1024]{1,0:T(8,128)(2,1)S(1)}, u32[]{:S(2)}, u32[]{:S(2)}) collective-permute-start(bf16[8,1024]{1,0:T(8,128)(2,1)S(1)} %collective-permute-done.4.refs_2_), channel_id=1, source_target_pairs={{0,1},{1,0},{4,5},{5,4},{8,9},{9,8},{12,13},{13,12},{2,3},{3,2},{6... | collective-permute-start | bytes 49160 | tf_op jit(solution)/shard_map/ppermute | solution.py:248
  15.4 0.4 %fusion.1.refs_4_ = f32[4,512]{1,0:T(4,128)S(1)} fusion(bf16[4,1024]{1,0:T(4,128)(2,1)S(1)} %collective-permute-done.2, bf16[512,1024]{1,0:T(8,128)(2,1)S(1)} %get-tuple-element.7), kind=kOutput, calls=%fused_computation.2 | convolution fusion | flops 4194304 | bytes 1064960 | tf_op jit(solution)/shard_map/ep,qp->eq/dot_general | solution.py:249
  15.8 0.0 collective-permute-done.6.refs_5_
  15.8 0.1 collective-permute-done.3.refs_1_
  15.9 0.4 %collective-permute-done.5.refs_3_ = bf16[8,1024]{1,0:T(8,128)(2,1)S(1)} collective-permute-done((bf16[8,1024]{1,0:T(8,128)(2,1)S(1)}, bf16[8,1024]{1,0:T(8,128)(2,1)S(1)}, u32[]{:S(2)}, u32[]{:S(2)}) %collective-permute-start.5) | collective-permute-done | bytes 16416 | tf_op jit(solution)/shard_map/ppermute | solution.py:248
  16.3 1.1 %shard_map.79 = (f32[128,1024]{1,0:T(8,128)}, f32[4,1024]{1,0:T(4,128)}) custom-call(bf16[8,1024]{1,0:T(8,128)(2,1)S(1)} %pad_maximum_fusion.refs_0_, bf16[8,1024]{1,0:T(8,128)(2,1)S(1)} %collective-permute-done.3.refs_1_, bf16[8,1024]{1,0:T(8,128)(2,1)S(1)} %collective-permute-done.4.refs_2_, bf16[8,1024]{1,0:T(8,128)(2,1)S(1)} %collective-permute-done.5.refs_3_, ...), custom_call_target="tpu_custom_call" | custom-call | tf_op jit(solution)/shard_map/pallas_call | solution.py:213
  (4 shorter events, 0.0 us)
Async XLA Ops:
  4.1 4.2 %collective-permute-start.1 = (f16[64,256]{1,0:T(8,128)(2,1)S(1)}, f16[64,256]{1,0:T(8,128)(2,1)S(1)}, u32[]{:S(2)}, u32[]{:S(2)}) collective-permute-start(f16[64,256]{1,0:T(8,128)(2,1)S(1)} %convert_element_type.9), channel_id=1, source_target_pairs={{0,3},{1,2},{2,1},{3,0},{4,7},{5,6},{6,5},{7,4},{8,11},{9,10},{10,... | collective-permute-start | bytes 98312 | tf_op jit(solution)/shard_map/ppermute | solution.py:234
  6.5 1.8 %collective-permute-start = (f16[64,256]{1,0:T(8,128)(2,1)S(1)}, f16[64,256]{1,0:T(8,128)(2,1)S(1)}, u32[]{:S(2)}, u32[]{:S(2)}) collective-permute-start(f16[64,256]{1,0:T(8,128)(2,1)S(1)} %convert_element_type.9), channel_id=1, source_target_pairs={{0,1},{1,0},{2,3},{3,2},{4,5},{5,4},{6,7},{7,6},{8,9},{9,8},{10,11... | collective-permute-start | bytes 98312 | tf_op jit(solution)/shard_map/ppermute | solution.py:235
  8.6 1.4 %collective-permute-start.2 = (bf16[4,1024]{1,0:T(4,128)(2,1)S(1)}, bf16[4,1024]{1,0:T(4,128)(2,1)S(1)}, u32[]{:S(2)}, u32[]{:S(2)}) collective-permute-start(bf16[4,1024]{1,0:T(4,128)(2,1)S(1)} %shard_map.78), channel_id=1, source_target_pairs={{0,1},{1,0},{2,3},{3,2},{4,5},{5,4},{6,7},{7,6},{8,9},{9,8},{10,11... | collective-permute-start | bytes 24584 | tf_op jit(solution)/shard_map/ppermute | solution.py:237
  10.0 4.9 %collective-permute-start.4 = (bf16[8,1024]{1,0:T(8,128)(2,1)S(1)}, bf16[8,1024]{1,0:T(8,128)(2,1)S(1)}, u32[]{:S(2)}, u32[]{:S(2)}) collective-permute-start(bf16[8,1024]{1,0:T(8,128)(2,1)S(1)} %pad_maximum_fusion.refs_0_), channel_id=1, source_target_pairs={{0,5},{1,9},{4,8},{5,13},{8,12},{9,0},{12,4},{13,1},{2,7},{3,11},{... | collective-permute-start | bytes 49160 | tf_op jit(solution)/shard_map/ppermute | solution.py:246
  12.2 3.8 %collective-permute-start.3 = (bf16[8,1024]{1,0:T(8,128)(2,1)S(1)}, bf16[8,1024]{1,0:T(8,128)(2,1)S(1)}, u32[]{:S(2)}, u32[]{:S(2)}) collective-permute-start(bf16[8,1024]{1,0:T(8,128)(2,1)S(1)} %pad_maximum_fusion.refs_0_), channel_id=1, source_target_pairs={{0,13},{1,12},{4,0},{5,1},{8,4},{9,5},{12,9},{13,8},{2,15},{3,14},... | collective-permute-start | bytes 49160 | tf_op jit(solution)/shard_map/ppermute | solution.py:247
  14.2 1.5 %collective-permute-start.6 = (f32[4,512]{1,0:T(4,128)S(1)}, f32[4,512]{1,0:T(4,128)S(1)}, u32[]{:S(2)}, u32[]{:S(2)}) collective-permute-start(f32[4,512]{1,0:T(4,128)S(1)} %fusion), channel_id=1, source_target_pairs={{0,1},{1,0},{4,5},{5,4},{8,9},{9,8},{12,13},{13,12},{2,3},{3,2},{6... | collective-permute-start | bytes 24584 | tf_op jit(solution)/shard_map/ppermute | solution.py:250
  14.9 1.4 %collective-permute-start.5 = (bf16[8,1024]{1,0:T(8,128)(2,1)S(1)}, bf16[8,1024]{1,0:T(8,128)(2,1)S(1)}, u32[]{:S(2)}, u32[]{:S(2)}) collective-permute-start(bf16[8,1024]{1,0:T(8,128)(2,1)S(1)} %collective-permute-done.4.refs_2_), channel_id=1, source_target_pairs={{0,1},{1,0},{4,5},{5,4},{8,9},{9,8},{12,13},{13,12},{2,3},{3,2},{6... | collective-permute-start | bytes 49160 | tf_op jit(solution)/shard_map/ppermute | solution.py:248

commit v20 on v17

--- a/solution.py
+++ b/solution.py
@@ -30,7 +30,7 @@
     rows, width = hidden.shape
     k_in = pin.shape[0]
     small = first_chunk(width)
-    half = (width - small) // 2
+    third = (width - small) // 3
 
     def copies_of(n):
         if isinstance(n, int) and n == 0:
@@ -38,7 +38,7 @@
         elif isinstance(n, int) and n == 1:
             return [pltpu.make_async_copy(proj_out, pout, sems.at[0, 1]), pltpu.make_async_copy(out_grad, og, sems.at[1, 1])]
         else:
-            lanes = pl.ds(small + (n - 2) * half, half)
+            lanes = pl.ds(small + (n - 2) * third, third)
         return [
             pltpu.make_async_copy(proj_in.at[:, lanes], pin.at[:, lanes], sems.at[0, n]),
             pltpu.make_async_copy(hidden.at[:, lanes], hid.at[:, lanes], sems.at[1, n]),
@@ -53,13 +53,13 @@
                                          preferred_element_type=jnp.float32))
         return tree_sum(terms)
 
-    steps = range(0 if small else 1, 4)
+    steps = range(0 if small else 1, 5)
     for n in steps:
         for copy in copies_of(n):
             copy.start()
-    bounds = pltpu.make_async_copy(lengths, limits, sems.at[0, 4])
+    bounds = pltpu.make_async_copy(lengths, limits, sems.at[0, 5])
     bounds.start()
-    fetch = pltpu.make_async_copy(tests, near_tests, sems.at[1, 4])
+    fetch = pltpu.make_async_copy(tests, near_tests, sems.at[1, 5])
     fetch.start()
     total = jnp.zeros((k_in, rows), jnp.float32)
     if small:
@@ -73,9 +73,9 @@
     def step(n, total):
         for copy in copies_of(n):
             copy.wait()
-        return total + partial(pin, hid, small + (n - 2) * half, half)
-
-    total = lax.fori_loop(2, 4, step, total)
+        return total + partial(pin, hid, small + (n - 2) * third, third)
+
+    total = lax.fori_loop(2, 5, step, total)
     bounds.wait()
     slot = lax.broadcasted_iota(jnp.int32, (1, rows), 1)
     limit = jnp.zeros((1, rows), jnp.int32)
@@ -104,7 +104,7 @@
             pltpu.VMEM((k_in, width), jnp.bfloat16),
             pltpu.VMEM((k_out, narrow), jnp.bfloat16),
             pltpu.SMEM(lengths.shape, jnp.int32),
-            pltpu.SemaphoreType.DMA((2, 5)),
+            pltpu.SemaphoreType.DMA((2, 6)),
         ],
         compiler_params=pltpu.CompilerParams(vmem_limit_bytes=24 << 20),
         cost_estimate=pl.CostEstimate(

time: 17.3 us -> 17.5 us (1.012)
  no operation moved by 1% of the time
where the time goes in v20:
time: 17.5 us; the launch traced here: 17.3 us
  starting transfers between devices  9.14 us (52%)
  Pallas kernels  4.68 us (27%)
  waiting for transfers between devices  2.04 us (12%)
  matrix products  0.74 us (4%)
  between operations  0.67 us (4%)
    pallas_call x1, Pallas kernels, project(): pl.pallas_call(functools.partial(project_kernel, scales), out_shape=(jax....  3.4 us
    ppermute x1, starting transfers between devices, per_device(): far = lax.ppermute(sent, ('mp', 'sub'), [(0, 3), (1, 2), (2, 1), (3, 0)])  2.44 us
    ppermute x1, starting transfers between devices, per_device(): fetched = lax.ppermute(held, group, list(enumerate(SWAPPED_SEND)))  2.19 us
    ppermute x1, starting transfers between devices, per_device(): direct = lax.ppermute(held, group, list(enumerate(DIRECT_SEND)))  2.1 us
    ppermute x1, waiting for transfers between devices, per_device(): far = lax.ppermute(sent, ('mp', 'sub'), [(0, 3), (1, 2), (2, 1), (3, 0)])  1.1 us
    pallas_call x1, Pallas kernels, finish(): pl.pallas_call(functools.partial(finish_kernel, examples, len(pieces), le...  1.05 us
    ppermute x1, starting transfers between devices, per_device(): near = lax.ppermute(sent, 'sub', [(0, 1), (1, 0)])  0.67 us
    ppermute x1, starting transfers between devices, per_device(): raw = [own, lax.ppermute(for_other, group, swap)]  0.61 us
  transfers between devices with their start and end apart: 7, of which 4 were waited for; matrix products, arithmetic and copies ran while one was open for 4% of the time, Pallas kernels for 0%

profile of v20, /device:TPU:0, one launch (start us, length us, event | category | flops | bytes accessed | tf_op | source)
XLA Modules:
  0.0 17.3 jit_solution(7366602779036378805)
XLA Ops:
  0.6 3.4 %shard_map.77 = (f32[64,256]{1,0:T(8,128)S(1)}, bf16[512,1024]{1,0:T(8,128)(2,1)S(1)}) custom-call(bf16[256,7168]{1,0:T(8,128)(2,1)} %hidden.1, bf16[256,2048]{1,0:T(8,128)(2,1)} %out_grad.1, s32[4]{0:T(128)} %lengths.1, bf16[32,7168]{1,0:T(8,128)(2,1)} %bitcast.6, bf16[32,2048]{1,0:T(8,128)(2,1)} %bitcast.7, bf16[512,1024]{1,0:T(8,128)(2,1)} %tests.1), custom_call_target="tpu_custom_call" | custom-call | flops 150994944 | bytes 5308416 | tf_op jit(solution)/shard_map/pallas_call | solution.py:93
  4.1 2.4 %collective-permute-start.1 = (f16[64,256]{1,0:T(8,128)(2,1)S(1)}, f16[64,256]{1,0:T(8,128)(2,1)S(1)}, u32[]{:S(2)}, u32[]{:S(2)}) collective-permute-start(f16[64,256]{1,0:T(8,128)(2,1)S(1)} %convert_element_type.9), channel_id=1, source_target_pairs={{0,3},{1,2},{2,1},{3,0},{4,7},{5,6},{6,5},{7,4},{8,11},{9,10},{10,... | collective-permute-start | bytes 98312 | tf_op jit(solution)/shard_map/ppermute | solution.py:234
  6.5 0.7 %collective-permute-start = (f16[64,256]{1,0:T(8,128)(2,1)S(1)}, f16[64,256]{1,0:T(8,128)(2,1)S(1)}, u32[]{:S(2)}, u32[]{:S(2)}) collective-permute-start(f16[64,256]{1,0:T(8,128)(2,1)S(1)} %convert_element_type.9), channel_id=1, source_target_pairs={{0,1},{1,0},{2,3},{3,2},{4,5},{5,4},{6,7},{7,6},{8,9},{9,8},{10,11... | collective-permute-start | bytes 98312 | tf_op jit(solution)/shard_map/ppermute | solution.py:235
  7.2 1.1 %collective-permute-done.1 = f16[64,256]{1,0:T(8,128)(2,1)S(1)} collective-permute-done((f16[64,256]{1,0:T(8,128)(2,1)S(1)}, f16[64,256]{1,0:T(8,128)(2,1)S(1)}, u32[]{:S(2)}, u32[]{:S(2)}) %collective-permute-start.1) | collective-permute-done | bytes 32800 | tf_op jit(solution)/shard_map/ppermute | solution.py:234
  8.3 0.0 collective-permute-done
  8.3 0.2 %shard_map.78 = bf16[4,1024]{1,0:T(4,128)(2,1)S(1)} custom-call(f32[64,256]{1,0:T(8,128)S(1)} %convert_element_type.10.refs_0_, f32[64,256]{1,0:T(8,128)S(1)} %convert_element_type.11.refs_1_), custom_call_target="tpu_custom_call" | custom-call | flops 8589934592 | tf_op jit(solution)/shard_map/pallas_call | solution.py:156
  8.5 0.6 %collective-permute-start.2 = (bf16[4,1024]{1,0:T(4,128)(2,1)S(1)}, bf16[4,1024]{1,0:T(4,128)(2,1)S(1)}, u32[]{:S(2)}, u32[]{:S(2)}) collective-permute-start(bf16[4,1024]{1,0:T(4,128)(2,1)S(1)} %shard_map.78), channel_id=1, source_target_pairs={{0,1},{1,0},{2,3},{3,2},{4,5},{5,4},{6,7},{7,6},{8,9},{9,8},{10,11... | collective-permute-start | bytes 24584 | tf_op jit(solution)/shard_map/ppermute | solution.py:237
  9.1 0.4 %fusion = f32[4,512]{1,0:T(4,128)S(1)} fusion(bf16[4,1024]{1,0:T(4,128)(2,1)S(1)} %shard_map.78, bf16[512,1024]{1,0:T(8,128)(2,1)S(1)} %get-tuple-element.7), kind=kOutput, calls=%fused_computation.1 | convolution fusion | flops 4194304 | bytes 1064960 | tf_op jit(solution)/shard_map/ep,qp->eq/dot_general | solution.py:243
  9.5 0.5 %collective-permute-done.2 = bf16[4,1024]{1,0:T(4,128)(2,1)S(1)} collective-permute-done((bf16[4,1024]{1,0:T(4,128)(2,1)S(1)}, bf16[4,1024]{1,0:T(4,128)(2,1)S(1)}, u32[]{:S(2)}, u32[]{:S(2)}) %collective-permute-start.2) | collective-permute-done | bytes 8224 | tf_op jit(solution)/shard_map/ppermute | solution.py:237
  9.9 2.2 %collective-permute-start.4 = (bf16[8,1024]{1,0:T(8,128)(2,1)S(1)}, bf16[8,1024]{1,0:T(8,128)(2,1)S(1)}, u32[]{:S(2)}, u32[]{:S(2)}) collective-permute-start(bf16[8,1024]{1,0:T(8,128)(2,1)S(1)} %pad_maximum_fusion.refs_0_), channel_id=1, source_target_pairs={{0,5},{1,9},{4,8},{5,13},{8,12},{9,0},{12,4},{13,1},{2,7},{3,11},{... | collective-permute-start | bytes 49160 | tf_op jit(solution)/shard_map/ppermute | solution.py:246
  12.1 2.1 %collective-permute-start.3 = (bf16[8,1024]{1,0:T(8,128)(2,1)S(1)}, bf16[8,1024]{1,0:T(8,128)(2,1)S(1)}, u32[]{:S(2)}, u32[]{:S(2)}) collective-permute-start(bf16[8,1024]{1,0:T(8,128)(2,1)S(1)} %pad_maximum_fusion.refs_0_), channel_id=1, source_target_pairs={{0,13},{1,12},{4,0},{5,1},{8,4},{9,5},{12,9},{13,8},{2,15},{3,14},... | collective-permute-start | bytes 49160 | tf_op jit(solution)/shard_map/ppermute | solution.py:247
  14.2 0.6 %collective-permute-start.6 = (f32[4,512]{1,0:T(4,128)S(1)}, f32[4,512]{1,0:T(4,128)S(1)}, u32[]{:S(2)}, u32[]{:S(2)}) collective-permute-start(f32[4,512]{1,0:T(4,128)S(1)} %fusion), channel_id=1, source_target_pairs={{0,1},{1,0},{4,5},{5,4},{8,9},{9,8},{12,13},{13,12},{2,3},{3,2},{6... | collective-permute-start | bytes 24584 | tf_op jit(solution)/shard_map/ppermute | solution.py:250
  14.8 0.0 collective-permute-done.4.refs_2_
  14.8 0.6 %collective-permute-start.5 = (bf16[8,1024]{1,0:T(8,128)(2,1)S(1)}, bf16[8,1024]{1,0:T(8,128)(2,1)S(1)}, u32[]{:S(2)}, u32[]{:S(2)}) collective-permute-start(bf16[8,1024]{1,0:T(8,128)(2,1)S(1)} %collective-permute-done.4.refs_2_), channel_id=1, source_target_pairs={{0,1},{1,0},{4,5},{5,4},{8,9},{9,8},{12,13},{13,12},{2,3},{3,2},{6... | collective-permute-start | bytes 49160 | tf_op jit(solution)/shard_map/ppermute | solution.py:248
  15.4 0.4 %fusion.1.refs_4_ = f32[4,512]{1,0:T(4,128)S(1)} fusion(bf16[4,1024]{1,0:T(4,128)(2,1)S(1)} %collective-permute-done.2, bf16[512,1024]{1,0:T(8,128)(2,1)S(1)} %get-tuple-element.7), kind=kOutput, calls=%fused_computation.2 | convolution fusion | flops 4194304 | bytes 1064960 | tf_op jit(solution)/shard_map/ep,qp->eq/dot_general | solution.py:249
  15.8 0.0 collective-permute-done.6.refs_5_
  15.8 0.1 collective-permute-done.3.refs_1_
  15.9 0.4 %collective-permute-done.5.refs_3_ = bf16[8,1024]{1,0:T(8,128)(2,1)S(1)} collective-permute-done((bf16[8,1024]{1,0:T(8,128)(2,1)S(1)}, bf16[8,1024]{1,0:T(8,128)(2,1)S(1)}, u32[]{:S(2)}, u32[]{:S(2)}) %collective-permute-start.5) | collective-permute-done | bytes 16416 | tf_op jit(solution)/shard_map/ppermute | solution.py:248
  16.3 1.1 %shard_map.79 = (f32[128,1024]{1,0:T(8,128)}, f32[4,1024]{1,0:T(4,128)}) custom-call(bf16[8,1024]{1,0:T(8,128)(2,1)S(1)} %pad_maximum_fusion.refs_0_, bf16[8,1024]{1,0:T(8,128)(2,1)S(1)} %collective-permute-done.3.refs_1_, bf16[8,1024]{1,0:T(8,128)(2,1)S(1)} %collective-permute-done.4.refs_2_, bf16[8,1024]{1,0:T(8,128)(2,1)S(1)} %collective-permute-done.5.refs_3_, ...), custom_call_target="tpu_custom_call" | custom-call | tf_op jit(solution)/shard_map/pallas_call | solution.py:213
  (4 shorter events, 0.0 us)
Async XLA Ops:
  4.1 4.2 %collective-permute-start.1 = (f16[64,256]{1,0:T(8,128)(2,1)S(1)}, f16[64,256]{1,0:T(8,128)(2,1)S(1)}, u32[]{:S(2)}, u32[]{:S(2)}) collective-permute-start(f16[64,256]{1,0:T(8,128)(2,1)S(1)} %convert_element_type.9), channel_id=1, source_target_pairs={{0,3},{1,2},{2,1},{3,0},{4,7},{5,6},{6,5},{7,4},{8,11},{9,10},{10,... | collective-permute-start | bytes 98312 | tf_op jit(solution)/shard_map/ppermute | solution.py:234
  6.5 1.8 %collective-permute-start = (f16[64,256]{1,0:T(8,128)(2,1)S(1)}, f16[64,256]{1,0:T(8,128)(2,1)S(1)}, u32[]{:S(2)}, u32[]{:S(2)}) collective-permute-start(f16[64,256]{1,0:T(8,128)(2,1)S(1)} %convert_element_type.9), channel_id=1, source_target_pairs={{0,1},{1,0},{2,3},{3,2},{4,5},{5,4},{6,7},{7,6},{8,9},{9,8},{10,11... | collective-permute-start | bytes 98312 | tf_op jit(solution)/shard_map/ppermute | solution.py:235
  8.5 1.4 %collective-permute-start.2 = (bf16[4,1024]{1,0:T(4,128)(2,1)S(1)}, bf16[4,1024]{1,0:T(4,128)(2,1)S(1)}, u32[]{:S(2)}, u32[]{:S(2)}) collective-permute-start(bf16[4,1024]{1,0:T(4,128)(2,1)S(1)} %shard_map.78), channel_id=1, source_target_pairs={{0,1},{1,0},{2,3},{3,2},{4,5},{5,4},{6,7},{7,6},{8,9},{9,8},{10,11... | collective-permute-start | bytes 24584 | tf_op jit(solution)/shard_map/ppermute | solution.py:237
  9.9 4.9 %collective-permute-start.4 = (bf16[8,1024]{1,0:T(8,128)(2,1)S(1)}, bf16[8,1024]{1,0:T(8,128)(2,1)S(1)}, u32[]{:S(2)}, u32[]{:S(2)}) collective-permute-start(bf16[8,1024]{1,0:T(8,128)(2,1)S(1)} %pad_maximum_fusion.refs_0_), channel_id=1, source_target_pairs={{0,5},{1,9},{4,8},{5,13},{8,12},{9,0},{12,4},{13,1},{2,7},{3,11},{... | collective-permute-start | bytes 49160 | tf_op jit(solution)/shard_map/ppermute | solution.py:246
  12.1 3.8 %collective-permute-start.3 = (bf16[8,1024]{1,0:T(8,128)(2,1)S(1)}, bf16[8,1024]{1,0:T(8,128)(2,1)S(1)}, u32[]{:S(2)}, u32[]{:S(2)}) collective-permute-start(bf16[8,1024]{1,0:T(8,128)(2,1)S(1)} %pad_maximum_fusion.refs_0_), channel_id=1, source_target_pairs={{0,13},{1,12},{4,0},{5,1},{8,4},{9,5},{12,9},{13,8},{2,15},{3,14},... | collective-permute-start | bytes 49160 | tf_op jit(solution)/shard_map/ppermute | solution.py:247
  14.2 1.5 %collective-permute-start.6 = (f32[4,512]{1,0:T(4,128)S(1)}, f32[4,512]{1,0:T(4,128)S(1)}, u32[]{:S(2)}, u32[]{:S(2)}) collective-permute-start(f32[4,512]{1,0:T(4,128)S(1)} %fusion), channel_id=1, source_target_pairs={{0,1},{1,0},{4,5},{5,4},{8,9},{9,8},{12,13},{13,12},{2,3},{3,2},{6... | collective-permute-start | bytes 24584 | tf_op jit(solution)/shard_map/ppermute | solution.py:250
  14.8 1.4 %collective-permute-start.5 = (bf16[8,1024]{1,0:T(8,128)(2,1)S(1)}, bf16[8,1024]{1,0:T(8,128)(2,1)S(1)}, u32[]{:S(2)}, u32[]{:S(2)}) collective-permute-start(bf16[8,1024]{1,0:T(8,128)(2,1)S(1)} %collective-permute-done.4.refs_2_), channel_id=1, source_target_pairs={{0,1},{1,0},{4,5},{5,4},{8,9},{9,8},{12,13},{13,12},{2,3},{3,2},{6... | collective-permute-start | bytes 49160 | tf_op jit(solution)/shard_map/ppermute | solution.py:248

commit v21 on v17

--- a/solution.py
+++ b/solution.py
@@ -8,7 +8,7 @@
 from jax.sharding import PartitionSpec as P
 
 SEQ = 64
-DEPTHS = (1024, 512, 256, 128)
+DEPTHS = (3072, 2048, 1536, 1024, 512, 256, 128)
 SWAPPED_SEND = (3, 5, 4, 7, 6, 0, 2, 1)
 DIRECT_SEND = (7, 6, 0, 1, 2, 3, 5, 4)
 CONTRACT_LAST = (((1,), (1,)), ((), ()))

time: 17.3 us -> 17.3 us (level)
  no operation moved by 1% of the time
where the time goes in v21:
time: 17.3 us; the launch traced here: 17.2 us
  starting transfers between devices  9.13 us (53%)
  Pallas kernels  4.54 us (26%)
  waiting for transfers between devices  2.04 us (12%)
  matrix products  0.74 us (4%)
  between operations  0.67 us (4%)
    pallas_call x1, Pallas kernels, project(): pl.pallas_call(functools.partial(project_kernel, scales), out_shape=(jax....  3.26 us
    ppermute x1, starting transfers between devices, per_device(): far = lax.ppermute(sent, ('mp', 'sub'), [(0, 3), (1, 2), (2, 1), (3, 0)])  2.44 us
    ppermute x1, starting transfers between devices, per_device(): fetched = lax.ppermute(held, group, list(enumerate(SWAPPED_SEND)))  2.18 us
    ppermute x1, starting transfers between devices, per_device(): direct = lax.ppermute(held, group, list(enumerate(DIRECT_SEND)))  2.1 us
    ppermute x1, waiting for transfers between devices, per_device(): far = lax.ppermute(sent, ('mp', 'sub'), [(0, 3), (1, 2), (2, 1), (3, 0)])  1.1 us
    pallas_call x1, Pallas kernels, finish(): pl.pallas_call(functools.partial(finish_kernel, examples, len(pieces), le...  1.05 us
    ppermute x1, starting transfers between devices, per_device(): near = lax.ppermute(sent, 'sub', [(0, 1), (1, 0)])  0.68 us
    ppermute x1, starting transfers between devices, per_device(): raw = [own, lax.ppermute(for_other, group, swap)]  0.61 us
  transfers between devices with their start and end apart: 7, of which 4 were waited for; matrix products, arithmetic and copies ran while one was open for 4% of the time, Pallas kernels for 0%

profile of v21, /device:TPU:0, one launch (start us, length us, event | category | flops | bytes accessed | tf_op | source)
XLA Modules:
  0.0 17.2 jit_solution(14272794751043839556)
XLA Ops:
  0.6 3.3 %shard_map.77 = (f32[64,256]{1,0:T(8,128)S(1)}, bf16[512,1024]{1,0:T(8,128)(2,1)S(1)}) custom-call(bf16[256,7168]{1,0:T(8,128)(2,1)} %hidden.1, bf16[256,2048]{1,0:T(8,128)(2,1)} %out_grad.1, s32[4]{0:T(128)} %lengths.1, bf16[32,7168]{1,0:T(8,128)(2,1)} %bitcast.6, bf16[32,2048]{1,0:T(8,128)(2,1)} %bitcast.7, bf16[512,1024]{1,0:T(8,128)(2,1)} %tests.1), custom_call_target="tpu_custom_call" | custom-call | flops 150994944 | bytes 5308416 | tf_op jit(solution)/shard_map/pallas_call | solution.py:93
  3.9 2.4 %collective-permute-start.1 = (f16[64,256]{1,0:T(8,128)(2,1)S(1)}, f16[64,256]{1,0:T(8,128)(2,1)S(1)}, u32[]{:S(2)}, u32[]{:S(2)}) collective-permute-start(f16[64,256]{1,0:T(8,128)(2,1)S(1)} %convert_element_type.9), channel_id=1, source_target_pairs={{0,3},{1,2},{2,1},{3,0},{4,7},{5,6},{6,5},{7,4},{8,11},{9,10},{10,... | collective-permute-start | bytes 98312 | tf_op jit(solution)/shard_map/ppermute | solution.py:234
  6.4 0.7 %collective-permute-start = (f16[64,256]{1,0:T(8,128)(2,1)S(1)}, f16[64,256]{1,0:T(8,128)(2,1)S(1)}, u32[]{:S(2)}, u32[]{:S(2)}) collective-permute-start(f16[64,256]{1,0:T(8,128)(2,1)S(1)} %convert_element_type.9), channel_id=1, source_target_pairs={{0,1},{1,0},{2,3},{3,2},{4,5},{5,4},{6,7},{7,6},{8,9},{9,8},{10,11... | collective-permute-start | bytes 98312 | tf_op jit(solution)/shard_map/ppermute | solution.py:235
  7.0 1.1 %collective-permute-done.1 = f16[64,256]{1,0:T(8,128)(2,1)S(1)} collective-permute-done((f16[64,256]{1,0:T(8,128)(2,1)S(1)}, f16[64,256]{1,0:T(8,128)(2,1)S(1)}, u32[]{:S(2)}, u32[]{:S(2)}) %collective-permute-start.1) | collective-permute-done | bytes 32800 | tf_op jit(solution)/shard_map/ppermute | solution.py:234
  8.2 0.0 collective-permute-done
  8.2 0.2 %shard_map.78 = bf16[4,1024]{1,0:T(4,128)(2,1)S(1)} custom-call(f32[64,256]{1,0:T(8,128)S(1)} %convert_element_type.10.refs_0_, f32[64,256]{1,0:T(8,128)S(1)} %convert_element_type.11.refs_1_), custom_call_target="tpu_custom_call" | custom-call | flops 8589934592 | tf_op jit(solution)/shard_map/pallas_call | solution.py:156
  8.4 0.6 %collective-permute-start.2 = (bf16[4,1024]{1,0:T(4,128)(2,1)S(1)}, bf16[4,1024]{1,0:T(4,128)(2,1)S(1)}, u32[]{:S(2)}, u32[]{:S(2)}) collective-permute-start(bf16[4,1024]{1,0:T(4,128)(2,1)S(1)} %shard_map.78), channel_id=1, source_target_pairs={{0,1},{1,0},{2,3},{3,2},{4,5},{5,4},{6,7},{7,6},{8,9},{9,8},{10,11... | collective-permute-start | bytes 24584 | tf_op jit(solution)/shard_map/ppermute | solution.py:237
  9.0 0.4 %fusion = f32[4,512]{1,0:T(4,128)S(1)} fusion(bf16[4,1024]{1,0:T(4,128)(2,1)S(1)} %shard_map.78, bf16[512,1024]{1,0:T(8,128)(2,1)S(1)} %get-tuple-element.7), kind=kOutput, calls=%fused_computation.1 | convolution fusion | flops 4194304 | bytes 1064960 | tf_op jit(solution)/shard_map/ep,qp->eq/dot_general | solution.py:243
  9.3 0.5 %collective-permute-done.2 = bf16[4,1024]{1,0:T(4,128)(2,1)S(1)} collective-permute-done((bf16[4,1024]{1,0:T(4,128)(2,1)S(1)}, bf16[4,1024]{1,0:T(4,128)(2,1)S(1)}, u32[]{:S(2)}, u32[]{:S(2)}) %collective-permute-start.2) | collective-permute-done | bytes 8224 | tf_op jit(solution)/shard_map/ppermute | solution.py:237
  9.8 2.2 %collective-permute-start.4 = (bf16[8,1024]{1,0:T(8,128)(2,1)S(1)}, bf16[8,1024]{1,0:T(8,128)(2,1)S(1)}, u32[]{:S(2)}, u32[]{:S(2)}) collective-permute-start(bf16[8,1024]{1,0:T(8,128)(2,1)S(1)} %pad_maximum_fusion.refs_0_), channel_id=1, source_target_pairs={{0,5},{1,9},{4,8},{5,13},{8,12},{9,0},{12,4},{13,1},{2,7},{3,11},{... | collective-permute-start | bytes 49160 | tf_op jit(solution)/shard_map/ppermute | solution.py:246
  12.0 2.1 %collective-permute-start.3 = (bf16[8,1024]{1,0:T(8,128)(2,1)S(1)}, bf16[8,1024]{1,0:T(8,128)(2,1)S(1)}, u32[]{:S(2)}, u32[]{:S(2)}) collective-permute-start(bf16[8,1024]{1,0:T(8,128)(2,1)S(1)} %pad_maximum_fusion.refs_0_), channel_id=1, source_target_pairs={{0,13},{1,12},{4,0},{5,1},{8,4},{9,5},{12,9},{13,8},{2,15},{3,14},... | collective-permute-start | bytes 49160 | tf_op jit(solution)/shard_map/ppermute | solution.py:247
  14.1 0.6 %collective-permute-start.6 = (f32[4,512]{1,0:T(4,128)S(1)}, f32[4,512]{1,0:T(4,128)S(1)}, u32[]{:S(2)}, u32[]{:S(2)}) collective-permute-start(f32[4,512]{1,0:T(4,128)S(1)} %fusion), channel_id=1, source_target_pairs={{0,1},{1,0},{4,5},{5,4},{8,9},{9,8},{12,13},{13,12},{2,3},{3,2},{6... | collective-permute-start | bytes 24584 | tf_op jit(solution)/shard_map/ppermute | solution.py:250
  14.7 0.0 collective-permute-done.4.refs_2_
  14.7 0.6 %collective-permute-start.5 = (bf16[8,1024]{1,0:T(8,128)(2,1)S(1)}, bf16[8,1024]{1,0:T(8,128)(2,1)S(1)}, u32[]{:S(2)}, u32[]{:S(2)}) collective-permute-start(bf16[8,1024]{1,0:T(8,128)(2,1)S(1)} %collective-permute-done.4.refs_2_), channel_id=1, source_target_pairs={{0,1},{1,0},{4,5},{5,4},{8,9},{9,8},{12,13},{13,12},{2,3},{3,2},{6... | collective-permute-start | bytes 49160 | tf_op jit(solution)/shard_map/ppermute | solution.py:248
  15.3 0.4 %fusion.1.refs_4_ = f32[4,512]{1,0:T(4,128)S(1)} fusion(bf16[4,1024]{1,0:T(4,128)(2,1)S(1)} %collective-permute-done.2, bf16[512,1024]{1,0:T(8,128)(2,1)S(1)} %get-tuple-element.7), kind=kOutput, calls=%fused_computation.2 | convolution fusion | flops 4194304 | bytes 1064960 | tf_op jit(solution)/shard_map/ep,qp->eq/dot_general | solution.py:249
  15.6 0.0 collective-permute-done.6.refs_5_
  15.6 0.1 collective-permute-done.3.refs_1_
  15.7 0.4 %collective-permute-done.5.refs_3_ = bf16[8,1024]{1,0:T(8,128)(2,1)S(1)} collective-permute-done((bf16[8,1024]{1,0:T(8,128)(2,1)S(1)}, bf16[8,1024]{1,0:T(8,128)(2,1)S(1)}, u32[]{:S(2)}, u32[]{:S(2)}) %collective-permute-start.5) | collective-permute-done | bytes 16416 | tf_op jit(solution)/shard_map/ppermute | solution.py:248
  16.1 1.1 %shard_map.79 = (f32[128,1024]{1,0:T(8,128)}, f32[4,1024]{1,0:T(4,128)}) custom-call(bf16[8,1024]{1,0:T(8,128)(2,1)S(1)} %pad_maximum_fusion.refs_0_, bf16[8,1024]{1,0:T(8,128)(2,1)S(1)} %collective-permute-done.3.refs_1_, bf16[8,1024]{1,0:T(8,128)(2,1)S(1)} %collective-permute-done.4.refs_2_, bf16[8,1024]{1,0:T(8,128)(2,1)S(1)} %collective-permute-done.5.refs_3_, ...), custom_call_target="tpu_custom_call" | custom-call | tf_op jit(solution)/shard_map/pallas_call | solution.py:213
  (4 shorter events, 0.0 us)
Async XLA Ops:
  3.9 4.2 %collective-permute-start.1 = (f16[64,256]{1,0:T(8,128)(2,1)S(1)}, f16[64,256]{1,0:T(8,128)(2,1)S(1)}, u32[]{:S(2)}, u32[]{:S(2)}) collective-permute-start(f16[64,256]{1,0:T(8,128)(2,1)S(1)} %convert_element_type.9), channel_id=1, source_target_pairs={{0,3},{1,2},{2,1},{3,0},{4,7},{5,6},{6,5},{7,4},{8,11},{9,10},{10,... | collective-permute-start | bytes 98312 | tf_op jit(solution)/shard_map/ppermute | solution.py:234
  6.4 1.8 %collective-permute-start = (f16[64,256]{1,0:T(8,128)(2,1)S(1)}, f16[64,256]{1,0:T(8,128)(2,1)S(1)}, u32[]{:S(2)}, u32[]{:S(2)}) collective-permute-start(f16[64,256]{1,0:T(8,128)(2,1)S(1)} %convert_element_type.9), channel_id=1, source_target_pairs={{0,1},{1,0},{2,3},{3,2},{4,5},{5,4},{6,7},{7,6},{8,9},{9,8},{10,11... | collective-permute-start | bytes 98312 | tf_op jit(solution)/shard_map/ppermute | solution.py:235
  8.4 1.4 %collective-permute-start.2 = (bf16[4,1024]{1,0:T(4,128)(2,1)S(1)}, bf16[4,1024]{1,0:T(4,128)(2,1)S(1)}, u32[]{:S(2)}, u32[]{:S(2)}) collective-permute-start(bf16[4,1024]{1,0:T(4,128)(2,1)S(1)} %shard_map.78), channel_id=1, source_target_pairs={{0,1},{1,0},{2,3},{3,2},{4,5},{5,4},{6,7},{7,6},{8,9},{9,8},{10,11... | collective-permute-start | bytes 24584 | tf_op jit(solution)/shard_map/ppermute | solution.py:237
  9.8 4.9 %collective-permute-start.4 = (bf16[8,1024]{1,0:T(8,128)(2,1)S(1)}, bf16[8,1024]{1,0:T(8,128)(2,1)S(1)}, u32[]{:S(2)}, u32[]{:S(2)}) collective-permute-start(bf16[8,1024]{1,0:T(8,128)(2,1)S(1)} %pad_maximum_fusion.refs_0_), channel_id=1, source_target_pairs={{0,5},{1,9},{4,8},{5,13},{8,12},{9,0},{12,4},{13,1},{2,7},{3,11},{... | collective-permute-start | bytes 49160 | tf_op jit(solution)/shard_map/ppermute | solution.py:246
  12.0 3.8 %collective-permute-start.3 = (bf16[8,1024]{1,0:T(8,128)(2,1)S(1)}, bf16[8,1024]{1,0:T(8,128)(2,1)S(1)}, u32[]{:S(2)}, u32[]{:S(2)}) collective-permute-start(bf16[8,1024]{1,0:T(8,128)(2,1)S(1)} %pad_maximum_fusion.refs_0_), channel_id=1, source_target_pairs={{0,13},{1,12},{4,0},{5,1},{8,4},{9,5},{12,9},{13,8},{2,15},{3,14},... | collective-permute-start | bytes 49160 | tf_op jit(solution)/shard_map/ppermute | solution.py:247
  14.1 1.5 %collective-permute-start.6 = (f32[4,512]{1,0:T(4,128)S(1)}, f32[4,512]{1,0:T(4,128)S(1)}, u32[]{:S(2)}, u32[]{:S(2)}) collective-permute-start(f32[4,512]{1,0:T(4,128)S(1)} %fusion), channel_id=1, source_target_pairs={{0,1},{1,0},{4,5},{5,4},{8,9},{9,8},{12,13},{13,12},{2,3},{3,2},{6... | collective-permute-start | bytes 24584 | tf_op jit(solution)/shard_map/ppermute | solution.py:250
  14.7 1.4 %collective-permute-start.5 = (bf16[8,1024]{1,0:T(8,128)(2,1)S(1)}, bf16[8,1024]{1,0:T(8,128)(2,1)S(1)}, u32[]{:S(2)}, u32[]{:S(2)}) collective-permute-start(bf16[8,1024]{1,0:T(8,128)(2,1)S(1)} %collective-permute-done.4.refs_2_), channel_id=1, source_target_pairs={{0,1},{1,0},{4,5},{5,4},{8,9},{9,8},{12,13},{13,12},{2,3},{3,2},{6... | collective-permute-start | bytes 49160 | tf_op jit(solution)/shard_map/ppermute | solution.py:248

commit v22 on v21

--- a/solution.py
+++ b/solution.py
@@ -233,7 +233,7 @@
         sent = lax.optimization_barrier(both.astype(jnp.float16))
         far = lax.ppermute(sent, ("mp", "sub"), [(0, 3), (1, 2), (2, 1), (3, 0)])
         near = lax.ppermute(sent, "sub", [(0, 1), (1, 0)])
-        made = example_grads([near.astype(jnp.float32), far.astype(jnp.float32)], k_in, k_out, scales)
+        made = example_grads([far.astype(jnp.float32), near.astype(jnp.float32)], k_in, k_out, scales)
         grads = lax.ppermute(made, "sub", [(0, 1), (1, 0)])
     else:
         grads = example_grads([lax.psum(both, "mp")], k_in, k_out, scales)

time: 17.3 us -> 17.3 us (level)
  waiting for transfers between devices: 2.04 us -> 2.82 us
  starting transfers between devices: 9.13 us -> 8.39 us
    ppermute x1, waiting for transfers between devices: 1.1 us -> 1.66 us  [per_device(): far = lax.ppermute(sent, ('mp', 'sub'), [(0, 3), (1, 2), (2, 1), (3, 0)])]
    ppermute x1, starting transfers between devices: 0.56 us -> 0.18 us  [per_device(): grads = lax.ppermute(made, 'sub', [(0, 1), (1, 0)])]
    ppermute x1, starting transfers between devices: 2.18 us -> 1.81 us  [per_device(): fetched = lax.ppermute(held, group, list(enumerate(SWAPPED_SEND)))]
    ppermute x1, waiting for transfers between devices: 0.46 us -> 0.69 us  [per_device(): grads = lax.ppermute(made, 'sub', [(0, 1), (1, 0)])]
    ppermute x1, starting transfers between devices: 0.61 us -> 0.43 us  [per_device(): raw = [own, lax.ppermute(for_other, group, swap)]]
    ppermute x1, starting transfers between devices: 0.56 us -> 0.74 us  [per_device(): gathered = [held, direct, fetched, lax.ppermute(fetched, group, swap)]]
where the time goes in v22:
time: 17.3 us; the launch traced here: 17.2 us
  starting transfers between devices  8.39 us (48%)
  Pallas kernels  4.54 us (26%)
  waiting for transfers between devices  2.82 us (16%)
  matrix products  0.74 us (4%)
  between operations  0.67 us (4%)
    pallas_call x1, Pallas kernels, project(): pl.pallas_call(functools.partial(project_kernel, scales), out_shape=(jax....  3.26 us
    ppermute x1, starting transfers between devices, per_device(): far = lax.ppermute(sent, ('mp', 'sub'), [(0, 3), (1, 2), (2, 1), (3, 0)])  2.61 us
    ppermute x1, starting transfers between devices, per_device(): direct = lax.ppermute(held, group, list(enumerate(DIRECT_SEND)))  2.1 us
    ppermute x1, starting transfers between devices, per_device(): fetched = lax.ppermute(held, group, list(enumerate(SWAPPED_SEND)))  1.81 us
    ppermute x1, waiting for transfers between devices, per_device(): far = lax.ppermute(sent, ('mp', 'sub'), [(0, 3), (1, 2), (2, 1), (3, 0)])  1.66 us
    pallas_call x1, Pallas kernels, finish(): pl.pallas_call(functools.partial(finish_kernel, examples, len(pieces), le...  1.05 us
    ppermute x1, starting transfers between devices, per_device(): gathered = [held, direct, fetched, lax.ppermute(fetched, group, swap)]  0.74 us
    ppermute x1, waiting for transfers between devices, per_device(): grads = lax.ppermute(made, 'sub', [(0, 1), (1, 0)])  0.69 us
  transfers between devices with their start and end apart: 7, of which 4 were waited for; matrix products, arithmetic and copies ran while one was open for 4% of the time, Pallas kernels for 0%

profile of v22, /device:TPU:0, one launch (start us, length us, event | category | flops | bytes accessed | tf_op | source)
XLA Modules:
  0.0 17.2 jit_solution(3493541174236864667)
XLA Ops:
  0.6 3.3 %shard_map.77 = (f32[64,256]{1,0:T(8,128)S(1)}, bf16[512,1024]{1,0:T(8,128)(2,1)S(1)}) custom-call(bf16[256,7168]{1,0:T(8,128)(2,1)} %hidden.1, bf16[256,2048]{1,0:T(8,128)(2,1)} %out_grad.1, s32[4]{0:T(128)} %lengths.1, bf16[32,7168]{1,0:T(8,128)(2,1)} %bitcast.6, bf16[32,2048]{1,0:T(8,128)(2,1)} %bitcast.7, bf16[512,1024]{1,0:T(8,128)(2,1)} %tests.1), custom_call_target="tpu_custom_call" | custom-call | flops 150994944 | bytes 5308416 | tf_op jit(solution)/shard_map/pallas_call | solution.py:93
  3.9 0.5 %collective-permute-start.1 = (f16[64,256]{1,0:T(8,128)(2,1)S(1)}, f16[64,256]{1,0:T(8,128)(2,1)S(1)}, u32[]{:S(2)}, u32[]{:S(2)}) collective-permute-start(f16[64,256]{1,0:T(8,128)(2,1)S(1)} %convert_element_type.9), channel_id=1, source_target_pairs={{0,1},{1,0},{2,3},{3,2},{4,5},{5,4},{6,7},{7,6},{8,9},{9,8},{10,11... | collective-permute-start | bytes 98312 | tf_op jit(solution)/shard_map/ppermute | solution.py:235
  4.4 2.6 %collective-permute-start = (f16[64,256]{1,0:T(8,128)(2,1)S(1)}, f16[64,256]{1,0:T(8,128)(2,1)S(1)}, u32[]{:S(2)}, u32[]{:S(2)}) collective-permute-start(f16[64,256]{1,0:T(8,128)(2,1)S(1)} %convert_element_type.9), channel_id=1, source_target_pairs={{0,3},{1,2},{2,1},{3,0},{4,7},{5,6},{6,5},{7,4},{8,11},{9,10},{10,... | collective-permute-start | bytes 98312 | tf_op jit(solution)/shard_map/ppermute | solution.py:234
  7.1 0.0 collective-permute-done.1
  7.1 1.7 %collective-permute-done = f16[64,256]{1,0:T(8,128)(2,1)S(1)} collective-permute-done((f16[64,256]{1,0:T(8,128)(2,1)S(1)}, f16[64,256]{1,0:T(8,128)(2,1)S(1)}, u32[]{:S(2)}, u32[]{:S(2)}) %collective-permute-start) | collective-permute-done | bytes 32800 | tf_op jit(solution)/shard_map/ppermute | solution.py:234
  8.7 0.2 %shard_map.78 = bf16[4,1024]{1,0:T(4,128)(2,1)S(1)} custom-call(f32[64,256]{1,0:T(8,128)S(1)} %convert_element_type.10.refs_0_, f32[64,256]{1,0:T(8,128)S(1)} %convert_element_type.11.refs_1_), custom_call_target="tpu_custom_call" | custom-call | flops 8589934592 | tf_op jit(solution)/shard_map/pallas_call | solution.py:156
  9.0 0.2 %collective-permute-start.2 = (bf16[4,1024]{1,0:T(4,128)(2,1)S(1)}, bf16[4,1024]{1,0:T(4,128)(2,1)S(1)}, u32[]{:S(2)}, u32[]{:S(2)}) collective-permute-start(bf16[4,1024]{1,0:T(4,128)(2,1)S(1)} %shard_map.78), channel_id=1, source_target_pairs={{0,1},{1,0},{2,3},{3,2},{4,5},{5,4},{6,7},{7,6},{8,9},{9,8},{10,11... | collective-permute-start | bytes 24584 | tf_op jit(solution)/shard_map/ppermute | solution.py:237
  9.1 0.4 %fusion = f32[4,512]{1,0:T(4,128)S(1)} fusion(bf16[4,1024]{1,0:T(4,128)(2,1)S(1)} %shard_map.78, bf16[512,1024]{1,0:T(8,128)(2,1)S(1)} %get-tuple-element.7), kind=kOutput, calls=%fused_computation.1 | convolution fusion | flops 4194304 | bytes 1064960 | tf_op jit(solution)/shard_map/ep,qp->eq/dot_general | solution.py:243
  9.5 0.7 %collective-permute-done.2 = bf16[4,1024]{1,0:T(4,128)(2,1)S(1)} collective-permute-done((bf16[4,1024]{1,0:T(4,128)(2,1)S(1)}, bf16[4,1024]{1,0:T(4,128)(2,1)S(1)}, u32[]{:S(2)}, u32[]{:S(2)}) %collective-permute-start.2) | collective-permute-done | bytes 8224 | tf_op jit(solution)/shard_map/ppermute | solution.py:237
  10.2 1.8 %collective-permute-start.4 = (bf16[8,1024]{1,0:T(8,128)(2,1)S(1)}, bf16[8,1024]{1,0:T(8,128)(2,1)S(1)}, u32[]{:S(2)}, u32[]{:S(2)}) collective-permute-start(bf16[8,1024]{1,0:T(8,128)(2,1)S(1)} %pad_maximum_fusion.refs_0_), channel_id=1, source_target_pairs={{0,5},{1,9},{4,8},{5,13},{8,12},{9,0},{12,4},{13,1},{2,7},{3,11},{... | collective-permute-start | bytes 49160 | tf_op jit(solution)/shard_map/ppermute | solution.py:246
  12.0 2.1 %collective-permute-start.3 = (bf16[8,1024]{1,0:T(8,128)(2,1)S(1)}, bf16[8,1024]{1,0:T(8,128)(2,1)S(1)}, u32[]{:S(2)}, u32[]{:S(2)}) collective-permute-start(bf16[8,1024]{1,0:T(8,128)(2,1)S(1)} %pad_maximum_fusion.refs_0_), channel_id=1, source_target_pairs={{0,13},{1,12},{4,0},{5,1},{8,4},{9,5},{12,9},{13,8},{2,15},{3,14},... | collective-permute-start | bytes 49160 | tf_op jit(solution)/shard_map/ppermute | solution.py:247
  14.1 0.4 %collective-permute-start.6 = (f32[4,512]{1,0:T(4,128)S(1)}, f32[4,512]{1,0:T(4,128)S(1)}, u32[]{:S(2)}, u32[]{:S(2)}) collective-permute-start(f32[4,512]{1,0:T(4,128)S(1)} %fusion), channel_id=1, source_target_pairs={{0,1},{1,0},{4,5},{5,4},{8,9},{9,8},{12,13},{13,12},{2,3},{3,2},{6... | collective-permute-start | bytes 24584 | tf_op jit(solution)/shard_map/ppermute | solution.py:250
  14.6 0.0 collective-permute-done.4.refs_2_
  14.6 0.7 %collective-permute-start.5 = (bf16[8,1024]{1,0:T(8,128)(2,1)S(1)}, bf16[8,1024]{1,0:T(8,128)(2,1)S(1)}, u32[]{:S(2)}, u32[]{:S(2)}) collective-permute-start(bf16[8,1024]{1,0:T(8,128)(2,1)S(1)} %collective-permute-done.4.refs_2_), channel_id=1, source_target_pairs={{0,1},{1,0},{4,5},{5,4},{8,9},{9,8},{12,13},{13,12},{2,3},{3,2},{6... | collective-permute-start | bytes 49160 | tf_op jit(solution)/shard_map/ppermute | solution.py:248
  15.3 0.4 %fusion.1.refs_4_ = f32[4,512]{1,0:T(4,128)S(1)} fusion(bf16[4,1024]{1,0:T(4,128)(2,1)S(1)} %collective-permute-done.2, bf16[512,1024]{1,0:T(8,128)(2,1)S(1)} %get-tuple-element.7), kind=kOutput, calls=%fused_computation.2 | convolution fusion | flops 4194304 | bytes 1064960 | tf_op jit(solution)/shard_map/ep,qp->eq/dot_general | solution.py:249
  15.7 0.0 collective-permute-done.6.refs_5_
  15.7 0.1 collective-permute-done.3.refs_1_
  15.8 0.4 %collective-permute-done.5.refs_3_ = bf16[8,1024]{1,0:T(8,128)(2,1)S(1)} collective-permute-done((bf16[8,1024]{1,0:T(8,128)(2,1)S(1)}, bf16[8,1024]{1,0:T(8,128)(2,1)S(1)}, u32[]{:S(2)}, u32[]{:S(2)}) %collective-permute-start.5) | collective-permute-done | bytes 16416 | tf_op jit(solution)/shard_map/ppermute | solution.py:248
  16.1 1.1 %shard_map.79 = (f32[128,1024]{1,0:T(8,128)}, f32[4,1024]{1,0:T(4,128)}) custom-call(bf16[8,1024]{1,0:T(8,128)(2,1)S(1)} %pad_maximum_fusion.refs_0_, bf16[8,1024]{1,0:T(8,128)(2,1)S(1)} %collective-permute-done.3.refs_1_, bf16[8,1024]{1,0:T(8,128)(2,1)S(1)} %collective-permute-done.4.refs_2_, bf16[8,1024]{1,0:T(8,128)(2,1)S(1)} %collective-permute-done.5.refs_3_, ...), custom_call_target="tpu_custom_call" | custom-call | tf_op jit(solution)/shard_map/pallas_call | solution.py:213
  (4 shorter events, 0.0 us)
Async XLA Ops:
  3.9 3.1 %collective-permute-start.1 = (f16[64,256]{1,0:T(8,128)(2,1)S(1)}, f16[64,256]{1,0:T(8,128)(2,1)S(1)}, u32[]{:S(2)}, u32[]{:S(2)}) collective-permute-start(f16[64,256]{1,0:T(8,128)(2,1)S(1)} %convert_element_type.9), channel_id=1, source_target_pairs={{0,1},{1,0},{2,3},{3,2},{4,5},{5,4},{6,7},{7,6},{8,9},{9,8},{10,11... | collective-permute-start | bytes 98312 | tf_op jit(solution)/shard_map/ppermute | solution.py:235
  4.4 4.3 %collective-permute-start = (f16[64,256]{1,0:T(8,128)(2,1)S(1)}, f16[64,256]{1,0:T(8,128)(2,1)S(1)}, u32[]{:S(2)}, u32[]{:S(2)}) collective-permute-start(f16[64,256]{1,0:T(8,128)(2,1)S(1)} %convert_element_type.9), channel_id=1, source_target_pairs={{0,3},{1,2},{2,1},{3,0},{4,7},{5,6},{6,5},{7,4},{8,11},{9,10},{10,... | collective-permute-start | bytes 98312 | tf_op jit(solution)/shard_map/ppermute | solution.py:234
  9.0 1.2 %collective-permute-start.2 = (bf16[4,1024]{1,0:T(4,128)(2,1)S(1)}, bf16[4,1024]{1,0:T(4,128)(2,1)S(1)}, u32[]{:S(2)}, u32[]{:S(2)}) collective-permute-start(bf16[4,1024]{1,0:T(4,128)(2,1)S(1)} %shard_map.78), channel_id=1, source_target_pairs={{0,1},{1,0},{2,3},{3,2},{4,5},{5,4},{6,7},{7,6},{8,9},{9,8},{10,11... | collective-permute-start | bytes 24584 | tf_op jit(solution)/shard_map/ppermute | solution.py:237
  10.2 4.3 %collective-permute-start.4 = (bf16[8,1024]{1,0:T(8,128)(2,1)S(1)}, bf16[8,1024]{1,0:T(8,128)(2,1)S(1)}, u32[]{:S(2)}, u32[]{:S(2)}) collective-permute-start(bf16[8,1024]{1,0:T(8,128)(2,1)S(1)} %pad_maximum_fusion.refs_0_), channel_id=1, source_target_pairs={{0,5},{1,9},{4,8},{5,13},{8,12},{9,0},{12,4},{13,1},{2,7},{3,11},{... | collective-permute-start | bytes 49160 | tf_op jit(solution)/shard_map/ppermute | solution.py:246
  12.0 3.8 %collective-permute-start.3 = (bf16[8,1024]{1,0:T(8,128)(2,1)S(1)}, bf16[8,1024]{1,0:T(8,128)(2,1)S(1)}, u32[]{:S(2)}, u32[]{:S(2)}) collective-permute-start(bf16[8,1024]{1,0:T(8,128)(2,1)S(1)} %pad_maximum_fusion.refs_0_), channel_id=1, source_target_pairs={{0,13},{1,12},{4,0},{5,1},{8,4},{9,5},{12,9},{13,8},{2,15},{3,14},... | collective-permute-start | bytes 49160 | tf_op jit(solution)/shard_map/ppermute | solution.py:247
  14.1 1.5 %collective-permute-start.6 = (f32[4,512]{1,0:T(4,128)S(1)}, f32[4,512]{1,0:T(4,128)S(1)}, u32[]{:S(2)}, u32[]{:S(2)}) collective-permute-start(f32[4,512]{1,0:T(4,128)S(1)} %fusion), channel_id=1, source_target_pairs={{0,1},{1,0},{4,5},{5,4},{8,9},{9,8},{12,13},{13,12},{2,3},{3,2},{6... | collective-permute-start | bytes 24584 | tf_op jit(solution)/shard_map/ppermute | solution.py:250
  14.6 1.6 %collective-permute-start.5 = (bf16[8,1024]{1,0:T(8,128)(2,1)S(1)}, bf16[8,1024]{1,0:T(8,128)(2,1)S(1)}, u32[]{:S(2)}, u32[]{:S(2)}) collective-permute-start(bf16[8,1024]{1,0:T(8,128)(2,1)S(1)} %collective-permute-done.4.refs_2_), channel_id=1, source_target_pairs={{0,1},{1,0},{4,5},{5,4},{8,9},{9,8},{12,13},{13,12},{2,3},{3,2},{6... | collective-permute-start | bytes 49160 | tf_op jit(solution)/shard_map/ppermute | solution.py:248
